TPU v7x, 32 devices: a whole 2x2x4 slice. The times are simulated.
32 devices in a mesh: ctx: 8 (over z, x), head: 4 (over y, core).
Axes of the slice: x: 2, y: 2, z: 4, core: 2. Of those that a mesh axis runs over, the one named last changes fastest.
Arguments:
- states: bfloat16 [4096, 2048], P(('ctx', 'head')), may hold values from -6 to 6
- shared_kv: bfloat16 [4096, 2048], P(('ctx', 'head')), may hold values from -6 to 6
- norm_gain: float32 [2048], replicated, may hold values from 0.25 to 1.75
- kv_gain: float32 [2048], replicated, may hold values from 0.25 to 1.75
- ffn_gain: float32 [2048], replicated, may hold values from 0.25 to 1.75
- query_weight: bfloat16 [2048, 2048], P(('ctx', 'head')), may hold values from -0.125 to 0.125
- key_weight: bfloat16 [2048, 2048], P(('ctx', 'head')), may hold values from -0.125 to 0.125
- value_weight: bfloat16 [2048, 2048], P(('ctx', 'head')), may hold values from -0.125 to 0.125
- out_weight: bfloat16 [2048, 2048], P(('ctx', 'head')), may hold values from -2 to 2
- gate_weight: bfloat16 [2048, 5504], P(None, ('ctx', 'head')), may hold values from -0.125 to 0.125
- up_weight: bfloat16 [2048, 5504], P(None, ('ctx', 'head')), may hold values from -0.125 to 0.125
- down_weight: bfloat16 [5504, 2048], P(('ctx', 'head')), may hold values from -0.078125 to 0.078125
- span_order: int32 [16], replicated, may hold values from 0 to 15, each once
- grad_output: bfloat16 [4096, 2048], P(('ctx', 'head')), may hold values from -6 to 6
Outputs:
- output: bfloat16 [4096, 2048], P(('ctx', 'head'))
- grad_states: bfloat16 [4096, 2048], P(('ctx', 'head'))
- grad_shared: bfloat16 [4096, 2048], P(('ctx', 'head'))
- grad_norm_gain: float32 [2048], P(('ctx', 'head'))
- grad_kv_gain: float32 [2048], P(('ctx', 'head'))
- grad_ffn_gain: float32 [2048], P(('ctx', 'head'))
- grad_query: float32 [2048, 2048], P('ctx', 'head')
- grad_key: float32 [2048, 2048], P('ctx', 'head')
- grad_value: float32 [2048, 2048], P('ctx', 'head')
- grad_out: float32 [2048, 2048], P('head', 'ctx')
- grad_gate: float32 [2048, 5504], P(None, ('ctx', 'head'))
- grad_up: float32 [2048, 5504], P(None, ('ctx', 'head'))
- grad_down: float32 [5504, 2048], P(('ctx', 'head'))
Inputs may be any that keep to these rules, and one draw needn't show every extreme that they name: A permutation: each number of 0 to 15 once; token rows r * 256 to r * 256 + 255 hold the positions from span_order[r] * 256 on.
All inputs are finite; a program needn't handle non-finite values.
Results may differ from a plain program's by a relative error of at most 0.02.
Values may be sent and summed in bfloat16 or wider, within the bound.
No kernel may reach another device: no remote copies, remote signals or barrier semaphores. Data moves between devices by JAX's collectives and lax.ppermute only.
A program may use at most 320 MiB of HBM per device.

v0:
```python
import jax
import jax.numpy as jnp
from jax import lax
from jax.sharding import PartitionSpec as P

HD = 128


EPSILON = 1e-06
MASKED = -1e30


def normalize(values, gain_vec):
    factor = lax.rsqrt(jnp.mean(values * values, axis=-1, keepdims=True) + EPSILON)
    plain_rows = values * factor
    return (plain_rows, factor, plain_rows * gain_vec)


def norm_backward(grad_normed, plain_rows, factor, gain_vec):
    scaled = grad_normed * gain_vec
    gain_part = jnp.sum(grad_normed * plain_rows, axis=0)
    grad_input = factor * (
        scaled - plain_rows * jnp.mean(scaled * plain_rows, axis=-1, keepdims=True)
    )
    return (gain_part, grad_input)


def matmul(left_side, right_side):
    return jnp.dot(left_side, right_side, preferred_element_type=jnp.float32)


def matmul_right_t(left_side, right_side):
    return lax.dot_general(
        left_side, right_side, (((1,), (1,)), ((), ())), preferred_element_type=jnp.float32
    )


def matmul_left_t(left_side, right_side):
    return lax.dot_general(
        left_side, right_side, (((0,), (0,)), ((), ())), preferred_element_type=jnp.float32
    )


def sort_spans(source_rows, order_list, span_rows):
    shaped = source_rows.reshape(-1, span_rows, source_rows.shape[1])
    return jnp.take(shaped, order_list, axis=0).reshape(source_rows.shape)


def arrange(span_order, rows_local):
    span_rows = rows_local // 2
    group_index = lax.axis_index("ctx")
    first_rank = span_order[2 * group_index]
    second_rank = span_order[2 * group_index + 1]
    local_rows = lax.iota(jnp.int32, rows_local)
    query_pos = jnp.where(
        local_rows < span_rows,
        first_rank * span_rows + local_rows,
        second_rank * span_rows + local_rows - span_rows,
    )
    rank_list = lax.iota(jnp.int32, span_order.shape[0])
    inverse = jnp.sum(
        jnp.where(span_order[None, :] == rank_list[:, None], rank_list[None, :], 0), axis=1
    )
    block_rows = 4 * span_rows
    blocks_used = (
        jnp.maximum(first_rank, second_rank) * span_rows + span_rows + block_rows - 1
    ) // block_rows
    return (query_pos, inverse, block_rows, blocks_used, span_rows)


def block_scores(query_split, key_sorted, row_start, query_pos, block_rows):
    heads_dev = query_split.shape[1]
    key_block = lax.dynamic_slice_in_dim(key_sorted, row_start, block_rows, 0).reshape(
        block_rows, heads_dev, HD
    )
    scores = jnp.einsum(
        "qhd,khd->hqk", query_split, key_block, preferred_element_type=jnp.float32
    ) * HD ** (-0.5)
    key_pos = row_start + lax.iota(jnp.int32, block_rows)
    visible = key_pos[None, None, :] <= query_pos[None, :, None]
    return (jnp.where(visible, scores, MASKED), key_block)


def value_slice(value_sorted, row_start, block_rows, heads_dev):
    return lax.dynamic_slice_in_dim(value_sorted, row_start, block_rows, 0).reshape(
        block_rows, heads_dev, HD
    )


def attention_forward(query_heads, key_sorted, value_sorted, query_pos, block_rows, blocks_used):
    rows_local, features = query_heads.shape
    heads_dev = features // HD
    query_split = query_heads.reshape(rows_local, heads_dev, HD)

    def max_step(block_index, running):
        running_max, running_sum = running
        scores, unused = block_scores(
            query_split, key_sorted, block_index * block_rows, query_pos, block_rows
        )
        new_max = jnp.maximum(running_max, jnp.max(scores, axis=-1))
        new_sum = running_sum * jnp.exp(running_max - new_max) + jnp.sum(
            jnp.exp(scores - new_max[:, :, None]), axis=-1
        )
        return (new_max, new_sum)

    start_max = jnp.full((heads_dev, rows_local), MASKED, jnp.float32)
    start_sum = jnp.zeros((heads_dev, rows_local), jnp.float32)
    final_max, final_sum = lax.fori_loop(0, blocks_used, max_step, (start_max, start_sum))
    log_total = final_max + jnp.log(final_sum)

    def mix_step(block_index, mixed_heads):
        row_start = block_index * block_rows
        scores, unused = block_scores(query_split, key_sorted, row_start, query_pos, block_rows)
        weights = jnp.exp(scores - log_total[:, :, None]).astype(jnp.bfloat16)
        value_block = value_slice(value_sorted, row_start, block_rows, heads_dev)
        return mixed_heads + jnp.einsum(
            "hqk,khd->qhd", weights, value_block, preferred_element_type=jnp.float32
        )

    mixed_heads = lax.fori_loop(
        0, blocks_used, mix_step, jnp.zeros((rows_local, heads_dev, HD), jnp.float32)
    )
    return (mixed_heads, log_total)


def row_statistic(grad_heads, mixed_heads):
    rows_local, heads_dev, unused = mixed_heads.shape
    grad_split = grad_heads.reshape(rows_local, heads_dev, HD)
    return jnp.transpose(jnp.sum(grad_split.astype(jnp.float32) * mixed_heads, axis=-1))


def attention_backward(
    query_heads,
    grad_heads,
    row_delta,
    log_total,
    key_sorted,
    value_sorted,
    query_pos,
    block_rows,
    blocks_used,
):
    rows_local, features = query_heads.shape
    heads_dev = features // HD
    score_scale = HD ** (-0.5)
    query_split = query_heads.reshape(rows_local, heads_dev, HD)
    grad_split = grad_heads.reshape(rows_local, heads_dev, HD)

    def grad_step(block_index, running):
        grad_query, grad_keys = running
        row_start = block_index * block_rows
        scores, key_block = block_scores(query_split, key_sorted, row_start, query_pos, block_rows)
        prob_full = jnp.exp(scores - log_total[:, :, None])
        value_block = value_slice(value_sorted, row_start, block_rows, heads_dev)
        grad_probs = jnp.einsum(
            "qhd,khd->hqk", grad_split, value_block, preferred_element_type=jnp.float32
        )
        grad_scores = (prob_full * (grad_probs - row_delta[:, :, None])).astype(jnp.bfloat16)
        grad_query = (
            grad_query
            + jnp.einsum("hqk,khd->qhd", grad_scores, key_block, preferred_element_type=jnp.float32)
            * score_scale
        )
        prob_low = prob_full.astype(jnp.bfloat16)
        grad_key_block = (
            jnp.einsum("hqk,qhd->khd", grad_scores, query_split, preferred_element_type=jnp.float32)
            * score_scale
        )
        grad_value_block = jnp.einsum(
            "hqk,qhd->khd", prob_low, grad_split, preferred_element_type=jnp.float32
        )
        update = jnp.concatenate(
            [
                grad_key_block.reshape(block_rows, features),
                grad_value_block.reshape(block_rows, features),
            ],
            axis=1,
        )
        grad_keys = lax.dynamic_update_slice_in_dim(grad_keys, update, row_start, 0)
        return (grad_query, grad_keys)

    start_query = jnp.zeros((rows_local, heads_dev, HD), jnp.float32)
    start_keys = jnp.zeros((key_sorted.shape[0], 2 * features), jnp.float32)
    grad_query, grad_keys = lax.fori_loop(0, blocks_used, grad_step, (start_query, start_keys))
    return (grad_query.reshape(rows_local, features), grad_keys)


def feed_forward(rows_in, rows_grad, weight_gate, weight_up, weight_down):
    gate_act = matmul(rows_in, weight_gate)
    up_act = matmul(rows_in, weight_up)
    sigmoid = jax.nn.sigmoid(gate_act)
    silu_act = gate_act * sigmoid
    hidden = (silu_act * up_act).astype(jnp.bfloat16)
    branch = matmul(hidden, weight_down)
    grad_hidden = matmul_right_t(rows_grad, weight_down)
    grad_gate = (grad_hidden * up_act * sigmoid * (1.0 + gate_act * (1.0 - sigmoid))).astype(
        jnp.bfloat16
    )
    grad_up = (grad_hidden * silu_act).astype(jnp.bfloat16)
    grad_input = matmul_right_t(grad_gate, weight_gate) + matmul_right_t(grad_up, weight_up)

    def unit_term(row_start, row_count):
        return jnp.concatenate(
            [
                matmul_left_t(grad_gate, rows_in),
                matmul_left_t(grad_up, rows_in),
                matmul_left_t(hidden, rows_grad),
            ],
            axis=1,
        )

    return (branch, grad_input, unit_term)


def per_device(
    states,
    shared_kv,
    norm_gain,
    kv_gain,
    ffn_gain,
    query_weight,
    key_weight,
    value_weight,
    out_weight,
    gate_weight,
    up_weight,
    down_weight,
    span_order,
    grad_output,
):
    width_model = query_weight.shape[1]
    state_rows = states.astype(jnp.float32)
    shared_rows = shared_kv.astype(jnp.float32)
    plain_one, factor_one, normed_one = normalize(state_rows, norm_gain)
    plain_kv, factor_kv, normed_kv = normalize(shared_rows, kv_gain)
    normed_low = normed_one.astype(jnp.bfloat16)
    shared_low = normed_kv.astype(jnp.bfloat16)
    full_query, full_key, full_value, full_out = (
        lax.all_gather(query_weight, ("ctx", "head"), axis=0, tiled=True),
        lax.all_gather(key_weight, ("ctx", "head"), axis=0, tiled=True),
        lax.all_gather(value_weight, ("ctx", "head"), axis=0, tiled=True),
        lax.all_gather(out_weight, ("ctx", "head"), axis=0, tiled=True),
    )
    queries = matmul(normed_low, full_query).astype(jnp.bfloat16)
    keys_tok = matmul(shared_low, full_key).astype(jnp.bfloat16)
    values_tok = matmul(shared_low, full_value).astype(jnp.bfloat16)
    query_heads, key_heads, value_heads = (
        lax.all_to_all(queries, "head", split_axis=1, concat_axis=0, tiled=True),
        lax.all_to_all(keys_tok, "head", split_axis=1, concat_axis=0, tiled=True),
        lax.all_to_all(values_tok, "head", split_axis=1, concat_axis=0, tiled=True),
    )
    key_all, value_all = (
        lax.all_gather(key_heads, "ctx", axis=0, tiled=True),
        lax.all_gather(value_heads, "ctx", axis=0, tiled=True),
    )
    rows_local, features = query_heads.shape
    query_pos, inverse, block_rows, blocks_used, span_rows = arrange(span_order, rows_local)
    key_sorted = sort_spans(key_all, inverse, span_rows)
    value_sorted = sort_spans(value_all, inverse, span_rows)
    mixed_heads, log_total = attention_forward(
        query_heads, key_sorted, value_sorted, query_pos, block_rows, blocks_used
    )
    attended_heads = mixed_heads.reshape(rows_local, features).astype(jnp.bfloat16)
    attended = lax.all_to_all(attended_heads, "head", split_axis=0, concat_axis=1, tiled=True)
    residual = state_rows + matmul(attended, full_out)
    plain_two, factor_two, normed_two = normalize(residual, ffn_gain)
    ffn_low = normed_two.astype(jnp.bfloat16)
    part_gate, part_up, part_down = (
        lax.all_gather(gate_weight, "ctx", axis=1, tiled=True),
        lax.all_gather(up_weight, "ctx", axis=1, tiled=True),
        lax.all_gather(down_weight, "ctx", axis=0, tiled=True),
    )
    group_in, group_grad, group_normed, group_shared = (
        lax.all_gather(ffn_low, "head", axis=0, tiled=True),
        lax.all_gather(grad_output, "head", axis=0, tiled=True),
        lax.all_gather(normed_low, "head", axis=0, tiled=True),
        lax.all_gather(shared_low, "head", axis=0, tiled=True),
    )
    partial_out, partial_grad, unit_term = feed_forward(
        group_in, group_grad, part_gate, part_up, part_down
    )
    branch, grad_ffn = (
        lax.psum_scatter(
            partial_out.astype(jnp.bfloat16), "head", scatter_dimension=0, tiled=True
        ).astype(jnp.float32),
        lax.psum_scatter(
            partial_grad.astype(jnp.bfloat16), "head", scatter_dimension=0, tiled=True
        ).astype(jnp.float32),
    )
    ffn_grads = lax.psum_scatter(
        unit_term(jnp.int32(0), gate_weight.shape[1] * lax.axis_size("ctx")).astype(jnp.bfloat16),
        "ctx",
        scatter_dimension=0,
        tiled=True,
    ).astype(jnp.float32)
    output = (residual + branch).astype(jnp.bfloat16)
    grad_rows = grad_output.astype(jnp.float32)
    gain_two, grad_norm_two = norm_backward(grad_ffn, plain_two, factor_two, ffn_gain)
    grad_residual = grad_rows + grad_norm_two
    grad_branch = grad_residual.astype(jnp.bfloat16)
    grad_attended = matmul_right_t(grad_branch, full_out).astype(jnp.bfloat16)
    grad_heads = lax.all_to_all(grad_attended, "head", split_axis=1, concat_axis=0, tiled=True)
    group_branch = lax.all_gather(grad_branch, "head", axis=0, tiled=True)
    row_delta = row_statistic(grad_heads, mixed_heads)
    grad_query_heads, grad_keys_sorted = attention_backward(
        query_heads,
        grad_heads,
        row_delta,
        log_total,
        key_sorted,
        value_sorted,
        query_pos,
        block_rows,
        blocks_used,
    )
    grad_keys_rows = sort_spans(grad_keys_sorted, span_order, span_rows)
    summed = lax.psum_scatter(
        grad_keys_rows.astype(jnp.bfloat16), "ctx", scatter_dimension=0, tiled=True
    ).astype(jnp.float32)
    grad_k_low = summed[:, :features].astype(jnp.bfloat16)
    grad_v_low = summed[:, features:].astype(jnp.bfloat16)
    grad_q_low = grad_query_heads.astype(jnp.bfloat16)
    grad_q_tok, grad_k_tok, grad_v_tok = (
        lax.all_to_all(grad_q_low, "head", split_axis=0, concat_axis=1, tiled=True),
        lax.all_to_all(grad_k_low, "head", split_axis=0, concat_axis=1, tiled=True),
        lax.all_to_all(grad_v_low, "head", split_axis=0, concat_axis=1, tiled=True),
    )
    grad_normed = matmul_right_t(grad_q_tok, full_query)
    grad_shared_normed = matmul_right_t(grad_k_tok, full_key) + matmul_right_t(
        grad_v_tok, full_value
    )
    gain_one, grad_in_one = norm_backward(grad_normed, plain_one, factor_one, norm_gain)
    gain_kv, grad_in_kv = norm_backward(grad_shared_normed, plain_kv, factor_kv, kv_gain)
    grad_states = (grad_residual + grad_in_one).astype(jnp.bfloat16)
    grad_shared = grad_in_kv.astype(jnp.bfloat16)
    attn_grads = lax.psum_scatter(
        jnp.concatenate(
            [
                matmul_left_t(group_normed, grad_q_low),
                matmul_left_t(group_shared, grad_k_low),
                matmul_left_t(group_shared, grad_v_low),
                matmul_left_t(group_branch, attended_heads),
            ],
            axis=1,
        ).astype(jnp.bfloat16),
        "ctx",
        scatter_dimension=0,
        tiled=True,
    ).astype(jnp.float32)
    gain_stack = jnp.stack([gain_one, gain_kv, gain_two])
    gain_sums = lax.psum_scatter(gain_stack, ("ctx", "head"), scatter_dimension=1, tiled=True)
    grad_query = attn_grads[:, 0:features]
    grad_key = attn_grads[:, features : 2 * features]
    grad_value = attn_grads[:, 2 * features : 3 * features]
    grad_out = jnp.transpose(attn_grads[:, 3 * features : 4 * features])
    grad_gate = jnp.transpose(ffn_grads[:, 0:width_model])
    grad_up = jnp.transpose(ffn_grads[:, width_model : 2 * width_model])
    grad_down = ffn_grads[:, 2 * width_model : 3 * width_model]
    return (
        output,
        grad_states,
        grad_shared,
        gain_sums[0],
        gain_sums[1],
        gain_sums[2],
        grad_query,
        grad_key,
        grad_value,
        grad_out,
        grad_gate,
        grad_up,
        grad_down,
    )


def solution(mesh):
    in_specs = (
        P(("ctx", "head"), None),
        P(("ctx", "head"), None),
        P(),
        P(),
        P(),
        P(("ctx", "head"), None),
        P(("ctx", "head"), None),
        P(("ctx", "head"), None),
        P(("ctx", "head"), None),
        P(None, ("ctx", "head")),
        P(None, ("ctx", "head")),
        P(("ctx", "head"), None),
        P(),
        P(("ctx", "head"), None),
    )
    out_specs = (
        P(("ctx", "head"), None),
        P(("ctx", "head"), None),
        P(("ctx", "head"), None),
        P(("ctx", "head")),
        P(("ctx", "head")),
        P(("ctx", "head")),
        P("ctx", "head"),
        P("ctx", "head"),
        P("ctx", "head"),
        P("head", "ctx"),
        P(None, ("ctx", "head")),
        P(None, ("ctx", "head")),
        P(("ctx", "head"), None),
    )
    return jax.shard_map(
        per_device, mesh=mesh, in_specs=in_specs, out_specs=out_specs, check_vma=False
    )
```

profile of v0, /device:TPU:0, one launch (start us, length us, event | category | flops | bytes accessed | tf_op | source)
XLA Modules:
  0.0 1725.1 jit_solution(17552821238304764119)
XLA Ops:
  12.5 78.7 %all-gather.22.cloned.1.call-done = bf16[2048,2048]{1,0:T(8,128)(2,1)} async-done(((bf16[64,2048]{1,0:T(8,128)(2,1)}), bf16[2048,2048]{1,0:T(8,128)(2,1)}) %all-gather.22.cloned.1.call-update) | async-done | bytes 8388624 | tf_op jit(solution)/shard_map/all_gather | solution.py:240
  95.9 13.8 all_to_all.140
  109.7 61.8 %all-gather.18.cloned.1.call-done = bf16[2048,2048]{1,0:T(8,128)(2,1)} async-done(((bf16[64,2048]{1,0:T(8,128)(2,1)}), bf16[2048,2048]{1,0:T(8,128)(2,1)}) %all-gather.18.cloned.1.call-update) | async-done | bytes 8388624 | tf_op jit(solution)/shard_map/all_gather | solution.py:241
  176.3 13.9 all_to_all.141
  194.1 57.9 %all-gather.26.cloned.1.call-done = bf16[2048,2048]{1,0:T(8,128)(2,1)} async-done(((bf16[64,2048]{1,0:T(8,128)(2,1)}), bf16[2048,2048]{1,0:T(8,128)(2,1)}) %all-gather.26.cloned.1.call-update) | async-done | bytes 8388624 | tf_op jit(solution)/shard_map/all_gather | solution.py:239
  264.3 5.5 all-to-all-done.2
  270.0 56.0 %all-gather.24.cloned.1.call-done = bf16[4096,512]{1,0:T(8,128)(2,1)} async-done(((bf16[512,512]{1,0:T(8,128)(2,1)}), bf16[4096,512]{1,0:T(8,128)(2,1)}) %all-gather.24.cloned.1.call-update) | async-done | bytes 4194320 | tf_op jit(solution)/shard_map/all_gather | solution.py:253
  331.0 68.7 %all-gather.20.cloned.1.call-done = bf16[4096,512]{1,0:T(8,128)(2,1)} async-done(((bf16[512,512]{1,0:T(8,128)(2,1)}), bf16[4096,512]{1,0:T(8,128)(2,1)}) %all-gather.20.cloned.1.call-update) | async-done | bytes 4194320 | tf_op jit(solution)/shard_map/all_gather | solution.py:254
  404.6 7.6 broadcast_select_fusion
  412.2 6.4 copy.191
  418.6 10.8 while.37
  429.4 6.4 copy.190
  436.9 15.0 while.38
  439.3 5.3 fusion.165
  453.8 17.2 all_to_all.142
  471.2 12.3 all-gather.28.cloned.1.call-done
  490.3 86.3 %all-gather.40.cloned.1.call-done = bf16[8,172,2048]{2,1,0:T(8,128)(2,1)} async-done(((bf16[1,172,2048]{2,1,0:T(8,128)(2,1)}), bf16[8,172,2048]{2,1,0:T(8,128)(2,1)}) %all-gather.40.cloned.1.call-update) | async-done | bytes 5636112 | tf_op jit(solution)/shard_map/all_gather | solution.py:269
  576.5 5.9 reshape.310
  582.4 87.2 %all-gather.42.cloned.1.call-done = bf16[8,172,2048]{2,1,0:T(8,128)(2,1)} async-done(((bf16[1,172,2048]{2,1,0:T(8,128)(2,1)}), bf16[8,172,2048]{2,1,0:T(8,128)(2,1)}) %all-gather.42.cloned.1.call-update) | async-done | bytes 5636112 | tf_op jit(solution)/shard_map/all_gather | solution.py:270
  669.6 5.9 reshape.312
  675.5 87.2 %all-gather.44.cloned.1.call-done = bf16[8,172,2048]{2,1,0:T(8,128)(2,1)} async-done(((bf16[1,172,2048]{2,1,0:T(8,128)(2,1)}), bf16[8,172,2048]{2,1,0:T(8,128)(2,1)}) %all-gather.44.cloned.1.call-update) | async-done | bytes 5636112 | tf_op jit(solution)/shard_map/all_gather | solution.py:271
  762.6 5.9 reshape.314
  768.5 16.9 all-gather.30.cloned.1.call-done
  785.4 8.1 fusion.79
  793.5 7.7 fusion.78
  801.2 8.4 all-gather.32.cloned.1.call-done
  809.6 10.2 multiply_convert_fusion
  819.8 6.6 fusion.80
  826.4 16.9 add_convert_fusion
  844.1 30.8 %reduce-scatter.12.cloned.1.call-done = bf16[128,2048]{1,0:T(8,128)(2,1)} async-done(((bf16[512,2048]{1,0:T(8,128)(2,1)}), bf16[128,2048]{1,0:T(8,128)(2,1)}) %reduce-scatter.12.cloned.1.call-update) | async-done | bytes 524304 | tf_op jit(solution)/shard_map/reduce_scatter | solution.py:286
  878.4 6.5 convolution_convert_fusion.8
  890.5 13.3 all-to-all-done.4
  910.7 43.9 %while.39 = (s32[]{:T(128)}, f32[512,4,128]{0,2,1:T(8,128)S(1)}, bf16[4096,1024]{1,0:T(8,128)(2,1)}, s32[]{:T(128)}, bf16[4096,512]{0,1:T(8,128)(2,1)}, /*index=...) while((s32[]{:T(128)}, f32[512,4,128]{0,2,1:T(8,128)S(1)}, ...), condition=%wide.region_15.17_spmd.clone, body=%wide.region_14.16_spmd.clone.sunk | while | flops 2711621120 | bytes 65573076 | solution.py:184
  954.5 8.2 gather_fusion
  962.7 7.5 fusion.38
  971.6 7.2 convolution_convert_fusion.7
  992.7 169.3 %reduce-scatter.14.cloned.1.call-done = bf16[512,1024]{1,0:T(8,128)(2,1)} async-done(((bf16[4096,1024]{1,0:T(8,128)(2,1)}), bf16[512,1024]{1,0:T(8,128)(2,1)}) %reduce-scatter.14.cloned.1.call-update) | async-done | bytes 1048592 | tf_op jit(solution)/shard_map/reduce_scatter | solution.py:317
  1167.8 8.1 fusion.67
  1175.9 13.5 all-gather.38.cloned.1.call-done
  1197.6 20.1 %all-gather.36.cloned.1.call-done = bf16[512,2048]{1,0:T(8,128)(2,1)} async-done(((bf16[128,2048]{1,0:T(8,128)(2,1)}), bf16[512,2048]{1,0:T(8,128)(2,1)}) %all-gather.36.cloned.1.call-update) | async-done | bytes 2097168 | tf_op jit(solution)/shard_map/all_gather | solution.py:277
  1225.4 7.0 fusion.81
  1232.5 7.4 fusion.58
  1241.5 7.2 pad_maximum_fusion.2
  1248.7 5.3 convolution_convert_fusion
  1260.7 13.3 pad_maximum_fusion.1
  1274.0 403.3 %fusion.6 = bf16[176,6144]{1,0:T(8,128)(2,1)} fusion(bf16[1376,6144]{1,0:T(8,128)(2,1)} %pad_maximum_fusion.1), kind=kCustom, calls=%all-reduce-scatter | all-reduce-scatter fusion | flops 8650753 | bytes 19071488
  1680.9 6.8 collective-permute-done
  1687.7 13.8 concatenate.14
  (270 shorter events, 193.3 us)
Async XLA Ops:
  7.2 84.0 %all-gather.22.cloned.1.call-start = ((), (), s32[]{:S(2)}) async-start(), calls=%async_computation.15 | async-start | bytes 8650752 | tf_op jit(solution)/shard_map/all_gather | solution.py:240
  7.9 163.6 %all-gather.18.cloned.1.call-start = ((), (), s32[]{:S(2)}) async-start(), calls=%async_computation.13 | async-start | bytes 8650752 | tf_op jit(solution)/shard_map/all_gather | solution.py:241
  8.7 243.3 %all-gather.26.cloned.1.call-start = ((), (), s32[]{:S(2)}) async-start(), calls=%async_computation.17 | async-start | bytes 8650752 | tf_op jit(solution)/shard_map/all_gather | solution.py:239
  9.4 316.6 %all-gather.24.cloned.1.call-start = ((), (), s32[]{:S(2)}) async-start(), calls=%async_computation.16 | async-start | bytes 4718592 | tf_op jit(solution)/shard_map/all_gather | solution.py:253
  12.5 159.0 %copy-start.2 = (bf16[128,2048]{1,0:T(8,128)(2,1)}, bf16[128,2048]{1,0:T(8,128)(2,1)S(1)}, u32[]{:S(2)}) copy-start(bf16[128,2048]{1,0:T(8,128)(2,1)S(1)} %fusion.53) | copy-start | bytes 1572868
  109.7 290.0 %all-gather.20.cloned.1.call-start = ((), (), s32[]{:S(2)}) async-start(), calls=%async_computation.14 | async-start | bytes 4718592 | tf_op jit(solution)/shard_map/all_gather | solution.py:254
  176.2 16.9 copy-start.36
  176.2 17.0 copy-start.3
  176.2 17.7 %copy-start.25 = (f32[2048]{0:T(1024)S(1)}, f32[2048]{0:T(1024)}, u32[]{:S(2)}) copy-start(f32[2048]{0:T(1024)} %param.24) | copy-start | bytes 24580
  190.2 293.3 %all-gather.28.cloned.1.call-start = ((), (), s32[]{:S(2)}) async-start(), calls=%async_computation.18 | async-start | bytes 8650752 | tf_op jit(solution)/shard_map/all_gather | solution.py:242
  190.8 385.7 %all-gather.40.cloned.1.call-start = ((), (), s32[]{:S(2)}) async-start(), calls=%async_computation.28 | async-start | bytes 6488064 | tf_op jit(solution)/shard_map/all_gather | solution.py:269
  191.6 478.0 %all-gather.42.cloned.1.call-start = ((), (), s32[]{:S(2)}) async-start(), calls=%async_computation.29 | async-start | bytes 6488064 | tf_op jit(solution)/shard_map/all_gather | solution.py:270
  192.3 570.3 %all-gather.44.cloned.1.call-start = ((), (), s32[]{:S(2)}) async-start(), calls=%async_computation.30 | async-start | bytes 6488064 | tf_op jit(solution)/shard_map/all_gather | solution.py:271
  194.1 62.5 %copy-start.8 = (bf16[128,2048]{1,0:T(8,128)(2,1)}, bf16[128,2048]{1,0:T(8,128)(2,1)S(1)}, u32[]{:S(2)}) copy-start(bf16[128,2048]{1,0:T(8,128)(2,1)S(1)} %fusion.61) | copy-start | bytes 1572868
  257.5 12.3 all-to-all-start.2
  261.0 524.5 %all-gather.30.cloned.1.call-start = ((), (), s32[]{:S(2)}) async-start(), calls=%async_computation.19 | async-start | bytes 2621440 | tf_op jit(solution)/shard_map/all_gather | solution.py:274
  269.9 61.1 %copy-start.14 = (bf16[512,4,128]{2,1,0:T(4,128)(2,1)}, bf16[512,4,128]{2,1,0:T(4,128)(2,1)S(1)}, u32[]{:S(2)}) copy-start(bf16[512,4,128]{2,1,0:T(4,128)(2,1)S(1)} %reshape.279) | copy-start | bytes 1572868
  451.9 31.6 %copy-start.4 = (bf16[128,2048]{1,0:T(8,128)(2,1)S(1)}, bf16[128,2048]{1,0:T(8,128)(2,1)}, u32[]{:S(2)}) copy-start(bf16[128,2048]{1,0:T(8,128)(2,1)} %param.22) | copy-start | bytes 1572868
  453.3 30.2 %copy-start.19 = (bf16[512,4,128]{0,2,1:T(8,128)(2,1)}, bf16[512,4,128]{0,2,1:T(8,128)(2,1)S(1)}, u32[]{:S(2)}) copy-start(bf16[512,4,128]{0,2,1:T(8,128)(2,1)S(1)} %convert_element_type.116) | copy-start | bytes 1572868
  488.3 388.6 %copy-start = (f32[128,2048]{1,0:T(8,128)}, f32[128,2048]{1,0:T(8,128)S(1)}, u32[]{:S(2)}) copy-start(f32[128,2048]{1,0:T(8,128)S(1)} %get-tuple-element.528) | copy-start | bytes 3145732
  488.3 388.6 %copy-start.28 = (f32[128]{0:T(128)}, f32[128]{0:T(128)S(1)}, u32[]{:S(2)}) copy-start(f32[128]{0:T(128)S(1)} %add_rsqrt_fusion) | copy-start | bytes 1540
  489.5 320.1 %all-gather.32.cloned.1.call-start = ((), (), s32[]{:S(2)}) async-start(), calls=%async_computation.21 | async-start | bytes 2621440 | tf_op jit(solution)/shard_map/all_gather | solution.py:275
  490.2 384.7 %reduce-scatter.12.cloned.1.call-start = ((), (), s32[]{:S(2)}) async-start(), calls=%async_computation.22 | async-start | bytes 2621440 | tf_op jit(solution)/shard_map/reduce_scatter | solution.py:286
  785.4 8.1 copy-start.38
  843.3 33.6 %copy-start.10 = (bf16[128,2048]{1,0:T(8,128)(2,1)S(1)}, bf16[128,2048]{1,0:T(8,128)(2,1)}, u32[]{:S(2)}) copy-start(bf16[128,2048]{1,0:T(8,128)(2,1)} %param.35) | copy-start | bytes 1572868
  843.3 140.4 %all-gather.34.cloned.1.call-start = ((), (), s32[]{:S(2)}) async-start(), calls=%async_computation.24 | async-start | bytes 2621440 | tf_op jit(solution)/shard_map/all_gather | solution.py:276
  876.9 7.9 copy-start.34
  878.3 11.0 copy-start.15
  884.8 20.2 %copy-start.6 = (f32[512,4,128]{0,2,1:T(8,128)S(1)}, f32[512,4,128]{0,2,1:T(8,128)}, u32[]{:S(2)}) copy-start(f32[512,4,128]{0,2,1:T(8,128)} %get-tuple-element.157) | copy-start | bytes 3145732
  885.7 18.1 %all-to-all-start.4 = ((bf16[128,4,512]{2,0,1:T(8,128)(2,1)}), bf16[128,4,512]{2,0,1:T(8,128)(2,1)S(1)}, u32[]{:S(2)}, u32[]{:S(2)}) async-start(bf16[128,4,512]{2,0,1:T(8,128)(2,1)} %bitcast.180), calls=%async_computation.6 | async-start | bytes 1048576 | tf_op jit(solution)/shard_map/all_to_all | solution.py:302
  889.2 272.9 %reduce-scatter.14.cloned.1.call-start = ((), (), s32[]{:S(2)}) async-start(), calls=%async_computation.23 | async-start | bytes 9437184 | tf_op jit(solution)/shard_map/reduce_scatter | solution.py:317
  970.3 219.1 %all-gather.38.cloned.1.call-start = ((), (), s32[]{:S(2)}) async-start(), calls=%async_computation.26 | async-start | bytes 2621440 | tf_op jit(solution)/shard_map/all_gather | solution.py:303
  970.9 246.8 %all-gather.36.cloned.1.call-start = ((), (), s32[]{:S(2)}) async-start(), calls=%async_computation.25 | async-start | bytes 2621440 | tf_op jit(solution)/shard_map/all_gather | solution.py:277
  971.5 734.5 %reduce-scatter.10.cloned.1.call-start = ((), (), s32[]{:S(2)}) async-start(), calls=%async_computation.20 | async-start | bytes 2621440 | tf_op jit(solution)/shard_map/reduce_scatter | solution.py:283
  980.2 12.3 all-to-all-start.5
  987.9 179.9 %copy-start.5 = (bf16[128,2048]{1,0:T(8,128)(2,1)S(1)}, bf16[128,2048]{1,0:T(8,128)(2,1)}, u32[]{:S(2)}) copy-start(bf16[128,2048]{1,0:T(8,128)(2,1)} %param.22) | copy-start | bytes 1572868
  987.9 179.9 %copy-start.26 = (f32[2048]{0:T(1024)S(1)}, f32[2048]{0:T(1024)}, u32[]{:S(2)}) copy-start(f32[2048]{0:T(1024)} %param.24) | copy-start | bytes 24580
  987.9 179.9 %copy-start.31 = (f32[128]{0:T(128)S(1)}, f32[128]{0:T(128)}, u32[]{:S(2)}) copy-start(f32[128]{0:T(128)} %copy-done.30) | copy-start | bytes 1540
  1164.3 29.3 %all-to-all-start.6 = ((bf16[4,128,512]{2,1,0:T(8,128)(2,1)}), bf16[4,128,512]{2,1,0:T(8,128)(2,1)S(1)}, u32[]{:S(2)}, u32[]{:S(2)}) async-start(bf16[4,128,512]{2,1,0:T(8,128)(2,1)} %bitcast.25), calls=%async_computation.9 | async-start | bytes 1048576 | tf_op jit(solution)/shard_map/all_to_all | solution.py:325
  1167.8 21.5 %copy-start.20 = (bf16[512,4,128]{0,2,1:T(8,128)(2,1)S(1)}, bf16[512,4,128]{0,2,1:T(8,128)(2,1)}, u32[]{:S(2)}) copy-start(bf16[512,4,128]{0,2,1:T(8,128)(2,1)} %copy-done.19) | copy-start | bytes 1572868
  1189.4 28.3 %copy-start.21 = (bf16[512,1024]{1,0:T(8,128)(2,1)S(1)}, bf16[512,1024]{1,0:T(8,128)(2,1)}, u32[]{:S(2)}) copy-start(bf16[512,1024]{1,0:T(8,128)(2,1)} %reduce-scatter.14.cloned.1.call-done) | copy-start | bytes 3145732
  1193.6 31.5 %all-to-all-start.7 = ((bf16[4,128,512]{2,1,0:T(8,128)(2,1)}), bf16[4,128,512]{2,1,0:T(8,128)(2,1)S(1)}, u32[]{:S(2)}, u32[]{:S(2)}) async-start(bf16[4,128,512]{2,1,0:T(8,128)(2,1)} %bitcast.28), calls=%async_computation.10 | async-start | bytes 1048576 | tf_op jit(solution)/shard_map/all_to_all | solution.py:326
  1197.1 513.2 %reduce-scatter.18.cloned.1.call-start = ((), (), s32[]{:S(2)}) async-start(), calls=%async_computation.31 | async-start | bytes 1081344
  1225.4 7.1 copy-start.7
  1232.5 7.4 copy-start.27
  1241.3 471.8 %reduce-scatter.16.cloned.1.call-start = ((), (), s32[]{:S(2)}) async-start(), calls=%async_computation.27 | async-start | bytes 9437184 | tf_op jit(solution)/shard_map/reduce_scatter | solution.py:336
  1274.0 405.7 %copy-start.37 = (u32[32]{0:T(128)S(1)}, u32[32]{0:T(128)}, u32[]{:S(2)}) copy-start(u32[32]{0:T(128)} %constant.134) | copy-start | bytes 388
  1678.3 9.3 collective-permute-start
  (21 other events, 81.9 us)
Sparse Core Ops, SparseCore 0:
  10.9 80.2 all-gather.21
  94.0 77.4 all-gather.17
  174.4 77.5 all-gather.25
  254.0 71.9 all-gather.23
  327.9 71.6 all-gather.19
  402.4 81.1 all-gather.27
  485.7 90.7 all-gather.39
  578.7 90.8 all-gather.41
  671.8 90.8 all-gather.43
  764.6 20.7 all-gather.29
  787.0 22.5 all-gather.31
  843.4 31.4 reduce-scatter.11
  877.1 28.1 all-gather.33
  970.4 191.6 reduce-scatter.13
  1164.1 25.2 all-gather.37
  1191.3 26.2 all-gather.35
  1220.0 30.5 reduce-scatter.9
  1252.8 185.1 reduce-scatter.17
  1441.6 239.5 reduce-scatter.15
where the time goes:
time: 1740 us; the launch traced here: 1730 us
  waiting for transfers between devices  892 us (51%)
  blocking collectives  448 us (26%)
  matrix products  173 us (10%)
  local copies, waits for them, and re-layouts  111 us (6%)
  other arithmetic  61.2 us (4%)
  starting transfers between devices  20 us (1%)
  between operations  18.3 us (1%)
    unnamed x1, blocking collectives  403 us
    reduce_scatter x1, waiting for transfers between devices, per_device(): lax.psum_scatter(grad_keys_rows.astype(jnp.bfloat16), 'ctx', scatter_dime...  169 us
    all_gather x1, waiting for transfers between devices, per_device(): lax.all_gather(down_weight, 'ctx', axis=0, tiled=True)  87.2 us
    all_gather x1, waiting for transfers between devices, per_device(): lax.all_gather(up_weight, 'ctx', axis=1, tiled=True)  87.2 us
    all_gather x1, waiting for transfers between devices, per_device(): lax.all_gather(gate_weight, 'ctx', axis=1, tiled=True)  86.3 us
    all_gather x1, waiting for transfers between devices, per_device(): lax.all_gather(key_weight, ('ctx', 'head'), axis=0, tiled=True)  78.7 us
    all_gather x1, waiting for transfers between devices, per_device(): lax.all_gather(value_heads, 'ctx', axis=0, tiled=True)  68.7 us
    dot_general x7, matrix products, matmul_right_t(): lax.dot_general(left_side, right_side, (((1,), (1,)), ((), ())), preferre...  62.5 us
  transfers between devices with their start and end apart: 25, of which 19 were waited for; matrix products, arithmetic and copies ran while one was open for 41% of the time, Pallas kernels for 0%

commit v1 on v0

v1 whole, which is shorter than its diff:
```python
import math

import jax
import jax.numpy as jnp
from jax import lax
from jax.experimental import pallas as pl
from jax.experimental.pallas import tpu as pltpu
from jax.sharding import Mesh, PartitionSpec as P

HD = 128
EPSILON = 1e-06
LOW = jnp.bfloat16
HIGH = jnp.float32
LOG2E = math.log2(math.e)
SCORE_SCALE = HD ** (-0.5)
ALL = ("z", "x", "y", "c")


def hop(values, axis, steps=1):
    size = lax.axis_size(axis)
    return lax.ppermute(values, axis, [(i, (i + steps) % size) for i in range(size)])


def gather_x_first(piece):
    pieces = []
    for step in range(lax.axis_size("x")):
        if step:
            piece = hop(piece, "x")
        pieces += [piece, hop(piece, "y")]
    return pieces


def gather_y_first(piece):
    other = hop(piece, "y")
    pieces = []
    for step in range(lax.axis_size("x")):
        if step:
            piece, other = hop(piece, "x"), hop(other, "x")
        pieces += [piece, other]
    return pieces


def add_low(first, second):
    return (first.astype(HIGH) + second.astype(HIGH)).astype(LOW)


def ring_sum(parts, axis):
    size = len(parts)
    total = parts[1 % size]
    for step in range(1, size):
        total = add_low(parts[(step + 1) % size], hop(total, axis))
    return total


def sum_y_first(parts):
    size = lax.axis_size("x")
    merged = [add_low(parts[2 * s], hop(parts[2 * s + 1], "y")) for s in range(size)]
    return ring_sum(merged, "x")


def sum_x_first(parts):
    size = lax.axis_size("x")
    near = ring_sum([parts[2 * s] for s in range(size)], "x")
    far = ring_sum([parts[2 * s + 1] for s in range(size)], "x")
    return add_low(near, hop(far, "y"))


def gather_rows(rows):
    blocks = []
    for step in range(lax.axis_size("z")):
        if step:
            rows = hop(rows, "z")
        blocks += [rows, hop(rows, "c")]
    return jnp.concatenate(blocks, axis=0)


def sum_rows(partial_of, rows_local):
    size = lax.axis_size("z")
    total = None
    for step in range(1, size + 1):
        block = partial_of(step % size)
        mine = block[:rows_local] + hop(block[rows_local:].astype(LOW), "c").astype(HIGH)
        if total is None:
            total = mine.astype(LOW)
        else:
            total = mine + hop(total, "z").astype(HIGH)
            if step < size:
                total = total.astype(LOW)
    return total


def normalize(values, gain_vec):
    factor = lax.rsqrt(jnp.mean(values * values, axis=-1, keepdims=True) + EPSILON)
    plain_rows = values * factor
    return (plain_rows, factor, plain_rows * gain_vec)


def norm_backward(grad_normed, plain_rows, factor, gain_vec):
    scaled = grad_normed * gain_vec
    gain_part = jnp.sum(grad_normed * plain_rows, axis=0)
    grad_input = factor * (
        scaled - plain_rows * jnp.mean(scaled * plain_rows, axis=-1, keepdims=True)
    )
    return (gain_part, grad_input)


def matmul(left_side, right_side):
    return jnp.dot(left_side, right_side, preferred_element_type=HIGH)


def matmul_right_t(left_side, right_side):
    return lax.dot_general(
        left_side, right_side, (((1,), (1,)), ((), ())), preferred_element_type=HIGH
    )


def matmul_left_t(left_side, right_side):
    return lax.dot_general(
        left_side, right_side, (((0,), (0,)), ((), ())), preferred_element_type=HIGH
    )


def pad_units(rows):
    extra = -rows.shape[0] % 16
    return jnp.pad(rows, ((0, extra), (0, 0)))


def split_units(count):
    return -(-count // 32) * 16


def diagonal_visible(core, span_rows, key_axis):
    half = span_rows // 2

    def place(axis):
        index = lax.broadcasted_iota(jnp.int32, (span_rows, span_rows), axis)
        flipped = jnp.where(index < half, index + half, index - half)
        return jnp.where(core == 0, index, flipped)

    return place(key_axis) <= place(1 - key_axis)


def forward_kernel(
    place_ref, rank_ref, core_ref, query_ref, key_ref, value_ref, mixed_ref, lse_ref, score_ref
):
    span_rows = query_ref.shape[0]
    heads = query_ref.shape[1] // HD
    rank = rank_ref[pl.program_id(1)]
    columns = [slice(h * HD, (h + 1) * HD) for h in range(heads)]

    def block_scores(step, h):
        start = pl.multiple_of(place_ref[step] * span_rows, span_rows)
        keys = key_ref[pl.ds(start, span_rows), columns[h]]
        return matmul_right_t(query_ref[:, columns[h]], keys) * (SCORE_SCALE * LOG2E)

    def fold(values, operation):
        folded = values[:, :HD]
        for at in range(HD, span_rows, HD):
            folded = operation(folded, values[:, at : at + HD])
        return folded

    def score_step(step, maxima):
        new = []
        for h in range(heads):
            scores = block_scores(step, h)
            score_ref[h, step] = scores
            new.append(jnp.maximum(maxima[h], fold(scores, jnp.maximum)))
        return tuple(new)

    start = tuple(jnp.full((span_rows, HD), -jnp.inf, HIGH) for _ in range(heads))
    maxima = lax.fori_loop(0, rank, score_step, start)
    visible = diagonal_visible(core_ref[0], span_rows, 1)
    tops = []
    for h in range(heads):
        scores = jnp.where(visible, block_scores(rank, h), -jnp.inf)
        score_ref[h, rank] = scores
        top = jnp.maximum(maxima[h], fold(scores, jnp.maximum))
        tops.append(jnp.max(top, axis=1, keepdims=True))

    def mix_step(step, running):
        new = []
        start = pl.multiple_of(place_ref[step] * span_rows, span_rows)
        for h in range(heads):
            total, mixed = running[h]
            weights = jnp.exp2(score_ref[h, step] - tops[h])
            values = value_ref[pl.ds(start, span_rows), columns[h]]
            new.append(
                (total + fold(weights, jnp.add), mixed + matmul(weights.astype(LOW), values))
            )
        return tuple(new)

    zero = jnp.zeros((span_rows, HD), HIGH)
    sums = lax.fori_loop(0, rank + 1, mix_step, tuple((zero, zero) for _ in range(heads)))
    for h in range(heads):
        total = jnp.sum(sums[h][0], axis=1, keepdims=True)
        mixed_ref[:, columns[h]] = (sums[h][1] / total).astype(LOW)
        lse = jnp.broadcast_to(tops[h] + jnp.log2(total), (span_rows, HD))
        lse_ref[h] = jnp.transpose(lse)[:8, :]


def backward_kernel(
    place_ref,
    rank_ref,
    core_ref,
    query_ref,
    grad_ref,
    mixed_ref,
    lse_ref,
    key_ref,
    value_ref,
    grad_query_ref,
    grad_key_ref,
    grad_value_ref,
    key_sum_ref,
    value_sum_ref,
):
    heads = query_ref.shape[1] // HD
    spans = query_ref.shape[0] // rank_ref.shape[0]
    span_rows = spans
    columns = [slice(h * HD, (h + 1) * HD) for h in range(heads)]
    key_sum_ref[...] = jnp.zeros_like(key_sum_ref)
    value_sum_ref[...] = jnp.zeros_like(value_sum_ref)

    def query_span(at, carry):
        first = pl.multiple_of(at * span_rows, span_rows)
        here = pl.ds(first, span_rows)
        rank = rank_ref[at]
        delta = []
        lse = []
        for h in range(heads):
            product = grad_ref[here, columns[h]].astype(HIGH) * mixed_ref[
                here, columns[h]
            ].astype(HIGH)
            delta.append(jnp.sum(jnp.transpose(product), axis=0, keepdims=True))
            lse.append(lse_ref[h, :1, here])

        def block(step, grad_query, visible):
            start = pl.multiple_of(place_ref[step] * span_rows, span_rows)
            there = pl.ds(start, span_rows)
            new = []
            for h in range(heads):
                query = query_ref[here, columns[h]]
                grad = grad_ref[here, columns[h]]
                keys = key_ref[there, columns[h]]
                values = value_ref[there, columns[h]]
                scores = matmul_right_t(keys, query) * (SCORE_SCALE * LOG2E)
                weights = jnp.exp2(scores - lse[h])
                if visible is not None:
                    weights = jnp.where(visible, weights, 0.0)
                grad_weights = matmul_right_t(values, grad)
                grad_scores = (weights * (grad_weights - delta[h])).astype(LOW)
                value_sum_ref[there, columns[h]] += matmul(weights.astype(LOW), grad)
                key_sum_ref[there, columns[h]] += matmul(grad_scores, query)
                new.append(grad_query[h] + matmul_left_t(grad_scores, keys))
            return tuple(new)

        start = tuple(jnp.zeros((span_rows, HD), HIGH) for _ in range(heads))
        grad_query = lax.fori_loop(0, rank, lambda s, g: block(s, g, None), start)
        visible = diagonal_visible(core_ref[0], span_rows, 0)
        grad_query = block(rank, grad_query, visible)
        for h in range(heads):
            grad_query_ref[here, columns[h]] = (grad_query[h] * SCORE_SCALE).astype(LOW)
        return carry

    lax.fori_loop(0, rank_ref.shape[0], query_span, 0)
    grad_key_ref[...] = (key_sum_ref[...] * SCORE_SCALE).astype(LOW)
    grad_value_ref[...] = value_sum_ref[...].astype(LOW)


def heads_at_once(key_rows, features):
    return features // HD if key_rows <= 4096 else 1


def attention_forward(scalars, queries, keys, values):
    rows, features = queries.shape
    key_rows = keys.shape[0]
    own_spans = scalars[1].shape[0]
    span_rows = rows // own_spans
    heads = heads_at_once(key_rows, features)
    width = heads * HD
    pairs = rows * key_rows * features
    return pl.pallas_call(
        forward_kernel,
        out_shape=(
            jax.ShapeDtypeStruct((rows, features), LOW),
            jax.ShapeDtypeStruct((features // HD, 8, rows), HIGH),
        ),
        grid_spec=pltpu.PrefetchScalarGridSpec(
            num_scalar_prefetch=3,
            grid=(features // width, own_spans),
            in_specs=[
                pl.BlockSpec((span_rows, width), lambda h, i, *_: (i, h)),
                pl.BlockSpec((key_rows, width), lambda h, i, *_: (0, h)),
                pl.BlockSpec((key_rows, width), lambda h, i, *_: (0, h)),
            ],
            out_specs=[
                pl.BlockSpec((span_rows, width), lambda h, i, *_: (i, h)),
                pl.BlockSpec((heads, 8, span_rows), lambda h, i, *_: (h, 0, i)),
            ],
            scratch_shapes=[
                pltpu.VMEM((heads, key_rows // span_rows, span_rows, span_rows), HIGH)
            ],
        ),
        compiler_params=pltpu.CompilerParams(vmem_limit_bytes=56 * 2**20),
        cost_estimate=pl.CostEstimate(
            flops=2 * pairs, bytes_accessed=4 * key_rows * features, transcendentals=pairs // 256
        ),
        name="attention_forward",
    )(*scalars, queries, keys, values)


def attention_backward(scalars, queries, grads, mixed, lse, keys, values):
    rows, features = queries.shape
    key_rows = keys.shape[0]
    heads = heads_at_once(key_rows, features)
    width = heads * HD
    pairs = rows * key_rows * features
    own = pl.BlockSpec((rows, width), lambda h, *_: (0, h))
    other = pl.BlockSpec((key_rows, width), lambda h, *_: (0, h))
    return pl.pallas_call(
        backward_kernel,
        out_shape=(
            jax.ShapeDtypeStruct((rows, features), LOW),
            jax.ShapeDtypeStruct((key_rows, features), LOW),
            jax.ShapeDtypeStruct((key_rows, features), LOW),
        ),
        grid_spec=pltpu.PrefetchScalarGridSpec(
            num_scalar_prefetch=3,
            grid=(features // width,),
            in_specs=[
                own,
                own,
                own,
                pl.BlockSpec((heads, 8, rows), lambda h, *_: (h, 0, 0)),
                other,
                other,
            ],
            out_specs=[own, other, other],
            scratch_shapes=[pltpu.VMEM((key_rows, width), HIGH)] * 2,
        ),
        compiler_params=pltpu.CompilerParams(vmem_limit_bytes=56 * 2**20),
        cost_estimate=pl.CostEstimate(
            flops=5 * pairs, bytes_accessed=8 * key_rows * features, transcendentals=pairs // 256
        ),
        name="attention_backward",
    )(*scalars, queries, grads, mixed, lse, keys, values)


def per_device(
    states,
    shared_kv,
    norm_gain,
    kv_gain,
    ffn_gain,
    query_weight,
    key_weight,
    value_weight,
    out_weight,
    gate_weight,
    up_weight,
    down_weight,
    span_order,
    grad_output,
):
    z, x, y, c = (lax.axis_index(name) for name in ALL)
    size_x = lax.axis_size("x")
    sides = 2 * size_x
    rows_local, width_model = states.shape
    weight_rows = query_weight.shape[0]
    units_local = gate_weight.shape[1]
    own_width = width_model // 8

    side = jnp.arange(sides, dtype=jnp.int32)
    side_owner = jnp.mod(x - side // 2, size_x) * 2 + jnp.bitwise_xor(y, side % 2)
    back = jnp.arange(4, dtype=jnp.int32)
    back_owner = jnp.mod(z - back, 4)

    def own_columns(weights):
        count = weights.shape[0]
        pair = 2 * own_width
        blocks = []
        for step in range(4):
            start = jnp.mod(z + step, 4) * pair
            block = lax.dynamic_slice_in_dim(weights, start, pair, 2)
            if step:
                block = hop(block, "z", step)
            keep = lax.dynamic_slice_in_dim(block, c * own_width, own_width, 2)
            give = lax.dynamic_slice_in_dim(block, (1 - c) * own_width, own_width, 2)
            blocks += [keep, hop(give, "c")]
        return [jnp.stack([b[i] for b in blocks]) for i in range(count)]

    spot = jnp.arange(8 * sides, dtype=jnp.int32)
    spot_z, spot_x, spot_y, spot_c = (
        spot // (4 * size_x),
        (spot // 4) % size_x,
        (spot // 2) % 2,
        spot % 2,
    )
    row_order = (
        (jnp.mod(x - spot_x, size_x) * 2 + jnp.bitwise_xor(y, spot_y)) * 4 + jnp.mod(z - spot_z, 4)
    ) * 2 + jnp.bitwise_xor(c, spot_c)

    def all_rows(pieces):
        stacked = jnp.concatenate(pieces, axis=0)
        return jnp.take(stacked, row_order, axis=0).reshape(width_model, own_width)

    state_rows = states.astype(HIGH)
    shared_rows = shared_kv.astype(HIGH)
    plain_kv, factor_kv, normed_kv = normalize(shared_rows, kv_gain)
    plain_one, factor_one, normed_one = normalize(state_rows, norm_gain)
    normed_low = normed_one.astype(LOW)
    shared_low = normed_kv.astype(LOW)

    key_slice, value_slice = own_columns(jnp.stack([key_weight, value_weight]))
    group_shared = gather_rows(shared_low)
    weight_key = all_rows(gather_x_first(key_slice))
    weight_value = all_rows(gather_y_first(value_slice))
    (query_slice,) = own_columns(query_weight[None])
    weight_query = all_rows(gather_x_first(query_slice))
    out_pieces = jnp.take(
        jnp.stack(gather_y_first(out_weight)), jnp.argsort(side_owner), axis=0
    ).reshape(2, size_x // 2, 2, weight_rows, width_model)
    out_keep = lax.dynamic_index_in_dim(out_pieces, c, 0, keepdims=False)
    out_got = hop(lax.dynamic_index_in_dim(out_pieces, 1 - c, 0, keepdims=False), "c")
    weight_out = jnp.where(
        c == 0, jnp.stack([out_keep, out_got], axis=2), jnp.stack([out_got, out_keep], axis=2)
    ).reshape(own_width, width_model)

    keys_own = matmul(group_shared, weight_key).astype(LOW)
    values_own = matmul(group_shared, weight_value).astype(LOW)
    keys_all = jnp.concatenate(gather_x_first(keys_own), axis=0)
    values_all = jnp.concatenate(gather_y_first(values_own), axis=0)
    group_normed = gather_rows(normed_low)
    queries = matmul(group_normed, weight_query).astype(LOW)

    span_of = (back_owner[None, :] * sides + side_owner[:, None]).reshape(-1)
    ranks = jnp.take(span_order, span_of)
    spans = span_order.shape[0]
    listed = jnp.arange(spans, dtype=jnp.int32)
    place = jnp.sum(jnp.where(ranks[None, :] == listed[:, None], listed[None, :], 0), axis=1)
    scalars = (place, ranks[:4], c.reshape(1).astype(jnp.int32))

    mixed, lse = attention_forward(scalars, queries, keys_all, values_all)

    gate_rows = pad_units(jnp.transpose(gate_weight))
    up_rows = pad_units(jnp.transpose(up_weight))
    down_rows = pad_units(down_weight)
    cut = split_units(gate_rows.shape[0])
    weight_gate = jnp.concatenate(gather_x_first(gate_rows), axis=0)
    weight_up = jnp.concatenate(gather_y_first(up_rows), axis=0)
    down_first = gather_x_first(down_rows[:cut])
    down_second = gather_y_first(down_rows[cut:])
    weight_down = jnp.concatenate(
        [part for pair in zip(down_first, down_second) for part in pair], axis=0
    )
    group_grad = gather_rows(grad_output)

    pair_rows = 2 * rows_local

    def rows_of(values, r):
        return values[r * pair_rows : (r + 1) * pair_rows]

    residual = state_rows + sum_rows(
        lambda r: matmul(rows_of(mixed, r), weight_out), rows_local
    )
    plain_two, factor_two, normed_two = normalize(residual, ffn_gain)
    group_in = gather_rows(normed_two.astype(LOW))

    gate_act = matmul_right_t(group_in, weight_gate)
    up_act = matmul_right_t(group_in, weight_up)
    grad_hidden = matmul_right_t(group_grad, weight_down)
    sigmoid = jax.nn.sigmoid(gate_act)
    silu_act = gate_act * sigmoid
    hidden = (silu_act * up_act).astype(LOW)
    grad_gate_act = (
        grad_hidden * up_act * sigmoid * (1.0 + gate_act * (1.0 - sigmoid))
    ).astype(LOW)
    grad_up_act = (grad_hidden * silu_act).astype(LOW)
    grad_ffn = sum_rows(
        lambda r: matmul(rows_of(grad_gate_act, r), weight_gate)
        + matmul(rows_of(grad_up_act, r), weight_up),
        rows_local,
    )
    branch = sum_rows(lambda r: matmul(rows_of(hidden, r), weight_down), rows_local)
    output = (residual + branch).astype(LOW)

    def unit_parts(values):
        step = values.shape[0] // sides
        return [values[s * step : (s + 1) * step] for s in range(sides)]

    gate_parts = unit_parts(matmul_left_t(grad_gate_act, group_in).astype(LOW))
    up_parts = unit_parts(matmul_left_t(grad_up_act, group_in).astype(LOW))
    down_parts = unit_parts(matmul_left_t(hidden, group_grad).astype(LOW))
    grad_gate = jnp.transpose(sum_y_first(gate_parts)[:units_local].astype(HIGH))
    grad_up = jnp.transpose(sum_x_first(up_parts)[:units_local].astype(HIGH))
    grad_down = jnp.concatenate(
        [sum_y_first([p[:cut] for p in down_parts]), sum_x_first([p[cut:] for p in down_parts])],
        axis=0,
    )[:units_local].astype(HIGH)

    gain_two, grad_norm_two = norm_backward(grad_ffn, plain_two, factor_two, ffn_gain)
    grad_residual = grad_output.astype(HIGH) + grad_norm_two
    group_branch = gather_rows(grad_residual.astype(LOW))
    grad_mixed = matmul_right_t(group_branch, weight_out).astype(LOW)

    grad_queries, key_terms, value_terms = attention_backward(
        scalars, queries, grad_mixed, mixed, lse, keys_all, values_all
    )
    grad_keys = sum_y_first(unit_parts(key_terms))
    grad_values = sum_x_first(unit_parts(value_terms))
    grad_normed = sum_rows(
        lambda r: matmul_right_t(rows_of(grad_queries, r), weight_query), rows_local
    )
    grad_shared_normed = sum_rows(
        lambda r: matmul_right_t(rows_of(grad_keys, r), weight_key)
        + matmul_right_t(rows_of(grad_values, r), weight_value),
        rows_local,
    )
    gain_one, grad_in_one = norm_backward(grad_normed, plain_one, factor_one, norm_gain)
    gain_kv, grad_in_kv = norm_backward(grad_shared_normed, plain_kv, factor_kv, kv_gain)
    grad_states = (grad_residual + grad_in_one).astype(LOW)
    grad_shared = grad_in_kv.astype(LOW)

    def side_parts(values):
        chunks = values.reshape(sides, -1, values.shape[1])
        return [
            lax.dynamic_index_in_dim(chunks, side_owner[s], 0, keepdims=False)
            for s in range(sides)
        ]

    to_layout = [
        [
            (
                ((za * size_x + xa) * 2 + ya) * 2 + ca,
                (4 * xa + 2 * ya + (ca ^ flip)) * 4 + za,
            )
            for za in range(4)
            for xa in range(size_x)
            for ya in range(2)
            for ca in range(2)
        ]
        for flip in range(2)
    ]

    def layout(summed):
        halves = summed.reshape(2, -1, summed.shape[1])
        got = []
        for flip in range(2):
            send = lax.dynamic_index_in_dim(
                halves, jnp.bitwise_xor(c, flip), 0, keepdims=False
            )
            got.append(lax.ppermute(send, ALL, to_layout[flip]))
        even = x % 2 == 0
        first = jnp.where(even, got[0], got[1])
        second = jnp.where(even, got[1], got[0])
        return jnp.concatenate([first, second], axis=1).astype(HIGH)

    grad_out = jnp.transpose(
        layout(sum_x_first(side_parts(matmul_left_t(group_branch, mixed).astype(LOW))))
    )
    grad_query = layout(
        sum_y_first(side_parts(matmul_left_t(group_normed, grad_queries).astype(LOW)))
    )
    grad_key = layout(
        sum_y_first(side_parts(matmul_left_t(group_shared, grad_keys).astype(LOW)))
    )
    grad_value = layout(
        sum_x_first(side_parts(matmul_left_t(group_shared, grad_values).astype(LOW)))
    )

    gain_stack = jnp.stack([gain_one, gain_kv, gain_two])
    gain_sums = lax.psum_scatter(gain_stack, ALL, scatter_dimension=1, tiled=True)
    return (
        output,
        grad_states,
        grad_shared,
        gain_sums[0],
        gain_sums[1],
        gain_sums[2],
        grad_query,
        grad_key,
        grad_value,
        grad_out,
        grad_gate,
        grad_up,
        grad_down,
    )


def solution(mesh):
    size_ctx, size_head = mesh.shape["ctx"], mesh.shape["head"]
    fine = Mesh(mesh.devices.reshape(4, size_ctx // 4, 2, size_head // 2), ALL)
    rows = P(ALL, None)
    ctx, head = ("z", "x"), ("y", "c")
    in_specs = (
        rows,
        rows,
        P(),
        P(),
        P(),
        rows,
        rows,
        rows,
        rows,
        P(None, ALL),
        P(None, ALL),
        rows,
        P(),
        rows,
    )
    out_specs = (
        rows,
        rows,
        rows,
        P(ALL),
        P(ALL),
        P(ALL),
        P(ctx, head),
        P(ctx, head),
        P(ctx, head),
        P(head, ctx),
        P(None, ALL),
        P(None, ALL),
        rows,
    )
    return jax.shard_map(
        per_device, mesh=fine, in_specs=in_specs, out_specs=out_specs, check_vma=False
    )
```

time: 1740 us -> 1050 us (0.60)
  blocking collectives: 448 us -> 0 us
  waiting for transfers between devices: 892 us -> 540 us
  starting transfers between devices: 20 us -> 183 us
  matrix products: 173 us -> 67.1 us
  Pallas kernels: 0 us -> 51.4 us
    all_gather x14 -> x0, waiting for transfers between devices: 655 us -> none  [the longest x1 87.2 us: per_device(): lax.all_gather(down_weight, 'ctx', axis=0, tiled=True)]
    ppermute x0 -> x153, waiting for transfers between devices: none -> 410 us  [the longest x145 407 us: hop(): lax.ppermute(values, axis, [(i, (i + steps) % size) for i in range(size)])]
    unnamed x1 -> x0, blocking collectives: 403 us -> none
    reduce_scatter x4 -> x0, waiting for transfers between devices: 200 us -> none  [the longest x1 169 us: per_device(): lax.psum_scatter(grad_keys_rows.astype(jnp.bfloat16), 'ctx', scatter_dime...]
    ppermute x0 -> x153, starting transfers between devices: none -> 183 us  [the longest x145 171 us: hop(): lax.ppermute(values, axis, [(i, (i + steps) % size) for i in range(size)])]
    unnamed x21 -> x2, waiting for transfers between devices: 14 us -> 130 us
    dot_general x21 -> x19, matrix products: 83.4 us -> 30 us  [matmul(): return jnp.dot(left_side, right_side, preferred_element_type=HIGH)]
    pallas_call x0 -> x2, Pallas kernels: none -> 51.4 us  [the longest x1 30.9 us: attention_backward(): pl.pallas_call(backward_kernel, out_shape=(jax.ShapeDtypeStruct((rows, fe...]
  transfers between devices with their start and end apart: 25 -> 154, of which waited for: 19 -> 59; matrix products, arithmetic and copies ran while one was open for 41% -> 19% of each run, Pallas kernels for 0% -> 2%
where the time goes in v1:
time: 1050 us; the launch traced here: 1030 us
  waiting for transfers between devices  540 us (51%)
  starting transfers between devices  183 us (17%)
  local copies, waits for them, and re-layouts  100 us (10%)
  matrix products  67.1 us (6%)
  other arithmetic  62.5 us (6%)
  Pallas kernels  51.4 us (5%)
  between operations  24.4 us (2%)
    ppermute x145, waiting for transfers between devices, hop(): lax.ppermute(values, axis, [(i, (i + steps) % size) for i in range(size)])  407 us
    ppermute x145, starting transfers between devices, hop(): lax.ppermute(values, axis, [(i, (i + steps) % size) for i in range(size)])  171 us
    unnamed x2, waiting for transfers between devices  130 us
    unnamed x221, local copies, waits for them, and re-layouts  54.6 us
    pallas_call x1, Pallas kernels, attention_backward(): pl.pallas_call(backward_kernel, out_shape=(jax.ShapeDtypeStruct((rows, fe...  30.9 us
    dot_general x19, matrix products, matmul(): return jnp.dot(left_side, right_side, preferred_element_type=HIGH)  30 us
  transfers between devices with their start and end apart: 154, of which 59 were waited for; matrix products, arithmetic and copies ran while one was open for 19% of the time, Pallas kernels for 2%

profile of v1, /device:TPU:0, one launch (start us, length us, event | category | flops | bytes accessed | tf_op | source)
XLA Modules:
  0.0 1027.9 jit_solution(17053686983894206703)
XLA Ops:
  53.4 4.9 collective-permute-done.8
  86.1 6.7 collective-permute-done.14
  149.1 9.4 collective-permute-done.20
  164.2 14.9 %collective-permute-done.22 = bf16[128,2048]{1,0:T(8,128)(2,1)S(1)} collective-permute-done((bf16[128,2048]{1,0:T(8,128)(2,1)}, bf16[128,2048]{1,0:T(8,128)(2,1)S(1)}, u32[]{:S(2)}, u32[]{:S(2)}) %collective-permute-start.22) | collective-permute-done | bytes 524320 | tf_op jit(solution)/shard_map/ppermute | solution.py:21
  187.9 9.2 collective-permute-done.35
  202.6 8.7 collective-permute-done.34
  211.4 9.9 collective-permute-done.36
  226.8 20.5 %attention_forward.1 = (bf16[1024,256]{1,0:T(8,128)(2,1)}, f32[2,8,1024]{2,1,0:T(8,128)}) custom-call(s32[16]{0:T(128)} %select_reduce_fusion.place_ref, s32[4]{0:T(128)} %bitcast.214, s32[1]{0:T(128)} %bitcast.1.core_ref, bf16[1024,256]{1,0:T(8,128)(2,1)} %convolution_convert_fusion.10.query_ref, bf16[4096,256]{1,0:T(8,128)(2,1)} %pad_maximum_fusion.2.key_ref, ...), custom_call_target="tpu_custom_call" | custom-call | flops 2147483648 | bytes 4194304 | tf_op jit(solution)/shard_map/attention_forward/pallas_call | solution.py:282
  254.9 12.3 %collective-permute-done.51 = bf16[128,2048]{1,0:T(8,128)(2,1)S(1)} collective-permute-done((bf16[128,2048]{1,0:T(8,128)(2,1)S(1)}, bf16[128,2048]{1,0:T(8,128)(2,1)S(1)}, u32[]{:S(2)}, u32[]{:S(2)}) %collective-permute-start.51) | collective-permute-done | bytes 524320 | tf_op jit(solution)/shard_map/ppermute | solution.py:21
  271.1 12.8 %collective-permute-done.52 = bf16[128,2048]{1,0:T(8,128)(2,1)S(1)} collective-permute-done((bf16[128,2048]{1,0:T(8,128)(2,1)S(1)}, bf16[128,2048]{1,0:T(8,128)(2,1)S(1)}, u32[]{:S(2)}, u32[]{:S(2)}) %collective-permute-start.52) | collective-permute-done | bytes 524320 | tf_op jit(solution)/shard_map/ppermute | solution.py:21
  288.7 6.5 collective-permute-done.83
  295.2 11.2 %collective-permute-done.53 = bf16[128,2048]{1,0:T(8,128)(2,1)S(1)} collective-permute-done((bf16[128,2048]{1,0:T(8,128)(2,1)S(1)}, bf16[128,2048]{1,0:T(8,128)(2,1)S(1)}, u32[]{:S(2)}, u32[]{:S(2)}) %collective-permute-start.53) | collective-permute-done | bytes 524320 | tf_op jit(solution)/shard_map/ppermute | solution.py:21
  309.4 8.3 collective-permute-done.85
  318.3 10.2 collective-permute-done.55
  328.8 15.1 %collective-permute-done.57 = bf16[128,2048]{1,0:T(8,128)(2,1)S(1)} collective-permute-done((bf16[128,2048]{1,0:T(8,128)(2,1)S(1)}, bf16[128,2048]{1,0:T(8,128)(2,1)S(1)}, u32[]{:S(2)}, u32[]{:S(2)}) %collective-permute-start.57) | collective-permute-done | bytes 524320 | tf_op jit(solution)/shard_map/ppermute | solution.py:21
  346.3 12.0 %collective-permute-done.59 = bf16[128,2048]{1,0:T(8,128)(2,1)S(1)} collective-permute-done((bf16[128,2048]{1,0:T(8,128)(2,1)S(1)}, bf16[128,2048]{1,0:T(8,128)(2,1)S(1)}, u32[]{:S(2)}, u32[]{:S(2)}) %collective-permute-start.59) | collective-permute-done | bytes 524320 | tf_op jit(solution)/shard_map/ppermute | solution.py:21
  363.2 15.3 %collective-permute-done.66 = bf16[176,2048]{1,0:T(8,128)(2,1)S(1)} collective-permute-done((bf16[176,2048]{1,0:T(8,128)(2,1)S(1)}, bf16[176,2048]{1,0:T(8,128)(2,1)S(1)}, u32[]{:S(2)}, u32[]{:S(2)}) %collective-permute-start.66) | collective-permute-done | bytes 720928 | tf_op jit(solution)/shard_map/ppermute | solution.py:21
  381.7 11.1 %collective-permute-done.63 = bf16[176,2048]{1,0:T(8,128)(2,1)S(1)} collective-permute-done((bf16[176,2048]{1,0:T(8,128)(2,1)S(1)}, bf16[176,2048]{1,0:T(8,128)(2,1)S(1)}, u32[]{:S(2)}, u32[]{:S(2)}) %collective-permute-start.63) | collective-permute-done | bytes 720928 | tf_op jit(solution)/shard_map/ppermute | solution.py:21
  396.0 6.0 multiply_convert_fusion.1
  411.1 6.3 collective-permute-start.150
  451.7 7.9 collective-permute-done.152
  459.7 6.6 collective-permute-done.145
  466.7 9.6 collective-permute-done.77
  478.3 7.6 collective-permute-done.91
  486.1 5.1 collective-permute-done.142
  491.5 11.0 %collective-permute-done.78 = bf16[128,2048]{1,0:T(8,128)(2,1)S(1)} collective-permute-done((bf16[128,2048]{1,0:T(8,128)(2,1)S(1)}, bf16[128,2048]{1,0:T(8,128)(2,1)S(1)}, u32[]{:S(2)}, u32[]{:S(2)}) %collective-permute-start.78) | collective-permute-done | bytes 524320 | tf_op jit(solution)/shard_map/ppermute | solution.py:21
  504.9 6.3 collective-permute-done.92
  513.7 16.4 %collective-permute-done.149 = bf16[96,2048]{1,0:T(8,128)(2,1)S(1)} collective-permute-done((bf16[96,2048]{1,0:T(8,128)(2,1)S(1)}, bf16[96,2048]{1,0:T(8,128)(2,1)S(1)}, u32[]{:S(2)}, u32[]{:S(2)}) %collective-permute-start.149) | collective-permute-done | bytes 393248 | tf_op jit(solution)/shard_map/ppermute | solution.py:21
  535.3 10.4 %collective-permute-done.93 = bf16[128,2048]{1,0:T(8,128)(2,1)S(1)} collective-permute-done((bf16[128,2048]{1,0:T(8,128)(2,1)S(1)}, bf16[128,2048]{1,0:T(8,128)(2,1)S(1)}, u32[]{:S(2)}, u32[]{:S(2)}) %collective-permute-start.93) | collective-permute-done | bytes 524320 | tf_op jit(solution)/shard_map/ppermute | solution.py:21
  549.8 15.1 %collective-permute-done.146 = bf16[176,2048]{1,0:T(8,128)(2,1)S(1)} collective-permute-done((bf16[176,2048]{1,0:T(8,128)(2,1)S(1)}, bf16[176,2048]{1,0:T(8,128)(2,1)S(1)}, u32[]{:S(2)}, u32[]{:S(2)}) %collective-permute-start.146) | collective-permute-done | bytes 720928 | tf_op jit(solution)/shard_map/ppermute | solution.py:21
  568.4 14.2 %collective-permute-done.97 = bf16[128,2048]{1,0:T(8,128)(2,1)S(1)} collective-permute-done((bf16[128,2048]{1,0:T(8,128)(2,1)S(1)}, bf16[128,2048]{1,0:T(8,128)(2,1)S(1)}, u32[]{:S(2)}, u32[]{:S(2)}) %collective-permute-start.97) | collective-permute-done | bytes 524320 | tf_op jit(solution)/shard_map/ppermute | solution.py:21
  583.2 15.1 %collective-permute-done.99 = bf16[128,2048]{1,0:T(8,128)(2,1)S(1)} collective-permute-done((bf16[128,2048]{1,0:T(8,128)(2,1)S(1)}, bf16[128,2048]{1,0:T(8,128)(2,1)S(1)}, u32[]{:S(2)}, u32[]{:S(2)}) %collective-permute-start.99) | collective-permute-done | bytes 524320 | tf_op jit(solution)/shard_map/ppermute | solution.py:21
  603.8 30.9 %attention_backward.1 = (bf16[1024,256]{1,0:T(8,128)(2,1)}, bf16[4096,256]{1,0:T(8,128)(2,1)}, bf16[4096,256]{1,0:T(8,128)(2,1)}) custom-call(s32[16]{0:T(128)} %select_reduce_fusion.place_ref, s32[4]{0:T(128)} %bitcast.215, s32[1]{0:T(128)} %bitcast.1.core_ref, bf16[1024,256]{1,0:T(8,128)(2,1)} %convolution_convert_fusion.10.query_ref, ...), custom_call_target="tpu_custom_call" | custom-call | flops 5368709120 | bytes 8388608 | tf_op jit(solution)/shard_map/attention_backward/pallas_call | solution.py:320
  643.4 8.7 collective-permute-start.121
  655.7 7.9 collective-permute-start.138
  670.7 11.3 %collective-permute-done.138 = bf16[512,256]{1,0:T(8,128)(2,1)S(1)} collective-permute-done((bf16[512,256]{1,0:T(8,128)(2,1)S(1)}, bf16[512,256]{1,0:T(8,128)(2,1)S(1)}, u32[]{:S(2)}, u32[]{:S(2)}) %collective-permute-start.138) | collective-permute-done | bytes 262176 | tf_op jit(solution)/shard_map/ppermute | solution.py:21
  684.3 7.2 collective-permute-done.123
  708.7 20.3 %collective-permute-start.113 = (bf16[1024,256]{1,0:T(8,128)(2,1)}, bf16[1024,256]{1,0:T(8,128)(2,1)}, u32[]{:S(2)}, u32[]{:S(2)}) collective-permute-start(bf16[1024,256]{1,0:T(8,128)(2,1)} %add_convert_fusion.7), channel_id=1, source_target_pairs={{0,2},{2,0},{1,3},{3,1},{4,6},{6,4},{5,7},{7,5},{8,10},{10,8},{9,1... | collective-permute-start | bytes 1572872 | tf_op jit(solution)/shard_map/ppermute | solution.py:21
  731.5 9.9 collective-permute-done.113
  748.5 6.2 collective-permute-done.110
  764.8 5.0 collective-permute-done.127
  782.0 5.1 collective-permute-done.133
  802.3 26.0 %collective-permute-start.118 = (bf16[128,2048]{1,0:T(8,128)(2,1)}, bf16[128,2048]{1,0:T(8,128)(2,1)S(1)}, u32[]{:S(2)}, u32[]{:S(2)}) collective-permute-start(bf16[128,2048]{1,0:T(8,128)(2,1)} %fusion.24), channel_id=1, source_target_pairs={{0,8},{8,16},{16,24},{24,0},{1,9},{9,17},{17,25},{25,1},{2,10},{10... | collective-permute-start | bytes 1572872 | tf_op jit(solution)/shard_map/ppermute | solution.py:21
  830.9 8.3 collective-permute-start.115
  849.7 6.4 collective-permute-done.107
  857.9 8.6 collective-permute-done.119
  870.5 12.2 %collective-permute-done.120 = bf16[128,2048]{1,0:T(8,128)(2,1)S(1)} collective-permute-done((bf16[128,2048]{1,0:T(8,128)(2,1)S(1)}, bf16[128,2048]{1,0:T(8,128)(2,1)S(1)}, u32[]{:S(2)}, u32[]{:S(2)}) %collective-permute-start.120) | collective-permute-done | bytes 524320 | tf_op jit(solution)/shard_map/ppermute | solution.py:21
  888.3 129.8 %reduce-scatter.4.cloned.1.call-done = f32[64,3]{1,0:T(8,128)} async-done(((f32[2048,3]{1,0:T(8,128)}), f32[64,3]{1,0:T(8,128)}) %reduce-scatter.4.cloned.1.call-update) | async-done | bytes 784
  (675 shorter events, 363.2 us)
Async XLA Ops:
  7.2 1010.9 %reduce-scatter.4.cloned.1.call-start = ((), (), s32[]{:S(2)}) async-start(), calls=%async_computation.1 | async-start | bytes 1081344
  7.2 100.0 %collective-permute-start.44 = (bf16[64,2048]{1,0:T(8,128)(2,1)}, bf16[64,2048]{1,0:T(8,128)(2,1)}, u32[]{:S(2)}, u32[]{:S(2)}) collective-permute-start(bf16[64,2048]{1,0:T(8,128)(2,1)} %param.24), channel_id=1, source_target_pairs={{0,4},{4,0},{1,5},{5,1},{2,6},{6,2},{3,7},{7,3},{8,12},{12,8},{9,1... | collective-permute-start | bytes 786440 | tf_op jit(solution)/shard_map/ppermute | solution.py:21
  10.3 91.4 %collective-permute-start.43 = (bf16[64,2048]{1,0:T(8,128)(2,1)}, bf16[64,2048]{1,0:T(8,128)(2,1)}, u32[]{:S(2)}, u32[]{:S(2)}) collective-permute-start(bf16[64,2048]{1,0:T(8,128)(2,1)} %param.24), channel_id=1, source_target_pairs={{0,2},{2,0},{1,3},{3,1},{4,6},{6,4},{5,7},{7,5},{8,10},{10,8},{9,1... | collective-permute-start | bytes 786440 | tf_op jit(solution)/shard_map/ppermute | solution.py:21
  13.3 38.7 %collective-permute-start.7 = (bf16[1,64,256]{2,1,0:T(8,128)(2,1)}, bf16[1,64,256]{2,1,0:T(8,128)(2,1)}, u32[]{:S(2)}, u32[]{:S(2)}) collective-permute-start(bf16[1,64,256]{2,1,0:T(8,128)(2,1)} %dynamic-slice_bitcast_fusion.13), channel_id=1, source_target_pairs={{0,1},{1,0},{2,3},{3,2},{4,5},{5,4},{6,7},{7,6},{8,9},{9,8},{10,11... | collective-permute-start | bytes 98312 | tf_op jit(solution)/shard_map/ppermute | solution.py:21
  14.9 44.1 %collective-permute-start.24 = (bf16[2,64,256]{2,1,0:T(8,128)(2,1)}, bf16[2,64,256]{2,1,0:T(8,128)(2,1)}, u32[]{:S(2)}, u32[]{:S(2)}) collective-permute-start(bf16[2,64,256]{2,1,0:T(8,128)(2,1)} %get-tuple-element.132), channel_id=1, source_target_pairs={{0,1},{1,0},{2,3},{3,2},{4,5},{5,4},{6,7},{7,6},{8,9},{9,8},{10,11... | collective-permute-start | bytes 196616 | tf_op jit(solution)/shard_map/ppermute | solution.py:21
  16.9 54.7 %collective-permute-start.12 = (bf16[1,64,512]{2,1,0:T(8,128)(2,1)}, bf16[1,64,512]{2,1,0:T(8,128)(2,1)}, u32[]{:S(2)}, u32[]{:S(2)}) collective-permute-start(bf16[1,64,512]{2,1,0:T(8,128)(2,1)} %get-tuple-element.152), channel_id=1, source_target_pairs={{0,24},{8,0},{16,8},{24,16},{1,25},{9,1},{17,9},{25,17},{2,26},{10... | collective-permute-start | bytes 196616 | tf_op jit(solution)/shard_map/ppermute | solution.py:21
  101.7 182.5 %collective-permute-start.80 = (bf16[128,2048]{1,0:T(8,128)(2,1)}, bf16[128,2048]{1,0:T(8,128)(2,1)}, u32[]{:S(2)}, u32[]{:S(2)}) collective-permute-start(bf16[128,2048]{1,0:T(8,128)(2,1)} %param.29), channel_id=1, source_target_pairs={{0,1},{1,0},{2,3},{3,2},{4,5},{5,4},{6,7},{7,6},{8,9},{9,8},{10,11... | collective-permute-start | bytes 1572872 | tf_op jit(solution)/shard_map/ppermute | solution.py:21
  147.7 32.4 %collective-permute-start.5 = (bf16[128,2048]{1,0:T(8,128)(2,1)}, bf16[128,2048]{1,0:T(8,128)(2,1)S(1)}, u32[]{:S(2)}, u32[]{:S(2)}) collective-permute-start(bf16[128,2048]{1,0:T(8,128)(2,1)} %collective-permute-done.3), channel_id=1, source_target_pairs={{0,8},{8,16},{16,24},{24,0},{1,9},{9,17},{17,25},{25,1},{2,10},{10... | collective-permute-start | bytes 1572872 | tf_op jit(solution)/shard_map/ppermute | solution.py:21
  186.1 25.1 %collective-permute-start.34 = (bf16[1024,256]{1,0:T(8,128)(2,1)S(1)}, bf16[1024,256]{1,0:T(8,128)(2,1)S(1)}, u32[]{:S(2)}, u32[]{:S(2)}) collective-permute-start(bf16[1024,256]{1,0:T(8,128)(2,1)S(1)} %convolution_convert_fusion.9), channel_id=1, source_target_pairs={{0,2},{2,0},{1,3},{3,1},{4,6},{6,4},{5,7},{7,5},{8,10},{10,8},{9,1... | collective-permute-start | bytes 1572872 | tf_op jit(solution)/shard_map/ppermute | solution.py:21
  187.4 36.0 %collective-permute-start.41 = (bf16[1024,256]{1,0:T(8,128)(2,1)S(1)}, bf16[1024,256]{1,0:T(8,128)(2,1)S(1)}, u32[]{:S(2)}, u32[]{:S(2)}) collective-permute-start(bf16[1024,256]{1,0:T(8,128)(2,1)S(1)} %convolution_convert_fusion.8), channel_id=1, source_target_pairs={{0,4},{4,0},{1,5},{5,1},{2,6},{6,2},{3,7},{7,3},{8,12},{12,8},{9,1... | collective-permute-start | bytes 1572872 | tf_op jit(solution)/shard_map/ppermute | solution.py:21
  211.2 57.8 %collective-permute-start.81 = (bf16[128,2048]{1,0:T(8,128)(2,1)}, bf16[128,2048]{1,0:T(8,128)(2,1)}, u32[]{:S(2)}, u32[]{:S(2)}) collective-permute-start(bf16[128,2048]{1,0:T(8,128)(2,1)} %param.29), channel_id=1, source_target_pairs={{0,8},{8,16},{16,24},{24,0},{1,9},{9,17},{17,25},{25,1},{2,10},{10... | collective-permute-start | bytes 1572872 | tf_op jit(solution)/shard_map/ppermute | solution.py:21
  221.3 46.1 %collective-permute-start.70 = (bf16[80,2048]{1,0:T(8,128)(2,1)}, bf16[80,2048]{1,0:T(8,128)(2,1)}, u32[]{:S(2)}, u32[]{:S(2)}) collective-permute-start(bf16[80,2048]{1,0:T(8,128)(2,1)} %get-tuple-element.125), channel_id=1, source_target_pairs={{0,4},{4,0},{1,5},{5,1},{2,6},{6,2},{3,7},{7,3},{8,12},{12,8},{9,1... | collective-permute-start | bytes 983048 | tf_op jit(solution)/shard_map/ppermute | solution.py:21
  223.3 25.5 %collective-permute-start.68 = (bf16[80,2048]{1,0:T(8,128)(2,1)}, bf16[80,2048]{1,0:T(8,128)(2,1)S(1)}, u32[]{:S(2)}, u32[]{:S(2)}) collective-permute-start(bf16[80,2048]{1,0:T(8,128)(2,1)} %get-tuple-element.125), channel_id=1, source_target_pairs={{0,2},{2,0},{1,3},{3,1},{4,6},{6,4},{5,7},{7,5},{8,10},{10,8},{9,1... | collective-permute-start | bytes 983048 | tf_op jit(solution)/shard_map/ppermute | solution.py:21
  223.9 27.2 %collective-permute-start.69 = (bf16[96,2048]{1,0:T(8,128)(2,1)}, bf16[96,2048]{1,0:T(8,128)(2,1)}, u32[]{:S(2)}, u32[]{:S(2)}) collective-permute-start(bf16[96,2048]{1,0:T(8,128)(2,1)} %get-tuple-element.127), channel_id=1, source_target_pairs={{0,4},{4,0},{1,5},{5,1},{2,6},{6,2},{3,7},{7,3},{8,12},{12,8},{9,1... | collective-permute-start | bytes 1179656 | tf_op jit(solution)/shard_map/ppermute | solution.py:21
  252.8 91.3 %collective-permute-start.64 = (bf16[176,2048]{1,0:T(8,128)(2,1)S(1)}, bf16[176,2048]{1,0:T(8,128)(2,1)S(1)}, u32[]{:S(2)}, u32[]{:S(2)}) collective-permute-start(bf16[176,2048]{1,0:T(8,128)(2,1)S(1)} %copy-done.33), channel_id=1, source_target_pairs={{0,2},{2,0},{1,3},{3,1},{4,6},{6,4},{5,7},{7,5},{8,10},{10,8},{9,1... | collective-permute-start | bytes 2162696 | tf_op jit(solution)/shard_map/ppermute | solution.py:21
  307.2 51.2 %collective-permute-start.62 = (bf16[176,2048]{1,0:T(8,128)(2,1)S(1)}, bf16[176,2048]{1,0:T(8,128)(2,1)S(1)}, u32[]{:S(2)}, u32[]{:S(2)}) collective-permute-start(bf16[176,2048]{1,0:T(8,128)(2,1)S(1)} %copy-done.32), channel_id=1, source_target_pairs={{0,4},{4,0},{1,5},{5,1},{2,6},{6,2},{3,7},{7,3},{8,12},{12,8},{9,1... | collective-permute-start | bytes 2162696 | tf_op jit(solution)/shard_map/ppermute | solution.py:21
  317.7 26.1 %collective-permute-start.54 = (bf16[128,2048]{1,0:T(8,128)(2,1)S(1)}, bf16[128,2048]{1,0:T(8,128)(2,1)S(1)}, u32[]{:S(2)}, u32[]{:S(2)}) collective-permute-start(bf16[128,2048]{1,0:T(8,128)(2,1)S(1)} %get-tuple-element.88), channel_id=1, source_target_pairs={{0,1},{1,0},{2,3},{3,2},{4,5},{5,4},{6,7},{7,6},{8,9},{9,8},{10,11... | collective-permute-start | bytes 1572872 | tf_op jit(solution)/shard_map/ppermute | solution.py:21
  346.2 32.2 %collective-permute-start.66 = (bf16[176,2048]{1,0:T(8,128)(2,1)S(1)}, bf16[176,2048]{1,0:T(8,128)(2,1)S(1)}, u32[]{:S(2)}, u32[]{:S(2)}) collective-permute-start(bf16[176,2048]{1,0:T(8,128)(2,1)S(1)} %collective-permute-done.64), channel_id=1, source_target_pairs={{0,4},{4,0},{1,5},{5,1},{2,6},{6,2},{3,7},{7,3},{8,12},{12,8},{9,1... | collective-permute-start | bytes 2162696 | tf_op jit(solution)/shard_map/ppermute | solution.py:21
  360.5 32.3 %collective-permute-start.63 = (bf16[176,2048]{1,0:T(8,128)(2,1)S(1)}, bf16[176,2048]{1,0:T(8,128)(2,1)S(1)}, u32[]{:S(2)}, u32[]{:S(2)}) collective-permute-start(bf16[176,2048]{1,0:T(8,128)(2,1)S(1)} %collective-permute-done.62), channel_id=1, source_target_pairs={{0,2},{2,0},{1,3},{3,1},{4,6},{6,4},{5,7},{7,5},{8,10},{10,8},{9,1... | collective-permute-start | bytes 2162696 | tf_op jit(solution)/shard_map/ppermute | solution.py:21
  411.1 40.5 %collective-permute-start.150 = (bf16[80,2048]{1,0:T(8,128)(2,1)}, bf16[80,2048]{1,0:T(8,128)(2,1)S(1)}, u32[]{:S(2)}, u32[]{:S(2)}) collective-permute-start(bf16[80,2048]{1,0:T(8,128)(2,1)} %get-tuple-element.102), channel_id=1, source_target_pairs={{0,4},{4,0},{1,5},{5,1},{2,6},{6,2},{3,7},{7,3},{8,12},{12,8},{9,1... | collective-permute-start | bytes 983048 | tf_op jit(solution)/shard_map/ppermute | solution.py:21
  417.4 29.2 %collective-permute-start.151 = (bf16[80,2048]{1,0:T(8,128)(2,1)}, bf16[80,2048]{1,0:T(8,128)(2,1)S(1)}, u32[]{:S(2)}, u32[]{:S(2)}) collective-permute-start(bf16[80,2048]{1,0:T(8,128)(2,1)} %get-tuple-element.103), channel_id=1, source_target_pairs={{0,4},{4,0},{1,5},{5,1},{2,6},{6,2},{3,7},{7,3},{8,12},{12,8},{9,1... | collective-permute-start | bytes 983048 | tf_op jit(solution)/shard_map/ppermute | solution.py:21
  417.5 96.1 %collective-permute-start.147 = (bf16[96,2048]{1,0:T(8,128)(2,1)S(1)}, bf16[96,2048]{1,0:T(8,128)(2,1)S(1)}, u32[]{:S(2)}, u32[]{:S(2)}) collective-permute-start(bf16[96,2048]{1,0:T(8,128)(2,1)S(1)} %get-tuple-element.100), channel_id=1, source_target_pairs={{0,2},{2,0},{1,3},{3,1},{4,6},{6,4},{5,7},{7,5},{8,10},{10,8},{9,1... | collective-permute-start | bytes 1179656 | tf_op jit(solution)/shard_map/ppermute | solution.py:21
  419.3 28.1 %collective-permute-start.148 = (bf16[96,2048]{1,0:T(8,128)(2,1)}, bf16[96,2048]{1,0:T(8,128)(2,1)S(1)}, u32[]{:S(2)}, u32[]{:S(2)}) collective-permute-start(bf16[96,2048]{1,0:T(8,128)(2,1)} %get-tuple-element.101), channel_id=1, source_target_pairs={{0,2},{2,0},{1,3},{3,1},{4,6},{6,4},{5,7},{7,5},{8,10},{10,8},{9,1... | collective-permute-start | bytes 1179656 | tf_op jit(solution)/shard_map/ppermute | solution.py:21
  419.6 27.9 %collective-permute-start.76 = (bf16[128,2048]{1,0:T(8,128)(2,1)S(1)}, bf16[128,2048]{1,0:T(8,128)(2,1)S(1)}, u32[]{:S(2)}, u32[]{:S(2)}) collective-permute-start(bf16[128,2048]{1,0:T(8,128)(2,1)S(1)} %slice.866), channel_id=1, source_target_pairs={{0,1},{1,0},{2,3},{3,2},{4,5},{5,4},{6,7},{7,6},{8,9},{9,8},{10,11... | collective-permute-start | bytes 1572872 | tf_op jit(solution)/shard_map/ppermute | solution.py:21
  451.7 26.5 %collective-permute-start.89 = (bf16[128,2048]{1,0:T(8,128)(2,1)S(1)}, bf16[128,2048]{1,0:T(8,128)(2,1)S(1)}, u32[]{:S(2)}, u32[]{:S(2)}) collective-permute-start(bf16[128,2048]{1,0:T(8,128)(2,1)S(1)} %slice.863), channel_id=1, source_target_pairs={{0,1},{1,0},{2,3},{3,2},{4,5},{5,4},{6,7},{7,6},{8,9},{9,8},{10,11... | collective-permute-start | bytes 1572872 | tf_op jit(solution)/shard_map/ppermute | solution.py:21
  466.6 24.8 %collective-permute-start.74 = (bf16[128,2048]{1,0:T(8,128)(2,1)S(1)}, bf16[128,2048]{1,0:T(8,128)(2,1)S(1)}, u32[]{:S(2)}, u32[]{:S(2)}) collective-permute-start(bf16[128,2048]{1,0:T(8,128)(2,1)S(1)} %slice.868), channel_id=1, source_target_pairs={{0,1},{1,0},{2,3},{3,2},{4,5},{5,4},{6,7},{7,6},{8,9},{9,8},{10,11... | collective-permute-start | bytes 1572872 | tf_op jit(solution)/shard_map/ppermute | solution.py:21
  491.4 40.1 %collective-permute-start.73 = (bf16[128,2048]{1,0:T(8,128)(2,1)S(1)}, bf16[128,2048]{1,0:T(8,128)(2,1)S(1)}, u32[]{:S(2)}, u32[]{:S(2)}) collective-permute-start(bf16[128,2048]{1,0:T(8,128)(2,1)S(1)} %slice.869), channel_id=1, source_target_pairs={{0,1},{1,0},{2,3},{3,2},{4,5},{5,4},{6,7},{7,6},{8,9},{9,8},{10,11... | collective-permute-start | bytes 1572872 | tf_op jit(solution)/shard_map/ppermute | solution.py:21
  502.5 30.7 %collective-permute-start.87 = (bf16[128,2048]{1,0:T(8,128)(2,1)S(1)}, bf16[128,2048]{1,0:T(8,128)(2,1)S(1)}, u32[]{:S(2)}, u32[]{:S(2)}) collective-permute-start(bf16[128,2048]{1,0:T(8,128)(2,1)S(1)} %slice.865), channel_id=1, source_target_pairs={{0,1},{1,0},{2,3},{3,2},{4,5},{5,4},{6,7},{7,6},{8,9},{9,8},{10,11... | collective-permute-start | bytes 1572872 | tf_op jit(solution)/shard_map/ppermute | solution.py:21
  502.7 47.1 %collective-permute-start.144 = (bf16[176,2048]{1,0:T(8,128)(2,1)S(1)}, bf16[176,2048]{1,0:T(8,128)(2,1)S(1)}, u32[]{:S(2)}, u32[]{:S(2)}) collective-permute-start(bf16[176,2048]{1,0:T(8,128)(2,1)S(1)} %get-tuple-element.106), channel_id=1, source_target_pairs={{0,4},{4,0},{1,5},{5,1},{2,6},{6,2},{3,7},{7,3},{8,12},{12,8},{9,1... | collective-permute-start | bytes 2162696 | tf_op jit(solution)/shard_map/ppermute | solution.py:21
  531.5 35.4 %collective-permute-start.141 = (bf16[176,2048]{1,0:T(8,128)(2,1)S(1)}, bf16[176,2048]{1,0:T(8,128)(2,1)S(1)}, u32[]{:S(2)}, u32[]{:S(2)}) collective-permute-start(bf16[176,2048]{1,0:T(8,128)(2,1)S(1)} %get-tuple-element.109), channel_id=1, source_target_pairs={{0,2},{2,0},{1,3},{3,1},{4,6},{6,4},{5,7},{7,5},{8,10},{10,8},{9,1... | collective-permute-start | bytes 2162696 | tf_op jit(solution)/shard_map/ppermute | solution.py:21
  533.3 31.7 %collective-permute-start.146 = (bf16[176,2048]{1,0:T(8,128)(2,1)S(1)}, bf16[176,2048]{1,0:T(8,128)(2,1)S(1)}, u32[]{:S(2)}, u32[]{:S(2)}) collective-permute-start(bf16[176,2048]{1,0:T(8,128)(2,1)S(1)} %add_convert_fusion.1), channel_id=1, source_target_pairs={{0,2},{2,0},{1,3},{3,1},{4,6},{6,4},{5,7},{7,5},{8,10},{10,8},{9,1... | collective-permute-start | bytes 2162696 | tf_op jit(solution)/shard_map/ppermute | solution.py:21
  533.6 33.4 %collective-permute-start.143 = (bf16[176,2048]{1,0:T(8,128)(2,1)S(1)}, bf16[176,2048]{1,0:T(8,128)(2,1)S(1)}, u32[]{:S(2)}, u32[]{:S(2)}) collective-permute-start(bf16[176,2048]{1,0:T(8,128)(2,1)S(1)} %add_convert_fusion.4), channel_id=1, source_target_pairs={{0,4},{4,0},{1,5},{5,1},{2,6},{6,2},{3,7},{7,3},{8,12},{12,8},{9,1... | collective-permute-start | bytes 2162696 | tf_op jit(solution)/shard_map/ppermute | solution.py:21
  638.7 30.2 %collective-permute-start.136 = (bf16[512,256]{1,0:T(8,128)(2,1)S(1)}, bf16[512,256]{1,0:T(8,128)(2,1)S(1)}, u32[]{:S(2)}, u32[]{:S(2)}) collective-permute-start(bf16[512,256]{1,0:T(8,128)(2,1)S(1)} %get-tuple-element.114), channel_id=1, source_target_pairs={{0,4},{4,0},{1,5},{5,1},{2,6},{6,2},{3,7},{7,3},{8,12},{12,8},{9,1... | collective-permute-start | bytes 786440 | tf_op jit(solution)/shard_map/ppermute | solution.py:21
  643.4 40.7 %collective-permute-start.121 = (bf16[512,256]{1,0:T(8,128)(2,1)}, bf16[512,256]{1,0:T(8,128)(2,1)}, u32[]{:S(2)}, u32[]{:S(2)}) collective-permute-start(bf16[512,256]{1,0:T(8,128)(2,1)} %get-tuple-element.120), channel_id=1, source_target_pairs={{0,2},{2,0},{1,3},{3,1},{4,6},{6,4},{5,7},{7,5},{8,10},{10,8},{9,1... | collective-permute-start | bytes 786440 | tf_op jit(solution)/shard_map/ppermute | solution.py:21
  653.2 93.3 %collective-permute-start.108 = (bf16[1024,256]{1,0:T(8,128)(2,1)}, bf16[1024,256]{1,0:T(8,128)(2,1)}, u32[]{:S(2)}, u32[]{:S(2)}) collective-permute-start(bf16[1024,256]{1,0:T(8,128)(2,1)} %get-tuple-element.110), channel_id=1, source_target_pairs={{0,2},{2,0},{1,3},{3,1},{4,6},{6,4},{5,7},{7,5},{8,10},{10,8},{9,1... | collective-permute-start | bytes 1572872 | tf_op jit(solution)/shard_map/ppermute | solution.py:21
  655.7 26.2 %collective-permute-start.138 = (bf16[512,256]{1,0:T(8,128)(2,1)S(1)}, bf16[512,256]{1,0:T(8,128)(2,1)S(1)}, u32[]{:S(2)}, u32[]{:S(2)}) collective-permute-start(bf16[512,256]{1,0:T(8,128)(2,1)S(1)} %fusion.57), channel_id=1, source_target_pairs={{0,2},{2,0},{1,3},{3,1},{4,6},{6,4},{5,7},{7,5},{8,10},{10,8},{9,1... | collective-permute-start | bytes 786440 | tf_op jit(solution)/shard_map/ppermute | solution.py:21
  668.9 62.5 %collective-permute-start.111 = (bf16[1024,256]{1,0:T(8,128)(2,1)}, bf16[1024,256]{1,0:T(8,128)(2,1)}, u32[]{:S(2)}, u32[]{:S(2)}) collective-permute-start(bf16[1024,256]{1,0:T(8,128)(2,1)} %get-tuple-element.112), channel_id=1, source_target_pairs={{0,4},{4,0},{1,5},{5,1},{2,6},{6,2},{3,7},{7,3},{8,12},{12,8},{9,1... | collective-permute-start | bytes 1572872 | tf_op jit(solution)/shard_map/ppermute | solution.py:21
  692.7 37.4 %collective-permute-start.140 = (bf16[256,256]{0,1:T(8,128)(2,1)S(1)}, bf16[256,256]{0,1:T(8,128)(2,1)S(1)}, u32[]{:S(2)}, u32[]{:S(2)}) collective-permute-start(bf16[256,256]{0,1:T(8,128)(2,1)S(1)} %bitcast.203), channel_id=1, source_target_pairs={{0,4},{1,0},{2,12},{3,8},{4,20},{5,16},{6,28},{7,24},{8,5},{9,1},{... | collective-permute-start | bytes 393224 | tf_op jit(solution)/shard_map/ppermute | solution.py:552
  708.7 32.7 %collective-permute-start.113 = (bf16[1024,256]{1,0:T(8,128)(2,1)}, bf16[1024,256]{1,0:T(8,128)(2,1)}, u32[]{:S(2)}, u32[]{:S(2)}) collective-permute-start(bf16[1024,256]{1,0:T(8,128)(2,1)} %add_convert_fusion.7), channel_id=1, source_target_pairs={{0,2},{2,0},{1,3},{3,1},{4,6},{6,4},{5,7},{7,5},{8,10},{10,8},{9,1... | collective-permute-start | bytes 1572872 | tf_op jit(solution)/shard_map/ppermute | solution.py:21
  730.1 119.6 %collective-permute-start.101 = (bf16[128,2048]{1,0:T(8,128)(2,1)}, bf16[128,2048]{1,0:T(8,128)(2,1)}, u32[]{:S(2)}, u32[]{:S(2)}) collective-permute-start(bf16[128,2048]{1,0:T(8,128)(2,1)} %slice.861), channel_id=1, source_target_pairs={{0,1},{1,0},{2,3},{3,2},{4,5},{5,4},{6,7},{7,6},{8,9},{9,8},{10,11... | collective-permute-start | bytes 1572872 | tf_op jit(solution)/shard_map/ppermute | solution.py:21
  730.1 29.5 %collective-permute-start.103 = (bf16[128,2048]{1,0:T(8,128)(2,1)}, bf16[128,2048]{1,0:T(8,128)(2,1)S(1)}, u32[]{:S(2)}, u32[]{:S(2)}) collective-permute-start(bf16[128,2048]{1,0:T(8,128)(2,1)} %slice.859), channel_id=1, source_target_pairs={{0,1},{1,0},{2,3},{3,2},{4,5},{5,4},{6,7},{7,6},{8,9},{9,8},{10,11... | collective-permute-start | bytes 1572872 | tf_op jit(solution)/shard_map/ppermute | solution.py:21
  731.4 59.6 %collective-permute-start.102 = (bf16[128,2048]{1,0:T(8,128)(2,1)}, bf16[128,2048]{1,0:T(8,128)(2,1)S(1)}, u32[]{:S(2)}, u32[]{:S(2)}) collective-permute-start(bf16[128,2048]{1,0:T(8,128)(2,1)} %slice.860), channel_id=1, source_target_pairs={{0,1},{1,0},{2,3},{3,2},{4,5},{5,4},{6,7},{7,6},{8,9},{9,8},{10,11... | collective-permute-start | bytes 1572872 | tf_op jit(solution)/shard_map/ppermute | solution.py:21
  787.1 52.1 %collective-permute-start.116 = (bf16[128,2048]{1,0:T(8,128)(2,1)}, bf16[128,2048]{1,0:T(8,128)(2,1)}, u32[]{:S(2)}, u32[]{:S(2)}) collective-permute-start(bf16[128,2048]{1,0:T(8,128)(2,1)} %slice.855), channel_id=1, source_target_pairs={{0,1},{1,0},{2,3},{3,2},{4,5},{5,4},{6,7},{7,6},{8,9},{9,8},{10,11... | collective-permute-start | bytes 1572872 | tf_op jit(solution)/shard_map/ppermute | solution.py:21
  795.3 33.9 %collective-permute-start.135 = (bf16[256,256]{0,1:T(8,128)(2,1)}, bf16[256,256]{0,1:T(8,128)(2,1)S(1)}, u32[]{:S(2)}, u32[]{:S(2)}) collective-permute-start(bf16[256,256]{0,1:T(8,128)(2,1)} %bitcast.204), channel_id=1, source_target_pairs={{0,4},{1,0},{2,12},{3,8},{4,20},{5,16},{6,28},{7,24},{8,5},{9,1},{... | collective-permute-start | bytes 393224 | tf_op jit(solution)/shard_map/ppermute | solution.py:552
  801.6 29.3 %collective-permute-start.134 = (bf16[256,256]{0,1:T(8,128)(2,1)S(1)}, bf16[256,256]{0,1:T(8,128)(2,1)S(1)}, u32[]{:S(2)}, u32[]{:S(2)}) collective-permute-start(bf16[256,256]{0,1:T(8,128)(2,1)S(1)} %bitcast.207), channel_id=1, source_target_pairs={{0,0},{1,4},{2,8},{3,12},{4,16},{5,20},{6,24},{7,28},{8,1},{9,5},{... | collective-permute-start | bytes 393224 | tf_op jit(solution)/shard_map/ppermute | solution.py:552
  802.3 37.7 %collective-permute-start.118 = (bf16[128,2048]{1,0:T(8,128)(2,1)}, bf16[128,2048]{1,0:T(8,128)(2,1)S(1)}, u32[]{:S(2)}, u32[]{:S(2)}) collective-permute-start(bf16[128,2048]{1,0:T(8,128)(2,1)} %fusion.24), channel_id=1, source_target_pairs={{0,8},{8,16},{16,24},{24,0},{1,9},{9,17},{17,25},{25,1},{2,10},{10... | collective-permute-start | bytes 1572872 | tf_op jit(solution)/shard_map/ppermute | solution.py:21
  829.2 41.2 %collective-permute-start.114 = (bf16[128,2048]{1,0:T(8,128)(2,1)}, bf16[128,2048]{1,0:T(8,128)(2,1)}, u32[]{:S(2)}, u32[]{:S(2)}) collective-permute-start(bf16[128,2048]{1,0:T(8,128)(2,1)} %slice.857), channel_id=1, source_target_pairs={{0,1},{1,0},{2,3},{3,2},{4,5},{5,4},{6,7},{7,6},{8,9},{9,8},{10,11... | collective-permute-start | bytes 1572872 | tf_op jit(solution)/shard_map/ppermute | solution.py:21
  830.9 27.0 %collective-permute-start.115 = (bf16[128,2048]{1,0:T(8,128)(2,1)}, bf16[128,2048]{1,0:T(8,128)(2,1)}, u32[]{:S(2)}, u32[]{:S(2)}) collective-permute-start(bf16[128,2048]{1,0:T(8,128)(2,1)} %slice.856), channel_id=1, source_target_pairs={{0,1},{1,0},{2,3},{3,2},{4,5},{5,4},{6,7},{7,6},{8,9},{9,8},{10,11... | collective-permute-start | bytes 1572872 | tf_op jit(solution)/shard_map/ppermute | solution.py:21
  (181 other events, 2749.5 us)
Sparse Core Ops, SparseCore 0:
  886.0 132.0 reduce-scatter.3

commit v2 on v1

v2 whole, which is shorter than its diff:
```python
import math

import jax
import jax.numpy as jnp
from jax import lax
from jax.experimental import pallas as pl
from jax.experimental.pallas import tpu as pltpu
from jax.sharding import Mesh, PartitionSpec as P

HD = 128
EPSILON = 1e-06
LOW = jnp.bfloat16
HIGH = jnp.float32
LOG2E = math.log2(math.e)
SCORE_SCALE = HD ** (-0.5)
ALL = ("z", "x", "y", "c")


def add_low(first, second):
    return (first.astype(HIGH) + second.astype(HIGH)).astype(LOW)


def after(values, *earlier):
    return lax.optimization_barrier((values, earlier))[0]


def hop(values, axis, steps=1):
    size = lax.axis_size(axis)
    return lax.ppermute(values, axis, [(i, (i + steps) % size) for i in range(size)])


def gather_task(first, second):
    size = lax.axis_size("x")
    firsts, seconds, first_over, second_over = [first], [second], [], []
    for stage in range(size):
        wanted = [("y", firsts[stage], first_over)]
        if stage == 0:
            wanted.append(("y", second, second_over))
        if stage < size - 1:
            wanted += [("x", firsts[stage], firsts), ("x", seconds[stage], seconds)]
        if stage:
            wanted.append(("x", second_over[stage - 1], second_over))
        yield wanted
    return (
        [piece for pair in zip(firsts, first_over) for piece in pair],
        [piece for pair in zip(seconds, second_over) for piece in pair],
    )


def sum_task(first, second):
    size = lax.axis_size("x")
    got, far, near = [], [], []
    over = [[] for _ in range(size)]
    far_total, near_total = second[3], second[2]
    for step in range(1, size):
        wanted = [("x", far_total, far), ("x", near_total, near)]
        if step == 1:
            wanted += [("y", first[2 * s + 1], over[s]) for s in range(1, size)]
            wanted.append(("y", first[1], over[0]))
        yield wanted
        at = 2 * ((step + 1) % size)
        far_total, near_total = add_low(second[at + 1], far[-1]), add_low(second[at], near[-1])
    merged = [add_low(first[2 * s], over[s][0]) for s in range(size)]
    total = merged[1]
    for step in range(1, size):
        wanted = [("x", total, got)]
        if step == 1:
            wanted.append(("y", far_total, far))
        yield wanted
        total = add_low(merged[(step + 1) % size], got[-1])
    return total, add_low(near_total, far[-1])


class Ticks:
    BYTES = 9 * 2**16

    def __init__(self):
        self.tasks = []
        self.over_z = ()
        self.sides = [(), ()]
        self.sent = None

    def add(self, task):
        entry = {"task": task, "wanted": None, "open": 0, "result": None}
        self.tasks.append(entry)
        self.advance(entry)
        return entry

    def advance(self, entry):
        try:
            entry["wanted"] = list(next(entry["task"]))
            entry["open"] = len(entry["wanted"])
        except StopIteration as stop:
            entry["result"] = stop.value
            self.tasks.remove(entry)

    def tick(self, *moves, room=1):
        got = []
        for values, steps in moves:
            self.sent = after(values, self.over_z, self.sides[-2])
            got.append(hop(self.sent, "z", steps))
        left = {"x": room * self.BYTES, "y": room * self.BYTES}
        arrived = []
        finished = []
        for entry in self.tasks:
            later = []
            for axis, values, into in entry["wanted"]:
                if left[axis] >= min(values.nbytes, self.BYTES):
                    left[axis] -= values.nbytes
                    into.append(hop(after(values, self.sides[-1]), axis))
                    arrived.append(into[-1])
                    entry["open"] -= 1
                else:
                    later.append((axis, values, into))
            entry["wanted"] = later
            if not entry["open"]:
                finished.append(entry)
        self.over_z = tuple(got) or self.over_z
        self.sides = self.sides[-1:] + [tuple(arrived)]
        for entry in finished:
            self.advance(entry)
        return got

    def finish(self, *entries):
        while any(entry["result"] is None for entry in entries):
            self.tick()
        return [entry["result"] for entry in entries]

    def gather_rows(self, rows):
        blocks = [rows]
        for _ in range(1, lax.axis_size("z")):
            blocks += self.tick((blocks[-1], 1))
        return self.both_cores(blocks)

    def both_cores(self, blocks):
        blocks = blocks[1:] + blocks[:1]
        return jnp.concatenate(blocks + [hop(block, "c") for block in blocks], axis=0)


class RowSum:
    def __init__(self, ticks, terms_of, inputs, rows_local):
        self.ticks = ticks
        self.rows = rows_local
        self.half = inputs[0].shape[0] // 2
        self.terms_of = terms_of
        self.inputs = inputs
        self.count = 0
        self.total = self.terms(inputs, 0, 1)[0].astype(LOW)

    def terms(self, inputs, start, stop):
        start, stop = start * self.rows, stop * self.rows
        far = self.terms_of(*(v[self.half + start : self.half + stop] for v in inputs))
        near = self.terms_of(*(v[start:stop] for v in inputs))
        got = hop(far.astype(LOW), "c").astype(HIGH)
        return [
            near[at : at + self.rows] + got[at : at + self.rows]
            for at in range(0, stop - start, self.rows)
        ]

    def step(self):
        (got,) = self.ticks.tick((self.total, 1))
        self.sent = self.ticks.sent
        if not self.count:
            inputs = after(tuple(self.inputs), self.sent)
            self.rest = self.terms(inputs, 1, lax.axis_size("z"))
        self.total = self.rest[self.count] + got.astype(HIGH)
        self.count += 1
        if self.count < len(self.rest):
            self.total = self.total.astype(LOW)
        return got

    def finish(self):
        while self.count < 3:
            self.step()
        return self.total


def place_blocks(pieces, places, widths):
    count, rows, width = pieces[0].shape
    total = len(pieces) * count

    def kernel(place_ref, *refs):
        ins, outs = refs[: len(pieces)], refs[len(pieces) :]
        for at in range(total):
            start = 0
            for out, size in zip(outs, widths):
                out[place_ref[at]] = ins[at // count][at % count, :, start : start + size]
                start += size

    shapes = [(total, rows, size) for size in widths]
    placed = pl.pallas_call(
        kernel,
        out_shape=[jax.ShapeDtypeStruct(shape, pieces[0].dtype) for shape in shapes],
        grid_spec=pltpu.PrefetchScalarGridSpec(
            num_scalar_prefetch=1,
            grid=(1,),
            in_specs=[pl.BlockSpec((count, rows, width), lambda i, *_: (0, 0, 0))] * len(pieces),
            out_specs=[pl.BlockSpec(shape, lambda i, *_: (0, 0, 0)) for shape in shapes],
        ),
        compiler_params=pltpu.CompilerParams(vmem_limit_bytes=48 * 2**20),
        cost_estimate=pl.CostEstimate(
            flops=0, bytes_accessed=4 * total * rows * width, transcendentals=0
        ),
        name="place_blocks",
    )(places, *pieces)
    return [out.reshape(total * rows, -1) for out in placed]


def normalize(values, gain_vec):
    factor = lax.rsqrt(jnp.mean(values * values, axis=-1, keepdims=True) + EPSILON)
    plain_rows = values * factor
    return (plain_rows, factor, plain_rows * gain_vec)


def norm_backward(grad_normed, plain_rows, factor, gain_vec):
    scaled = grad_normed * gain_vec
    gain_part = jnp.sum(grad_normed * plain_rows, axis=0)
    grad_input = factor * (
        scaled - plain_rows * jnp.mean(scaled * plain_rows, axis=-1, keepdims=True)
    )
    return (gain_part, grad_input)


def matmul(left_side, right_side):
    return jnp.dot(left_side, right_side, preferred_element_type=HIGH)


def matmul_right_t(left_side, right_side):
    return lax.dot_general(
        left_side, right_side, (((1,), (1,)), ((), ())), preferred_element_type=HIGH
    )


def matmul_left_t(left_side, right_side):
    return lax.dot_general(
        left_side, right_side, (((0,), (0,)), ((), ())), preferred_element_type=HIGH
    )


def pad_units(rows):
    extra = -rows.shape[0] % 16
    return jnp.pad(rows, ((0, extra), (0, 0)))


def quarters(count):
    tiles = count // 16
    return [16 * (tiles * i // 4) for i in range(5)]


def diagonal_visible(core, span_rows, key_axis):
    half = span_rows // 2

    def place(axis):
        index = lax.broadcasted_iota(jnp.int32, (span_rows, span_rows), axis)
        flipped = jnp.where(index < half, index + half, index - half)
        return jnp.where(core == 0, index, flipped)

    return place(key_axis) <= place(1 - key_axis)


def forward_kernel(
    place_ref, rank_ref, core_ref, query_ref, key_ref, value_ref, mixed_ref, lse_ref, score_ref
):
    half_rows = query_ref.shape[1]
    span_rows = 2 * half_rows
    heads = query_ref.shape[2] // HD
    rank = rank_ref[pl.program_id(1)]
    columns = [slice(h * HD, (h + 1) * HD) for h in range(heads)]

    def span(ref, step, h):
        side = place_ref[step] // 4
        start = pl.multiple_of((place_ref[step] % 4) * half_rows, half_rows)
        return ref[side, :, pl.ds(start, half_rows), columns[h]].reshape(span_rows, HD)

    def block_scores(step, h):
        query = query_ref[:, :, columns[h]].reshape(span_rows, HD)
        return matmul_right_t(query, span(key_ref, step, h)) * (SCORE_SCALE * LOG2E)

    def fold(values, operation):
        folded = values[:, :HD]
        for at in range(HD, span_rows, HD):
            folded = operation(folded, values[:, at : at + HD])
        return folded

    def score_step(step, maxima, count):
        new = []
        for h in range(heads):
            top = maxima[h]
            for at in range(count):
                scores = block_scores(step + at, h)
                score_ref[h, step + at] = scores
                top = jnp.maximum(top, fold(scores, jnp.maximum))
            new.append(top)
        return tuple(new)

    maxima = tuple(jnp.full((span_rows, HD), -jnp.inf, HIGH) for _ in range(heads))
    maxima = lax.fori_loop(0, rank // 2, lambda p, m: score_step(2 * p, m, 2), maxima)
    maxima = lax.fori_loop(rank // 2 * 2, rank, lambda p, m: score_step(p, m, 1), maxima)
    visible = diagonal_visible(core_ref[0], span_rows, 1)
    tops = []
    for h in range(heads):
        scores = jnp.where(visible, block_scores(rank, h), -jnp.inf)
        score_ref[h, rank] = scores
        top = jnp.maximum(maxima[h], fold(scores, jnp.maximum))
        tops.append(jnp.max(top, axis=1, keepdims=True))

    def mix_step(step, running, count):
        new = []
        for h in range(heads):
            total, mixed = running[h]
            for at in range(count):
                weights = jnp.exp2(score_ref[h, step + at] - tops[h])
                total = total + fold(weights, jnp.add)
                mixed = mixed + matmul(weights.astype(LOW), span(value_ref, step + at, h))
            new.append((total, mixed))
        return tuple(new)

    zero = jnp.zeros((span_rows, HD), HIGH)
    sums = tuple((zero, zero) for _ in range(heads))
    blocks = rank + 1
    sums = lax.fori_loop(0, blocks // 2, lambda p, r: mix_step(2 * p, r, 2), sums)
    sums = lax.fori_loop(blocks // 2 * 2, blocks, lambda p, r: mix_step(p, r, 1), sums)
    for h in range(heads):
        total = jnp.sum(sums[h][0], axis=1, keepdims=True)
        mixed = (sums[h][1] / total).astype(LOW)
        mixed_ref[:, :, columns[h]] = mixed.reshape(2, half_rows, HD)
        lse = jnp.broadcast_to(tops[h] + jnp.log2(total), (span_rows, HD))
        lse_ref[h] = jnp.transpose(lse)[:8, :]


def backward_kernel(
    place_ref,
    rank_ref,
    core_ref,
    query_ref,
    grad_ref,
    mixed_ref,
    lse_ref,
    key_ref,
    value_ref,
    grad_query_ref,
    grad_key_ref,
    grad_value_ref,
    key_sum_ref,
    value_sum_ref,
):
    heads = query_ref.shape[2] // HD
    half_rows = query_ref.shape[1] // rank_ref.shape[0]
    span_rows = 2 * half_rows
    columns = [slice(h * HD, (h + 1) * HD) for h in range(heads)]
    key_sum_ref[...] = jnp.zeros_like(key_sum_ref)
    value_sum_ref[...] = jnp.zeros_like(value_sum_ref)

    def query_span(at, carry):
        here = pl.ds(pl.multiple_of(at * half_rows, half_rows), half_rows)
        lanes = pl.ds(pl.multiple_of(at * span_rows, span_rows), span_rows)
        rank = rank_ref[at]

        def own(ref, h):
            return ref[:, here, columns[h]].reshape(span_rows, HD)

        delta = []
        lse = []
        for h in range(heads):
            product = own(grad_ref, h).astype(HIGH) * own(mixed_ref, h).astype(HIGH)
            delta.append(jnp.sum(jnp.transpose(product), axis=0, keepdims=True))
            lse.append(lse_ref[h, :1, lanes])

        def block(step, grad_query, visible):
            side = place_ref[step] // 4
            start = pl.multiple_of((place_ref[step] % 4) * half_rows, half_rows)
            there = pl.ds(start, half_rows)
            new = []
            for h in range(heads):
                query = own(query_ref, h)
                grad = own(grad_ref, h)
                keys = key_ref[side, :, there, columns[h]].reshape(span_rows, HD)
                values = value_ref[side, :, there, columns[h]].reshape(span_rows, HD)
                scores = matmul_right_t(keys, query) * (SCORE_SCALE * LOG2E)
                weights = jnp.exp2(scores - lse[h])
                if visible is not None:
                    weights = jnp.where(visible, weights, 0.0)
                grad_weights = matmul_right_t(values, grad)
                grad_scores = (weights * (grad_weights - delta[h])).astype(LOW)
                value_term = matmul(weights.astype(LOW), grad)
                key_term = matmul(grad_scores, query)
                value_sum_ref[side, :, there, columns[h]] += value_term.reshape(2, half_rows, HD)
                key_sum_ref[side, :, there, columns[h]] += key_term.reshape(2, half_rows, HD)
                new.append(grad_query[h] + matmul_left_t(grad_scores, keys))
            return tuple(new)

        start = tuple(jnp.zeros((span_rows, HD), HIGH) for _ in range(heads))
        grad_query = lax.fori_loop(
            0, rank // 2, lambda p, g: block(2 * p + 1, block(2 * p, g, None), None), start
        )
        grad_query = lax.fori_loop(
            rank // 2 * 2, rank, lambda p, g: block(p, g, None), grad_query
        )
        visible = diagonal_visible(core_ref[0], span_rows, 0)
        grad_query = block(rank, grad_query, visible)
        for h in range(heads):
            result = (grad_query[h] * SCORE_SCALE).astype(LOW)
            grad_query_ref[:, here, columns[h]] = result.reshape(2, half_rows, HD)
        return carry

    lax.fori_loop(0, rank_ref.shape[0], query_span, 0)
    grad_key_ref[...] = (key_sum_ref[...] * SCORE_SCALE).astype(LOW)
    grad_value_ref[...] = value_sum_ref[...].astype(LOW)


def heads_at_once(key_rows, features):
    return features // HD if key_rows <= 4096 else 1


def attention_forward(scalars, queries, keys, values):
    rows, features = queries.shape
    key_rows = keys.shape[0]
    own_spans = scalars[1].shape[0]
    half_rows = rows // own_spans // 2
    span_rows = 2 * half_rows
    heads = heads_at_once(key_rows, features)
    width = heads * HD
    pairs = rows * key_rows * features
    sides = key_rows // rows
    own = pl.BlockSpec((2, half_rows, width), lambda h, i, *_: (0, i, h))
    other = pl.BlockSpec((sides, 2, rows // 2, width), lambda h, i, *_: (0, 0, 0, h))
    mixed, lse = pl.pallas_call(
        forward_kernel,
        out_shape=(
            jax.ShapeDtypeStruct((2, rows // 2, features), LOW),
            jax.ShapeDtypeStruct((features // HD, 8, rows), HIGH),
        ),
        grid_spec=pltpu.PrefetchScalarGridSpec(
            num_scalar_prefetch=3,
            grid=(features // width, own_spans),
            in_specs=[own, other, other],
            out_specs=[own, pl.BlockSpec((heads, 8, span_rows), lambda h, i, *_: (h, 0, i))],
            scratch_shapes=[
                pltpu.VMEM((heads, key_rows // span_rows, span_rows, span_rows), HIGH)
            ],
        ),
        compiler_params=pltpu.CompilerParams(vmem_limit_bytes=56 * 2**20),
        cost_estimate=pl.CostEstimate(
            flops=2 * pairs, bytes_accessed=4 * key_rows * features, transcendentals=pairs // 256
        ),
        name="attention_forward",
    )(
        *scalars,
        queries.reshape(2, rows // 2, features),
        keys.reshape(sides, 2, rows // 2, features),
        values.reshape(sides, 2, rows // 2, features),
    )
    return mixed.reshape(rows, features), lse


def attention_backward(scalars, head, queries, grads, mixed, lse, keys, values):
    rows, features = queries.shape
    key_rows = keys.shape[0]
    pairs = rows * key_rows * HD
    sides = key_rows // rows
    own_shape = (2, rows // 2, features)
    key_shape = (sides, 2, rows // 2, features)
    own_part, key_part = own_shape[:2] + (HD,), key_shape[:3] + (HD,)
    own = pl.BlockSpec(own_part, lambda i, *_: (0, 0, head))
    other = pl.BlockSpec(key_part, lambda i, *_: (0, 0, 0, head))
    own_out = pl.BlockSpec(own_part, lambda i, *_: (0, 0, 0))
    other_out = pl.BlockSpec(key_part, lambda i, *_: (0, 0, 0, 0))
    grad_queries, grad_keys, grad_values = pl.pallas_call(
        backward_kernel,
        out_shape=(
            jax.ShapeDtypeStruct(own_part, LOW),
            jax.ShapeDtypeStruct(key_part, LOW),
            jax.ShapeDtypeStruct(key_part, LOW),
        ),
        grid_spec=pltpu.PrefetchScalarGridSpec(
            num_scalar_prefetch=3,
            grid=(1,),
            in_specs=[
                own,
                own,
                own,
                pl.BlockSpec((1, 8, rows), lambda i, *_: (head, 0, 0)),
                other,
                other,
            ],
            out_specs=[own_out, other_out, other_out],
            scratch_shapes=[pltpu.VMEM(key_part, HIGH)] * 2,
        ),
        compiler_params=pltpu.CompilerParams(vmem_limit_bytes=56 * 2**20),
        cost_estimate=pl.CostEstimate(
            flops=5 * pairs, bytes_accessed=8 * key_rows * HD, transcendentals=pairs // 256
        ),
        name="attention_backward",
    )(
        *scalars,
        queries.reshape(own_shape),
        grads.reshape(own_shape),
        mixed.reshape(own_shape),
        lse,
        keys.reshape(key_shape),
        values.reshape(key_shape),
    )
    return (
        grad_queries.reshape(rows, HD),
        grad_keys.reshape(key_rows, HD),
        grad_values.reshape(key_rows, HD),
    )


def per_device(
    states,
    shared_kv,
    norm_gain,
    kv_gain,
    ffn_gain,
    query_weight,
    key_weight,
    value_weight,
    out_weight,
    gate_weight,
    up_weight,
    down_weight,
    span_order,
    grad_output,
):
    z, x, y, c = (lax.axis_index(name) for name in ALL)
    size_x = lax.axis_size("x")
    sides = 2 * size_x
    rows_local, width_model = states.shape
    weight_rows = query_weight.shape[0]
    units_local = gate_weight.shape[1]
    own_width = width_model // 8

    side = jnp.arange(sides, dtype=jnp.int32)
    side_owner = jnp.mod(x - side // 2, size_x) * 2 + jnp.bitwise_xor(y, side % 2)
    back = jnp.mod(jnp.arange(4, dtype=jnp.int32) + 1, 4)
    back_owner = jnp.mod(z - back, 4)

    ticks = Ticks()

    block = jnp.arange(8 * sides, dtype=jnp.int32)
    block_half, block_side = block // (4 * sides), block // 4 % sides
    block_back = 2 * block_half + block // 2 % 2
    block_place = (
        (jnp.mod(z - block_back, 4) * size_x + jnp.mod(x - block_side // 2, size_x)) * 2
        + jnp.bitwise_xor(y, block_side % 2)
    ) * 2 + jnp.bitwise_xor(c, block % 2)

    state_rows = states.astype(HIGH)
    shared_rows = shared_kv.astype(HIGH)
    plain_kv, factor_kv, normed_kv = normalize(shared_rows, kv_gain)
    plain_one, factor_one, normed_one = normalize(state_rows, norm_gain)
    shared_low = normed_kv.astype(LOW)
    normed_low = normed_one.astype(LOW)

    with jax.named_scope("weight_columns"):
        pair = 2 * own_width
        stacked = jnp.stack([key_weight, value_weight, query_weight], axis=1)
        cut = [
            lax.dynamic_slice_in_dim(stacked, jnp.mod(z + step, 4) * pair, pair, 2)
            for step in range(4)
        ]
        shared_next, *over = ticks.tick((shared_low, 1), (cut[1], 1), (cut[2], 2), (cut[3], 3))
        columns = []
        for part in [cut[0]] + over:
            keep = lax.dynamic_slice_in_dim(part, c * own_width, own_width, 2)
            give = lax.dynamic_slice_in_dim(part, (1 - c) * own_width, own_width, 2)
            columns += [keep, hop(give, "c")]
        columns = jnp.stack(columns).reshape(8, weight_rows, 3 * own_width)
    with jax.named_scope("shared_rows"):
        weight_task = ticks.add(gather_task(columns[:4], columns[4:]))
        shared_blocks = [shared_low, shared_next]
        for _ in range(2):
            shared_blocks += ticks.tick((shared_blocks[-1], 1))
        group_shared = ticks.both_cores(shared_blocks)
    with jax.named_scope("weight_columns"):
        first, second = ticks.finish(weight_task)[0]
        weight_kv, weight_query = place_blocks(
            first + second, block_place, (2 * own_width, own_width)
        )
    with jax.named_scope("keys_values"):
        keys_own = matmul(group_shared, weight_kv[:, :own_width]).astype(LOW)
        values_own = matmul(group_shared, weight_kv[:, own_width:]).astype(LOW)
        keys_task = ticks.add(gather_task(keys_own, values_own))
    with jax.named_scope("out_weight"):
        out_task = ticks.add(
            gather_task(out_weight[: weight_rows // 2], out_weight[weight_rows // 2 :])
        )
    with jax.named_scope("normed_rows"):
        group_normed = ticks.gather_rows(normed_low)
        queries = matmul(group_normed, weight_query).astype(LOW)
    with jax.named_scope("grad_output_rows"):
        grad_back, grad_ahead = ticks.tick((grad_output, 1), (grad_output, -1))
    with jax.named_scope("keys_values"):
        ((keys_all, values_all),) = ticks.finish(keys_task)
        keys_all, values_all = jnp.concatenate(keys_all), jnp.concatenate(values_all)

    span_of = (back_owner[None, :] * sides + side_owner[:, None]).reshape(-1)
    ranks = jnp.take(span_order, span_of)
    spans = span_order.shape[0]
    listed = jnp.arange(spans, dtype=jnp.int32)
    place = jnp.sum(jnp.where(ranks[None, :] == listed[:, None], listed[None, :], 0), axis=1)
    scalars = (place, ranks[:4], c.reshape(1).astype(jnp.int32))

    with jax.named_scope("unit_weights"):
        late = (keys_all, values_all)
        unit_rows = jnp.concatenate(
            [
                pad_units(jnp.transpose(after(gate_weight, *late))),
                pad_units(jnp.transpose(after(up_weight, *late))),
                pad_units(after(down_weight, *late)),
            ],
            axis=0,
        )
        cuts = quarters(unit_rows.shape[0])
        chunks = [unit_rows[cuts[i] : cuts[i + 1]] for i in range(4)]
        unit_tasks = [ticks.add(gather_task(chunks[i], chunks[i + 1])) for i in (0, 2)]
    with jax.named_scope("grad_output_rows"):
        (grad_far,) = ticks.tick((grad_back, 1), room=2)
        group_grad = ticks.both_cores([grad_output, grad_back, grad_far, grad_ahead])
    mixed, lse = attention_forward(scalars, queries, keys_all, values_all)

    with jax.named_scope("out_weight"):
        whole = jnp.arange(sides, dtype=jnp.int32)
        whole_side = jnp.mod(x - whole // 2, size_x) * 2 + jnp.bitwise_xor(y, whole % 2)
        out_pieces = [
            part for pair in zip(*ticks.finish(out_task)[0]) for part in pair
        ]
        out_pieces = jnp.stack(out_pieces).reshape(sides, weight_rows, width_model)
        out_pieces = jnp.take(out_pieces, whole_side, axis=0).reshape(
            2, size_x // 2, 2, weight_rows, width_model
        )
        out_keep = lax.dynamic_index_in_dim(out_pieces, c, 0, keepdims=False)
        out_give = lax.dynamic_index_in_dim(out_pieces, 1 - c, 0, keepdims=False)
        out_got = hop(out_give, "c")
        weight_out = jnp.where(
            c == 0, jnp.stack([out_keep, out_got], axis=2), jnp.stack([out_got, out_keep], axis=2)
        ).reshape(own_width, width_model)

    with jax.named_scope("attention_sum"):
        attention_sum = RowSum(ticks, lambda v: matmul(v, weight_out), [mixed], rows_local)
        residual = state_rows + attention_sum.finish()
    plain_two, factor_two, normed_two = normalize(residual, ffn_gain)
    with jax.named_scope("normed_two_rows"):
        group_in = ticks.gather_rows(normed_two.astype(LOW))
    with jax.named_scope("unit_weights"):
        gathered = [pieces for result in ticks.finish(*unit_tasks) for pieces in result]
        units_padded = unit_rows.shape[0] // 3

        def units_of(which):
            low, high = which * units_padded, (which + 1) * units_padded
            rows = []
            for s in range(sides):
                for i in range(4):
                    start, stop = max(low, cuts[i]), min(high, cuts[i + 1])
                    if start < stop:
                        rows.append(gathered[i][s][start - cuts[i] : stop - cuts[i]])
            return jnp.concatenate(rows, axis=0)

        weight_gate, weight_up, weight_down = (units_of(which) for which in range(3))

    gate_act = matmul_right_t(group_in, weight_gate)
    up_act = matmul_right_t(group_in, weight_up)
    grad_hidden = matmul_right_t(group_grad, weight_down)
    sigmoid = jax.nn.sigmoid(gate_act)
    silu_act = gate_act * sigmoid
    hidden = (silu_act * up_act).astype(LOW)
    grad_gate_act = (
        grad_hidden * up_act * sigmoid * (1.0 + gate_act * (1.0 - sigmoid))
    ).astype(LOW)
    grad_up_act = (grad_hidden * silu_act).astype(LOW)
    with jax.named_scope("ffn_grad_sum"):
        ffn_grad_sum = RowSum(
            ticks,
            lambda g, u: matmul(g, weight_gate) + matmul(u, weight_up),
            [grad_gate_act, grad_up_act],
            rows_local,
        )
        ffn_grad_sum.step()
        ffn_grad_sum.step()
        sent = ffn_grad_sum.sent

    def unit_parts(values):
        step = values.shape[0] // sides
        return [values[s * step : (s + 1) * step] for s in range(sides)]

    with jax.named_scope("unit_weight_sums"):
        unit_terms = [
            unit_parts(matmul_left_t(after(left, sent), right).astype(LOW))
            for left, right in (
                (grad_gate_act, group_in),
                (grad_up_act, group_in),
                (hidden, group_grad),
            )
        ]

        def chunk_parts(i):
            parts = []
            for s in range(sides):
                rows = []
                for which in range(3):
                    low = which * units_padded
                    start, stop = max(low, cuts[i]), min(low + units_padded, cuts[i + 1])
                    if start < stop:
                        rows.append(unit_terms[which][s][start - low : stop - low])
                parts.append(jnp.concatenate(rows, axis=0))
            return parts

        unit_sum_tasks = [
            ticks.add(sum_task(chunk_parts(i), chunk_parts(i + 1))) for i in (0, 2)
        ]

    with jax.named_scope("ffn_grad_sum"):
        grad_ffn = ffn_grad_sum.finish()
    gain_two, grad_norm_two = norm_backward(grad_ffn, plain_two, factor_two, ffn_gain)
    grad_residual = grad_output.astype(HIGH) + grad_norm_two
    with jax.named_scope("branch_rows"):
        group_branch = ticks.gather_rows(grad_residual.astype(LOW))
    grad_mixed = matmul_right_t(group_branch, weight_out).astype(LOW)
    with jax.named_scope("ffn_sum"):
        ffn_sum = RowSum(
            ticks,
            lambda v: matmul(v, weight_down),
            [after(hidden, grad_residual)],
            rows_local,
        )
    head_terms = []
    key_tasks = []
    backward_inputs = (queries, grad_mixed, mixed)
    for head in range(own_width // HD):
        if ffn_sum.count < 2:
            with jax.named_scope("ffn_sum"):
                backward_inputs = after(backward_inputs, ticks.over_z)
                ffn_sum.step()
        terms = attention_backward(
            scalars, head, *after(backward_inputs, ffn_sum.sent), lse, keys_all, values_all
        )
        head_terms.append(terms[0])
        with jax.named_scope("grad_keys_values"):
            key_tasks.append(ticks.add(sum_task(unit_parts(terms[1]), unit_parts(terms[2]))))
    grad_queries = jnp.concatenate(head_terms, axis=1)

    def side_parts(values, k):
        chunks = values.reshape(2 * sides, -1, values.shape[1])
        return [
            lax.dynamic_index_in_dim(
                chunks,
                2 * jnp.bitwise_xor(jnp.bitwise_xor(side_owner[s], z), 2 * k) + k,
                0,
                keepdims=False,
            )
            for s in range(sides)
        ]

    def chunk_sums(values):
        return sum_task(side_parts(values, 0), side_parts(values, 1))

    to_layout = [
        [
            (
                ((za * size_x + xa) * 2 + ya) * 2 + ca,
                (2 * ((2 * xa + ya) ^ za ^ (2 * (ca ^ flip))) + (ca ^ flip)) * 4 + za,
            )
            for za in range(4)
            for xa in range(size_x)
            for ya in range(2)
            for ca in range(2)
        ]
        for flip in range(2)
    ]

    def layout(summed):
        sent = jnp.where(c == 0, summed[0], summed[1]), jnp.where(c == 0, summed[1], summed[0])
        got = [lax.ppermute(sent[flip], ALL, to_layout[flip]) for flip in range(2)]
        even = x % 2 == 0
        first = jnp.where(even, got[0], got[1]).astype(HIGH)
        second = jnp.where(even, got[1], got[0]).astype(HIGH)
        return [
            jnp.concatenate([part[:, at : at + own_width] for part in (first, second)], axis=1)
            for at in range(0, first.shape[1], own_width)
        ]

    with jax.named_scope("normed_sum"):
        normed_sum = RowSum(
            ticks, lambda v: matmul_right_t(v, weight_query), [grad_queries], rows_local
        )
        normed_sum.step()
        sent = normed_sum.sent
    with jax.named_scope("query_weight_sum"):
        query_terms = matmul_left_t(after(group_normed, sent), grad_queries).astype(LOW)
    with jax.named_scope("out_weight_sum"):
        out_terms = matmul_left_t(after(group_branch, sent), mixed).astype(LOW)
    with jax.named_scope("normed_sum"):
        grad_normed = normed_sum.finish()
    with jax.named_scope("ffn_sum"):
        output = (residual + ffn_sum.finish()).astype(LOW)
    with jax.named_scope("grad_keys_values"):
        parts = ticks.finish(*key_tasks)
        grad_kv = jnp.concatenate(
            [part[0] for part in parts] + [part[1] for part in parts], axis=1
        )
    with jax.named_scope("query_out_weight_sum"):
        query_out_task = ticks.add(
            chunk_sums(jnp.concatenate([query_terms, out_terms], axis=1))
        )
    with jax.named_scope("shared_sum"):
        shared_sum = RowSum(
            ticks, lambda v: matmul_right_t(v, weight_kv), [grad_kv], rows_local
        )
        shared_sum.step()
        sent = shared_sum.sent
    with jax.named_scope("key_value_weight_sum"):
        kv_terms = matmul_left_t(after(group_shared, sent), grad_kv).astype(LOW)
        kv_task = ticks.add(chunk_sums(kv_terms))
    with jax.named_scope("shared_sum"):
        grad_shared_normed = shared_sum.finish()
    with jax.named_scope("weight_layout"):
        query_out_sum, kv_sum = ticks.finish(query_out_task, kv_task)
        grad_query, grad_out = layout(query_out_sum)
        grad_key, grad_value = layout(kv_sum)
        grad_out = jnp.transpose(grad_out)
    with jax.named_scope("unit_weight_sums"):
        sums = [part for result in ticks.finish(*unit_sum_tasks) for part in result]
        whole = jnp.concatenate(sums, axis=0).astype(HIGH)
        grad_gate, grad_up, grad_down = (
            whole[w * units_padded : w * units_padded + units_local] for w in range(3)
        )
        grad_gate, grad_up = jnp.transpose(grad_gate), jnp.transpose(grad_up)

    gain_one, grad_in_one = norm_backward(grad_normed, plain_one, factor_one, norm_gain)
    gain_kv, grad_in_kv = norm_backward(grad_shared_normed, plain_kv, factor_kv, kv_gain)
    grad_states = (grad_residual + grad_in_one).astype(LOW)
    grad_shared = grad_in_kv.astype(LOW)

    devices = 8 * sides
    gain_terms = jnp.stack([g.reshape(devices, -1) for g in (gain_one, gain_kv, gain_two)], axis=1)
    gain_terms = lax.all_to_all(
        gain_terms.reshape(devices, -1), ALL, split_axis=0, concat_axis=0, tiled=True
    )
    gain_sums = jnp.sum(gain_terms, axis=0).reshape(3, -1)
    return (
        output,
        grad_states,
        grad_shared,
        gain_sums[0],
        gain_sums[1],
        gain_sums[2],
        grad_query,
        grad_key,
        grad_value,
        grad_out,
        grad_gate,
        grad_up,
        grad_down,
    )


def solution(mesh):
    size_ctx, size_head = mesh.shape["ctx"], mesh.shape["head"]
    fine = Mesh(mesh.devices.reshape(4, size_ctx // 4, 2, size_head // 2), ALL)
    rows = P(ALL, None)
    ctx, head = ("z", "x"), ("y", "c")
    in_specs = (
        rows,
        rows,
        P(),
        P(),
        P(),
        rows,
        rows,
        rows,
        rows,
        P(None, ALL),
        P(None, ALL),
        rows,
        P(),
        rows,
    )
    out_specs = (
        rows,
        rows,
        rows,
        P(ALL),
        P(ALL),
        P(ALL),
        P(ctx, head),
        P(ctx, head),
        P(ctx, head),
        P(head, ctx),
        P(None, ALL),
        P(None, ALL),
        rows,
    )
    return jax.shard_map(
        per_device, mesh=fine, in_specs=in_specs, out_specs=out_specs, check_vma=False
    )
```

time: 1050 us -> 767 us (0.73); the launches traced: 1030 us -> 771 us
  waiting for transfers between devices: 540 us -> 329 us
  local copies, waits for them, and re-layouts: 100 us -> 62.6 us
  between operations: 24.4 us -> 6.15 us
  Pallas kernels: 51.4 us -> 38.6 us
  matrix products: 67.1 us -> 78 us
    unnamed x2 -> x0, waiting for transfers between devices: 130 us -> none
    ppermute x145 -> x134, waiting for transfers between devices: 407 us -> 322 us  [hop(): lax.ppermute(values, axis, [(i, (i + steps) % size) for i in range(size)])]
    unnamed x221 -> x286, local copies, waits for them, and re-layouts: 54.6 us -> 32.5 us
    all_to_all x0 -> x1, starting transfers between devices: none -> 15.5 us  [per_device(): lax.all_to_all(gain_terms.reshape(devices, -1), ALL, split_axis=0, concat...]
    pallas_call x2 -> x4, Pallas kernels: 51.4 us -> 38.6 us  [the longest x2 24.4 us: attention_backward(): pl.pallas_call(backward_kernel, out_shape=(jax.ShapeDtypeStruct(own_part,...]
    gather x4 -> x1, local copies, waits for them, and re-layouts: 11.2 us -> 0.61 us  [per_device(): jnp.take(out_pieces, whole_side, axis=0)]
    ppermute x145 -> x134, starting transfers between devices: 171 us -> 165 us  [hop(): lax.ppermute(values, axis, [(i, (i + steps) % size) for i in range(size)])]
    dot_general x16 -> x12, matrix products: 20.1 us -> 26.4 us  [matmul_right_t(): lax.dot_general(left_side, right_side, (((1,), (1,)), ((), ())), preferre...]
  transfers between devices with their start and end apart: 154 -> 139, of which waited for: 59 -> 66; matrix products, arithmetic and copies ran while one was open for 19% -> 21% of each run, Pallas kernels for 2% -> 5%
where the time goes in v2:
time: 767 us; the launch traced here: 771 us
  waiting for transfers between devices  329 us (43%)
  starting transfers between devices  191 us (25%)
  matrix products  78 us (10%)
  other arithmetic  65.7 us (9%)
  local copies, waits for them, and re-layouts  62.6 us (8%)
  Pallas kernels  38.6 us (5%)
    ppermute x134, waiting for transfers between devices, hop(): lax.ppermute(values, axis, [(i, (i + steps) % size) for i in range(size)])  322 us
    ppermute x134, starting transfers between devices, hop(): lax.ppermute(values, axis, [(i, (i + steps) % size) for i in range(size)])  165 us
    dot_general x19, matrix products, matmul(): return jnp.dot(left_side, right_side, preferred_element_type=HIGH)  36.2 us
    unnamed x286, local copies, waits for them, and re-layouts  32.5 us
    dot_general x12, matrix products, matmul_right_t(): lax.dot_general(left_side, right_side, (((1,), (1,)), ((), ())), preferre...  26.4 us
    pallas_call x2, Pallas kernels, attention_backward(): pl.pallas_call(backward_kernel, out_shape=(jax.ShapeDtypeStruct(own_part,...  24.4 us
    convert_element_type x18, other arithmetic, add_low(): return (first.astype(HIGH) + second.astype(HIGH)).astype(LOW)  18.6 us
    all_to_all x1, starting transfers between devices, per_device(): lax.all_to_all(gain_terms.reshape(devices, -1), ALL, split_axis=0, concat...  15.5 us
  transfers between devices with their start and end apart: 139, of which 66 were waited for; matrix products, arithmetic and copies ran while one was open for 21% of the time, Pallas kernels for 5%

profile of v2, /device:TPU:0, one launch (start us, length us, event | category | flops | bytes accessed | tf_op | source)
XLA Modules:
  0.0 770.9 jit_solution(3842341194216756959)
XLA Ops:
  18.0 12.6 %collective-permute-done.2 = bf16[64,3,512]{2,0,1:T(8,128)(2,1)S(1)} collective-permute-done((bf16[64,3,512]{2,0,1:T(8,128)(2,1)S(1)}, bf16[64,3,512]{2,0,1:T(8,128)(2,1)S(1)}, u32[]{:S(2)}, u32[]{:S(2)}) %collective-permute-start.2) | collective-permute-done | bytes 196640 | tf_op jit(solution)/shard_map/weight_columns/ppermute | solution.py:29
  40.1 4.9 collective-permute-start.4
  50.8 5.9 collective-permute-done.4
  62.6 6.5 collective-permute-done.15.refs_3_
  72.2 4.9 collective-permute-start.14
  81.5 7.2 collective-permute-done.14
  95.7 7.7 %collective-permute-done.17 = bf16[128,2048]{1,0:T(8,128)(2,1)S(1)} collective-permute-done((bf16[128,2048]{1,0:T(8,128)(2,1)S(1)}, bf16[128,2048]{1,0:T(8,128)(2,1)S(1)}, u32[]{:S(2)}, u32[]{:S(2)}) %collective-permute-start.17) | collective-permute-done | bytes 524320 | tf_op jit(solution)/shard_map/normed_rows/ppermute | solution.py:29
  108.5 8.9 %collective-permute-done.24 = bf16[128,2048]{1,0:T(8,128)(2,1)S(1)} collective-permute-done((bf16[128,2048]{1,0:T(8,128)(2,1)S(1)}, bf16[128,2048]{1,0:T(8,128)(2,1)S(1)}, u32[]{:S(2)}, u32[]{:S(2)}) %collective-permute-start.24) | collective-permute-done | bytes 524320 | tf_op jit(solution)/shard_map/normed_rows/ppermute | solution.py:29
  121.5 7.9 %collective-permute-done.32 = bf16[1024,256]{1,0:T(8,128)(2,1)S(1)} collective-permute-done((bf16[1024,256]{1,0:T(8,128)(2,1)}, bf16[1024,256]{1,0:T(8,128)(2,1)S(1)}, u32[]{:S(2)}, u32[]{:S(2)}) %collective-permute-start.32) | collective-permute-done | bytes 524320 | tf_op jit(solution)/shard_map/normed_rows/ppermute | solution.py:29
  136.1 5.2 collective-permute-done.42
  153.6 12.1 %attention_forward.1 = (bf16[2,512,256]{2,1,0:T(8,128)(2,1)}, f32[2,8,1024]{2,1,0:T(8,128)}) custom-call(s32[16]{0:T(128)} %select_reduce_fusion.place_ref, s32[4]{0:T(128)} %bitcast.245, s32[1]{0:T(128)} %bitcast.1.core_ref, bf16[2,512,256]{2,1,0:T(8,128)(2,1)} %bitcast.240, bf16[4,2,512,256]{3,2,1,0:T(8,128)(2,1)} %bitcast.217, ...), custom_call_target="tpu_custom_call" | custom-call | flops 2147483648 | bytes 4194304 | tf_op jit(solution)/shard_map/attention_forward/pallas_call | solution.py:427
  165.9 7.7 collective-permute-start.48
  173.5 7.2 collective-permute-start.46
  180.9 15.2 %collective-permute-done.37 = bf16[32,2048]{1,0:T(8,128)(2,1)S(1)} collective-permute-done((bf16[32,2048]{1,0:T(8,128)(2,1)S(1)}, bf16[32,2048]{1,0:T(8,128)(2,1)S(1)}, u32[]{:S(2)}, u32[]{:S(2)}) %collective-permute-start.37) | collective-permute-done | bytes 131104 | tf_op jit(solution)/shard_map/grad_output_rows/ppermute | solution.py:29
  196.4 4.8 collective-permute-done.38
  228.7 7.0 collective-permute-done.52
  240.7 6.3 collective-permute-done.55
  252.0 4.5 collective-permute-done.45
  256.8 15.4 %collective-permute-done.50 = bf16[128,2048]{1,0:T(8,128)(2,1)S(1)} collective-permute-done((bf16[128,2048]{1,0:T(8,128)(2,1)S(1)}, bf16[128,2048]{1,0:T(8,128)(2,1)S(1)}, u32[]{:S(2)}, u32[]{:S(2)}) %collective-permute-start.50) | collective-permute-done | bytes 524320 | tf_op jit(solution)/shard_map/attention_sum/ppermute | solution.py:29
  274.9 12.2 %collective-permute-done.53 = bf16[128,2048]{1,0:T(8,128)(2,1)S(1)} collective-permute-done((bf16[128,2048]{1,0:T(8,128)(2,1)S(1)}, bf16[128,2048]{1,0:T(8,128)(2,1)S(1)}, u32[]{:S(2)}, u32[]{:S(2)}) %collective-permute-start.53) | collective-permute-done | bytes 524320 | tf_op jit(solution)/shard_map/attention_sum/ppermute | solution.py:29
  287.8 13.7 %collective-permute-done.56 = bf16[128,2048]{1,0:T(8,128)(2,1)S(1)} collective-permute-done((bf16[128,2048]{1,0:T(8,128)(2,1)S(1)}, bf16[128,2048]{1,0:T(8,128)(2,1)S(1)}, u32[]{:S(2)}, u32[]{:S(2)}) %collective-permute-start.56) | collective-permute-done | bytes 524320 | tf_op jit(solution)/shard_map/normed_two_rows/ppermute | solution.py:29
  301.6 12.7 %collective-permute-done.59 = bf16[128,2048]{1,0:T(8,128)(2,1)S(1)} collective-permute-done((bf16[128,2048]{1,0:T(8,128)(2,1)S(1)}, bf16[128,2048]{1,0:T(8,128)(2,1)S(1)}, u32[]{:S(2)}, u32[]{:S(2)}) %collective-permute-start.59) | collective-permute-done | bytes 524320 | tf_op jit(solution)/shard_map/normed_two_rows/ppermute | solution.py:29
  315.2 11.0 %collective-permute-done.62 = bf16[128,2048]{1,0:T(8,128)(2,1)S(1)} collective-permute-done((bf16[128,2048]{1,0:T(8,128)(2,1)S(1)}, bf16[128,2048]{1,0:T(8,128)(2,1)S(1)}, u32[]{:S(2)}, u32[]{:S(2)}) %collective-permute-start.62) | collective-permute-done | bytes 524320 | tf_op jit(solution)/shard_map/normed_two_rows/ppermute | solution.py:29
  331.4 5.0 fusion.173
  336.5 5.8 multiply_convert_fusion
  352.4 4.5 add_convert_fusion
  369.2 7.4 collective-permute-done.73
  396.8 9.9 %collective-permute-done.79 = bf16[128,2048]{1,0:T(8,128)(2,1)S(1)} collective-permute-done((bf16[128,2048]{1,0:T(8,128)(2,1)S(1)}, bf16[128,2048]{1,0:T(8,128)(2,1)S(1)}, u32[]{:S(2)}, u32[]{:S(2)}) %collective-permute-start.79) | collective-permute-done | bytes 524320 | tf_op jit(solution)/shard_map/ffn_grad_sum/ppermute | solution.py:29
  425.2 8.0 %collective-permute-done.77 = bf16[128,2048]{1,0:T(8,128)(2,1)} collective-permute-done((bf16[128,2048]{1,0:T(8,128)(2,1)}, bf16[128,2048]{1,0:T(8,128)(2,1)}, u32[]{:S(2)}, u32[]{:S(2)}) %collective-permute-start.77) | collective-permute-done | bytes 524320 | tf_op jit(solution)/shard_map/branch_rows/ppermute | solution.py:29
  454.1 9.2 %collective-permute-done.83 = bf16[128,2048]{1,0:T(8,128)(2,1)S(1)} collective-permute-done((bf16[128,2048]{1,0:T(8,128)(2,1)S(1)}, bf16[128,2048]{1,0:T(8,128)(2,1)S(1)}, u32[]{:S(2)}, u32[]{:S(2)}) %collective-permute-start.83) | collective-permute-done | bytes 524320 | tf_op jit(solution)/shard_map/branch_rows/ppermute | solution.py:29
  474.2 12.2 %attention_backward.2 = (bf16[2,512,128]{2,1,0:T(8,128)(2,1)}, bf16[4,2,512,128]{3,2,1,0:T(8,128)(2,1)}, bf16[4,2,512,128]{3,2,1,0:T(8,128)(2,1)}) custom-call(s32[16]{0:T(128)} %select_reduce_fusion.place_ref, s32[4]{0:T(128)} %bitcast.246, s32[1]{0:T(128)} %bitcast.1.core_ref, bf16[2,512,256]{2,1,0:T(8,128)(2,1)} %bitcast.241, ...), custom_call_target="tpu_custom_call" | custom-call | flops 2684354560 | bytes 4194304 | tf_op jit(solution)/shard_map/attention_backward/pallas_call | solution.py:468
  490.5 7.7 collective-permute-start.103
  498.3 7.8 %collective-permute-start.105 = (bf16[1024,128]{1,0:T(8,128)(2,1)S(1)}, bf16[1024,128]{1,0:T(8,128)(2,1)S(1)}, u32[]{:S(2)}, u32[]{:S(2)}) collective-permute-start(bf16[1024,128]{1,0:T(8,128)(2,1)S(1)} %bitcast.236), channel_id=1, source_target_pairs={{0,2},{2,0},{1,3},{3,1},{4,6},{6,4},{5,7},{7,5},{8,10},{10,8},{9,1... | collective-permute-start | bytes 786440 | tf_op jit(solution)/shard_map/normed_sum/ppermute | solution.py:29
  513.2 4.5 collective-permute-done.106
  531.8 12.2 %attention_backward.3 = (bf16[2,512,128]{2,1,0:T(8,128)(2,1)}, bf16[4,2,512,128]{3,2,1,0:T(8,128)(2,1)}, bf16[4,2,512,128]{3,2,1,0:T(8,128)(2,1)}) custom-call(s32[16]{0:T(128)} %select_reduce_fusion.place_ref, s32[4]{0:T(128)} %bitcast.247, s32[1]{0:T(128)} %bitcast.1.core_ref, bf16[2,512,256]{2,1,0:T(8,128)(2,1)} %bitcast.242, ...), custom_call_target="tpu_custom_call" | custom-call | flops 2684354560 | bytes 4194304 | tf_op jit(solution)/shard_map/attention_backward/pallas_call | solution.py:468
  546.1 7.5 collective-permute-start.110
  555.5 8.1 %collective-permute-start.111 = (bf16[1024,128]{1,0:T(8,128)(2,1)S(1)}, bf16[1024,128]{1,0:T(8,128)(2,1)S(1)}, u32[]{:S(2)}, u32[]{:S(2)}) collective-permute-start(bf16[1024,128]{1,0:T(8,128)(2,1)S(1)} %bitcast.239), channel_id=1, source_target_pairs={{0,2},{2,0},{1,3},{3,1},{4,6},{6,4},{5,7},{7,5},{8,10},{10,8},{9,1... | collective-permute-start | bytes 786440 | tf_op jit(solution)/shard_map/normed_sum/ppermute | solution.py:29
  564.3 4.2 collective-permute-done.111
  612.7 7.1 collective-permute-start.129
  623.8 11.7 %collective-permute-done.102 = bf16[128,2048]{1,0:T(8,128)(2,1)S(1)} collective-permute-done((bf16[128,2048]{1,0:T(8,128)(2,1)S(1)}, bf16[128,2048]{1,0:T(8,128)(2,1)S(1)}, u32[]{:S(2)}, u32[]{:S(2)}) %collective-permute-start.102) | collective-permute-done | bytes 524320 | tf_op jit(solution)/shard_map/normed_sum/ppermute | solution.py:29
  644.1 8.8 %collective-permute-done.107 = bf16[128,2048]{1,0:T(8,128)(2,1)} collective-permute-done((bf16[128,2048]{1,0:T(8,128)(2,1)}, bf16[128,2048]{1,0:T(8,128)(2,1)}, u32[]{:S(2)}, u32[]{:S(2)}) %collective-permute-start.107) | collective-permute-done | bytes 524320 | tf_op jit(solution)/shard_map/normed_sum/ppermute | solution.py:29
  657.8 6.6 collective-permute-done.112
  667.8 7.2 collective-permute-start.130
  675.0 14.0 %collective-permute-start.131 = (bf16[256,512]{1,0:T(8,128)(2,1)S(1)}, bf16[256,512]{1,0:T(8,128)(2,1)S(1)}, u32[]{:S(2)}, u32[]{:S(2)}) collective-permute-start(bf16[256,512]{1,0:T(8,128)(2,1)S(1)} %get-tuple-element.246), channel_id=1, source_target_pairs={{0,2},{2,0},{1,3},{3,1},{4,6},{6,4},{5,7},{7,5},{8,10},{10,8},{9,1... | collective-permute-start | bytes 786440 | tf_op jit(solution)/shard_map/shared_sum/ppermute | solution.py:29
  719.6 13.1 %collective-permute-done.120 = bf16[128,2048]{1,0:T(8,128)(2,1)S(1)} collective-permute-done((bf16[128,2048]{1,0:T(8,128)(2,1)S(1)}, bf16[128,2048]{1,0:T(8,128)(2,1)S(1)}, u32[]{:S(2)}, u32[]{:S(2)}) %collective-permute-start.120) | collective-permute-done | bytes 524320 | tf_op jit(solution)/shard_map/shared_sum/ppermute | solution.py:29
  736.6 9.3 %collective-permute-done.125 = bf16[128,2048]{1,0:T(8,128)(2,1)S(1)} collective-permute-done((bf16[128,2048]{1,0:T(8,128)(2,1)S(1)}, bf16[128,2048]{1,0:T(8,128)(2,1)S(1)}, u32[]{:S(2)}, u32[]{:S(2)}) %collective-permute-start.125) | collective-permute-done | bytes 524320 | tf_op jit(solution)/shard_map/shared_sum/ppermute | solution.py:29
  747.3 15.5 %all-to-all-start = ((f32[32,1,192]{2,1,0:T(1,128)}), f32[32,1,192]{2,1,0:T(1,128)S(1)}, u32[]{:S(2)}, u32[]{:S(2)}) async-start(f32[32,1,192]{2,1,0:T(1,128)} %all_to_all.8), calls=%async_computation | async-start | bytes 65536 | tf_op jit(solution)/shard_map/all_to_all | solution.py:837
  764.0 6.1 all-to-all-done
  (712 shorter events, 349.7 us)
Async XLA Ops:
  4.0 36.0 %collective-permute-start = (bf16[128,2048]{1,0:T(8,128)(2,1)}, bf16[128,2048]{1,0:T(8,128)(2,1)}, u32[]{:S(2)}, u32[]{:S(2)}) collective-permute-start(bf16[128,2048]{1,0:T(8,128)(2,1)} %fusion.15), channel_id=1, source_target_pairs={{0,8},{8,16},{16,24},{24,0},{1,9},{9,17},{17,25},{25,1},{2,10},{10... | collective-permute-start | bytes 1572872 | tf_op jit(solution)/shard_map/weight_columns/ppermute | solution.py:29
  8.6 22.0 %collective-permute-start.2 = (bf16[64,3,512]{2,0,1:T(8,128)(2,1)S(1)}, bf16[64,3,512]{2,0,1:T(8,128)(2,1)S(1)}, u32[]{:S(2)}, u32[]{:S(2)}) collective-permute-start(bf16[64,3,512]{2,0,1:T(8,128)(2,1)S(1)} %get-tuple-element.381), channel_id=1, source_target_pairs={{0,16},{8,24},{16,0},{24,8},{1,17},{9,25},{17,1},{25,9},{2,18},{10... | collective-permute-start | bytes 589832 | tf_op jit(solution)/shard_map/weight_columns/ppermute | solution.py:29
  11.2 19.6 %collective-permute-start.3 = (bf16[64,3,512]{2,0,1:T(8,128)(2,1)S(1)}, bf16[64,3,512]{2,0,1:T(8,128)(2,1)S(1)}, u32[]{:S(2)}, u32[]{:S(2)}) collective-permute-start(bf16[64,3,512]{2,0,1:T(8,128)(2,1)S(1)} %get-tuple-element.380), channel_id=1, source_target_pairs={{0,24},{8,0},{16,8},{24,16},{1,25},{9,1},{17,9},{25,17},{2,26},{10... | collective-permute-start | bytes 589832 | tf_op jit(solution)/shard_map/weight_columns/ppermute | solution.py:29
  12.6 21.4 %collective-permute-start.1 = (bf16[64,3,512]{2,0,1:T(8,128)(2,1)S(1)}, bf16[64,3,512]{2,0,1:T(8,128)(2,1)S(1)}, u32[]{:S(2)}, u32[]{:S(2)}) collective-permute-start(bf16[64,3,512]{2,0,1:T(8,128)(2,1)S(1)} %get-tuple-element.382), channel_id=1, source_target_pairs={{0,8},{8,16},{16,24},{24,0},{1,9},{9,17},{17,25},{25,1},{2,10},{10... | collective-permute-start | bytes 589832 | tf_op jit(solution)/shard_map/weight_columns/ppermute | solution.py:29
  39.0 38.2 %collective-permute-start.21 = (bf16[128,2048]{1,0:T(8,128)(2,1)}, bf16[128,2048]{1,0:T(8,128)(2,1)}, u32[]{:S(2)}, u32[]{:S(2)}) collective-permute-start(bf16[128,2048]{1,0:T(8,128)(2,1)} %fusion.15), channel_id=1, source_target_pairs={{0,1},{1,0},{2,3},{3,2},{4,5},{5,4},{6,7},{7,6},{8,9},{9,8},{10,11... | collective-permute-start | bytes 1572872 | tf_op jit(solution)/shard_map/shared_rows/ppermute | solution.py:29
  39.3 107.9 %collective-permute-start.28 = (bf16[128,2048]{1,0:T(8,128)(2,1)}, bf16[128,2048]{1,0:T(8,128)(2,1)}, u32[]{:S(2)}, u32[]{:S(2)}) collective-permute-start(bf16[128,2048]{1,0:T(8,128)(2,1)} %fusion.22), channel_id=1, source_target_pairs={{0,1},{1,0},{2,3},{3,2},{4,5},{5,4},{6,7},{7,6},{8,9},{9,8},{10,11... | collective-permute-start | bytes 1572872 | tf_op jit(solution)/shard_map/normed_rows/ppermute | solution.py:29
  40.1 16.6 %collective-permute-start.4 = (bf16[128,2048]{1,0:T(8,128)(2,1)}, bf16[128,2048]{1,0:T(8,128)(2,1)S(1)}, u32[]{:S(2)}, u32[]{:S(2)}) collective-permute-start(bf16[128,2048]{1,0:T(8,128)(2,1)} %collective-permute-done), channel_id=1, source_target_pairs={{0,8},{8,16},{16,24},{24,0},{1,9},{9,17},{17,25},{25,1},{2,10},{10... | collective-permute-start | bytes 1572872 | tf_op jit(solution)/shard_map/shared_rows/ppermute | solution.py:29
  72.2 16.5 %collective-permute-start.14 = (bf16[128,2048]{1,0:T(8,128)(2,1)}, bf16[128,2048]{1,0:T(8,128)(2,1)S(1)}, u32[]{:S(2)}, u32[]{:S(2)}) collective-permute-start(bf16[128,2048]{1,0:T(8,128)(2,1)} %fusion.22), channel_id=1, source_target_pairs={{0,8},{8,16},{16,24},{24,0},{1,9},{9,17},{17,25},{25,1},{2,10},{10... | collective-permute-start | bytes 1572872 | tf_op jit(solution)/shard_map/normed_rows/ppermute | solution.py:29
  119.0 22.3 %collective-permute-start.42 = (bf16[128,2048]{1,0:T(8,128)(2,1)}, bf16[128,2048]{1,0:T(8,128)(2,1)S(1)}, u32[]{:S(2)}, u32[]{:S(2)}) collective-permute-start(bf16[128,2048]{1,0:T(8,128)(2,1)} %param.27), channel_id=1, source_target_pairs={{0,24},{8,0},{16,8},{24,16},{1,25},{9,1},{17,9},{25,17},{2,26},{10... | collective-permute-start | bytes 1572872 | tf_op jit(solution)/shard_map/grad_output_rows/ppermute | solution.py:29
  119.1 23.9 %collective-permute-start.41 = (bf16[128,2048]{1,0:T(8,128)(2,1)}, bf16[128,2048]{1,0:T(8,128)(2,1)}, u32[]{:S(2)}, u32[]{:S(2)}) collective-permute-start(bf16[128,2048]{1,0:T(8,128)(2,1)} %param.27), channel_id=1, source_target_pairs={{0,8},{8,16},{16,24},{24,0},{1,9},{9,17},{17,25},{25,1},{2,10},{10... | collective-permute-start | bytes 1572872 | tf_op jit(solution)/shard_map/grad_output_rows/ppermute | solution.py:29
  121.5 23.2 %collective-permute-start.27 = (bf16[128,2048]{1,0:T(8,128)(2,1)S(1)}, bf16[128,2048]{1,0:T(8,128)(2,1)S(1)}, u32[]{:S(2)}, u32[]{:S(2)}) collective-permute-start(bf16[128,2048]{1,0:T(8,128)(2,1)S(1)} %collective-permute-done.24), channel_id=1, source_target_pairs={{0,1},{1,0},{2,3},{3,2},{4,5},{5,4},{6,7},{7,6},{8,9},{9,8},{10,11... | collective-permute-start | bytes 1572872 | tf_op jit(solution)/shard_map/normed_rows/ppermute | solution.py:29
  129.4 36.3 %collective-permute-start.35 = (bf16[32,2048]{1,0:T(8,128)(2,1)}, bf16[32,2048]{1,0:T(8,128)(2,1)S(1)}, u32[]{:S(2)}, u32[]{:S(2)}) collective-permute-start(bf16[32,2048]{1,0:T(8,128)(2,1)} %get-tuple-element.147), channel_id=1, source_target_pairs={{0,4},{4,0},{1,5},{5,1},{2,6},{6,2},{3,7},{7,3},{8,12},{12,8},{9,1... | collective-permute-start | bytes 393224 | tf_op jit(solution)/shard_map/grad_output_rows/ppermute | solution.py:29
  141.3 24.5 %collective-permute-start.33 = (bf16[32,2048]{1,0:T(8,128)(2,1)}, bf16[32,2048]{1,0:T(8,128)(2,1)S(1)}, u32[]{:S(2)}, u32[]{:S(2)}) collective-permute-start(bf16[32,2048]{1,0:T(8,128)(2,1)} %get-tuple-element.147), channel_id=1, source_target_pairs={{0,2},{2,0},{1,3},{3,1},{4,6},{6,4},{5,7},{7,5},{8,10},{10,8},{9,1... | collective-permute-start | bytes 393224 | tf_op jit(solution)/shard_map/grad_output_rows/ppermute | solution.py:29
  143.1 22.8 %collective-permute-start.36 = (bf16[32,2048]{1,0:T(8,128)(2,1)S(1)}, bf16[32,2048]{1,0:T(8,128)(2,1)S(1)}, u32[]{:S(2)}, u32[]{:S(2)}) collective-permute-start(bf16[32,2048]{1,0:T(8,128)(2,1)S(1)} %copy-done.86), channel_id=1, source_target_pairs={{0,4},{4,0},{1,5},{5,1},{2,6},{6,2},{3,7},{7,3},{8,12},{12,8},{9,1... | collective-permute-start | bytes 393224 | tf_op jit(solution)/shard_map/grad_output_rows/ppermute | solution.py:29
  144.7 21.2 %collective-permute-start.34 = (bf16[32,2048]{1,0:T(8,128)(2,1)S(1)}, bf16[32,2048]{1,0:T(8,128)(2,1)S(1)}, u32[]{:S(2)}, u32[]{:S(2)}) collective-permute-start(bf16[32,2048]{1,0:T(8,128)(2,1)S(1)} %copy-done.86), channel_id=1, source_target_pairs={{0,2},{2,0},{1,3},{3,1},{4,6},{6,4},{5,7},{7,5},{8,10},{10,8},{9,1... | collective-permute-start | bytes 393224 | tf_op jit(solution)/shard_map/grad_output_rows/ppermute | solution.py:29
  147.2 55.5 %collective-permute-start.43 = (bf16[128,2048]{1,0:T(8,128)(2,1)}, bf16[128,2048]{1,0:T(8,128)(2,1)}, u32[]{:S(2)}, u32[]{:S(2)}) collective-permute-start(bf16[128,2048]{1,0:T(8,128)(2,1)} %collective-permute-done.41), channel_id=1, source_target_pairs={{0,8},{8,16},{16,24},{24,0},{1,9},{9,17},{17,25},{25,1},{2,10},{10... | collective-permute-start | bytes 1572872 | tf_op jit(solution)/shard_map/grad_output_rows/ppermute | solution.py:29
  165.7 43.2 %collective-permute-start.67 = (bf16[128,2048]{1,0:T(8,128)(2,1)}, bf16[128,2048]{1,0:T(8,128)(2,1)}, u32[]{:S(2)}, u32[]{:S(2)}) collective-permute-start(bf16[128,2048]{1,0:T(8,128)(2,1)} %collective-permute-done.41), channel_id=1, source_target_pairs={{0,1},{1,0},{2,3},{3,2},{4,5},{5,4},{6,7},{7,6},{8,9},{9,8},{10,11... | collective-permute-start | bytes 1572872 | tf_op jit(solution)/shard_map/grad_output_rows/ppermute | solution.py:29
  165.9 45.0 %collective-permute-start.48 = (bf16[128,2048]{1,0:T(8,128)(2,1)}, bf16[128,2048]{1,0:T(8,128)(2,1)}, u32[]{:S(2)}, u32[]{:S(2)}) collective-permute-start(bf16[128,2048]{1,0:T(8,128)(2,1)} %get-tuple-element.156), channel_id=1, source_target_pairs={{0,4},{4,0},{1,5},{5,1},{2,6},{6,2},{3,7},{7,3},{8,12},{12,8},{9,1... | collective-permute-start | bytes 1572872 | tf_op jit(solution)/shard_map/grad_output_rows/ppermute | solution.py:29
  173.5 37.8 %collective-permute-start.46 = (bf16[128,2048]{1,0:T(8,128)(2,1)}, bf16[128,2048]{1,0:T(8,128)(2,1)}, u32[]{:S(2)}, u32[]{:S(2)}) collective-permute-start(bf16[128,2048]{1,0:T(8,128)(2,1)} %get-tuple-element.156), channel_id=1, source_target_pairs={{0,2},{2,0},{1,3},{3,1},{4,6},{6,4},{5,7},{7,5},{8,10},{10,8},{9,1... | collective-permute-start | bytes 1572872 | tf_op jit(solution)/shard_map/grad_output_rows/ppermute | solution.py:29
  208.9 16.0 %collective-permute-start.70 = (bf16[128,2048]{1,0:T(8,128)(2,1)}, bf16[128,2048]{1,0:T(8,128)(2,1)S(1)}, u32[]{:S(2)}, u32[]{:S(2)}) collective-permute-start(bf16[128,2048]{1,0:T(8,128)(2,1)} %param.27), channel_id=1, source_target_pairs={{0,1},{1,0},{2,3},{3,2},{4,5},{5,4},{6,7},{7,6},{8,9},{9,8},{10,11... | collective-permute-start | bytes 1572872 | tf_op jit(solution)/shard_map/grad_output_rows/ppermute | solution.py:29
  240.0 16.4 %collective-permute-start.45 = (bf16[128,2048]{1,0:T(8,128)(2,1)S(1)}, bf16[128,2048]{1,0:T(8,128)(2,1)S(1)}, u32[]{:S(2)}, u32[]{:S(2)}) collective-permute-start(bf16[128,2048]{1,0:T(8,128)(2,1)S(1)} %add_convert_fusion.13), channel_id=1, source_target_pairs={{0,8},{8,16},{16,24},{24,0},{1,9},{9,17},{17,25},{25,1},{2,10},{10... | collective-permute-start | bytes 1572872 | tf_op jit(solution)/shard_map/attention_sum/ppermute | solution.py:29
  248.7 23.8 %collective-permute-start.58 = (bf16[144,2048]{1,0:T(8,128)(2,1)S(1)}, bf16[144,2048]{1,0:T(8,128)(2,1)S(1)}, u32[]{:S(2)}, u32[]{:S(2)}) collective-permute-start(bf16[144,2048]{1,0:T(8,128)(2,1)S(1)} %copy-done.51), channel_id=1, source_target_pairs={{0,4},{4,0},{1,5},{5,1},{2,6},{6,2},{3,7},{7,3},{8,12},{12,8},{9,1... | collective-permute-start | bytes 1769480 | tf_op jit(solution)/shard_map/attention_sum/ppermute | solution.py:29
  249.0 23.5 %collective-permute-start.57 = (bf16[144,2048]{1,0:T(8,128)(2,1)S(1)}, bf16[144,2048]{1,0:T(8,128)(2,1)S(1)}, u32[]{:S(2)}, u32[]{:S(2)}) collective-permute-start(bf16[144,2048]{1,0:T(8,128)(2,1)S(1)} %copy-done.51), channel_id=1, source_target_pairs={{0,2},{2,0},{1,3},{3,1},{4,6},{6,4},{5,7},{7,5},{8,10},{10,8},{9,1... | collective-permute-start | bytes 1769480 | tf_op jit(solution)/shard_map/attention_sum/ppermute | solution.py:29
  272.5 29.0 %collective-permute-start.60 = (bf16[128,2048]{1,0:T(8,128)(2,1)S(1)}, bf16[128,2048]{1,0:T(8,128)(2,1)S(1)}, u32[]{:S(2)}, u32[]{:S(2)}) collective-permute-start(bf16[128,2048]{1,0:T(8,128)(2,1)S(1)} %collective-permute-done.55), channel_id=1, source_target_pairs={{0,2},{2,0},{1,3},{3,1},{4,6},{6,4},{5,7},{7,5},{8,10},{10,8},{9,1... | collective-permute-start | bytes 1572872 | tf_op jit(solution)/shard_map/normed_two_rows/ppermute | solution.py:29
  274.0 27.6 %collective-permute-start.61 = (bf16[144,2048]{1,0:T(8,128)(2,1)S(1)}, bf16[144,2048]{1,0:T(8,128)(2,1)S(1)}, u32[]{:S(2)}, u32[]{:S(2)}) collective-permute-start(bf16[144,2048]{1,0:T(8,128)(2,1)S(1)} %collective-permute-done.57), channel_id=1, source_target_pairs={{0,4},{4,0},{1,5},{5,1},{2,6},{6,2},{3,7},{7,3},{8,12},{12,8},{9,1... | collective-permute-start | bytes 1769480 | tf_op jit(solution)/shard_map/normed_two_rows/ppermute | solution.py:29
  360.3 16.3 %collective-permute-start.73 = (bf16[128,2048]{1,0:T(8,128)(2,1)}, bf16[128,2048]{1,0:T(8,128)(2,1)S(1)}, u32[]{:S(2)}, u32[]{:S(2)}) collective-permute-start(bf16[128,2048]{1,0:T(8,128)(2,1)} %fusion.6), channel_id=1, source_target_pairs={{0,8},{8,16},{16,24},{24,0},{1,9},{9,17},{17,25},{25,1},{2,10},{10... | collective-permute-start | bytes 1572872 | tf_op jit(solution)/shard_map/ffn_grad_sum/ppermute | solution.py:29
  376.8 19.8 %collective-permute-start.74 = (bf16[128,2048]{1,0:T(8,128)(2,1)S(1)}, bf16[128,2048]{1,0:T(8,128)(2,1)S(1)}, u32[]{:S(2)}, u32[]{:S(2)}) collective-permute-start(bf16[128,2048]{1,0:T(8,128)(2,1)S(1)} %fusion.48), channel_id=1, source_target_pairs={{0,8},{8,16},{16,24},{24,0},{1,9},{9,17},{17,25},{25,1},{2,10},{10... | collective-permute-start | bytes 1572872 | tf_op jit(solution)/shard_map/ffn_grad_sum/ppermute | solution.py:29
  416.7 18.7 %collective-permute-start.76 = (bf16[128,2048]{1,0:T(8,128)(2,1)}, bf16[128,2048]{1,0:T(8,128)(2,1)}, u32[]{:S(2)}, u32[]{:S(2)}) collective-permute-start(bf16[128,2048]{1,0:T(8,128)(2,1)} %convolution_convert_fusion.12), channel_id=1, source_target_pairs={{0,1},{1,0},{2,3},{3,2},{4,5},{5,4},{6,7},{7,6},{8,9},{9,8},{10,11... | collective-permute-start | bytes 1572872 | tf_op jit(solution)/shard_map/ffn_sum/ppermute | solution.py:29
  416.8 16.4 %collective-permute-start.77 = (bf16[128,2048]{1,0:T(8,128)(2,1)}, bf16[128,2048]{1,0:T(8,128)(2,1)}, u32[]{:S(2)}, u32[]{:S(2)}) collective-permute-start(bf16[128,2048]{1,0:T(8,128)(2,1)} %get-tuple-element.177), channel_id=1, source_target_pairs={{0,8},{8,16},{16,24},{24,0},{1,9},{9,17},{17,25},{25,1},{2,10},{10... | collective-permute-start | bytes 1572872 | tf_op jit(solution)/shard_map/branch_rows/ppermute | solution.py:29
  435.5 33.0 %collective-permute-start.91 = (bf16[128,2048]{1,0:T(8,128)(2,1)}, bf16[128,2048]{1,0:T(8,128)(2,1)S(1)}, u32[]{:S(2)}, u32[]{:S(2)}) collective-permute-start(bf16[128,2048]{1,0:T(8,128)(2,1)} %collective-permute-done.77), channel_id=1, source_target_pairs={{0,1},{1,0},{2,3},{3,2},{4,5},{5,4},{6,7},{7,6},{8,9},{9,8},{10,11... | collective-permute-start | bytes 1572872 | tf_op jit(solution)/shard_map/branch_rows/ppermute | solution.py:29
  448.8 20.3 %collective-permute-start.92 = (bf16[128,2048]{1,0:T(8,128)(2,1)S(1)}, bf16[128,2048]{1,0:T(8,128)(2,1)S(1)}, u32[]{:S(2)}, u32[]{:S(2)}) collective-permute-start(bf16[128,2048]{1,0:T(8,128)(2,1)S(1)} %collective-permute-done.80), channel_id=1, source_target_pairs={{0,1},{1,0},{2,3},{3,2},{4,5},{5,4},{6,7},{7,6},{8,9},{9,8},{10,11... | collective-permute-start | bytes 1572872 | tf_op jit(solution)/shard_map/branch_rows/ppermute | solution.py:29
  449.8 19.8 %collective-permute-start.97 = (bf16[128,2048]{1,0:T(8,128)(2,1)S(1)}, bf16[128,2048]{1,0:T(8,128)(2,1)S(1)}, u32[]{:S(2)}, u32[]{:S(2)}) collective-permute-start(bf16[128,2048]{1,0:T(8,128)(2,1)S(1)} %copy-done.63), channel_id=1, source_target_pairs={{0,2},{2,0},{1,3},{3,1},{4,6},{6,4},{5,7},{7,5},{8,10},{10,8},{9,1... | collective-permute-start | bytes 1572872 | tf_op jit(solution)/shard_map/ffn_sum/ppermute | solution.py:29
  450.8 18.9 %collective-permute-start.96 = (bf16[144,2048]{1,0:T(8,128)(2,1)S(1)}, bf16[144,2048]{1,0:T(8,128)(2,1)S(1)}, u32[]{:S(2)}, u32[]{:S(2)}) collective-permute-start(bf16[144,2048]{1,0:T(8,128)(2,1)S(1)} %copy-done.52), channel_id=1, source_target_pairs={{0,4},{4,0},{1,5},{5,1},{2,6},{6,2},{3,7},{7,3},{8,12},{12,8},{9,1... | collective-permute-start | bytes 1769480 | tf_op jit(solution)/shard_map/ffn_sum/ppermute | solution.py:29
  469.1 20.1 %collective-permute-start.87 = (bf16[128,2048]{1,0:T(8,128)(2,1)}, bf16[128,2048]{1,0:T(8,128)(2,1)}, u32[]{:S(2)}, u32[]{:S(2)}) collective-permute-start(bf16[128,2048]{1,0:T(8,128)(2,1)} %fusion.3), channel_id=1, source_target_pairs={{0,8},{8,16},{16,24},{24,0},{1,9},{9,17},{17,25},{25,1},{2,10},{10... | collective-permute-start | bytes 1572872 | tf_op jit(solution)/shard_map/ffn_sum/ppermute | solution.py:29
  469.6 57.4 %collective-permute-start.86 = (bf16[384,2048]{1,0:T(8,128)(2,1)}, bf16[384,2048]{1,0:T(8,128)(2,1)}, u32[]{:S(2)}, u32[]{:S(2)}) collective-permute-start(bf16[384,2048]{1,0:T(8,128)(2,1)} %convolution_convert_fusion.4), channel_id=1, source_target_pairs={{0,1},{1,0},{2,3},{3,2},{4,5},{5,4},{6,7},{7,6},{8,9},{9,8},{10,11... | collective-permute-start | bytes 4718600 | tf_op jit(solution)/shard_map/ffn_sum/ppermute | solution.py:29
  469.7 19.5 %collective-permute-start.100 = (bf16[128,2048]{1,0:T(8,128)(2,1)}, bf16[128,2048]{1,0:T(8,128)(2,1)}, u32[]{:S(2)}, u32[]{:S(2)}) collective-permute-start(bf16[128,2048]{1,0:T(8,128)(2,1)} %add_convert_fusion.10), channel_id=1, source_target_pairs={{0,4},{4,0},{1,5},{5,1},{2,6},{6,2},{3,7},{7,3},{8,12},{12,8},{9,1... | collective-permute-start | bytes 1572872 | tf_op jit(solution)/shard_map/ffn_sum/ppermute | solution.py:29
  470.7 19.8 %collective-permute-start.101 = (bf16[144,2048]{1,0:T(8,128)(2,1)}, bf16[144,2048]{1,0:T(8,128)(2,1)S(1)}, u32[]{:S(2)}, u32[]{:S(2)}) collective-permute-start(bf16[144,2048]{1,0:T(8,128)(2,1)} %add_convert_fusion.3), channel_id=1, source_target_pairs={{0,2},{2,0},{1,3},{3,1},{4,6},{6,4},{5,7},{7,5},{8,10},{10,8},{9,1... | collective-permute-start | bytes 1769480 | tf_op jit(solution)/shard_map/ffn_sum/ppermute | solution.py:29
  490.5 17.7 %collective-permute-start.103 = (bf16[1024,128]{1,0:T(8,128)(2,1)S(1)}, bf16[1024,128]{1,0:T(8,128)(2,1)S(1)}, u32[]{:S(2)}, u32[]{:S(2)}) collective-permute-start(bf16[1024,128]{1,0:T(8,128)(2,1)S(1)} %bitcast.237), channel_id=1, source_target_pairs={{0,4},{4,0},{1,5},{5,1},{2,6},{6,2},{3,7},{7,3},{8,12},{12,8},{9,1... | collective-permute-start | bytes 786440 | tf_op jit(solution)/shard_map/normed_sum/ppermute | solution.py:29
  531.8 42.2 %collective-permute-start.90 = (bf16[128,2048]{1,0:T(8,128)(2,1)S(1)}, bf16[128,2048]{1,0:T(8,128)(2,1)S(1)}, u32[]{:S(2)}, u32[]{:S(2)}) collective-permute-start(bf16[128,2048]{1,0:T(8,128)(2,1)S(1)} %fusion.41), channel_id=1, source_target_pairs={{0,8},{8,16},{16,24},{24,0},{1,9},{9,17},{17,25},{25,1},{2,10},{10... | collective-permute-start | bytes 1572872 | tf_op jit(solution)/shard_map/ffn_sum/ppermute | solution.py:29
  546.1 18.3 %collective-permute-start.110 = (bf16[1024,128]{1,0:T(8,128)(2,1)S(1)}, bf16[1024,128]{1,0:T(8,128)(2,1)S(1)}, u32[]{:S(2)}, u32[]{:S(2)}) collective-permute-start(bf16[1024,128]{1,0:T(8,128)(2,1)S(1)} %bitcast.238), channel_id=1, source_target_pairs={{0,4},{4,0},{1,5},{5,1},{2,6},{6,2},{3,7},{7,3},{8,12},{12,8},{9,1... | collective-permute-start | bytes 786440 | tf_op jit(solution)/shard_map/normed_sum/ppermute | solution.py:29
  585.8 34.7 %collective-permute-start.98 = (bf16[384,2048]{1,0:T(8,128)(2,1)S(1)}, bf16[384,2048]{1,0:T(8,128)(2,1)S(1)}, u32[]{:S(2)}, u32[]{:S(2)}) collective-permute-start(bf16[384,2048]{1,0:T(8,128)(2,1)S(1)} %convolution_convert_fusion.6), channel_id=1, source_target_pairs={{0,1},{1,0},{2,3},{3,2},{4,5},{5,4},{6,7},{7,6},{8,9},{9,8},{10,11... | collective-permute-start | bytes 4718600 | tf_op jit(solution)/shard_map/normed_sum/ppermute | solution.py:29
  600.8 20.1 %collective-permute-start.99 = (bf16[128,2048]{1,0:T(8,128)(2,1)S(1)}, bf16[128,2048]{1,0:T(8,128)(2,1)S(1)}, u32[]{:S(2)}, u32[]{:S(2)}) collective-permute-start(bf16[128,2048]{1,0:T(8,128)(2,1)S(1)} %copy-done.60), channel_id=1, source_target_pairs={{0,8},{8,16},{16,24},{24,0},{1,9},{9,17},{17,25},{25,1},{2,10},{10... | collective-permute-start | bytes 1572872 | tf_op jit(solution)/shard_map/normed_sum/ppermute | solution.py:29
  636.5 16.4 %collective-permute-start.107 = (bf16[128,2048]{1,0:T(8,128)(2,1)}, bf16[128,2048]{1,0:T(8,128)(2,1)}, u32[]{:S(2)}, u32[]{:S(2)}) collective-permute-start(bf16[128,2048]{1,0:T(8,128)(2,1)} %fusion.39), channel_id=1, source_target_pairs={{0,8},{8,16},{16,24},{24,0},{1,9},{9,17},{17,25},{25,1},{2,10},{10... | collective-permute-start | bytes 1572872 | tf_op jit(solution)/shard_map/normed_sum/ppermute | solution.py:29
  667.8 23.4 %collective-permute-start.130 = (bf16[256,512]{1,0:T(8,128)(2,1)S(1)}, bf16[256,512]{1,0:T(8,128)(2,1)S(1)}, u32[]{:S(2)}, u32[]{:S(2)}) collective-permute-start(bf16[256,512]{1,0:T(8,128)(2,1)S(1)} %get-tuple-element.245), channel_id=1, source_target_pairs={{0,4},{4,0},{1,5},{5,1},{2,6},{6,2},{3,7},{7,3},{8,12},{12,8},{9,1... | collective-permute-start | bytes 786440 | tf_op jit(solution)/shard_map/shared_sum/ppermute | solution.py:29
  675.0 18.3 %collective-permute-start.131 = (bf16[256,512]{1,0:T(8,128)(2,1)S(1)}, bf16[256,512]{1,0:T(8,128)(2,1)S(1)}, u32[]{:S(2)}, u32[]{:S(2)}) collective-permute-start(bf16[256,512]{1,0:T(8,128)(2,1)S(1)} %get-tuple-element.246), channel_id=1, source_target_pairs={{0,2},{2,0},{1,3},{3,1},{4,6},{6,4},{5,7},{7,5},{8,10},{10,8},{9,1... | collective-permute-start | bytes 786440 | tf_op jit(solution)/shard_map/shared_sum/ppermute | solution.py:29
  691.2 23.5 %collective-permute-start.118 = (bf16[384,2048]{1,0:T(8,128)(2,1)}, bf16[384,2048]{1,0:T(8,128)(2,1)}, u32[]{:S(2)}, u32[]{:S(2)}) collective-permute-start(bf16[384,2048]{1,0:T(8,128)(2,1)} %convolution_convert_fusion.5), channel_id=1, source_target_pairs={{0,1},{1,0},{2,3},{3,2},{4,5},{5,4},{6,7},{7,6},{8,9},{9,8},{10,11... | collective-permute-start | bytes 4718600 | tf_op jit(solution)/shard_map/shared_sum/ppermute | solution.py:29
  696.9 19.6 %collective-permute-start.119 = (bf16[128,2048]{1,0:T(8,128)(2,1)S(1)}, bf16[128,2048]{1,0:T(8,128)(2,1)S(1)}, u32[]{:S(2)}, u32[]{:S(2)}) collective-permute-start(bf16[128,2048]{1,0:T(8,128)(2,1)S(1)} %copy-done.59), channel_id=1, source_target_pairs={{0,8},{8,16},{16,24},{24,0},{1,9},{9,17},{17,25},{25,1},{2,10},{10... | collective-permute-start | bytes 1572872 | tf_op jit(solution)/shard_map/shared_sum/ppermute | solution.py:29
  747.3 22.8 %all-to-all-start = ((f32[32,1,192]{2,1,0:T(1,128)}), f32[32,1,192]{2,1,0:T(1,128)S(1)}, u32[]{:S(2)}, u32[]{:S(2)}) async-start(f32[32,1,192]{2,1,0:T(1,128)} %all_to_all.8), calls=%async_computation | async-start | bytes 65536 | tf_op jit(solution)/shard_map/all_to_all | solution.py:837
  (202 other events, 2846.3 us)

commit v3 on v2

--- a/solution.py
+++ b/solution.py
@@ -27,6 +27,11 @@
 def hop(values, axis, steps=1):
     size = lax.axis_size(axis)
     return lax.ppermute(values, axis, [(i, (i + steps) % size) for i in range(size)])
+
+
+def both_cores(blocks):
+    blocks = blocks[1:] + blocks[:1]
+    return blocks + [hop(block, "c") for block in blocks]
 
 
 def gather_task(first, second):
@@ -80,9 +85,9 @@
         self.sides = [(), ()]
         self.sent = None
 
-    def add(self, task):
+    def add(self, task, urgent=False):
         entry = {"task": task, "wanted": None, "open": 0, "result": None}
-        self.tasks.append(entry)
+        self.tasks.insert(0 if urgent else len(self.tasks), entry)
         self.advance(entry)
         return entry
 
@@ -94,12 +99,14 @@
             entry["result"] = stop.value
             self.tasks.remove(entry)
 
-    def tick(self, *moves, room=1):
+    def tick(self, *moves, room=1, lock=True, hold=False):
         got = []
         for values, steps in moves:
             self.sent = after(values, self.over_z, self.sides[-2])
             got.append(hop(self.sent, "z", steps))
         left = {"x": room * self.BYTES, "y": room * self.BYTES}
+        before = self.over_z if lock else ()
+        places = []
         arrived = []
         finished = []
         for entry in self.tasks:
@@ -107,7 +114,8 @@
             for axis, values, into in entry["wanted"]:
                 if left[axis] >= min(values.nbytes, self.BYTES):
                     left[axis] -= values.nbytes
-                    into.append(hop(after(values, self.sides[-1]), axis))
+                    into.append(hop(after(values, self.sides[-1], before), axis))
+                    places.append((into, len(into) - 1))
                     arrived.append(into[-1])
                     entry["open"] -= 1
                 else:
@@ -117,9 +125,20 @@
                 finished.append(entry)
         self.over_z = tuple(got) or self.over_z
         self.sides = self.sides[-1:] + [tuple(arrived)]
+        self.held = (places, finished)
+        if not hold:
+            self.release()
+        return got
+
+    def release(self, *earlier):
+        places, finished = self.held
+        if earlier:
+            for into, at in places:
+                into[at] = after(into[at], earlier)
         for entry in finished:
+            self.tasks.remove(entry)
+            self.tasks.append(entry)
             self.advance(entry)
-        return got
 
     def finish(self, *entries):
         while any(entry["result"] is None for entry in entries):
@@ -130,11 +149,10 @@
         blocks = [rows]
         for _ in range(1, lax.axis_size("z")):
             blocks += self.tick((blocks[-1], 1))
-        return self.both_cores(blocks)
-
-    def both_cores(self, blocks):
-        blocks = blocks[1:] + blocks[:1]
-        return jnp.concatenate(blocks + [hop(block, "c") for block in blocks], axis=0)
+        return self.join_cores(blocks)
+
+    def join_cores(self, blocks):
+        return jnp.concatenate(both_cores(blocks), axis=0)
 
 
 class RowSum:
@@ -143,31 +161,23 @@
         self.rows = rows_local
         self.half = inputs[0].shape[0] // 2
         self.terms_of = terms_of
-        self.inputs = inputs
+        self.inputs = tuple(inputs)
         self.count = 0
-        self.total = self.terms(inputs, 0, 1)[0].astype(LOW)
-
-    def terms(self, inputs, start, stop):
-        start, stop = start * self.rows, stop * self.rows
-        far = self.terms_of(*(v[self.half + start : self.half + stop] for v in inputs))
-        near = self.terms_of(*(v[start:stop] for v in inputs))
-        got = hop(far.astype(LOW), "c").astype(HIGH)
-        return [
-            near[at : at + self.rows] + got[at : at + self.rows]
-            for at in range(0, stop - start, self.rows)
-        ]
+        self.total = self.terms(self.inputs, 0).astype(LOW)
+
+    def terms(self, inputs, block):
+        near, far = block * self.rows, self.half + block * self.rows
+        far_terms = self.terms_of(*(v[far : far + self.rows] for v in inputs))
+        got = hop(far_terms.astype(LOW), "c")
+        return self.terms_of(*(v[near : near + self.rows] for v in inputs)) + got.astype(HIGH)
 
     def step(self):
         (got,) = self.ticks.tick((self.total, 1))
         self.sent = self.ticks.sent
-        if not self.count:
-            inputs = after(tuple(self.inputs), self.sent)
-            self.rest = self.terms(inputs, 1, lax.axis_size("z"))
-        self.total = self.rest[self.count] + got.astype(HIGH)
         self.count += 1
-        if self.count < len(self.rest):
+        self.total = self.terms(after(self.inputs, self.sent), self.count) + got.astype(HIGH)
+        if self.count < 3:
             self.total = self.total.astype(LOW)
-        return got
 
     def finish(self):
         while self.count < 3:
@@ -333,21 +343,22 @@
     rank_ref,
     core_ref,
     query_ref,
-    grad_ref,
     mixed_ref,
     lse_ref,
     key_ref,
     value_ref,
-    grad_query_ref,
-    grad_key_ref,
-    grad_value_ref,
-    key_sum_ref,
-    value_sum_ref,
+    weight_ref,
+    *refs,
 ):
+    *branch_refs, grad_query_ref, grad_key_ref, grad_value_ref = refs[:-3]
+    grad_ref, key_sum_ref, value_sum_ref = refs[-3:]
     heads = query_ref.shape[2] // HD
     half_rows = query_ref.shape[1] // rank_ref.shape[0]
     span_rows = 2 * half_rows
     columns = [slice(h * HD, (h + 1) * HD) for h in range(heads)]
+    for at, ref in enumerate(branch_refs):
+        rows = slice(at % 4 * half_rows, (at % 4 + 1) * half_rows)
+        grad_ref[at // 4, rows, :] = matmul_right_t(ref[...], weight_ref[...]).astype(LOW)
     key_sum_ref[...] = jnp.zeros_like(key_sum_ref)
     value_sum_ref[...] = jnp.zeros_like(value_sum_ref)
 
@@ -441,7 +452,7 @@
         ),
         compiler_params=pltpu.CompilerParams(vmem_limit_bytes=56 * 2**20),
         cost_estimate=pl.CostEstimate(
-            flops=2 * pairs, bytes_accessed=4 * key_rows * features, transcendentals=pairs // 256
+            flops=20 * pairs, bytes_accessed=4 * key_rows * features, transcendentals=pairs // 256
         ),
         name="attention_forward",
     )(
@@ -453,57 +464,62 @@
     return mixed.reshape(rows, features), lse
 
 
-def attention_backward(scalars, head, queries, grads, mixed, lse, keys, values):
+def attention_backward(scalars, queries, mixed, lse, keys, values, weight_out, branch_blocks):
     rows, features = queries.shape
     key_rows = keys.shape[0]
-    pairs = rows * key_rows * HD
+    heads = heads_at_once(key_rows, features)
+    width = heads * HD
+    pairs = rows * key_rows * features
     sides = key_rows // rows
     own_shape = (2, rows // 2, features)
     key_shape = (sides, 2, rows // 2, features)
-    own_part, key_part = own_shape[:2] + (HD,), key_shape[:3] + (HD,)
-    own = pl.BlockSpec(own_part, lambda i, *_: (0, 0, head))
-    other = pl.BlockSpec(key_part, lambda i, *_: (0, 0, 0, head))
-    own_out = pl.BlockSpec(own_part, lambda i, *_: (0, 0, 0))
-    other_out = pl.BlockSpec(key_part, lambda i, *_: (0, 0, 0, 0))
+    once = pl.Buffered(1)
+    own_part, key_part = own_shape[:2] + (width,), key_shape[:3] + (width,)
+    own = pl.BlockSpec(own_part, lambda h, *_: (0, 0, h))
+    other = pl.BlockSpec(key_part, lambda h, *_: (0, 0, 0, h))
+    other_in = pl.BlockSpec(key_part, lambda h, *_: (0, 0, 0, h), pipeline_mode=once)
+    block = pl.BlockSpec(branch_blocks[0].shape, lambda h, *_: (0, 0), pipeline_mode=once)
     grad_queries, grad_keys, grad_values = pl.pallas_call(
         backward_kernel,
         out_shape=(
-            jax.ShapeDtypeStruct(own_part, LOW),
-            jax.ShapeDtypeStruct(key_part, LOW),
-            jax.ShapeDtypeStruct(key_part, LOW),
+            jax.ShapeDtypeStruct(own_shape, LOW),
+            jax.ShapeDtypeStruct(key_shape, LOW),
+            jax.ShapeDtypeStruct(key_shape, LOW),
         ),
         grid_spec=pltpu.PrefetchScalarGridSpec(
             num_scalar_prefetch=3,
-            grid=(1,),
+            grid=(features // width,),
             in_specs=[
                 own,
                 own,
-                own,
-                pl.BlockSpec((1, 8, rows), lambda i, *_: (head, 0, 0)),
-                other,
-                other,
-            ],
-            out_specs=[own_out, other_out, other_out],
-            scratch_shapes=[pltpu.VMEM(key_part, HIGH)] * 2,
+                pl.BlockSpec((heads, 8, rows), lambda h, *_: (h, 0, 0)),
+                other_in,
+                other_in,
+                pl.BlockSpec((width, weight_out.shape[1]), lambda h, *_: (h, 0)),
+            ]
+            + [block] * len(branch_blocks),
+            out_specs=[own, other, other],
+            scratch_shapes=[pltpu.VMEM(own_part, LOW)] + [pltpu.VMEM(key_part, HIGH)] * 2,
         ),
         compiler_params=pltpu.CompilerParams(vmem_limit_bytes=56 * 2**20),
         cost_estimate=pl.CostEstimate(
-            flops=5 * pairs, bytes_accessed=8 * key_rows * HD, transcendentals=pairs // 256
+            flops=120 * pairs, bytes_accessed=8 * key_rows * features, transcendentals=pairs // 256
         ),
         name="attention_backward",
     )(
         *scalars,
         queries.reshape(own_shape),
-        grads.reshape(own_shape),
         mixed.reshape(own_shape),
         lse,
         keys.reshape(key_shape),
         values.reshape(key_shape),
+        weight_out,
+        *branch_blocks,
     )
     return (
-        grad_queries.reshape(rows, HD),
-        grad_keys.reshape(key_rows, HD),
-        grad_values.reshape(key_rows, HD),
+        grad_queries.reshape(rows, features),
+        grad_keys.reshape(key_rows, features),
+        grad_values.reshape(key_rows, features),
     )
 
 
@@ -553,46 +569,69 @@
     shared_low = normed_kv.astype(LOW)
     normed_low = normed_one.astype(LOW)
 
+    with jax.named_scope("out_weight"):
+        out_task = ticks.add(
+            gather_task(out_weight[: weight_rows // 2], out_weight[weight_rows // 2 :])
+        )
     with jax.named_scope("weight_columns"):
         pair = 2 * own_width
-        stacked = jnp.stack([key_weight, value_weight, query_weight], axis=1)
-        cut = [
-            lax.dynamic_slice_in_dim(stacked, jnp.mod(z + step, 4) * pair, pair, 2)
-            for step in range(4)
-        ]
-        shared_next, *over = ticks.tick((shared_low, 1), (cut[1], 1), (cut[2], 2), (cut[3], 3))
+        projections = (key_weight, value_weight, query_weight)
+
+        def cut(start, size, arrays):
+            return jnp.concatenate(
+                [lax.dynamic_slice_in_dim(v, start, size, 1) for v in arrays], axis=1
+            )
+
+        parts = [cut(jnp.mod(z + step, 4) * pair, pair, projections) for step in range(4)]
+        over = ticks.tick((parts[1], 1), (parts[2], 2), (parts[3], 3), lock=False)
         columns = []
-        for part in [cut[0]] + over:
-            keep = lax.dynamic_slice_in_dim(part, c * own_width, own_width, 2)
-            give = lax.dynamic_slice_in_dim(part, (1 - c) * own_width, own_width, 2)
-            columns += [keep, hop(give, "c")]
-        columns = jnp.stack(columns).reshape(8, weight_rows, 3 * own_width)
+        for part in [parts[0]] + over:
+            arrays = [part[:, i * pair : (i + 1) * pair] for i in range(3)]
+            columns.append(cut(c * own_width, own_width, arrays))
+            columns.append(hop(cut((1 - c) * own_width, own_width, arrays), "c"))
+        columns = jnp.stack(columns)
     with jax.named_scope("shared_rows"):
         weight_task = ticks.add(gather_task(columns[:4], columns[4:]))
-        shared_blocks = [shared_low, shared_next]
-        for _ in range(2):
-            shared_blocks += ticks.tick((shared_blocks[-1], 1))
-        group_shared = ticks.both_cores(shared_blocks)
+        shared_blocks = [shared_low]
+        for _ in range(3):
+            shared_blocks += ticks.tick((shared_blocks[-1], 1), lock=False)
+        group_shared = ticks.join_cores(shared_blocks)
     with jax.named_scope("weight_columns"):
         first, second = ticks.finish(weight_task)[0]
         weight_kv, weight_query = place_blocks(
             first + second, block_place, (2 * own_width, own_width)
         )
+    with jax.named_scope("out_weight"):
+        whole = jnp.arange(sides, dtype=jnp.int32)
+        whole_side = jnp.mod(x - whole // 2, size_x) * 2 + jnp.bitwise_xor(y, whole % 2)
+        out_pieces = ticks.finish(out_task)[0]
+        out_pieces = jnp.stack([part for pair in zip(*out_pieces) for part in pair])
+        out_pieces = jnp.take(
+            out_pieces.reshape(sides, weight_rows, width_model), whole_side, axis=0
+        ).reshape(2, size_x // 2, 2, weight_rows, width_model)
+        out_keep = lax.dynamic_index_in_dim(out_pieces, c, 0, keepdims=False)
+        out_give = lax.dynamic_index_in_dim(out_pieces, 1 - c, 0, keepdims=False)
+        out_got = hop(out_give, "c")
+        weight_out = jnp.where(
+            c == 0, jnp.stack([out_keep, out_got], axis=2), jnp.stack([out_got, out_keep], axis=2)
+        ).reshape(own_width, width_model)
+
     with jax.named_scope("keys_values"):
+        group_shared = after(group_shared, weight_out)
         keys_own = matmul(group_shared, weight_kv[:, :own_width]).astype(LOW)
         values_own = matmul(group_shared, weight_kv[:, own_width:]).astype(LOW)
         keys_task = ticks.add(gather_task(keys_own, values_own))
-    with jax.named_scope("out_weight"):
-        out_task = ticks.add(
-            gather_task(out_weight[: weight_rows // 2], out_weight[weight_rows // 2 :])
-        )
     with jax.named_scope("normed_rows"):
-        group_normed = ticks.gather_rows(normed_low)
+        normed_blocks = [normed_low]
+        for _ in range(3):
+            normed_blocks += ticks.tick((normed_blocks[-1], 1), lock=False)
+    with jax.named_scope("normed_rows"):
+        group_normed = ticks.join_cores(normed_blocks)
         queries = matmul(group_normed, weight_query).astype(LOW)
     with jax.named_scope("grad_output_rows"):
-        grad_back, grad_ahead = ticks.tick((grad_output, 1), (grad_output, -1))
+        grad_blocks = [grad_output] + ticks.tick((grad_output, 1))
     with jax.named_scope("keys_values"):
-        ((keys_all, values_all),) = ticks.finish(keys_task)
+        keys_all, values_all = after(ticks.finish(keys_task)[0], queries)
         keys_all, values_all = jnp.concatenate(keys_all), jnp.concatenate(values_all)
 
     span_of = (back_owner[None, :] * sides + side_owner[:, None]).reshape(-1)
@@ -616,27 +655,10 @@
         chunks = [unit_rows[cuts[i] : cuts[i + 1]] for i in range(4)]
         unit_tasks = [ticks.add(gather_task(chunks[i], chunks[i + 1])) for i in (0, 2)]
     with jax.named_scope("grad_output_rows"):
-        (grad_far,) = ticks.tick((grad_back, 1), room=2)
-        group_grad = ticks.both_cores([grad_output, grad_back, grad_far, grad_ahead])
+        grad_blocks += ticks.tick((grad_blocks[-1], 1), (grad_output, -1))
     mixed, lse = attention_forward(scalars, queries, keys_all, values_all)
-
-    with jax.named_scope("out_weight"):
-        whole = jnp.arange(sides, dtype=jnp.int32)
-        whole_side = jnp.mod(x - whole // 2, size_x) * 2 + jnp.bitwise_xor(y, whole % 2)
-        out_pieces = [
-            part for pair in zip(*ticks.finish(out_task)[0]) for part in pair
-        ]
-        out_pieces = jnp.stack(out_pieces).reshape(sides, weight_rows, width_model)
-        out_pieces = jnp.take(out_pieces, whole_side, axis=0).reshape(
-            2, size_x // 2, 2, weight_rows, width_model
-        )
-        out_keep = lax.dynamic_index_in_dim(out_pieces, c, 0, keepdims=False)
-        out_give = lax.dynamic_index_in_dim(out_pieces, 1 - c, 0, keepdims=False)
-        out_got = hop(out_give, "c")
-        weight_out = jnp.where(
-            c == 0, jnp.stack([out_keep, out_got], axis=2), jnp.stack([out_got, out_keep], axis=2)
-        ).reshape(own_width, width_model)
-
+    with jax.named_scope("grad_output_rows"):
+        group_grad = ticks.join_cores(grad_blocks)
     with jax.named_scope("attention_sum"):
         attention_sum = RowSum(ticks, lambda v: matmul(v, weight_out), [mixed], rows_local)
         residual = state_rows + attention_sum.finish()
@@ -669,6 +691,10 @@
         grad_hidden * up_act * sigmoid * (1.0 + gate_act * (1.0 - sigmoid))
     ).astype(LOW)
     grad_up_act = (grad_hidden * silu_act).astype(LOW)
+    def unit_parts(values):
+        step = values.shape[0] // sides
+        return [values[s * step : (s + 1) * step] for s in range(sides)]
+
     with jax.named_scope("ffn_grad_sum"):
         ffn_grad_sum = RowSum(
             ticks,
@@ -676,23 +702,12 @@
             [grad_gate_act, grad_up_act],
             rows_local,
         )
-        ffn_grad_sum.step()
-        ffn_grad_sum.step()
-        sent = ffn_grad_sum.sent
-
-    def unit_parts(values):
-        step = values.shape[0] // sides
-        return [values[s * step : (s + 1) * step] for s in range(sides)]
-
-    with jax.named_scope("unit_weight_sums"):
-        unit_terms = [
-            unit_parts(matmul_left_t(after(left, sent), right).astype(LOW))
-            for left, right in (
-                (grad_gate_act, group_in),
-                (grad_up_act, group_in),
-                (hidden, group_grad),
-            )
-        ]
+        unit_terms = []
+
+        def unit_window(left, right):
+            ffn_grad_sum.step()
+            terms = matmul_left_t(after(left, ffn_grad_sum.sent), right).astype(LOW)
+            unit_terms.append(unit_parts(terms))
 
         def chunk_parts(i):
             parts = []
@@ -703,51 +718,51 @@
                     start, stop = max(low, cuts[i]), min(low + units_padded, cuts[i + 1])
                     if start < stop:
                         rows.append(unit_terms[which][s][start - low : stop - low])
-                parts.append(jnp.concatenate(rows, axis=0))
+                parts.append(jnp.concatenate(rows, axis=0) if rows[1:] else rows[0])
             return parts
 
-        unit_sum_tasks = [
-            ticks.add(sum_task(chunk_parts(i), chunk_parts(i + 1))) for i in (0, 2)
-        ]
-
-    with jax.named_scope("ffn_grad_sum"):
+        unit_window(grad_gate_act, group_in)
+        unit_window(grad_up_act, group_in)
+        unit_sum_tasks = [ticks.add(sum_task(chunk_parts(0), chunk_parts(1)))]
+        unit_window(hidden, group_grad)
+        unit_sum_tasks.append(ticks.add(sum_task(chunk_parts(2), chunk_parts(3))))
         grad_ffn = ffn_grad_sum.finish()
+
     gain_two, grad_norm_two = norm_backward(grad_ffn, plain_two, factor_two, ffn_gain)
     grad_residual = grad_output.astype(HIGH) + grad_norm_two
     with jax.named_scope("branch_rows"):
-        group_branch = ticks.gather_rows(grad_residual.astype(LOW))
-    grad_mixed = matmul_right_t(group_branch, weight_out).astype(LOW)
+        branch_blocks = [grad_residual.astype(LOW)]
+        branch_blocks += ticks.tick((branch_blocks[-1], 1))
+        lined = jnp.arange(8, dtype=jnp.int32)
+        order = jnp.bitwise_xor(c, lined % 2) * 4 + jnp.mod(z - lined // 2 - 1, 4)
+        late_hidden = after(hidden, ticks.sent).reshape(8, rows_local, -1)
+        late_hidden = jnp.take(late_hidden, order, axis=0).reshape(8 * rows_local, -1)
+        branch_blocks += ticks.tick((branch_blocks[-1], 1))
+        terms = matmul(after(late_hidden, ticks.sent), weight_down).astype(LOW)
+        branch_blocks += ticks.tick((branch_blocks[-1], 1))
+        branch_both = both_cores(branch_blocks)
     with jax.named_scope("ffn_sum"):
-        ffn_sum = RowSum(
-            ticks,
-            lambda v: matmul(v, weight_down),
-            [after(hidden, grad_residual)],
-            rows_local,
-        )
-    head_terms = []
-    key_tasks = []
-    backward_inputs = (queries, grad_mixed, mixed)
-    for head in range(own_width // HD):
-        if ffn_sum.count < 2:
-            with jax.named_scope("ffn_sum"):
-                backward_inputs = after(backward_inputs, ticks.over_z)
-                ffn_sum.step()
-        terms = attention_backward(
-            scalars, head, *after(backward_inputs, ffn_sum.sent), lse, keys_all, values_all
-        )
-        head_terms.append(terms[0])
-        with jax.named_scope("grad_keys_values"):
-            key_tasks.append(ticks.add(sum_task(unit_parts(terms[1]), unit_parts(terms[2]))))
-    grad_queries = jnp.concatenate(head_terms, axis=1)
+        branch = lax.psum_scatter(
+            after(terms, branch_blocks[-1]), ("z", "c"), scatter_dimension=0, tiled=True
+        )
+        output = (residual + branch.astype(HIGH)).astype(LOW)
+    with jax.named_scope("unit_weight_sums"):
+        ticks.tick(room=2, lock=False, hold=True)
+    grad_queries, key_terms, value_terms = attention_backward(
+        scalars, queries, mixed, lse, keys_all, values_all, weight_out, branch_both
+    )
+
+    with jax.named_scope("unit_weight_sums"):
+        ticks.release(grad_queries)
 
     def side_parts(values, k):
-        chunks = values.reshape(2 * sides, -1, values.shape[1])
+        count = values.shape[0] // (2 * sides)
         return [
-            lax.dynamic_index_in_dim(
-                chunks,
-                2 * jnp.bitwise_xor(jnp.bitwise_xor(side_owner[s], z), 2 * k) + k,
+            lax.dynamic_slice_in_dim(
+                values,
+                (2 * jnp.bitwise_xor(jnp.bitwise_xor(side_owner[s], z), 2 * k) + k) * count,
+                count,
                 0,
-                keepdims=False,
             )
             for s in range(sides)
         ]
@@ -780,6 +795,10 @@
             for at in range(0, first.shape[1], own_width)
         ]
 
+    with jax.named_scope("grad_keys_values"):
+        keys_task = ticks.add(
+            sum_task(unit_parts(key_terms), unit_parts(value_terms)), urgent=True
+        )
     with jax.named_scope("normed_sum"):
         normed_sum = RowSum(
             ticks, lambda v: matmul_right_t(v, weight_query), [grad_queries], rows_local
@@ -789,16 +808,12 @@
     with jax.named_scope("query_weight_sum"):
         query_terms = matmul_left_t(after(group_normed, sent), grad_queries).astype(LOW)
     with jax.named_scope("out_weight_sum"):
-        out_terms = matmul_left_t(after(group_branch, sent), mixed).astype(LOW)
+        group_branch = jnp.concatenate(after(branch_both, sent), axis=0)
+        out_terms = matmul_left_t(group_branch, mixed).astype(LOW)
     with jax.named_scope("normed_sum"):
         grad_normed = normed_sum.finish()
-    with jax.named_scope("ffn_sum"):
-        output = (residual + ffn_sum.finish()).astype(LOW)
     with jax.named_scope("grad_keys_values"):
-        parts = ticks.finish(*key_tasks)
-        grad_kv = jnp.concatenate(
-            [part[0] for part in parts] + [part[1] for part in parts], axis=1
-        )
+        grad_kv = jnp.concatenate(ticks.finish(keys_task)[0], axis=1)
     with jax.named_scope("query_out_weight_sum"):
         query_out_task = ticks.add(
             chunk_sums(jnp.concatenate([query_terms, out_terms], axis=1))
@@ -807,6 +822,7 @@
         shared_sum = RowSum(
             ticks, lambda v: matmul_right_t(v, weight_kv), [grad_kv], rows_local
         )
+        shared_sum.total = after(shared_sum.total, branch)
         shared_sum.step()
         sent = shared_sum.sent
     with jax.named_scope("key_value_weight_sum"):

time: 767 us -> 634 us (0.83)
  the two profiles are of different devices: /device:TPU:0 before, /device:TPU:6 now
where the time goes in v3:
time: 634 us; the launch traced here: 625 us
  waiting for transfers between devices  273 us (43%)
  starting transfers between devices  104 us (16%)
  matrix products  74.6 us (12%)
  local copies, waits for them, and re-layouts  60 us (9%)
  Pallas kernels  50.4 us (8%)
  other arithmetic  42.5 us (7%)
  between operations  19.7 us (3%)
    ppermute x131, waiting for transfers between devices, hop(): lax.ppermute(values, axis, [(i, (i + steps) % size) for i in range(size)])  247 us
    ppermute x131, starting transfers between devices, hop(): lax.ppermute(values, axis, [(i, (i + steps) % size) for i in range(size)])  81.8 us
    pallas_call x1, Pallas kernels, attention_backward(): pl.pallas_call(backward_kernel, out_shape=(jax.ShapeDtypeStruct(own_shape...  31.9 us
    unnamed x249, local copies, waits for them, and re-layouts  31.5 us
    dot_general x19, matrix products, matmul_right_t(): lax.dot_general(left_side, right_side, (((1,), (1,)), ((), ())), preferre...  29.7 us
    dot_general x28, matrix products, matmul(): return jnp.dot(left_side, right_side, preferred_element_type=HIGH)  27.2 us
    ppermute x4, waiting for transfers between devices, layout(): got = [lax.ppermute(sent[flip], ALL, to_layout[flip]) for flip in range(2)]  26.1 us
    ppermute x4, starting transfers between devices, layout(): got = [lax.ppermute(sent[flip], ALL, to_layout[flip]) for flip in range(2)]  17.7 us
  transfers between devices with their start and end apart: 137, of which 57 were waited for; matrix products, arithmetic and copies ran while one was open for 25% of the time, Pallas kernels for 8%

profile of v3, /device:TPU:6, one launch (start us, length us, event | category | flops | bytes accessed | tf_op | source)
XLA Modules:
  0.0 624.8 jit_solution(8755985016268334584)
XLA Ops:
  33.0 4.8 collective-permute-done.2
  44.9 7.1 %collective-permute-done.3 = bf16[128,2048]{1,0:T(8,128)(2,1)} collective-permute-done((bf16[128,2048]{1,0:T(8,128)(2,1)}, bf16[128,2048]{1,0:T(8,128)(2,1)}, u32[]{:S(2)}, u32[]{:S(2)}) %collective-permute-start.3) | collective-permute-done | bytes 524320 | tf_op jit(solution)/shard_map/shared_rows/ppermute | solution.py:29
  58.7 6.6 %collective-permute-done.8 = bf16[128,2048]{1,0:T(8,128)(2,1)} collective-permute-done((bf16[128,2048]{1,0:T(8,128)(2,1)}, bf16[128,2048]{1,0:T(8,128)(2,1)}, u32[]{:S(2)}, u32[]{:S(2)}) %collective-permute-start.8) | collective-permute-done | bytes 524320 | tf_op jit(solution)/shard_map/shared_rows/ppermute | solution.py:29
  70.5 7.5 %collective-permute-done.22.refs_7_ = bf16[4,64,768]{2,1,0:T(8,128)(2,1)S(1)} collective-permute-done((bf16[4,64,768]{2,1,0:T(8,128)(2,1)S(1)}, bf16[4,64,768]{2,1,0:T(8,128)(2,1)S(1)}, u32[]{:S(2)}, u32[]{:S(2)}) %collective-permute-start.22) | collective-permute-done | bytes 393248 | tf_op jit(solution)/shard_map/shared_rows/ppermute | solution.py:29
  87.5 9.9 %collective-permute-done.20 = bf16[128,2048]{1,0:T(8,128)(2,1)S(1)} collective-permute-done((bf16[128,2048]{1,0:T(8,128)(2,1)S(1)}, bf16[128,2048]{1,0:T(8,128)(2,1)S(1)}, u32[]{:S(2)}, u32[]{:S(2)}) %collective-permute-start.20) | collective-permute-done | bytes 524320 | tf_op jit(solution)/shard_map/normed_rows/ppermute | solution.py:29
  102.4 10.5 %collective-permute-done.23 = bf16[128,2048]{1,0:T(8,128)(2,1)} collective-permute-done((bf16[128,2048]{1,0:T(8,128)(2,1)S(1)}, bf16[128,2048]{1,0:T(8,128)(2,1)}, u32[]{:S(2)}, u32[]{:S(2)}) %collective-permute-start.23) | collective-permute-done | bytes 524320 | tf_op jit(solution)/shard_map/normed_rows/ppermute | solution.py:29
  119.4 8.3 %collective-permute-done.31 = bf16[128,2048]{1,0:T(8,128)(2,1)} collective-permute-done((bf16[128,2048]{1,0:T(8,128)(2,1)}, bf16[128,2048]{1,0:T(8,128)(2,1)}, u32[]{:S(2)}, u32[]{:S(2)}) %collective-permute-start.31) | collective-permute-done | bytes 524320 | tf_op jit(solution)/shard_map/normed_rows/ppermute | solution.py:29
  133.2 10.3 %collective-permute-done.38 = bf16[1024,256]{1,0:T(8,128)(2,1)S(1)} collective-permute-done((bf16[1024,256]{1,0:T(8,128)(2,1)S(1)}, bf16[1024,256]{1,0:T(8,128)(2,1)S(1)}, u32[]{:S(2)}, u32[]{:S(2)}) %collective-permute-start.38) | collective-permute-done | bytes 524320 | tf_op jit(solution)/shard_map/normed_rows/ppermute | solution.py:29
  151.7 16.4 %attention_forward.1 = (bf16[2,512,256]{2,1,0:T(8,128)(2,1)}, f32[2,8,1024]{2,1,0:T(8,128)}) custom-call(s32[16]{0:T(128)} %select_reduce_fusion.place_ref, s32[4]{0:T(128)} %bitcast.222, s32[1]{0:T(128)} %bitcast.1.core_ref, bf16[2,512,256]{2,1,0:T(8,128)(2,1)} %bitcast.220, bf16[4,2,512,256]{3,2,1,0:T(8,128)(2,1)} %bitcast.213, ...), custom_call_target="tpu_custom_call" | custom-call | flops 21474836480 | bytes 4194304 | tf_op jit(solution)/shard_map/attention_forward/pallas_call | solution.py:438
  179.7 3.1 collective-permute-start.51
  183.1 7.5 %collective-permute-done.45 = bf16[128,2048]{1,0:T(8,128)(2,1)S(1)} collective-permute-done((bf16[128,2048]{1,0:T(8,128)(2,1)S(1)}, bf16[128,2048]{1,0:T(8,128)(2,1)S(1)}, u32[]{:S(2)}, u32[]{:S(2)}) %collective-permute-start.45) | collective-permute-done | bytes 524320 | tf_op jit(solution)/shard_map/attention_sum/ppermute | solution.py:29
  197.5 9.7 %collective-permute-done.49 = bf16[128,2048]{1,0:T(8,128)(2,1)S(1)} collective-permute-done((bf16[128,2048]{1,0:T(8,128)(2,1)S(1)}, bf16[128,2048]{1,0:T(8,128)(2,1)S(1)}, u32[]{:S(2)}, u32[]{:S(2)}) %collective-permute-start.49) | collective-permute-done | bytes 524320 | tf_op jit(solution)/shard_map/attention_sum/ppermute | solution.py:29
  215.7 7.3 %collective-permute-done.53 = bf16[128,2048]{1,0:T(8,128)(2,1)S(1)} collective-permute-done((bf16[128,2048]{1,0:T(8,128)(2,1)S(1)}, bf16[128,2048]{1,0:T(8,128)(2,1)S(1)}, u32[]{:S(2)}, u32[]{:S(2)}) %collective-permute-start.53) | collective-permute-done | bytes 524320 | tf_op jit(solution)/shard_map/attention_sum/ppermute | solution.py:29
  228.5 11.5 %collective-permute-done.56 = bf16[128,2048]{1,0:T(8,128)(2,1)S(1)} collective-permute-done((bf16[128,2048]{1,0:T(8,128)(2,1)S(1)}, bf16[128,2048]{1,0:T(8,128)(2,1)S(1)}, u32[]{:S(2)}, u32[]{:S(2)}) %collective-permute-start.56) | collective-permute-done | bytes 524320 | tf_op jit(solution)/shard_map/normed_two_rows/ppermute | solution.py:29
  244.2 11.1 %collective-permute-done.59 = bf16[128,2048]{1,0:T(8,128)(2,1)S(1)} collective-permute-done((bf16[128,2048]{1,0:T(8,128)(2,1)S(1)}, bf16[128,2048]{1,0:T(8,128)(2,1)S(1)}, u32[]{:S(2)}, u32[]{:S(2)}) %collective-permute-start.59) | collective-permute-done | bytes 524320 | tf_op jit(solution)/shard_map/normed_two_rows/ppermute | solution.py:29
  256.5 13.5 %collective-permute-done.62 = bf16[128,2048]{1,0:T(8,128)(2,1)S(1)} collective-permute-done((bf16[128,2048]{1,0:T(8,128)(2,1)S(1)}, bf16[128,2048]{1,0:T(8,128)(2,1)S(1)}, u32[]{:S(2)}, u32[]{:S(2)}) %collective-permute-start.62) | collective-permute-done | bytes 524320 | tf_op jit(solution)/shard_map/normed_two_rows/ppermute | solution.py:29
  272.0 3.2 fusion.198
  275.2 3.2 fusion.197
  278.4 4.3 multiply_convert_fusion
  286.8 3.4 convolution_convert_fusion.3
  294.0 8.5 %collective-permute-done.75 = bf16[128,2048]{1,0:T(8,128)(2,1)S(1)} collective-permute-done((bf16[128,2048]{1,0:T(8,128)(2,1)S(1)}, bf16[128,2048]{1,0:T(8,128)(2,1)S(1)}, u32[]{:S(2)}, u32[]{:S(2)}) %collective-permute-start.75) | collective-permute-done | bytes 524320 | tf_op jit(solution)/shard_map/ffn_grad_sum/ppermute | solution.py:29
  305.2 3.4 convolution_convert_fusion.2
  311.6 6.6 %collective-permute-done.77 = bf16[128,2048]{1,0:T(8,128)(2,1)S(1)} collective-permute-done((bf16[128,2048]{1,0:T(8,128)(2,1)S(1)}, bf16[128,2048]{1,0:T(8,128)(2,1)S(1)}, u32[]{:S(2)}, u32[]{:S(2)}) %collective-permute-start.77) | collective-permute-done | bytes 524320 | tf_op jit(solution)/shard_map/ffn_grad_sum/ppermute | solution.py:29
  321.3 3.4 convolution_convert_fusion.1
  335.0 3.6 collective-permute-done.81
  344.1 6.2 collective-permute-done.85
  359.4 10.9 %collective-permute-done.83.refs_1_ = bf16[128,2048]{1,0:T(8,128)(2,1)} collective-permute-done((bf16[128,2048]{1,0:T(8,128)(2,1)}, bf16[128,2048]{1,0:T(8,128)(2,1)}, u32[]{:S(2)}, u32[]{:S(2)}) %collective-permute-start.83) | collective-permute-done | bytes 524320 | tf_op jit(solution)/shard_map/branch_rows/ppermute | solution.py:29
  371.0 7.7 %convolution_convert_fusion = bf16[1024,2048]{1,0:T(8,128)(2,1)} fusion(bf16[1024,704]{0,1:T(8,128)(2,1)} %bitcast_select_fusion, bf16[704,2048]{1,0:T(8,128)(2,1)} %copy-done.64), kind=kOutput, calls=%fused_computation.19 | convolution fusion | flops 2954887168 | bytes 8519680 | tf_op jit(solution)/shard_map/branch_rows/dot_general | solution.py:235
  378.7 6.1 collective-permute-done.86.refs_2_
  388.6 9.4 %collective-permute-done.94 = bf16[144,2048]{1,0:T(8,128)(2,1)S(1)} collective-permute-done((bf16[144,2048]{1,0:T(8,128)(2,1)S(1)}, bf16[144,2048]{1,0:T(8,128)(2,1)S(1)}, u32[]{:S(2)}, u32[]{:S(2)}) %collective-permute-start.94) | collective-permute-done | bytes 589856 | tf_op jit(solution)/shard_map/branch_rows/ppermute | solution.py:29
  402.1 31.9 %attention_backward.1 = (bf16[2,512,256]{2,1,0:T(8,128)(2,1)}, bf16[4,2,512,256]{3,2,1,0:T(8,128)(2,1)}, bf16[4,2,512,256]{3,2,1,0:T(8,128)(2,1)}) custom-call(s32[16]{0:T(128)} %select_reduce_fusion.place_ref, s32[4]{0:T(128)} %bitcast.223, s32[1]{0:T(128)} %bitcast.1.core_ref, bf16[2,512,256]{2,1,0:T(8,128)(2,1)} %bitcast.221, ...), custom_call_target="tpu_custom_call" | custom-call | flops 128849018880 | bytes 8388608 | tf_op jit(solution)/shard_map/attention_backward/pallas_call | solution.py:482
  442.5 4.1 collective-permute-start.104
  446.6 3.8 collective-permute-start.105
  464.0 7.0 %collective-permute-done.97 = bf16[128,2048]{1,0:T(8,128)(2,1)S(1)} collective-permute-done((bf16[128,2048]{1,0:T(8,128)(2,1)S(1)}, bf16[128,2048]{1,0:T(8,128)(2,1)S(1)}, u32[]{:S(2)}, u32[]{:S(2)}) %collective-permute-start.97) | collective-permute-done | bytes 524320 | tf_op jit(solution)/shard_map/normed_sum/ppermute | solution.py:29
  473.2 11.3 %collective-permute-done.108 = bf16[1024,256]{1,0:T(8,128)(2,1)S(1)} collective-permute-done((bf16[1024,256]{1,0:T(8,128)(2,1)S(1)}, bf16[1024,256]{1,0:T(8,128)(2,1)S(1)}, u32[]{:S(2)}, u32[]{:S(2)}) %collective-permute-start.108) | collective-permute-done | bytes 524320 | tf_op jit(solution)/shard_map/normed_sum/ppermute | solution.py:29
  491.2 7.0 %collective-permute-done.111 = bf16[1024,256]{1,0:T(8,128)(2,1)S(1)} collective-permute-done((bf16[1024,256]{1,0:T(8,128)(2,1)S(1)}, bf16[1024,256]{1,0:T(8,128)(2,1)S(1)}, u32[]{:S(2)}, u32[]{:S(2)}) %collective-permute-start.111) | collective-permute-done | bytes 524320 | tf_op jit(solution)/shard_map/normed_sum/ppermute | solution.py:29
  498.8 3.1 collective-permute-done.107
  516.3 4.8 convolution_convert_fusion.4
  525.8 6.9 %collective-permute-done.114 = bf16[128,2048]{1,0:T(8,128)(2,1)S(1)} collective-permute-done((bf16[128,2048]{1,0:T(8,128)(2,1)}, bf16[128,2048]{1,0:T(8,128)(2,1)S(1)}, u32[]{:S(2)}, u32[]{:S(2)}) %collective-permute-start.114) | collective-permute-done | bytes 524320 | tf_op jit(solution)/shard_map/shared_sum/ppermute | solution.py:29
  538.5 4.3 collective-permute-done.124
  547.2 6.5 %collective-permute-start.125 = (bf16[256,512]{0,1:T(8,128)(2,1)S(1)}, bf16[256,512]{0,1:T(8,128)(2,1)S(1)}, u32[]{:S(2)}, u32[]{:S(2)}) collective-permute-start(bf16[256,512]{0,1:T(8,128)(2,1)S(1)} %get-tuple-element.347), channel_id=1, source_target_pairs={{0,0},{1,20},{2,8},{3,28},{4,16},{5,4},{6,24},{7,12},{8,9},{9,29},... | collective-permute-start | bytes 786440 | tf_op jit(solution)/shard_map/weight_layout/ppermute | solution.py:789
  558.1 17.7 %collective-permute-done.126 = bf16[256,512]{0,1:T(8,128)(2,1)S(1)} collective-permute-done((bf16[256,512]{0,1:T(8,128)(2,1)S(1)}, bf16[256,512]{0,1:T(8,128)(2,1)S(1)}, u32[]{:S(2)}, u32[]{:S(2)}) %collective-permute-start.126) | collective-permute-done | bytes 262176 | tf_op jit(solution)/shard_map/weight_layout/ppermute | solution.py:789
  579.7 3.6 collective-permute-done.129
  585.8 3.2 fusion.40
  589.9 4.8 all-to-all-start
  596.1 3.4 collective-permute-start.134
  599.6 5.9 collective-permute-start.133
  607.2 7.4 %collective-permute-done.134 = bf16[256,512]{0,1:T(8,128)(2,1)S(1)} collective-permute-done((bf16[256,512]{0,1:T(8,128)(2,1)S(1)}, bf16[256,512]{0,1:T(8,128)(2,1)S(1)}, u32[]{:S(2)}, u32[]{:S(2)}) %collective-permute-start.134) | collective-permute-done | bytes 262176 | tf_op jit(solution)/shard_map/weight_layout/ppermute | solution.py:789
  (670 shorter events, 243.4 us)
Async XLA Ops:
  7.3 508.9 %reduce-scatter.2.cloned.1.call-start = ((), (), s32[]{:S(2)}) async-start(), calls=%async_computation.2 | async-start | bytes 4718592 | tf_op jit(solution)/shard_map/ffn_sum/reduce_scatter | solution.py:745
  9.1 18.8 %collective-permute-start.4 = (bf16[32,2048]{1,0:T(8,128)(2,1)}, bf16[32,2048]{1,0:T(8,128)(2,1)}, u32[]{:S(2)}, u32[]{:S(2)}) collective-permute-start(bf16[32,2048]{1,0:T(8,128)(2,1)} %get-tuple-element.436), channel_id=1, source_target_pairs={{0,2},{2,0},{1,3},{3,1},{4,6},{6,4},{5,7},{7,5},{8,10},{10,8},{9,1... | collective-permute-start | bytes 393224 | tf_op jit(solution)/shard_map/weight_columns/ppermute | solution.py:29
  9.6 20.4 %collective-permute-start.6 = (bf16[32,2048]{1,0:T(8,128)(2,1)}, bf16[32,2048]{1,0:T(8,128)(2,1)S(1)}, u32[]{:S(2)}, u32[]{:S(2)}) collective-permute-start(bf16[32,2048]{1,0:T(8,128)(2,1)} %get-tuple-element.436), channel_id=1, source_target_pairs={{0,4},{4,0},{1,5},{5,1},{2,6},{6,2},{3,7},{7,3},{8,12},{12,8},{9,1... | collective-permute-start | bytes 393224 | tf_op jit(solution)/shard_map/weight_columns/ppermute | solution.py:29
  9.6 19.6 %collective-permute-start.5 = (bf16[32,2048]{1,0:T(8,128)(2,1)}, bf16[32,2048]{1,0:T(8,128)(2,1)S(1)}, u32[]{:S(2)}, u32[]{:S(2)}) collective-permute-start(bf16[32,2048]{1,0:T(8,128)(2,1)} %get-tuple-element.435), channel_id=1, source_target_pairs={{0,2},{2,0},{1,3},{3,1},{4,6},{6,4},{5,7},{7,5},{8,10},{10,8},{9,1... | collective-permute-start | bytes 393224 | tf_op jit(solution)/shard_map/weight_columns/ppermute | solution.py:29
  11.6 18.3 %collective-permute-start.7 = (bf16[32,2048]{1,0:T(8,128)(2,1)}, bf16[32,2048]{1,0:T(8,128)(2,1)}, u32[]{:S(2)}, u32[]{:S(2)}) collective-permute-start(bf16[32,2048]{1,0:T(8,128)(2,1)} %get-tuple-element.435), channel_id=1, source_target_pairs={{0,4},{4,0},{1,5},{5,1},{2,6},{6,2},{3,7},{7,3},{8,12},{12,8},{9,1... | collective-permute-start | bytes 393224 | tf_op jit(solution)/shard_map/weight_columns/ppermute | solution.py:29
  15.1 17.3 %collective-permute-start.1 = (bf16[64,1536]{1,0:T(8,128)(2,1)S(1)}, bf16[64,1536]{1,0:T(8,128)(2,1)S(1)}, u32[]{:S(2)}, u32[]{:S(2)}) collective-permute-start(bf16[64,1536]{1,0:T(8,128)(2,1)S(1)} %pad_maximum_fusion.13), channel_id=1, source_target_pairs={{0,16},{8,24},{16,0},{24,8},{1,17},{9,25},{17,1},{25,9},{2,18},{10... | collective-permute-start | bytes 589832 | tf_op jit(solution)/shard_map/weight_columns/ppermute | solution.py:29
  52.9 29.7 %collective-permute-start.27 = (bf16[128,2048]{1,0:T(8,128)(2,1)}, bf16[128,2048]{1,0:T(8,128)(2,1)}, u32[]{:S(2)}, u32[]{:S(2)}) collective-permute-start(bf16[128,2048]{1,0:T(8,128)(2,1)} %fusion.35), channel_id=1, source_target_pairs={{0,1},{1,0},{2,3},{3,2},{4,5},{5,4},{6,7},{7,6},{8,9},{9,8},{10,11... | collective-permute-start | bytes 1572872 | tf_op jit(solution)/shard_map/shared_rows/ppermute | solution.py:29
  66.4 63.5 %collective-permute-start.35 = (bf16[128,2048]{1,0:T(8,128)(2,1)}, bf16[128,2048]{1,0:T(8,128)(2,1)}, u32[]{:S(2)}, u32[]{:S(2)}) collective-permute-start(bf16[128,2048]{1,0:T(8,128)(2,1)} %fusion.42), channel_id=1, source_target_pairs={{0,1},{1,0},{2,3},{3,2},{4,5},{5,4},{6,7},{7,6},{8,9},{9,8},{10,11... | collective-permute-start | bytes 1572872 | tf_op jit(solution)/shard_map/normed_rows/ppermute | solution.py:29
  81.2 16.2 %collective-permute-start.20 = (bf16[128,2048]{1,0:T(8,128)(2,1)S(1)}, bf16[128,2048]{1,0:T(8,128)(2,1)S(1)}, u32[]{:S(2)}, u32[]{:S(2)}) collective-permute-start(bf16[128,2048]{1,0:T(8,128)(2,1)S(1)} %copy-done.53), channel_id=1, source_target_pairs={{0,8},{8,16},{16,24},{24,0},{1,9},{9,17},{17,25},{25,1},{2,10},{10... | collective-permute-start | bytes 1572872 | tf_op jit(solution)/shard_map/normed_rows/ppermute | solution.py:29
  100.2 17.6 %collective-permute-start.36 = (bf16[1024,256]{1,0:T(8,128)(2,1)}, bf16[1024,256]{1,0:T(8,128)(2,1)}, u32[]{:S(2)}, u32[]{:S(2)}) collective-permute-start(bf16[1024,256]{1,0:T(8,128)(2,1)} %convolution_convert_fusion.19), channel_id=1, source_target_pairs={{0,2},{2,0},{1,3},{3,1},{4,6},{6,4},{5,7},{7,5},{8,10},{10,8},{9,1... | collective-permute-start | bytes 1572872 | tf_op jit(solution)/shard_map/normed_rows/ppermute | solution.py:29
  100.9 17.5 %collective-permute-start.37 = (bf16[1024,256]{1,0:T(8,128)(2,1)}, bf16[1024,256]{1,0:T(8,128)(2,1)}, u32[]{:S(2)}, u32[]{:S(2)}) collective-permute-start(bf16[1024,256]{1,0:T(8,128)(2,1)} %convolution_convert_fusion.19), channel_id=1, source_target_pairs={{0,4},{4,0},{1,5},{5,1},{2,6},{6,2},{3,7},{7,3},{8,12},{12,8},{9,1... | collective-permute-start | bytes 1572872 | tf_op jit(solution)/shard_map/normed_rows/ppermute | solution.py:29
  129.2 18.0 %collective-permute-start.41 = (bf16[128,2048]{1,0:T(8,128)(2,1)S(1)}, bf16[128,2048]{1,0:T(8,128)(2,1)}, u32[]{:S(2)}, u32[]{:S(2)}) collective-permute-start(bf16[128,2048]{1,0:T(8,128)(2,1)S(1)} %copy-done.24), channel_id=1, source_target_pairs={{0,8},{8,16},{16,24},{24,0},{1,9},{9,17},{17,25},{25,1},{2,10},{10... | collective-permute-start | bytes 1572872 | tf_op jit(solution)/shard_map/grad_output_rows/ppermute | solution.py:29
  147.2 27.7 %collective-permute-start.46 = (bf16[128,2048]{1,0:T(8,128)(2,1)S(1)}, bf16[128,2048]{1,0:T(8,128)(2,1)}, u32[]{:S(2)}, u32[]{:S(2)}) collective-permute-start(bf16[128,2048]{1,0:T(8,128)(2,1)S(1)} %get-tuple-element.177), channel_id=1, source_target_pairs={{0,2},{2,0},{1,3},{3,1},{4,6},{6,4},{5,7},{7,5},{8,10},{10,8},{9,1... | collective-permute-start | bytes 1572872 | tf_op jit(solution)/shard_map/grad_output_rows/ppermute | solution.py:29
  147.5 27.3 %collective-permute-start.47 = (bf16[128,2048]{1,0:T(8,128)(2,1)S(1)}, bf16[128,2048]{1,0:T(8,128)(2,1)}, u32[]{:S(2)}, u32[]{:S(2)}) collective-permute-start(bf16[128,2048]{1,0:T(8,128)(2,1)S(1)} %get-tuple-element.177), channel_id=1, source_target_pairs={{0,4},{4,0},{1,5},{5,1},{2,6},{6,2},{3,7},{7,3},{8,12},{12,8},{9,1... | collective-permute-start | bytes 1572872 | tf_op jit(solution)/shard_map/grad_output_rows/ppermute | solution.py:29
  149.4 25.1 %collective-permute-start.43 = (bf16[128,2048]{1,0:T(8,128)(2,1)S(1)}, bf16[128,2048]{1,0:T(8,128)(2,1)}, u32[]{:S(2)}, u32[]{:S(2)}) collective-permute-start(bf16[128,2048]{1,0:T(8,128)(2,1)S(1)} %copy-done.24), channel_id=1, source_target_pairs={{0,24},{8,0},{16,8},{24,16},{1,25},{9,1},{17,9},{25,17},{2,26},{10... | collective-permute-start | bytes 1572872 | tf_op jit(solution)/shard_map/grad_output_rows/ppermute | solution.py:29
  149.5 25.0 %collective-permute-start.42 = (bf16[128,2048]{1,0:T(8,128)(2,1)}, bf16[128,2048]{1,0:T(8,128)(2,1)}, u32[]{:S(2)}, u32[]{:S(2)}) collective-permute-start(bf16[128,2048]{1,0:T(8,128)(2,1)} %collective-permute-done.41), channel_id=1, source_target_pairs={{0,8},{8,16},{16,24},{24,0},{1,9},{9,17},{17,25},{25,1},{2,10},{10... | collective-permute-start | bytes 1572872 | tf_op jit(solution)/shard_map/grad_output_rows/ppermute | solution.py:29
  171.3 26.0 %collective-permute-start.71 = (bf16[128,2048]{1,0:T(8,128)(2,1)S(1)}, bf16[128,2048]{1,0:T(8,128)(2,1)S(1)}, u32[]{:S(2)}, u32[]{:S(2)}) collective-permute-start(bf16[128,2048]{1,0:T(8,128)(2,1)S(1)} %copy-done.24), channel_id=1, source_target_pairs={{0,1},{1,0},{2,3},{3,2},{4,5},{5,4},{6,7},{7,6},{8,9},{9,8},{10,11... | collective-permute-start | bytes 1572872 | tf_op jit(solution)/shard_map/grad_output_rows/ppermute | solution.py:29
  174.8 16.2 %collective-permute-start.50 = (bf16[128,2048]{1,0:T(8,128)(2,1)S(1)}, bf16[128,2048]{1,0:T(8,128)(2,1)S(1)}, u32[]{:S(2)}, u32[]{:S(2)}) collective-permute-start(bf16[128,2048]{1,0:T(8,128)(2,1)S(1)} %get-tuple-element.181), channel_id=1, source_target_pairs={{0,2},{2,0},{1,3},{3,1},{4,6},{6,4},{5,7},{7,5},{8,10},{10,8},{9,1... | collective-permute-start | bytes 1572872 | tf_op jit(solution)/shard_map/attention_sum/ppermute | solution.py:29
  191.0 16.2 %collective-permute-start.49 = (bf16[128,2048]{1,0:T(8,128)(2,1)S(1)}, bf16[128,2048]{1,0:T(8,128)(2,1)S(1)}, u32[]{:S(2)}, u32[]{:S(2)}) collective-permute-start(bf16[128,2048]{1,0:T(8,128)(2,1)S(1)} %add_convert_fusion.16), channel_id=1, source_target_pairs={{0,8},{8,16},{16,24},{24,0},{1,9},{9,17},{17,25},{25,1},{2,10},{10... | collective-permute-start | bytes 1572872 | tf_op jit(solution)/shard_map/attention_sum/ppermute | solution.py:29
  223.8 48.2 %collective-permute-start.66 = (bf16[128,2048]{1,0:T(8,128)(2,1)S(1)}, bf16[128,2048]{1,0:T(8,128)(2,1)S(1)}, u32[]{:S(2)}, u32[]{:S(2)}) collective-permute-start(bf16[128,2048]{1,0:T(8,128)(2,1)S(1)} %multiply_convert_fusion.3), channel_id=1, source_target_pairs={{0,1},{1,0},{2,3},{3,2},{4,5},{5,4},{6,7},{7,6},{8,9},{9,8},{10,11... | collective-permute-start | bytes 1572872 | tf_op jit(solution)/shard_map/normed_two_rows/ppermute | solution.py:29
  240.0 30.3 %collective-permute-start.63 = (bf16[128,2048]{1,0:T(8,128)(2,1)S(1)}, bf16[128,2048]{1,0:T(8,128)(2,1)S(1)}, u32[]{:S(2)}, u32[]{:S(2)}) collective-permute-start(bf16[128,2048]{1,0:T(8,128)(2,1)S(1)} %collective-permute-done.56), channel_id=1, source_target_pairs={{0,1},{1,0},{2,3},{3,2},{4,5},{5,4},{6,7},{7,6},{8,9},{9,8},{10,11... | collective-permute-start | bytes 1572872 | tf_op jit(solution)/shard_map/normed_two_rows/ppermute | solution.py:29
  240.2 16.2 %collective-permute-start.72 = (bf16[144,2048]{1,0:T(8,128)(2,1)S(1)}, bf16[144,2048]{1,0:T(8,128)(2,1)S(1)}, u32[]{:S(2)}, u32[]{:S(2)}) collective-permute-start(bf16[144,2048]{1,0:T(8,128)(2,1)S(1)} %collective-permute-done.57), channel_id=1, source_target_pairs={{0,4},{4,0},{1,5},{5,1},{2,6},{6,2},{3,7},{7,3},{8,12},{12,8},{9,1... | collective-permute-start | bytes 1769480 | tf_op jit(solution)/shard_map/normed_two_rows/ppermute | solution.py:29
  335.0 63.6 %collective-permute-start.90 = (bf16[128,2048]{1,0:T(8,128)(2,1)S(1)}, bf16[128,2048]{1,0:T(8,128)(2,1)}, u32[]{:S(2)}, u32[]{:S(2)}) collective-permute-start(bf16[128,2048]{1,0:T(8,128)(2,1)S(1)} %fusion.177.refs_3_), channel_id=1, source_target_pairs={{0,1},{1,0},{2,3},{3,2},{4,5},{5,4},{6,7},{7,6},{8,9},{9,8},{10,11... | collective-permute-start | bytes 1572872 | tf_op jit(solution)/shard_map/branch_rows/ppermute | solution.py:29
  335.0 16.8 %collective-permute-start.80 = (bf16[128,2048]{1,0:T(8,128)(2,1)S(1)}, bf16[128,2048]{1,0:T(8,128)(2,1)}, u32[]{:S(2)}, u32[]{:S(2)}) collective-permute-start(bf16[128,2048]{1,0:T(8,128)(2,1)S(1)} %fusion.177.refs_3_), channel_id=1, source_target_pairs={{0,8},{8,16},{16,24},{24,0},{1,9},{9,17},{17,25},{25,1},{2,10},{10... | collective-permute-start | bytes 1572872 | tf_op jit(solution)/shard_map/branch_rows/ppermute | solution.py:29
  351.8 18.8 %collective-permute-start.93 = (bf16[128,2048]{1,0:T(8,128)(2,1)}, bf16[128,2048]{1,0:T(8,128)(2,1)}, u32[]{:S(2)}, u32[]{:S(2)}) collective-permute-start(bf16[128,2048]{1,0:T(8,128)(2,1)} %pad_maximum_fusion.5), channel_id=1, source_target_pairs={{0,2},{2,0},{1,3},{3,1},{4,6},{6,4},{5,7},{7,5},{8,10},{10,8},{9,1... | collective-permute-start | bytes 1572872 | tf_op jit(solution)/shard_map/branch_rows/ppermute | solution.py:29
  352.3 18.3 %collective-permute-start.92 = (bf16[144,2048]{1,0:T(8,128)(2,1)}, bf16[144,2048]{1,0:T(8,128)(2,1)S(1)}, u32[]{:S(2)}, u32[]{:S(2)}) collective-permute-start(bf16[144,2048]{1,0:T(8,128)(2,1)} %get-tuple-element.218), channel_id=1, source_target_pairs={{0,4},{4,0},{1,5},{5,1},{2,6},{6,2},{3,7},{7,3},{8,12},{12,8},{9,1... | collective-permute-start | bytes 1769480 | tf_op jit(solution)/shard_map/branch_rows/ppermute | solution.py:29
  359.4 39.2 %collective-permute-start.87 = (bf16[128,2048]{1,0:T(8,128)(2,1)}, bf16[128,2048]{1,0:T(8,128)(2,1)S(1)}, u32[]{:S(2)}, u32[]{:S(2)}) collective-permute-start(bf16[128,2048]{1,0:T(8,128)(2,1)} %collective-permute-done.80.refs_0_), channel_id=1, source_target_pairs={{0,1},{1,0},{2,3},{3,2},{4,5},{5,4},{6,7},{7,6},{8,9},{9,8},{10,11... | collective-permute-start | bytes 1572872 | tf_op jit(solution)/shard_map/branch_rows/ppermute | solution.py:29
  378.7 21.7 %collective-permute-start.88 = (bf16[128,2048]{1,0:T(8,128)(2,1)}, bf16[128,2048]{1,0:T(8,128)(2,1)}, u32[]{:S(2)}, u32[]{:S(2)}) collective-permute-start(bf16[128,2048]{1,0:T(8,128)(2,1)} %collective-permute-done.83.refs_1_), channel_id=1, source_target_pairs={{0,1},{1,0},{2,3},{3,2},{4,5},{5,4},{6,7},{7,6},{8,9},{9,8},{10,11... | collective-permute-start | bytes 1572872 | tf_op jit(solution)/shard_map/branch_rows/ppermute | solution.py:29
  385.3 16.8 %collective-permute-start.89 = (bf16[128,2048]{1,0:T(8,128)(2,1)}, bf16[128,2048]{1,0:T(8,128)(2,1)}, u32[]{:S(2)}, u32[]{:S(2)}) collective-permute-start(bf16[128,2048]{1,0:T(8,128)(2,1)} %collective-permute-done.86.refs_2_), channel_id=1, source_target_pairs={{0,1},{1,0},{2,3},{3,2},{4,5},{5,4},{6,7},{7,6},{8,9},{9,8},{10,11... | collective-permute-start | bytes 1572872 | tf_op jit(solution)/shard_map/branch_rows/ppermute | solution.py:29
  398.0 42.9 %collective-permute-start.98 = (bf16[128,2048]{1,0:T(8,128)(2,1)}, bf16[128,2048]{1,0:T(8,128)(2,1)S(1)}, u32[]{:S(2)}, u32[]{:S(2)}) collective-permute-start(bf16[128,2048]{1,0:T(8,128)(2,1)} %add_convert_fusion.13), channel_id=1, source_target_pairs={{0,4},{4,0},{1,5},{5,1},{2,6},{6,2},{3,7},{7,3},{8,12},{12,8},{9,1... | collective-permute-start | bytes 1572872 | tf_op jit(solution)/shard_map/unit_weight_sums/ppermute | solution.py:29
  398.6 38.9 %collective-permute-start.99 = (bf16[128,2048]{1,0:T(8,128)(2,1)}, bf16[128,2048]{1,0:T(8,128)(2,1)S(1)}, u32[]{:S(2)}, u32[]{:S(2)}) collective-permute-start(bf16[128,2048]{1,0:T(8,128)(2,1)} %add_convert_fusion.12), channel_id=1, source_target_pairs={{0,2},{2,0},{1,3},{3,1},{4,6},{6,4},{5,7},{7,5},{8,10},{10,8},{9,1... | collective-permute-start | bytes 1572872 | tf_op jit(solution)/shard_map/unit_weight_sums/ppermute | solution.py:29
  398.6 41.0 %collective-permute-start.100 = (bf16[128,2048]{1,0:T(8,128)(2,1)}, bf16[128,2048]{1,0:T(8,128)(2,1)S(1)}, u32[]{:S(2)}, u32[]{:S(2)}) collective-permute-start(bf16[128,2048]{1,0:T(8,128)(2,1)} %add_convert_fusion.11), channel_id=1, source_target_pairs={{0,4},{4,0},{1,5},{5,1},{2,6},{6,2},{3,7},{7,3},{8,12},{12,8},{9,1... | collective-permute-start | bytes 1572872 | tf_op jit(solution)/shard_map/unit_weight_sums/ppermute | solution.py:29
  400.4 42.1 %collective-permute-start.101 = (bf16[144,2048]{1,0:T(8,128)(2,1)S(1)}, bf16[144,2048]{1,0:T(8,128)(2,1)S(1)}, u32[]{:S(2)}, u32[]{:S(2)}) collective-permute-start(bf16[144,2048]{1,0:T(8,128)(2,1)S(1)} %add_convert_fusion.2), channel_id=1, source_target_pairs={{0,2},{2,0},{1,3},{3,1},{4,6},{6,4},{5,7},{7,5},{8,10},{10,8},{9,1... | collective-permute-start | bytes 1769480 | tf_op jit(solution)/shard_map/unit_weight_sums/ppermute | solution.py:29
  435.5 18.9 %collective-permute-start.91 = (bf16[128,2048]{1,0:T(8,128)(2,1)S(1)}, bf16[128,2048]{1,0:T(8,128)(2,1)S(1)}, u32[]{:S(2)}, u32[]{:S(2)}) collective-permute-start(bf16[128,2048]{1,0:T(8,128)(2,1)S(1)} %convolution_convert_fusion.14), channel_id=1, source_target_pairs={{0,1},{1,0},{2,3},{3,2},{4,5},{5,4},{6,7},{7,6},{8,9},{9,8},{10,11... | collective-permute-start | bytes 1572872 | tf_op jit(solution)/shard_map/normed_sum/ppermute | solution.py:29
  442.5 29.1 %collective-permute-start.104 = (bf16[1024,256]{1,0:T(8,128)(2,1)S(1)}, bf16[1024,256]{1,0:T(8,128)(2,1)S(1)}, u32[]{:S(2)}, u32[]{:S(2)}) collective-permute-start(bf16[1024,256]{1,0:T(8,128)(2,1)S(1)} %bitcast.211), channel_id=1, source_target_pairs={{0,4},{4,0},{1,5},{5,1},{2,6},{6,2},{3,7},{7,3},{8,12},{12,8},{9,1... | collective-permute-start | bytes 1572872 | tf_op jit(solution)/shard_map/normed_sum/ppermute | solution.py:29
  446.6 25.0 %collective-permute-start.105 = (bf16[1024,256]{1,0:T(8,128)(2,1)S(1)}, bf16[1024,256]{1,0:T(8,128)(2,1)S(1)}, u32[]{:S(2)}, u32[]{:S(2)}) collective-permute-start(bf16[1024,256]{1,0:T(8,128)(2,1)S(1)} %bitcast.212), channel_id=1, source_target_pairs={{0,2},{2,0},{1,3},{3,1},{4,6},{6,4},{5,7},{7,5},{8,10},{10,8},{9,1... | collective-permute-start | bytes 1572872 | tf_op jit(solution)/shard_map/normed_sum/ppermute | solution.py:29
  491.1 18.4 %collective-permute-start.106 = (bf16[128,2048]{1,0:T(8,128)(2,1)S(1)}, bf16[128,2048]{1,0:T(8,128)(2,1)S(1)}, u32[]{:S(2)}, u32[]{:S(2)}) collective-permute-start(bf16[128,2048]{1,0:T(8,128)(2,1)S(1)} %convolution_convert_fusion.11), channel_id=1, source_target_pairs={{0,1},{1,0},{2,3},{3,2},{4,5},{5,4},{6,7},{7,6},{8,9},{9,8},{10,11... | collective-permute-start | bytes 1572872 | tf_op jit(solution)/shard_map/normed_sum/ppermute | solution.py:29
  504.0 29.5 %collective-permute-start.120 = (bf16[256,512]{0,1:T(8,128)(2,1)}, bf16[256,512]{0,1:T(8,128)(2,1)S(1)}, u32[]{:S(2)}, u32[]{:S(2)}) collective-permute-start(bf16[256,512]{0,1:T(8,128)(2,1)} %get-tuple-element.257), channel_id=1, source_target_pairs={{0,2},{2,0},{1,3},{3,1},{4,6},{6,4},{5,7},{7,5},{8,10},{10,8},{9,1... | collective-permute-start | bytes 786440 | tf_op jit(solution)/shard_map/shared_sum/ppermute | solution.py:29
  505.0 28.6 %collective-permute-start.118 = (bf16[256,512]{0,1:T(8,128)(2,1)}, bf16[256,512]{0,1:T(8,128)(2,1)}, u32[]{:S(2)}, u32[]{:S(2)}) collective-permute-start(bf16[256,512]{0,1:T(8,128)(2,1)} %get-tuple-element.255), channel_id=1, source_target_pairs={{0,4},{4,0},{1,5},{5,1},{2,6},{6,2},{3,7},{7,3},{8,12},{12,8},{9,1... | collective-permute-start | bytes 786440 | tf_op jit(solution)/shard_map/shared_sum/ppermute | solution.py:29
  516.2 16.5 %collective-permute-start.114 = (bf16[128,2048]{1,0:T(8,128)(2,1)}, bf16[128,2048]{1,0:T(8,128)(2,1)S(1)}, u32[]{:S(2)}, u32[]{:S(2)}) collective-permute-start(bf16[128,2048]{1,0:T(8,128)(2,1)} %fusion.21), channel_id=1, source_target_pairs={{0,8},{8,16},{16,24},{24,0},{1,9},{9,17},{17,25},{25,1},{2,10},{10... | collective-permute-start | bytes 1572872 | tf_op jit(solution)/shard_map/shared_sum/ppermute | solution.py:29
  533.5 21.2 %collective-permute-start.116 = (bf16[128,2048]{1,0:T(8,128)(2,1)S(1)}, bf16[128,2048]{1,0:T(8,128)(2,1)S(1)}, u32[]{:S(2)}, u32[]{:S(2)}) collective-permute-start(bf16[128,2048]{1,0:T(8,128)(2,1)S(1)} %fusion.22), channel_id=1, source_target_pairs={{0,8},{8,16},{16,24},{24,0},{1,9},{9,17},{17,25},{25,1},{2,10},{10... | collective-permute-start | bytes 1572872 | tf_op jit(solution)/shard_map/shared_sum/ppermute | solution.py:29
  536.6 17.0 %collective-permute-start.127 = (bf16[256,512]{0,1:T(8,128)(2,1)S(1)}, bf16[256,512]{0,1:T(8,128)(2,1)S(1)}, u32[]{:S(2)}, u32[]{:S(2)}) collective-permute-start(bf16[256,512]{0,1:T(8,128)(2,1)S(1)} %get-tuple-element.263), channel_id=1, source_target_pairs={{0,4},{4,0},{1,5},{5,1},{2,6},{6,2},{3,7},{7,3},{8,12},{12,8},{9,1... | collective-permute-start | bytes 786440 | tf_op jit(solution)/shard_map/shared_sum/ppermute | solution.py:29
  545.2 30.5 %collective-permute-start.126 = (bf16[256,512]{0,1:T(8,128)(2,1)S(1)}, bf16[256,512]{0,1:T(8,128)(2,1)S(1)}, u32[]{:S(2)}, u32[]{:S(2)}) collective-permute-start(bf16[256,512]{0,1:T(8,128)(2,1)S(1)} %broadcast_select_fusion.3), channel_id=1, source_target_pairs={{0,20},{1,0},{2,28},{3,8},{4,4},{5,16},{6,12},{7,24},{8,29},{9,9},... | collective-permute-start | bytes 786440 | tf_op jit(solution)/shard_map/weight_layout/ppermute | solution.py:789
  547.2 28.7 %collective-permute-start.125 = (bf16[256,512]{0,1:T(8,128)(2,1)S(1)}, bf16[256,512]{0,1:T(8,128)(2,1)S(1)}, u32[]{:S(2)}, u32[]{:S(2)}) collective-permute-start(bf16[256,512]{0,1:T(8,128)(2,1)S(1)} %get-tuple-element.347), channel_id=1, source_target_pairs={{0,0},{1,20},{2,8},{3,28},{4,16},{5,4},{6,24},{7,12},{8,9},{9,29},... | collective-permute-start | bytes 786440 | tf_op jit(solution)/shard_map/weight_layout/ppermute | solution.py:789
  556.3 28.5 %collective-permute-start.122 = (bf16[128,2048]{1,0:T(8,128)(2,1)}, bf16[128,2048]{1,0:T(8,128)(2,1)}, u32[]{:S(2)}, u32[]{:S(2)}) collective-permute-start(bf16[128,2048]{1,0:T(8,128)(2,1)} %fusion.23), channel_id=1, source_target_pairs={{0,8},{8,16},{16,24},{24,0},{1,9},{9,17},{17,25},{25,1},{2,10},{10... | collective-permute-start | bytes 1572872 | tf_op jit(solution)/shard_map/shared_sum/ppermute | solution.py:29
  557.9 27.9 %collective-permute-start.121 = (bf16[128,2048]{1,0:T(8,128)(2,1)}, bf16[128,2048]{1,0:T(8,128)(2,1)}, u32[]{:S(2)}, u32[]{:S(2)}) collective-permute-start(bf16[128,2048]{1,0:T(8,128)(2,1)} %convolution_convert_fusion.7), channel_id=1, source_target_pairs={{0,1},{1,0},{2,3},{3,2},{4,5},{5,4},{6,7},{7,6},{8,9},{9,8},{10,11... | collective-permute-start | bytes 1572872 | tf_op jit(solution)/shard_map/shared_sum/ppermute | solution.py:29
  589.9 16.7 %all-to-all-start = ((f32[32,1,192]{2,1,0:T(1,128)}), f32[32,1,192]{2,1,0:T(1,128)S(1)}, u32[]{:S(2)}, u32[]{:S(2)}) async-start(f32[32,1,192]{2,1,0:T(1,128)} %all_to_all.8), calls=%async_computation.1 | async-start | bytes 65536 | tf_op jit(solution)/shard_map/all_to_all | solution.py:853
  596.1 18.5 %collective-permute-start.134 = (bf16[256,512]{0,1:T(8,128)(2,1)S(1)}, bf16[256,512]{0,1:T(8,128)(2,1)S(1)}, u32[]{:S(2)}, u32[]{:S(2)}) collective-permute-start(bf16[256,512]{0,1:T(8,128)(2,1)S(1)} %broadcast_select_fusion.1), channel_id=1, source_target_pairs={{0,20},{1,0},{2,28},{3,8},{4,4},{5,16},{6,12},{7,24},{8,29},{9,9},... | collective-permute-start | bytes 786440 | tf_op jit(solution)/shard_map/weight_layout/ppermute | solution.py:789
  (180 other events, 2216.6 us)
Sparse Core Ops, SparseCore 0:
  388.8 48.9 reduce-scatter.1

commit v4 on v3

--- a/solution.py
+++ b/solution.py
@@ -84,9 +84,11 @@
         self.over_z = ()
         self.sides = [(), ()]
         self.sent = None
+        self.held = []
+        self.places = []
 
     def add(self, task, urgent=False):
-        entry = {"task": task, "wanted": None, "open": 0, "result": None}
+        entry = {"task": task, "wanted": None, "open": 0, "result": None, "urgent": urgent}
         self.tasks.insert(0 if urgent else len(self.tasks), entry)
         self.advance(entry)
         return entry
@@ -99,14 +101,14 @@
             entry["result"] = stop.value
             self.tasks.remove(entry)
 
-    def tick(self, *moves, room=1, lock=True, hold=False):
+    def tick(self, *moves, room=1, lock=True):
         got = []
         for values, steps in moves:
             self.sent = after(values, self.over_z, self.sides[-2])
             got.append(hop(self.sent, "z", steps))
+        self.release(*([self.sent] if moves else []))
         left = {"x": room * self.BYTES, "y": room * self.BYTES}
         before = self.over_z if lock else ()
-        places = []
         arrived = []
         finished = []
         for entry in self.tasks:
@@ -115,7 +117,8 @@
                 if left[axis] >= min(values.nbytes, self.BYTES):
                     left[axis] -= values.nbytes
                     into.append(hop(after(values, self.sides[-1], before), axis))
-                    places.append((into, len(into) - 1))
+                    if not entry["urgent"]:
+                        self.places.append((into, len(into) - 1))
                     arrived.append(into[-1])
                     entry["open"] -= 1
                 else:
@@ -125,31 +128,40 @@
                 finished.append(entry)
         self.over_z = tuple(got) or self.over_z
         self.sides = self.sides[-1:] + [tuple(arrived)]
-        self.held = (places, finished)
-        if not hold:
-            self.release()
+        for entry in finished:
+            if entry["urgent"]:
+                self.advance(entry)
+            else:
+                self.held.append(entry)
         return got
 
     def release(self, *earlier):
-        places, finished = self.held
         if earlier:
-            for into, at in places:
+            for into, at in self.places:
                 into[at] = after(into[at], earlier)
-        for entry in finished:
+        held, self.held, self.places = self.held, [], []
+        for entry in held:
             self.tasks.remove(entry)
             self.tasks.append(entry)
             self.advance(entry)
 
     def finish(self, *entries):
+        self.release()
         while any(entry["result"] is None for entry in entries):
             self.tick()
+            self.release()
         return [entry["result"] for entry in entries]
 
-    def gather_rows(self, rows):
+    def gather_parts(self, rows):
         blocks = [rows]
         for _ in range(1, lax.axis_size("z")):
             blocks += self.tick((blocks[-1], 1))
-        return self.join_cores(blocks)
+            yield self.sent
+        yield both_cores(blocks)
+
+    def gather_rows(self, rows):
+        *_, blocks = self.gather_parts(rows)
+        return jnp.concatenate(blocks, axis=0)
 
     def join_cores(self, blocks):
         return jnp.concatenate(both_cores(blocks), axis=0)
@@ -171,17 +183,18 @@
         got = hop(far_terms.astype(LOW), "c")
         return self.terms_of(*(v[near : near + self.rows] for v in inputs)) + got.astype(HIGH)
 
-    def step(self):
-        (got,) = self.ticks.tick((self.total, 1))
+    def step(self, room=1):
+        (got,) = self.ticks.tick((self.total, 1), room=room)
         self.sent = self.ticks.sent
         self.count += 1
-        self.total = self.terms(after(self.inputs, self.sent), self.count) + got.astype(HIGH)
+        terms = lax.optimization_barrier(self.terms(after(self.inputs, self.sent), self.count))
+        self.total = terms + got.astype(HIGH)
         if self.count < 3:
             self.total = self.total.astype(LOW)
 
-    def finish(self):
+    def finish(self, room=1):
         while self.count < 3:
-            self.step()
+            self.step(room)
         return self.total
 
 
@@ -350,15 +363,22 @@
     weight_ref,
     *refs,
 ):
-    *branch_refs, grad_query_ref, grad_key_ref, grad_value_ref = refs[:-3]
-    grad_ref, key_sum_ref, value_sum_ref = refs[-3:]
+    *branch_refs, grad_query_ref, grad_key_ref, grad_value_ref = refs[:-4]
+    grad_ref, turned_ref, key_sum_ref, value_sum_ref = refs[-4:]
     heads = query_ref.shape[2] // HD
     half_rows = query_ref.shape[1] // rank_ref.shape[0]
     span_rows = 2 * half_rows
     columns = [slice(h * HD, (h + 1) * HD) for h in range(heads)]
-    for at, ref in enumerate(branch_refs):
-        rows = slice(at % 4 * half_rows, (at % 4 + 1) * half_rows)
-        grad_ref[at // 4, rows, :] = matmul_right_t(ref[...], weight_ref[...]).astype(LOW)
+    count = len(branch_refs) // 2
+    for core in range(2):
+        rows = [ref[...] for ref in branch_refs[core * count : (core + 1) * count]]
+        rows = jnp.concatenate(rows, axis=0)
+        grad_ref[core] = matmul_right_t(rows, weight_ref[...]).astype(LOW)
+    for h in range(heads):
+        for at in range(turned_ref.shape[1]):
+            rows = slice(at % 4 * half_rows, (at % 4 + 1) * half_rows)
+            keys = key_ref[at // 4, :, rows, columns[h]].reshape(span_rows, HD)
+            turned_ref[h, at] = jnp.transpose(keys)
     key_sum_ref[...] = jnp.zeros_like(key_sum_ref)
     value_sum_ref[...] = jnp.zeros_like(value_sum_ref)
 
@@ -397,10 +417,10 @@
                 key_term = matmul(grad_scores, query)
                 value_sum_ref[side, :, there, columns[h]] += value_term.reshape(2, half_rows, HD)
                 key_sum_ref[side, :, there, columns[h]] += key_term.reshape(2, half_rows, HD)
-                new.append(grad_query[h] + matmul_left_t(grad_scores, keys))
+                new.append(grad_query[h] + matmul(turned_ref[h, place_ref[step]], grad_scores))
             return tuple(new)
 
-        start = tuple(jnp.zeros((span_rows, HD), HIGH) for _ in range(heads))
+        start = tuple(jnp.zeros((HD, span_rows), HIGH) for _ in range(heads))
         grad_query = lax.fori_loop(
             0, rank // 2, lambda p, g: block(2 * p + 1, block(2 * p, g, None), None), start
         )
@@ -410,7 +430,7 @@
         visible = diagonal_visible(core_ref[0], span_rows, 0)
         grad_query = block(rank, grad_query, visible)
         for h in range(heads):
-            result = (grad_query[h] * SCORE_SCALE).astype(LOW)
+            result = (jnp.transpose(grad_query[h]) * SCORE_SCALE).astype(LOW)
             grad_query_ref[:, here, columns[h]] = result.reshape(2, half_rows, HD)
         return carry
 
@@ -499,7 +519,11 @@
             ]
             + [block] * len(branch_blocks),
             out_specs=[own, other, other],
-            scratch_shapes=[pltpu.VMEM(own_part, LOW)] + [pltpu.VMEM(key_part, HIGH)] * 2,
+            scratch_shapes=[
+                pltpu.VMEM(own_part, LOW),
+                pltpu.VMEM((heads, 4 * sides, HD, key_rows // (4 * sides)), LOW),
+            ]
+            + [pltpu.VMEM(key_part, HIGH)] * 2,
         ),
         compiler_params=pltpu.CompilerParams(vmem_limit_bytes=56 * 2**20),
         cost_estimate=pl.CostEstimate(
@@ -569,10 +593,6 @@
     shared_low = normed_kv.astype(LOW)
     normed_low = normed_one.astype(LOW)
 
-    with jax.named_scope("out_weight"):
-        out_task = ticks.add(
-            gather_task(out_weight[: weight_rows // 2], out_weight[weight_rows // 2 :])
-        )
     with jax.named_scope("weight_columns"):
         pair = 2 * own_width
         projections = (key_weight, value_weight, query_weight)
@@ -591,10 +611,15 @@
             columns.append(hop(cut((1 - c) * own_width, own_width, arrays), "c"))
         columns = jnp.stack(columns)
     with jax.named_scope("shared_rows"):
-        weight_task = ticks.add(gather_task(columns[:4], columns[4:]))
+        out_weight = after(out_weight, over)
+        out_task = ticks.add(
+            gather_task(out_weight[: weight_rows // 2], out_weight[weight_rows // 2 :]),
+            urgent=True,
+        )
+        weight_task = ticks.add(gather_task(columns[:4], columns[4:]), urgent=True)
         shared_blocks = [shared_low]
         for _ in range(3):
-            shared_blocks += ticks.tick((shared_blocks[-1], 1), lock=False)
+            shared_blocks += ticks.tick((shared_blocks[-1], 1), room=1.2, lock=False)
         group_shared = ticks.join_cores(shared_blocks)
     with jax.named_scope("weight_columns"):
         first, second = ticks.finish(weight_task)[0]
@@ -620,19 +645,21 @@
         group_shared = after(group_shared, weight_out)
         keys_own = matmul(group_shared, weight_kv[:, :own_width]).astype(LOW)
         values_own = matmul(group_shared, weight_kv[:, own_width:]).astype(LOW)
-        keys_task = ticks.add(gather_task(keys_own, values_own))
+        keys_task = ticks.add(gather_task(keys_own, values_own), urgent=True)
     with jax.named_scope("normed_rows"):
         normed_blocks = [normed_low]
         for _ in range(3):
             normed_blocks += ticks.tick((normed_blocks[-1], 1), lock=False)
     with jax.named_scope("normed_rows"):
         group_normed = ticks.join_cores(normed_blocks)
-        queries = matmul(group_normed, weight_query).astype(LOW)
     with jax.named_scope("grad_output_rows"):
         grad_blocks = [grad_output] + ticks.tick((grad_output, 1))
     with jax.named_scope("keys_values"):
-        keys_all, values_all = after(ticks.finish(keys_task)[0], queries)
-        keys_all, values_all = jnp.concatenate(keys_all), jnp.concatenate(values_all)
+        key_pieces, value_pieces = ticks.finish(keys_task)[0]
+        keys_all, values_all = jnp.concatenate(key_pieces), jnp.concatenate(value_pieces)
+    with jax.named_scope("queries"):
+        late_normed = after(group_normed, key_pieces[-1], value_pieces[-1])
+        queries = matmul(late_normed, weight_query).astype(LOW)
 
     span_of = (back_owner[None, :] * sides + side_owner[:, None]).reshape(-1)
     ranks = jnp.take(span_order, span_of)
@@ -691,6 +718,7 @@
         grad_hidden * up_act * sigmoid * (1.0 + gate_act * (1.0 - sigmoid))
     ).astype(LOW)
     grad_up_act = (grad_hidden * silu_act).astype(LOW)
+
     def unit_parts(values):
         step = values.shape[0] // sides
         return [values[s * step : (s + 1) * step] for s in range(sides)]
@@ -704,8 +732,8 @@
         )
         unit_terms = []
 
-        def unit_window(left, right):
-            ffn_grad_sum.step()
+        def unit_window(left, right, room=1):
+            ffn_grad_sum.step(room)
             terms = matmul_left_t(after(left, ffn_grad_sum.sent), right).astype(LOW)
             unit_terms.append(unit_parts(terms))
 
@@ -724,36 +752,32 @@
         unit_window(grad_gate_act, group_in)
         unit_window(grad_up_act, group_in)
         unit_sum_tasks = [ticks.add(sum_task(chunk_parts(0), chunk_parts(1)))]
-        unit_window(hidden, group_grad)
+        unit_window(hidden, group_grad, room=2)
         unit_sum_tasks.append(ticks.add(sum_task(chunk_parts(2), chunk_parts(3))))
         grad_ffn = ffn_grad_sum.finish()
 
     gain_two, grad_norm_two = norm_backward(grad_ffn, plain_two, factor_two, ffn_gain)
     grad_residual = grad_output.astype(HIGH) + grad_norm_two
     with jax.named_scope("branch_rows"):
-        branch_blocks = [grad_residual.astype(LOW)]
-        branch_blocks += ticks.tick((branch_blocks[-1], 1))
+        branch_moves = ticks.gather_parts(grad_residual.astype(LOW))
+        sent = next(branch_moves)
         lined = jnp.arange(8, dtype=jnp.int32)
         order = jnp.bitwise_xor(c, lined % 2) * 4 + jnp.mod(z - lined // 2 - 1, 4)
-        late_hidden = after(hidden, ticks.sent).reshape(8, rows_local, -1)
+        late_hidden = after(hidden, sent).reshape(8, rows_local, -1)
         late_hidden = jnp.take(late_hidden, order, axis=0).reshape(8 * rows_local, -1)
-        branch_blocks += ticks.tick((branch_blocks[-1], 1))
-        terms = matmul(after(late_hidden, ticks.sent), weight_down).astype(LOW)
-        branch_blocks += ticks.tick((branch_blocks[-1], 1))
-        branch_both = both_cores(branch_blocks)
+        terms = matmul(after(late_hidden, next(branch_moves)), weight_down).astype(LOW)
+        next(branch_moves)
+        branch_both = next(branch_moves)
     with jax.named_scope("ffn_sum"):
         branch = lax.psum_scatter(
-            after(terms, branch_blocks[-1]), ("z", "c"), scatter_dimension=0, tiled=True
+            after(terms, ticks.over_z), ("z", "c"), scatter_dimension=0, tiled=True
         )
         output = (residual + branch.astype(HIGH)).astype(LOW)
     with jax.named_scope("unit_weight_sums"):
-        ticks.tick(room=2, lock=False, hold=True)
+        ticks.tick(room=2, lock=False)
     grad_queries, key_terms, value_terms = attention_backward(
         scalars, queries, mixed, lse, keys_all, values_all, weight_out, branch_both
     )
-
-    with jax.named_scope("unit_weight_sums"):
-        ticks.release(grad_queries)
 
     def side_parts(values, k):
         count = values.shape[0] // (2 * sides)
@@ -813,26 +837,32 @@
     with jax.named_scope("normed_sum"):
         grad_normed = normed_sum.finish()
     with jax.named_scope("grad_keys_values"):
-        grad_kv = jnp.concatenate(ticks.finish(keys_task)[0], axis=1)
+        grad_keys, grad_values = ticks.finish(keys_task)[0]
     with jax.named_scope("query_out_weight_sum"):
         query_out_task = ticks.add(
             chunk_sums(jnp.concatenate([query_terms, out_terms], axis=1))
         )
     with jax.named_scope("shared_sum"):
+        weight_key, weight_value = weight_kv[:, :own_width], weight_kv[:, own_width:]
         shared_sum = RowSum(
-            ticks, lambda v: matmul_right_t(v, weight_kv), [grad_kv], rows_local
+            ticks,
+            lambda k, v: matmul_right_t(k, weight_key) + matmul_right_t(v, weight_value),
+            [grad_keys, grad_values],
+            rows_local,
         )
         shared_sum.total = after(shared_sum.total, branch)
         shared_sum.step()
         sent = shared_sum.sent
     with jax.named_scope("key_value_weight_sum"):
-        kv_terms = matmul_left_t(after(group_shared, sent), grad_kv).astype(LOW)
+        grad_kv = jnp.concatenate(after((grad_keys, grad_values), sent), axis=1)
+        kv_terms = matmul_left_t(group_shared, grad_kv).astype(LOW)
         kv_task = ticks.add(chunk_sums(kv_terms))
     with jax.named_scope("shared_sum"):
         grad_shared_normed = shared_sum.finish()
     with jax.named_scope("weight_layout"):
-        query_out_sum, kv_sum = ticks.finish(query_out_task, kv_task)
-        grad_query, grad_out = layout(query_out_sum)
+        (query_out_sum,) = ticks.finish(query_out_task)
+        grad_query, grad_out = layout(after(query_out_sum, grad_shared_normed))
+        (kv_sum,) = ticks.finish(kv_task)
         grad_key, grad_value = layout(kv_sum)
         grad_out = jnp.transpose(grad_out)
     with jax.named_scope("unit_weight_sums"):
@@ -843,6 +873,7 @@
         )
         grad_gate, grad_up = jnp.transpose(grad_gate), jnp.transpose(grad_up)
 
+    grad_normed = after(grad_normed, sent)
     gain_one, grad_in_one = norm_backward(grad_normed, plain_one, factor_one, norm_gain)
     gain_kv, grad_in_kv = norm_backward(grad_shared_normed, plain_kv, factor_kv, kv_gain)
     grad_states = (grad_residual + grad_in_one).astype(LOW)

time: 634 us -> 611 us (0.964)
  the two profiles are of different devices: /device:TPU:6 before, /device:TPU:0 now
where the time goes in v4:
time: 611 us; the launch traced here: 605 us
  waiting for transfers between devices  259 us (42%)
  starting transfers between devices  113 us (18%)
  matrix products  73 us (12%)
  Pallas kernels  51.6 us (8%)
  local copies, waits for them, and re-layouts  47.6 us (8%)
  other arithmetic  41.6 us (7%)
  between operations  20 us (3%)
    ppermute x131, waiting for transfers between devices, hop(): lax.ppermute(values, axis, [(i, (i + steps) % size) for i in range(size)])  255 us
    ppermute x131, starting transfers between devices, hop(): lax.ppermute(values, axis, [(i, (i + steps) % size) for i in range(size)])  92.5 us
    pallas_call x1, Pallas kernels, attention_backward(): pl.pallas_call(backward_kernel, out_shape=(jax.ShapeDtypeStruct(own_shape...  30.7 us
    dot_general x27, matrix products, matmul_right_t(): lax.dot_general(left_side, right_side, (((1,), (1,)), ((), ())), preferre...  28.4 us
    dot_general x28, matrix products, matmul(): return jnp.dot(left_side, right_side, preferred_element_type=HIGH)  25.6 us
    unnamed x231, local copies, waits for them, and re-layouts  21.9 us
    dot_general x6, matrix products, matmul_left_t(): lax.dot_general(left_side, right_side, (((0,), (0,)), ((), ())), preferre...  19 us
    pallas_call x1, Pallas kernels, attention_forward(): pl.pallas_call(forward_kernel, out_shape=(jax.ShapeDtypeStruct((2, rows /...  18.8 us
  transfers between devices with their start and end apart: 137, of which 61 were waited for; matrix products, arithmetic and copies ran while one was open for 23% of the time, Pallas kernels for 9%

profile of v4, /device:TPU:0, one launch (start us, length us, event | category | flops | bytes accessed | tf_op | source)
XLA Modules:
  0.0 605.4 jit_solution(8296467382953162670)
XLA Ops:
  9.4 5.1 collective-permute-start.2
  23.5 7.7 %collective-permute-done.1 = bf16[64,1536]{1,0:T(8,128)(2,1)S(1)} collective-permute-done((bf16[64,1536]{1,0:T(8,128)(2,1)S(1)}, bf16[64,1536]{1,0:T(8,128)(2,1)S(1)}, u32[]{:S(2)}, u32[]{:S(2)}) %collective-permute-start.1) | collective-permute-done | bytes 196640 | tf_op jit(solution)/shard_map/weight_columns/ppermute | solution.py:29
  38.9 3.2 collective-permute-done.10
  43.2 9.4 %collective-permute-done.7.refs_1_ = bf16[4,64,768]{2,1,0:T(8,128)(2,1)S(1)} collective-permute-done((bf16[4,64,768]{2,1,0:T(8,128)(2,1)S(1)}, bf16[4,64,768]{2,1,0:T(8,128)(2,1)S(1)}, u32[]{:S(2)}, u32[]{:S(2)}) %collective-permute-start.7) | collective-permute-done | bytes 393248 | tf_op jit(solution)/shard_map/shared_rows/ppermute | solution.py:29
  60.4 6.4 %collective-permute-done.19 = bf16[32,2048]{1,0:T(8,128)(2,1)S(1)} collective-permute-done((bf16[32,2048]{1,0:T(8,128)(2,1)S(1)}, bf16[32,2048]{1,0:T(8,128)(2,1)S(1)}, u32[]{:S(2)}, u32[]{:S(2)}) %collective-permute-start.19) | collective-permute-done | bytes 131104 | tf_op jit(solution)/shard_map/shared_rows/ppermute | solution.py:29
  77.4 6.9 %collective-permute-done.22.refs_7_ = bf16[4,64,768]{2,1,0:T(8,128)(2,1)S(1)} collective-permute-done((bf16[4,64,768]{2,1,0:T(8,128)(2,1)S(1)}, bf16[4,64,768]{2,1,0:T(8,128)(2,1)S(1)}, u32[]{:S(2)}, u32[]{:S(2)}) %collective-permute-start.22) | collective-permute-done | bytes 393248 | tf_op jit(solution)/shard_map/shared_rows/ppermute | solution.py:29
  95.6 8.1 %collective-permute-done.20 = bf16[128,2048]{1,0:T(8,128)(2,1)S(1)} collective-permute-done((bf16[128,2048]{1,0:T(8,128)(2,1)S(1)}, bf16[128,2048]{1,0:T(8,128)(2,1)S(1)}, u32[]{:S(2)}, u32[]{:S(2)}) %collective-permute-start.20) | collective-permute-done | bytes 524320 | tf_op jit(solution)/shard_map/normed_rows/ppermute | solution.py:29
  109.6 9.5 %collective-permute-done.23 = bf16[128,2048]{1,0:T(8,128)(2,1)} collective-permute-done((bf16[128,2048]{1,0:T(8,128)(2,1)S(1)}, bf16[128,2048]{1,0:T(8,128)(2,1)}, u32[]{:S(2)}, u32[]{:S(2)}) %collective-permute-start.23) | collective-permute-done | bytes 524320 | tf_op jit(solution)/shard_map/normed_rows/ppermute | solution.py:29
  123.9 10.0 %collective-permute-done.31 = bf16[128,2048]{1,0:T(8,128)(2,1)S(1)} collective-permute-done((bf16[128,2048]{1,0:T(8,128)(2,1)}, bf16[128,2048]{1,0:T(8,128)(2,1)S(1)}, u32[]{:S(2)}, u32[]{:S(2)}) %collective-permute-start.31) | collective-permute-done | bytes 524320 | tf_op jit(solution)/shard_map/normed_rows/ppermute | solution.py:29
  140.5 5.3 collective-permute-done.38
  156.9 18.8 %attention_forward.1 = (bf16[2,512,256]{2,1,0:T(8,128)(2,1)}, f32[2,8,1024]{2,1,0:T(8,128)}) custom-call(s32[16]{0:T(128)} %select_reduce_fusion.place_ref, s32[4]{0:T(128)} %bitcast.223, s32[1]{0:T(128)} %bitcast.1.core_ref, bf16[2,512,256]{2,1,0:T(8,128)(2,1)} %bitcast.221, bf16[4,2,512,256]{3,2,1,0:T(8,128)(2,1)} %bitcast.190, ...), custom_call_target="tpu_custom_call" | custom-call | flops 21474836480 | bytes 4194304 | tf_op jit(solution)/shard_map/attention_forward/pallas_call | solution.py:458
  179.1 6.3 %collective-permute-start.51 = (bf16[128,2048]{1,0:T(8,128)(2,1)S(1)}, bf16[128,2048]{1,0:T(8,128)(2,1)S(1)}, u32[]{:S(2)}, u32[]{:S(2)}) collective-permute-start(bf16[128,2048]{1,0:T(8,128)(2,1)S(1)} %get-tuple-element.198), channel_id=1, source_target_pairs={{0,4},{4,0},{1,5},{5,1},{2,6},{6,2},{3,7},{7,3},{8,12},{12,8},{9,1... | collective-permute-start | bytes 1572872 | tf_op jit(solution)/shard_map/attention_sum/ppermute | solution.py:29
  190.0 2.9 collective-permute-done.50
  192.9 4.2 collective-permute-done.51
  197.2 3.6 collective-permute-done.45
  206.3 14.0 %collective-permute-done.49 = bf16[128,2048]{1,0:T(8,128)(2,1)S(1)} collective-permute-done((bf16[128,2048]{1,0:T(8,128)(2,1)S(1)}, bf16[128,2048]{1,0:T(8,128)(2,1)S(1)}, u32[]{:S(2)}, u32[]{:S(2)}) %collective-permute-start.49) | collective-permute-done | bytes 524320 | tf_op jit(solution)/shard_map/attention_sum/ppermute | solution.py:29
  226.0 9.7 %collective-permute-done.53 = bf16[128,2048]{1,0:T(8,128)(2,1)S(1)} collective-permute-done((bf16[128,2048]{1,0:T(8,128)(2,1)S(1)}, bf16[128,2048]{1,0:T(8,128)(2,1)S(1)}, u32[]{:S(2)}, u32[]{:S(2)}) %collective-permute-start.53) | collective-permute-done | bytes 524320 | tf_op jit(solution)/shard_map/attention_sum/ppermute | solution.py:29
  239.5 13.0 %collective-permute-done.56 = bf16[128,2048]{1,0:T(8,128)(2,1)S(1)} collective-permute-done((bf16[128,2048]{1,0:T(8,128)(2,1)S(1)}, bf16[128,2048]{1,0:T(8,128)(2,1)S(1)}, u32[]{:S(2)}, u32[]{:S(2)}) %collective-permute-start.56) | collective-permute-done | bytes 524320 | tf_op jit(solution)/shard_map/normed_two_rows/ppermute | solution.py:29
  255.6 12.2 %collective-permute-done.59 = bf16[128,2048]{1,0:T(8,128)(2,1)S(1)} collective-permute-done((bf16[128,2048]{1,0:T(8,128)(2,1)S(1)}, bf16[128,2048]{1,0:T(8,128)(2,1)S(1)}, u32[]{:S(2)}, u32[]{:S(2)}) %collective-permute-start.59) | collective-permute-done | bytes 524320 | tf_op jit(solution)/shard_map/normed_two_rows/ppermute | solution.py:29
  268.4 14.1 %collective-permute-done.62 = bf16[128,2048]{1,0:T(8,128)(2,1)S(1)} collective-permute-done((bf16[128,2048]{1,0:T(8,128)(2,1)S(1)}, bf16[128,2048]{1,0:T(8,128)(2,1)S(1)}, u32[]{:S(2)}, u32[]{:S(2)}) %collective-permute-start.62) | collective-permute-done | bytes 524320 | tf_op jit(solution)/shard_map/normed_two_rows/ppermute | solution.py:29
  284.6 3.2 fusion.226
  287.8 3.2 fusion.225
  291.0 4.3 multiply_convert_fusion
  299.4 3.4 convolution_convert_fusion.3
  306.7 8.4 %collective-permute-done.75 = bf16[128,2048]{1,0:T(8,128)(2,1)S(1)} collective-permute-done((bf16[128,2048]{1,0:T(8,128)(2,1)S(1)}, bf16[128,2048]{1,0:T(8,128)(2,1)S(1)}, u32[]{:S(2)}, u32[]{:S(2)}) %collective-permute-start.75) | collective-permute-done | bytes 524320 | tf_op jit(solution)/shard_map/ffn_grad_sum/ppermute | solution.py:29
  315.3 3.4 convolution_convert_fusion.2
  324.6 5.6 collective-permute-done.77
  330.6 3.4 convolution_convert_fusion.1
  346.5 4.4 collective-permute-done.84
  350.9 8.6 %collective-permute-done.83 = bf16[128,2048]{1,0:T(8,128)(2,1)S(1)} collective-permute-done((bf16[128,2048]{1,0:T(8,128)(2,1)S(1)}, bf16[128,2048]{1,0:T(8,128)(2,1)S(1)}, u32[]{:S(2)}, u32[]{:S(2)}) %collective-permute-start.83) | collective-permute-done | bytes 524320 | tf_op jit(solution)/shard_map/ffn_grad_sum/ppermute | solution.py:29
  359.5 5.2 collective-permute-done.81
  374.0 4.1 collective-permute-done.87
  382.5 6.8 %convolution_convert_fusion = bf16[1024,2048]{1,0:T(8,128)(2,1)} fusion(bf16[1024,704]{0,1:T(8,128)(2,1)S(1)} %bitcast_select_fusion, bf16[704,2048]{1,0:T(8,128)(2,1)} %copy-done.67), kind=kOutput, calls=%fused_computation.19 | convolution fusion | flops 2954887168 | bytes 8519680 | tf_op jit(solution)/shard_map/branch_rows/dot_general | solution.py:248
  389.7 3.0 collective-permute-done.95
  400.4 3.0 collective-permute-done.88.refs_2_
  413.0 30.7 %attention_backward.1 = (bf16[2,512,256]{2,1,0:T(8,128)(2,1)}, bf16[4,2,512,256]{3,2,1,0:T(8,128)(2,1)}, bf16[4,2,512,256]{3,2,1,0:T(8,128)(2,1)}) custom-call(s32[16]{0:T(128)} %select_reduce_fusion.place_ref, s32[4]{0:T(128)} %bitcast.224, s32[1]{0:T(128)} %bitcast.1.core_ref, bf16[2,512,256]{2,1,0:T(8,128)(2,1)} %bitcast.222, ...), custom_call_target="tpu_custom_call" | custom-call | flops 128849018880 | bytes 8388608 | tf_op jit(solution)/shard_map/attention_backward/pallas_call | solution.py:502
  447.9 5.7 collective-permute-start.104
  466.8 3.4 collective-permute-done.99
  472.7 11.0 %collective-permute-done.108 = bf16[1024,256]{1,0:T(8,128)(2,1)S(1)} collective-permute-done((bf16[1024,256]{1,0:T(8,128)(2,1)S(1)}, bf16[1024,256]{1,0:T(8,128)(2,1)S(1)}, u32[]{:S(2)}, u32[]{:S(2)}) %collective-permute-start.108) | collective-permute-done | bytes 524320 | tf_op jit(solution)/shard_map/normed_sum/ppermute | solution.py:29
  491.8 5.9 collective-permute-done.110
  498.4 3.8 collective-permute-done.107
  510.9 6.2 %convolution_convert_fusion.4 = bf16[2048,512]{0,1:T(8,128)(2,1)} fusion(bf16[1024,2048]{1,0:T(8,128)(2,1)} %copy-done.75, bf16[1024,256]{1,0:T(8,128)(2,1)} %copy-done.26, bf16[1024,256]{1,0:T(8,128)(2,1)} %copy-done.28), kind=kOutput, calls=%fused_computation.23 | convolution fusion | flops 2150629376 | bytes 7340032 | tf_op jit(solution)/shard_map/key_value_weight_sum/dot_general | solution.py:258
  528.4 5.2 collective-permute-done.117
  541.1 3.3 collective-permute-done.116
  554.4 8.2 %collective-permute-done.132 = bf16[256,512]{0,1:T(8,128)(2,1)S(1)} collective-permute-done((bf16[256,512]{0,1:T(8,128)(2,1)S(1)}, bf16[256,512]{0,1:T(8,128)(2,1)S(1)}, u32[]{:S(2)}, u32[]{:S(2)}) %collective-permute-start.132) | collective-permute-done | bytes 262176 | tf_op jit(solution)/shard_map/shared_sum/ppermute | solution.py:29
  570.9 12.5 %collective-permute-start.130 = (bf16[256,512]{0,1:T(8,128)(2,1)}, bf16[256,512]{0,1:T(8,128)(2,1)}, u32[]{:S(2)}, u32[]{:S(2)}) collective-permute-start(bf16[256,512]{0,1:T(8,128)(2,1)} %get-tuple-element.471), channel_id=1, source_target_pairs={{0,20},{1,0},{2,28},{3,8},{4,4},{5,16},{6,12},{7,24},{8,29},{9,9},... | collective-permute-start | bytes 786440 | tf_op jit(solution)/shard_map/weight_layout/ppermute | solution.py:813
  584.4 2.9 all-to-all-start
  590.6 4.0 all-to-all-done
  (673 shorter events, 242.1 us)
Async XLA Ops:
  7.2 502.3 %reduce-scatter.2.cloned.1.call-start = ((), (), s32[]{:S(2)}) async-start(), calls=%async_computation.2 | async-start | bytes 4718592 | tf_op jit(solution)/shard_map/ffn_sum/reduce_scatter | solution.py:772
  14.6 16.7 %collective-permute-start.1 = (bf16[64,1536]{1,0:T(8,128)(2,1)S(1)}, bf16[64,1536]{1,0:T(8,128)(2,1)S(1)}, u32[]{:S(2)}, u32[]{:S(2)}) collective-permute-start(bf16[64,1536]{1,0:T(8,128)(2,1)S(1)} %pad_maximum_fusion.14), channel_id=1, source_target_pairs={{0,16},{8,24},{16,0},{24,8},{1,17},{9,25},{17,1},{25,9},{2,18},{10... | collective-permute-start | bytes 589832 | tf_op jit(solution)/shard_map/weight_columns/ppermute | solution.py:29
  14.7 16.6 %collective-permute-start = (bf16[64,1536]{1,0:T(8,128)(2,1)S(1)}, bf16[64,1536]{1,0:T(8,128)(2,1)S(1)}, u32[]{:S(2)}, u32[]{:S(2)}) collective-permute-start(bf16[64,1536]{1,0:T(8,128)(2,1)S(1)} %pad_maximum_fusion.13), channel_id=1, source_target_pairs={{0,8},{8,16},{16,24},{24,0},{1,9},{9,17},{17,25},{25,1},{2,10},{10... | collective-permute-start | bytes 589832 | tf_op jit(solution)/shard_map/weight_columns/ppermute | solution.py:29
  17.7 17.1 %collective-permute-start.5 = (bf16[64,768]{1,0:T(8,128)(2,1)S(1)}, bf16[64,768]{1,0:T(8,128)(2,1)S(1)}, u32[]{:S(2)}, u32[]{:S(2)}) collective-permute-start(bf16[64,768]{1,0:T(8,128)(2,1)S(1)} %pad_maximum_fusion.16), channel_id=1, source_target_pairs={{0,1},{1,0},{2,3},{3,2},{4,5},{5,4},{6,7},{7,6},{8,9},{9,8},{10,11... | collective-permute-start | bytes 294920 | tf_op jit(solution)/shard_map/weight_columns/ppermute | solution.py:29
  19.0 71.2 %collective-permute-start.27 = (bf16[128,2048]{1,0:T(8,128)(2,1)}, bf16[128,2048]{1,0:T(8,128)(2,1)}, u32[]{:S(2)}, u32[]{:S(2)}) collective-permute-start(bf16[128,2048]{1,0:T(8,128)(2,1)} %fusion.23), channel_id=1, source_target_pairs={{0,1},{1,0},{2,3},{3,2},{4,5},{5,4},{6,7},{7,6},{8,9},{9,8},{10,11... | collective-permute-start | bytes 1572872 | tf_op jit(solution)/shard_map/shared_rows/ppermute | solution.py:29
  37.9 17.7 %collective-permute-start.3 = (bf16[128,2048]{1,0:T(8,128)(2,1)}, bf16[128,2048]{1,0:T(8,128)(2,1)}, u32[]{:S(2)}, u32[]{:S(2)}) collective-permute-start(bf16[128,2048]{1,0:T(8,128)(2,1)} %fusion.23), channel_id=1, source_target_pairs={{0,8},{8,16},{16,24},{24,0},{1,9},{9,17},{17,25},{25,1},{2,10},{10... | collective-permute-start | bytes 1572872 | tf_op jit(solution)/shard_map/shared_rows/ppermute | solution.py:29
  54.5 18.4 %collective-permute-start.16 = (bf16[4,64,768]{2,1,0:T(8,128)(2,1)S(1)}, bf16[4,64,768]{2,1,0:T(8,128)(2,1)S(1)}, u32[]{:S(2)}, u32[]{:S(2)}) collective-permute-start(bf16[4,64,768]{2,1,0:T(8,128)(2,1)S(1)} %pad_maximum_fusion.12.refs_4_), channel_id=1, source_target_pairs={{0,2},{2,0},{1,3},{3,1},{4,6},{6,4},{5,7},{7,5},{8,10},{10,8},{9,1... | collective-permute-start | bytes 1179656 | tf_op jit(solution)/shard_map/shared_rows/ppermute | solution.py:29
  55.1 17.9 %collective-permute-start.17 = (bf16[4,64,768]{2,1,0:T(8,128)(2,1)S(1)}, bf16[4,64,768]{2,1,0:T(8,128)(2,1)S(1)}, u32[]{:S(2)}, u32[]{:S(2)}) collective-permute-start(bf16[4,64,768]{2,1,0:T(8,128)(2,1)S(1)} %pad_maximum_fusion.12.refs_4_), channel_id=1, source_target_pairs={{0,4},{4,0},{1,5},{5,1},{2,6},{6,2},{3,7},{7,3},{8,12},{12,8},{9,1... | collective-permute-start | bytes 1179656 | tf_op jit(solution)/shard_map/shared_rows/ppermute | solution.py:29
  71.2 16.1 %collective-permute-start.13 = (bf16[128,2048]{1,0:T(8,128)(2,1)}, bf16[128,2048]{1,0:T(8,128)(2,1)S(1)}, u32[]{:S(2)}, u32[]{:S(2)}) collective-permute-start(bf16[128,2048]{1,0:T(8,128)(2,1)} %collective-permute-done.4), channel_id=1, source_target_pairs={{0,8},{8,16},{16,24},{24,0},{1,9},{9,17},{17,25},{25,1},{2,10},{10... | collective-permute-start | bytes 1572872 | tf_op jit(solution)/shard_map/shared_rows/ppermute | solution.py:29
  76.2 77.5 %collective-permute-start.35 = (bf16[128,2048]{1,0:T(8,128)(2,1)}, bf16[128,2048]{1,0:T(8,128)(2,1)}, u32[]{:S(2)}, u32[]{:S(2)}) collective-permute-start(bf16[128,2048]{1,0:T(8,128)(2,1)} %fusion.30), channel_id=1, source_target_pairs={{0,1},{1,0},{2,3},{3,2},{4,5},{5,4},{6,7},{7,6},{8,9},{9,8},{10,11... | collective-permute-start | bytes 1572872 | tf_op jit(solution)/shard_map/normed_rows/ppermute | solution.py:29
  87.5 16.2 %collective-permute-start.20 = (bf16[128,2048]{1,0:T(8,128)(2,1)S(1)}, bf16[128,2048]{1,0:T(8,128)(2,1)S(1)}, u32[]{:S(2)}, u32[]{:S(2)}) collective-permute-start(bf16[128,2048]{1,0:T(8,128)(2,1)S(1)} %copy-done.50), channel_id=1, source_target_pairs={{0,8},{8,16},{16,24},{24,0},{1,9},{9,17},{17,25},{25,1},{2,10},{10... | collective-permute-start | bytes 1572872 | tf_op jit(solution)/shard_map/normed_rows/ppermute | solution.py:29
  149.8 28.6 %collective-permute-start.46 = (bf16[128,2048]{1,0:T(8,128)(2,1)}, bf16[128,2048]{1,0:T(8,128)(2,1)}, u32[]{:S(2)}, u32[]{:S(2)}) collective-permute-start(bf16[128,2048]{1,0:T(8,128)(2,1)} %get-tuple-element.194), channel_id=1, source_target_pairs={{0,2},{2,0},{1,3},{3,1},{4,6},{6,4},{5,7},{7,5},{8,10},{10,8},{9,1... | collective-permute-start | bytes 1572872 | tf_op jit(solution)/shard_map/grad_output_rows/ppermute | solution.py:29
  150.3 28.7 %collective-permute-start.47 = (bf16[128,2048]{1,0:T(8,128)(2,1)}, bf16[128,2048]{1,0:T(8,128)(2,1)}, u32[]{:S(2)}, u32[]{:S(2)}) collective-permute-start(bf16[128,2048]{1,0:T(8,128)(2,1)} %get-tuple-element.194), channel_id=1, source_target_pairs={{0,4},{4,0},{1,5},{5,1},{2,6},{6,2},{3,7},{7,3},{8,12},{12,8},{9,1... | collective-permute-start | bytes 1572872 | tf_op jit(solution)/shard_map/grad_output_rows/ppermute | solution.py:29
  150.3 28.7 %collective-permute-start.43 = (bf16[128,2048]{1,0:T(8,128)(2,1)S(1)}, bf16[128,2048]{1,0:T(8,128)(2,1)}, u32[]{:S(2)}, u32[]{:S(2)}) collective-permute-start(bf16[128,2048]{1,0:T(8,128)(2,1)S(1)} %copy-done.30), channel_id=1, source_target_pairs={{0,24},{8,0},{16,8},{24,16},{1,25},{9,1},{17,9},{25,17},{2,26},{10... | collective-permute-start | bytes 1572872 | tf_op jit(solution)/shard_map/grad_output_rows/ppermute | solution.py:29
  150.3 28.7 %collective-permute-start.42 = (bf16[128,2048]{1,0:T(8,128)(2,1)}, bf16[128,2048]{1,0:T(8,128)(2,1)}, u32[]{:S(2)}, u32[]{:S(2)}) collective-permute-start(bf16[128,2048]{1,0:T(8,128)(2,1)} %collective-permute-done.41), channel_id=1, source_target_pairs={{0,8},{8,16},{16,24},{24,0},{1,9},{9,17},{17,25},{25,1},{2,10},{10... | collective-permute-start | bytes 1572872 | tf_op jit(solution)/shard_map/grad_output_rows/ppermute | solution.py:29
  179.1 18.1 %collective-permute-start.51 = (bf16[128,2048]{1,0:T(8,128)(2,1)S(1)}, bf16[128,2048]{1,0:T(8,128)(2,1)S(1)}, u32[]{:S(2)}, u32[]{:S(2)}) collective-permute-start(bf16[128,2048]{1,0:T(8,128)(2,1)S(1)} %get-tuple-element.198), channel_id=1, source_target_pairs={{0,4},{4,0},{1,5},{5,1},{2,6},{6,2},{3,7},{7,3},{8,12},{12,8},{9,1... | collective-permute-start | bytes 1572872 | tf_op jit(solution)/shard_map/attention_sum/ppermute | solution.py:29
  200.8 19.6 %collective-permute-start.54 = (bf16[128,2048]{1,0:T(8,128)(2,1)S(1)}, bf16[128,2048]{1,0:T(8,128)(2,1)S(1)}, u32[]{:S(2)}, u32[]{:S(2)}) collective-permute-start(bf16[128,2048]{1,0:T(8,128)(2,1)S(1)} %get-tuple-element.202), channel_id=1, source_target_pairs={{0,2},{2,0},{1,3},{3,1},{4,6},{6,4},{5,7},{7,5},{8,10},{10,8},{9,1... | collective-permute-start | bytes 1572872 | tf_op jit(solution)/shard_map/attention_sum/ppermute | solution.py:29
  201.2 19.3 %collective-permute-start.55 = (bf16[128,2048]{1,0:T(8,128)(2,1)S(1)}, bf16[128,2048]{1,0:T(8,128)(2,1)S(1)}, u32[]{:S(2)}, u32[]{:S(2)}) collective-permute-start(bf16[128,2048]{1,0:T(8,128)(2,1)S(1)} %get-tuple-element.202), channel_id=1, source_target_pairs={{0,4},{4,0},{1,5},{5,1},{2,6},{6,2},{3,7},{7,3},{8,12},{12,8},{9,1... | collective-permute-start | bytes 1572872 | tf_op jit(solution)/shard_map/attention_sum/ppermute | solution.py:29
  204.1 16.2 %collective-permute-start.49 = (bf16[128,2048]{1,0:T(8,128)(2,1)S(1)}, bf16[128,2048]{1,0:T(8,128)(2,1)S(1)}, u32[]{:S(2)}, u32[]{:S(2)}) collective-permute-start(bf16[128,2048]{1,0:T(8,128)(2,1)S(1)} %add_convert_fusion.23), channel_id=1, source_target_pairs={{0,8},{8,16},{16,24},{24,0},{1,9},{9,17},{17,25},{25,1},{2,10},{10... | collective-permute-start | bytes 1572872 | tf_op jit(solution)/shard_map/attention_sum/ppermute | solution.py:29
  220.5 16.0 %collective-permute-start.57 = (bf16[144,2048]{1,0:T(8,128)(2,1)S(1)}, bf16[144,2048]{1,0:T(8,128)(2,1)S(1)}, u32[]{:S(2)}, u32[]{:S(2)}) collective-permute-start(bf16[144,2048]{1,0:T(8,128)(2,1)S(1)} %pad_slice_fusion), channel_id=1, source_target_pairs={{0,2},{2,0},{1,3},{3,1},{4,6},{6,4},{5,7},{7,5},{8,10},{10,8},{9,1... | collective-permute-start | bytes 1769480 | tf_op jit(solution)/shard_map/attention_sum/ppermute | solution.py:29
  236.3 48.2 %collective-permute-start.66 = (bf16[128,2048]{1,0:T(8,128)(2,1)S(1)}, bf16[128,2048]{1,0:T(8,128)(2,1)S(1)}, u32[]{:S(2)}, u32[]{:S(2)}) collective-permute-start(bf16[128,2048]{1,0:T(8,128)(2,1)S(1)} %multiply_convert_fusion.3), channel_id=1, source_target_pairs={{0,1},{1,0},{2,3},{3,2},{4,5},{5,4},{6,7},{7,6},{8,9},{9,8},{10,11... | collective-permute-start | bytes 1572872 | tf_op jit(solution)/shard_map/normed_two_rows/ppermute | solution.py:29
  236.4 16.1 %collective-permute-start.56 = (bf16[128,2048]{1,0:T(8,128)(2,1)S(1)}, bf16[128,2048]{1,0:T(8,128)(2,1)S(1)}, u32[]{:S(2)}, u32[]{:S(2)}) collective-permute-start(bf16[128,2048]{1,0:T(8,128)(2,1)S(1)} %multiply_convert_fusion.3), channel_id=1, source_target_pairs={{0,8},{8,16},{16,24},{24,0},{1,9},{9,17},{17,25},{25,1},{2,10},{10... | collective-permute-start | bytes 1572872 | tf_op jit(solution)/shard_map/normed_two_rows/ppermute | solution.py:29
  236.5 16.1 %collective-permute-start.61 = (bf16[128,2048]{1,0:T(8,128)(2,1)S(1)}, bf16[128,2048]{1,0:T(8,128)(2,1)S(1)}, u32[]{:S(2)}, u32[]{:S(2)}) collective-permute-start(bf16[128,2048]{1,0:T(8,128)(2,1)S(1)} %collective-permute-done.50), channel_id=1, source_target_pairs={{0,4},{4,0},{1,5},{5,1},{2,6},{6,2},{3,7},{7,3},{8,12},{12,8},{9,1... | collective-permute-start | bytes 1572872 | tf_op jit(solution)/shard_map/normed_two_rows/ppermute | solution.py:29
  252.5 30.3 %collective-permute-start.63 = (bf16[128,2048]{1,0:T(8,128)(2,1)S(1)}, bf16[128,2048]{1,0:T(8,128)(2,1)S(1)}, u32[]{:S(2)}, u32[]{:S(2)}) collective-permute-start(bf16[128,2048]{1,0:T(8,128)(2,1)S(1)} %collective-permute-done.56), channel_id=1, source_target_pairs={{0,1},{1,0},{2,3},{3,2},{4,5},{5,4},{6,7},{7,6},{8,9},{9,8},{10,11... | collective-permute-start | bytes 1572872 | tf_op jit(solution)/shard_map/normed_two_rows/ppermute | solution.py:29
  252.6 15.8 %collective-permute-start.72 = (bf16[144,2048]{1,0:T(8,128)(2,1)S(1)}, bf16[144,2048]{1,0:T(8,128)(2,1)S(1)}, u32[]{:S(2)}, u32[]{:S(2)}) collective-permute-start(bf16[144,2048]{1,0:T(8,128)(2,1)S(1)} %collective-permute-done.57), channel_id=1, source_target_pairs={{0,4},{4,0},{1,5},{5,1},{2,6},{6,2},{3,7},{7,3},{8,12},{12,8},{9,1... | collective-permute-start | bytes 1769480 | tf_op jit(solution)/shard_map/normed_two_rows/ppermute | solution.py:29
  299.1 16.0 %collective-permute-start.75 = (bf16[128,2048]{1,0:T(8,128)(2,1)S(1)}, bf16[128,2048]{1,0:T(8,128)(2,1)S(1)}, u32[]{:S(2)}, u32[]{:S(2)}) collective-permute-start(bf16[128,2048]{1,0:T(8,128)(2,1)S(1)} %add_convert_fusion.21), channel_id=1, source_target_pairs={{0,8},{8,16},{16,24},{24,0},{1,9},{9,17},{17,25},{25,1},{2,10},{10... | collective-permute-start | bytes 1572872 | tf_op jit(solution)/shard_map/ffn_grad_sum/ppermute | solution.py:29
  338.4 21.0 %collective-permute-start.83 = (bf16[128,2048]{1,0:T(8,128)(2,1)S(1)}, bf16[128,2048]{1,0:T(8,128)(2,1)S(1)}, u32[]{:S(2)}, u32[]{:S(2)}) collective-permute-start(bf16[128,2048]{1,0:T(8,128)(2,1)S(1)} %get-tuple-element.238), channel_id=1, source_target_pairs={{0,2},{2,0},{1,3},{3,1},{4,6},{6,4},{5,7},{7,5},{8,10},{10,8},{9,1... | collective-permute-start | bytes 1572872 | tf_op jit(solution)/shard_map/ffn_grad_sum/ppermute | solution.py:29
  339.4 20.0 %collective-permute-start.82 = (bf16[128,2048]{1,0:T(8,128)(2,1)S(1)}, bf16[128,2048]{1,0:T(8,128)(2,1)S(1)}, u32[]{:S(2)}, u32[]{:S(2)}) collective-permute-start(bf16[128,2048]{1,0:T(8,128)(2,1)S(1)} %pad_maximum_fusion.5), channel_id=1, source_target_pairs={{0,4},{4,0},{1,5},{5,1},{2,6},{6,2},{3,7},{7,3},{8,12},{12,8},{9,1... | collective-permute-start | bytes 1572872 | tf_op jit(solution)/shard_map/ffn_grad_sum/ppermute | solution.py:29
  342.9 21.7 %collective-permute-start.81 = (bf16[128,2048]{1,0:T(8,128)(2,1)S(1)}, bf16[128,2048]{1,0:T(8,128)(2,1)S(1)}, u32[]{:S(2)}, u32[]{:S(2)}) collective-permute-start(bf16[128,2048]{1,0:T(8,128)(2,1)S(1)} %pad_maximum_fusion.4), channel_id=1, source_target_pairs={{0,4},{4,0},{1,5},{5,1},{2,6},{6,2},{3,7},{7,3},{8,12},{12,8},{9,1... | collective-permute-start | bytes 1572872 | tf_op jit(solution)/shard_map/ffn_grad_sum/ppermute | solution.py:29
  346.5 27.6 %collective-permute-start.80 = (bf16[128,2048]{1,0:T(8,128)(2,1)S(1)}, bf16[128,2048]{1,0:T(8,128)(2,1)}, u32[]{:S(2)}, u32[]{:S(2)}) collective-permute-start(bf16[128,2048]{1,0:T(8,128)(2,1)S(1)} %get-tuple-element.285.refs_3_), channel_id=1, source_target_pairs={{0,8},{8,16},{16,24},{24,0},{1,9},{9,17},{17,25},{25,1},{2,10},{10... | collective-permute-start | bytes 1572872 | tf_op jit(solution)/shard_map/branch_rows/ppermute | solution.py:29
  350.9 59.9 %collective-permute-start.92 = (bf16[128,2048]{1,0:T(8,128)(2,1)S(1)}, bf16[128,2048]{1,0:T(8,128)(2,1)}, u32[]{:S(2)}, u32[]{:S(2)}) collective-permute-start(bf16[128,2048]{1,0:T(8,128)(2,1)S(1)} %get-tuple-element.285.refs_3_), channel_id=1, source_target_pairs={{0,1},{1,0},{2,3},{3,2},{4,5},{5,4},{6,7},{7,6},{8,9},{9,8},{10,11... | collective-permute-start | bytes 1572872 | tf_op jit(solution)/shard_map/branch_rows/ppermute | solution.py:29
  406.7 40.4 %collective-permute-start.100 = (bf16[128,2048]{1,0:T(8,128)(2,1)S(1)}, bf16[128,2048]{1,0:T(8,128)(2,1)S(1)}, u32[]{:S(2)}, u32[]{:S(2)}) collective-permute-start(bf16[128,2048]{1,0:T(8,128)(2,1)S(1)} %add_convert_fusion.14), channel_id=1, source_target_pairs={{0,4},{4,0},{1,5},{5,1},{2,6},{6,2},{3,7},{7,3},{8,12},{12,8},{9,1... | collective-permute-start | bytes 1572872 | tf_op jit(solution)/shard_map/unit_weight_sums/ppermute | solution.py:29
  410.8 36.4 %collective-permute-start.101 = (bf16[144,2048]{1,0:T(8,128)(2,1)S(1)}, bf16[144,2048]{1,0:T(8,128)(2,1)S(1)}, u32[]{:S(2)}, u32[]{:S(2)}) collective-permute-start(bf16[144,2048]{1,0:T(8,128)(2,1)S(1)} %add_convert_fusion.2), channel_id=1, source_target_pairs={{0,2},{2,0},{1,3},{3,1},{4,6},{6,4},{5,7},{7,5},{8,10},{10,8},{9,1... | collective-permute-start | bytes 1769480 | tf_op jit(solution)/shard_map/unit_weight_sums/ppermute | solution.py:29
  447.2 23.2 %collective-permute-start.105 = (bf16[1024,256]{1,0:T(8,128)(2,1)S(1)}, bf16[1024,256]{1,0:T(8,128)(2,1)S(1)}, u32[]{:S(2)}, u32[]{:S(2)}) collective-permute-start(bf16[1024,256]{1,0:T(8,128)(2,1)S(1)} %bitcast.197), channel_id=1, source_target_pairs={{0,2},{2,0},{1,3},{3,1},{4,6},{6,4},{5,7},{7,5},{8,10},{10,8},{9,1... | collective-permute-start | bytes 1572872 | tf_op jit(solution)/shard_map/normed_sum/ppermute | solution.py:29
  447.9 22.5 %collective-permute-start.104 = (bf16[1024,256]{1,0:T(8,128)(2,1)S(1)}, bf16[1024,256]{1,0:T(8,128)(2,1)S(1)}, u32[]{:S(2)}, u32[]{:S(2)}) collective-permute-start(bf16[1024,256]{1,0:T(8,128)(2,1)S(1)} %bitcast.198), channel_id=1, source_target_pairs={{0,4},{4,0},{1,5},{5,1},{2,6},{6,2},{3,7},{7,3},{8,12},{12,8},{9,1... | collective-permute-start | bytes 1572872 | tf_op jit(solution)/shard_map/normed_sum/ppermute | solution.py:29
  454.2 16.0 %collective-permute-start.99 = (bf16[128,2048]{1,0:T(8,128)(2,1)S(1)}, bf16[128,2048]{1,0:T(8,128)(2,1)S(1)}, u32[]{:S(2)}, u32[]{:S(2)}) collective-permute-start(bf16[128,2048]{1,0:T(8,128)(2,1)S(1)} %fusion.9), channel_id=1, source_target_pairs={{0,8},{8,16},{16,24},{24,0},{1,9},{9,17},{17,25},{25,1},{2,10},{10... | collective-permute-start | bytes 1572872 | tf_op jit(solution)/shard_map/normed_sum/ppermute | solution.py:29
  502.2 26.1 %collective-permute-start.120 = (bf16[256,512]{0,1:T(8,128)(2,1)}, bf16[256,512]{0,1:T(8,128)(2,1)}, u32[]{:S(2)}, u32[]{:S(2)}) collective-permute-start(bf16[256,512]{0,1:T(8,128)(2,1)} %get-tuple-element.293), channel_id=1, source_target_pairs={{0,2},{2,0},{1,3},{3,1},{4,6},{6,4},{5,7},{7,5},{8,10},{10,8},{9,1... | collective-permute-start | bytes 786440 | tf_op jit(solution)/shard_map/shared_sum/ppermute | solution.py:29
  504.4 24.0 %collective-permute-start.119 = (bf16[256,512]{0,1:T(8,128)(2,1)}, bf16[256,512]{0,1:T(8,128)(2,1)S(1)}, u32[]{:S(2)}, u32[]{:S(2)}) collective-permute-start(bf16[256,512]{0,1:T(8,128)(2,1)} %get-tuple-element.292), channel_id=1, source_target_pairs={{0,2},{2,0},{1,3},{3,1},{4,6},{6,4},{5,7},{7,5},{8,10},{10,8},{9,1... | collective-permute-start | bytes 786440 | tf_op jit(solution)/shard_map/shared_sum/ppermute | solution.py:29
  505.9 22.5 %collective-permute-start.118 = (bf16[256,512]{0,1:T(8,128)(2,1)}, bf16[256,512]{0,1:T(8,128)(2,1)}, u32[]{:S(2)}, u32[]{:S(2)}) collective-permute-start(bf16[256,512]{0,1:T(8,128)(2,1)} %get-tuple-element.291), channel_id=1, source_target_pairs={{0,4},{4,0},{1,5},{5,1},{2,6},{6,2},{3,7},{7,3},{8,12},{12,8},{9,1... | collective-permute-start | bytes 786440 | tf_op jit(solution)/shard_map/shared_sum/ppermute | solution.py:29
  509.6 17.5 %collective-permute-start.114 = (bf16[128,2048]{1,0:T(8,128)(2,1)}, bf16[128,2048]{1,0:T(8,128)(2,1)}, u32[]{:S(2)}, u32[]{:S(2)}) collective-permute-start(bf16[128,2048]{1,0:T(8,128)(2,1)} %fusion.10), channel_id=1, source_target_pairs={{0,8},{8,16},{16,24},{24,0},{1,9},{9,17},{17,25},{25,1},{2,10},{10... | collective-permute-start | bytes 1572872 | tf_op jit(solution)/shard_map/shared_sum/ppermute | solution.py:29
  528.3 16.2 %collective-permute-start.116 = (bf16[128,2048]{1,0:T(8,128)(2,1)S(1)}, bf16[128,2048]{1,0:T(8,128)(2,1)S(1)}, u32[]{:S(2)}, u32[]{:S(2)}) collective-permute-start(bf16[128,2048]{1,0:T(8,128)(2,1)S(1)} %add_convert_fusion.10), channel_id=1, source_target_pairs={{0,8},{8,16},{16,24},{24,0},{1,9},{9,17},{17,25},{25,1},{2,10},{10... | collective-permute-start | bytes 1572872 | tf_op jit(solution)/shard_map/shared_sum/ppermute | solution.py:29
  544.5 23.4 %collective-permute-start.122 = (bf16[128,2048]{1,0:T(8,128)(2,1)S(1)}, bf16[128,2048]{1,0:T(8,128)(2,1)S(1)}, u32[]{:S(2)}, u32[]{:S(2)}) collective-permute-start(bf16[128,2048]{1,0:T(8,128)(2,1)S(1)} %add_convert_fusion.9), channel_id=1, source_target_pairs={{0,8},{8,16},{16,24},{24,0},{1,9},{9,17},{17,25},{25,1},{2,10},{10... | collective-permute-start | bytes 1572872 | tf_op jit(solution)/shard_map/shared_sum/ppermute | solution.py:29
  548.6 16.7 %collective-permute-start.127 = (bf16[256,512]{0,1:T(8,128)(2,1)S(1)}, bf16[256,512]{0,1:T(8,128)(2,1)S(1)}, u32[]{:S(2)}, u32[]{:S(2)}) collective-permute-start(bf16[256,512]{0,1:T(8,128)(2,1)S(1)} %get-tuple-element.303), channel_id=1, source_target_pairs={{0,4},{4,0},{1,5},{5,1},{2,6},{6,2},{3,7},{7,3},{8,12},{12,8},{9,1... | collective-permute-start | bytes 786440 | tf_op jit(solution)/shard_map/shared_sum/ppermute | solution.py:29
  549.3 16.8 %collective-permute-start.128 = (bf16[256,512]{0,1:T(8,128)(2,1)S(1)}, bf16[256,512]{0,1:T(8,128)(2,1)S(1)}, u32[]{:S(2)}, u32[]{:S(2)}) collective-permute-start(bf16[256,512]{0,1:T(8,128)(2,1)S(1)} %get-tuple-element.306), channel_id=1, source_target_pairs={{0,2},{2,0},{1,3},{3,1},{4,6},{6,4},{5,7},{7,5},{8,10},{10,8},{9,1... | collective-permute-start | bytes 786440 | tf_op jit(solution)/shard_map/shared_sum/ppermute | solution.py:29
  562.9 20.5 %collective-permute-start.134 = (bf16[256,512]{0,1:T(8,128)(2,1)S(1)}, bf16[256,512]{0,1:T(8,128)(2,1)S(1)}, u32[]{:S(2)}, u32[]{:S(2)}) collective-permute-start(bf16[256,512]{0,1:T(8,128)(2,1)S(1)} %broadcast_select_fusion.1), channel_id=1, source_target_pairs={{0,20},{1,0},{2,28},{3,8},{4,4},{5,16},{6,12},{7,24},{8,29},{9,9},... | collective-permute-start | bytes 786440 | tf_op jit(solution)/shard_map/weight_layout/ppermute | solution.py:813
  565.3 18.0 %collective-permute-start.133 = (bf16[256,512]{0,1:T(8,128)(2,1)S(1)}, bf16[256,512]{0,1:T(8,128)(2,1)S(1)}, u32[]{:S(2)}, u32[]{:S(2)}) collective-permute-start(bf16[256,512]{0,1:T(8,128)(2,1)S(1)} %get-tuple-element.392), channel_id=1, source_target_pairs={{0,0},{1,20},{2,8},{3,28},{4,16},{5,4},{6,24},{7,12},{8,9},{9,29},... | collective-permute-start | bytes 786440 | tf_op jit(solution)/shard_map/weight_layout/ppermute | solution.py:813
  569.3 26.0 %collective-permute-start.129 = (bf16[256,512]{0,1:T(8,128)(2,1)}, bf16[256,512]{0,1:T(8,128)(2,1)S(1)}, u32[]{:S(2)}, u32[]{:S(2)}) collective-permute-start(bf16[256,512]{0,1:T(8,128)(2,1)} %get-tuple-element.470), channel_id=1, source_target_pairs={{0,0},{1,20},{2,8},{3,28},{4,16},{5,4},{6,24},{7,12},{8,9},{9,29},... | collective-permute-start | bytes 786440 | tf_op jit(solution)/shard_map/weight_layout/ppermute | solution.py:813
  570.9 24.4 %collective-permute-start.130 = (bf16[256,512]{0,1:T(8,128)(2,1)}, bf16[256,512]{0,1:T(8,128)(2,1)}, u32[]{:S(2)}, u32[]{:S(2)}) collective-permute-start(bf16[256,512]{0,1:T(8,128)(2,1)} %get-tuple-element.471), channel_id=1, source_target_pairs={{0,20},{1,0},{2,28},{3,8},{4,4},{5,16},{6,12},{7,24},{8,29},{9,9},... | collective-permute-start | bytes 786440 | tf_op jit(solution)/shard_map/weight_layout/ppermute | solution.py:813
  (174 other events, 1862.7 us)
Sparse Core Ops, SparseCore 0:
  403.6 48.7 reduce-scatter.1

commit v5 on v4

--- a/solution.py
+++ b/solution.py
@@ -14,6 +14,7 @@
 LOG2E = math.log2(math.e)
 SCORE_SCALE = HD ** (-0.5)
 ALL = ("z", "x", "y", "c")
+RUNS = (8, 4, 2, 1)
 
 
 def add_low(first, second):
@@ -281,6 +282,20 @@
     return place(key_axis) <= place(1 - key_axis)
 
 
+def in_runs(count, step, carry):
+    done = 0
+    for run in RUNS:
+        stop = count // run * run
+        first = done
+
+        def body(at, carry, run=run, first=first):
+            return step(first + run * at, carry, run)
+
+        carry = lax.fori_loop(0, (stop - done) // run, body, carry)
+        done = stop
+    return carry
+
+
 def forward_kernel(
     place_ref, rank_ref, core_ref, query_ref, key_ref, value_ref, mixed_ref, lse_ref, score_ref
 ):
@@ -317,8 +332,7 @@
         return tuple(new)
 
     maxima = tuple(jnp.full((span_rows, HD), -jnp.inf, HIGH) for _ in range(heads))
-    maxima = lax.fori_loop(0, rank // 2, lambda p, m: score_step(2 * p, m, 2), maxima)
-    maxima = lax.fori_loop(rank // 2 * 2, rank, lambda p, m: score_step(p, m, 1), maxima)
+    maxima = in_runs(rank, score_step, maxima)
     visible = diagonal_visible(core_ref[0], span_rows, 1)
     tops = []
     for h in range(heads):
@@ -341,8 +355,7 @@
     zero = jnp.zeros((span_rows, HD), HIGH)
     sums = tuple((zero, zero) for _ in range(heads))
     blocks = rank + 1
-    sums = lax.fori_loop(0, blocks // 2, lambda p, r: mix_step(2 * p, r, 2), sums)
-    sums = lax.fori_loop(blocks // 2 * 2, blocks, lambda p, r: mix_step(p, r, 1), sums)
+    sums = in_runs(blocks, mix_step, sums)
     for h in range(heads):
         total = jnp.sum(sums[h][0], axis=1, keepdims=True)
         mixed = (sums[h][1] / total).astype(LOW)
@@ -421,12 +434,12 @@
             return tuple(new)
 
         start = tuple(jnp.zeros((HD, span_rows), HIGH) for _ in range(heads))
-        grad_query = lax.fori_loop(
-            0, rank // 2, lambda p, g: block(2 * p + 1, block(2 * p, g, None), None), start
-        )
-        grad_query = lax.fori_loop(
-            rank // 2 * 2, rank, lambda p, g: block(p, g, None), grad_query
-        )
+        def blocks(first, grad_query, count):
+            for more in range(count):
+                grad_query = block(first + more, grad_query, None)
+            return grad_query
+
+        grad_query = in_runs(rank, blocks, start)
         visible = diagonal_visible(core_ref[0], span_rows, 0)
         grad_query = block(rank, grad_query, visible)
         for h in range(heads):

time: 611 us -> 612 us (level)
  Pallas kernels: 51.6 us -> 38.4 us
  starting transfers between devices: 113 us -> 123 us
    ppermute x131, starting transfers between devices: 92.5 us -> 102 us  [hop(): lax.ppermute(values, axis, [(i, (i + steps) % size) for i in range(size)])]
    pallas_call x1, Pallas kernels: 30.7 us -> 23 us  [attention_backward(): pl.pallas_call(backward_kernel, out_shape=(jax.ShapeDtypeStruct(own_shape...]
  transfers between devices with their start and end apart: 137 -> 137, of which waited for: 61 -> 62; matrix products, arithmetic and copies ran while one was open for 23% -> 23% of each run, Pallas kernels for 9% -> 6%
where the time goes in v5:
time: 612 us; the launch traced here: 606 us
  waiting for transfers between devices  263 us (43%)
  starting transfers between devices  123 us (20%)
  matrix products  73 us (12%)
  local copies, waits for them, and re-layouts  47.5 us (8%)
  other arithmetic  41.5 us (7%)
  Pallas kernels  38.4 us (6%)
  between operations  20.1 us (3%)
    ppermute x131, waiting for transfers between devices, hop(): lax.ppermute(values, axis, [(i, (i + steps) % size) for i in range(size)])  259 us
    ppermute x131, starting transfers between devices, hop(): lax.ppermute(values, axis, [(i, (i + steps) % size) for i in range(size)])  102 us
    dot_general x27, matrix products, matmul_right_t(): lax.dot_general(left_side, right_side, (((1,), (1,)), ((), ())), preferre...  28.4 us
    dot_general x28, matrix products, matmul(): return jnp.dot(left_side, right_side, preferred_element_type=HIGH)  25.6 us
    pallas_call x1, Pallas kernels, attention_backward(): pl.pallas_call(backward_kernel, out_shape=(jax.ShapeDtypeStruct(own_shape...  23 us
    unnamed x231, local copies, waits for them, and re-layouts  21.8 us
    dot_general x6, matrix products, matmul_left_t(): lax.dot_general(left_side, right_side, (((0,), (0,)), ((), ())), preferre...  19 us
    ppermute x4, starting transfers between devices, layout(): got = [lax.ppermute(sent[flip], ALL, to_layout[flip]) for flip in range(2)]  17.4 us
  transfers between devices with their start and end apart: 137, of which 62 were waited for; matrix products, arithmetic and copies ran while one was open for 23% of the time, Pallas kernels for 6%

profile of v5, /device:TPU:0, one launch (start us, length us, event | category | flops | bytes accessed | tf_op | source)
XLA Modules:
  0.0 606.1 jit_solution(3573520435484021871)
XLA Ops:
  9.4 5.1 collective-permute-start.2
  23.6 7.7 %collective-permute-done.1 = bf16[64,1536]{1,0:T(8,128)(2,1)S(1)} collective-permute-done((bf16[64,1536]{1,0:T(8,128)(2,1)S(1)}, bf16[64,1536]{1,0:T(8,128)(2,1)S(1)}, u32[]{:S(2)}, u32[]{:S(2)}) %collective-permute-start.1) | collective-permute-done | bytes 196640 | tf_op jit(solution)/shard_map/weight_columns/ppermute | solution.py:30
  38.9 3.2 collective-permute-done.10
  43.2 9.4 %collective-permute-done.7.refs_1_ = bf16[4,64,768]{2,1,0:T(8,128)(2,1)S(1)} collective-permute-done((bf16[4,64,768]{2,1,0:T(8,128)(2,1)S(1)}, bf16[4,64,768]{2,1,0:T(8,128)(2,1)S(1)}, u32[]{:S(2)}, u32[]{:S(2)}) %collective-permute-start.7) | collective-permute-done | bytes 393248 | tf_op jit(solution)/shard_map/shared_rows/ppermute | solution.py:30
  60.4 6.4 %collective-permute-done.19 = bf16[32,2048]{1,0:T(8,128)(2,1)S(1)} collective-permute-done((bf16[32,2048]{1,0:T(8,128)(2,1)S(1)}, bf16[32,2048]{1,0:T(8,128)(2,1)S(1)}, u32[]{:S(2)}, u32[]{:S(2)}) %collective-permute-start.19) | collective-permute-done | bytes 131104 | tf_op jit(solution)/shard_map/shared_rows/ppermute | solution.py:30
  77.4 6.9 %collective-permute-done.22.refs_7_ = bf16[4,64,768]{2,1,0:T(8,128)(2,1)S(1)} collective-permute-done((bf16[4,64,768]{2,1,0:T(8,128)(2,1)S(1)}, bf16[4,64,768]{2,1,0:T(8,128)(2,1)S(1)}, u32[]{:S(2)}, u32[]{:S(2)}) %collective-permute-start.22) | collective-permute-done | bytes 393248 | tf_op jit(solution)/shard_map/shared_rows/ppermute | solution.py:30
  95.6 8.1 %collective-permute-done.20 = bf16[128,2048]{1,0:T(8,128)(2,1)S(1)} collective-permute-done((bf16[128,2048]{1,0:T(8,128)(2,1)S(1)}, bf16[128,2048]{1,0:T(8,128)(2,1)S(1)}, u32[]{:S(2)}, u32[]{:S(2)}) %collective-permute-start.20) | collective-permute-done | bytes 524320 | tf_op jit(solution)/shard_map/normed_rows/ppermute | solution.py:30
  109.6 9.5 %collective-permute-done.23 = bf16[128,2048]{1,0:T(8,128)(2,1)} collective-permute-done((bf16[128,2048]{1,0:T(8,128)(2,1)S(1)}, bf16[128,2048]{1,0:T(8,128)(2,1)}, u32[]{:S(2)}, u32[]{:S(2)}) %collective-permute-start.23) | collective-permute-done | bytes 524320 | tf_op jit(solution)/shard_map/normed_rows/ppermute | solution.py:30
  123.9 10.0 %collective-permute-done.31 = bf16[128,2048]{1,0:T(8,128)(2,1)S(1)} collective-permute-done((bf16[128,2048]{1,0:T(8,128)(2,1)}, bf16[128,2048]{1,0:T(8,128)(2,1)S(1)}, u32[]{:S(2)}, u32[]{:S(2)}) %collective-permute-start.31) | collective-permute-done | bytes 524320 | tf_op jit(solution)/shard_map/normed_rows/ppermute | solution.py:30
  137.7 2.8 pad_maximum_fusion.1
  140.5 5.3 collective-permute-done.38
  157.2 13.3 %attention_forward.1 = (bf16[2,512,256]{2,1,0:T(8,128)(2,1)}, f32[2,8,1024]{2,1,0:T(8,128)}) custom-call(s32[16]{0:T(128)} %select_reduce_fusion.place_ref, s32[4]{0:T(128)} %bitcast.223, s32[1]{0:T(128)} %bitcast.1.core_ref, bf16[2,512,256]{2,1,0:T(8,128)(2,1)} %bitcast.221, bf16[4,2,512,256]{3,2,1,0:T(8,128)(2,1)} %bitcast.190, ...), custom_call_target="tpu_custom_call" | custom-call | flops 21474836480 | bytes 4194304 | tf_op jit(solution)/shard_map/attention_forward/pallas_call | solution.py:471
  174.5 8.0 %collective-permute-start.51 = (bf16[128,2048]{1,0:T(8,128)(2,1)S(1)}, bf16[128,2048]{1,0:T(8,128)(2,1)S(1)}, u32[]{:S(2)}, u32[]{:S(2)}) collective-permute-start(bf16[128,2048]{1,0:T(8,128)(2,1)S(1)} %get-tuple-element.198), channel_id=1, source_target_pairs={{0,4},{4,0},{1,5},{5,1},{2,6},{6,2},{3,7},{7,3},{8,12},{12,8},{9,1... | collective-permute-start | bytes 1572872 | tf_op jit(solution)/shard_map/attention_sum/ppermute | solution.py:30
  187.7 6.9 %collective-permute-done.51 = bf16[128,2048]{1,0:T(8,128)(2,1)S(1)} collective-permute-done((bf16[128,2048]{1,0:T(8,128)(2,1)S(1)}, bf16[128,2048]{1,0:T(8,128)(2,1)S(1)}, u32[]{:S(2)}, u32[]{:S(2)}) %collective-permute-start.51) | collective-permute-done | bytes 524320 | tf_op jit(solution)/shard_map/attention_sum/ppermute | solution.py:30
  194.6 3.6 collective-permute-done.45
  204.4 14.0 %collective-permute-done.49 = bf16[128,2048]{1,0:T(8,128)(2,1)S(1)} collective-permute-done((bf16[128,2048]{1,0:T(8,128)(2,1)S(1)}, bf16[128,2048]{1,0:T(8,128)(2,1)S(1)}, u32[]{:S(2)}, u32[]{:S(2)}) %collective-permute-start.49) | collective-permute-done | bytes 524320 | tf_op jit(solution)/shard_map/attention_sum/ppermute | solution.py:30
  223.4 10.5 %collective-permute-done.53 = bf16[128,2048]{1,0:T(8,128)(2,1)S(1)} collective-permute-done((bf16[128,2048]{1,0:T(8,128)(2,1)S(1)}, bf16[128,2048]{1,0:T(8,128)(2,1)S(1)}, u32[]{:S(2)}, u32[]{:S(2)}) %collective-permute-start.53) | collective-permute-done | bytes 524320 | tf_op jit(solution)/shard_map/attention_sum/ppermute | solution.py:30
  237.3 13.4 %collective-permute-done.56 = bf16[128,2048]{1,0:T(8,128)(2,1)S(1)} collective-permute-done((bf16[128,2048]{1,0:T(8,128)(2,1)S(1)}, bf16[128,2048]{1,0:T(8,128)(2,1)S(1)}, u32[]{:S(2)}, u32[]{:S(2)}) %collective-permute-start.56) | collective-permute-done | bytes 524320 | tf_op jit(solution)/shard_map/normed_two_rows/ppermute | solution.py:30
  253.0 13.0 %collective-permute-done.59 = bf16[128,2048]{1,0:T(8,128)(2,1)S(1)} collective-permute-done((bf16[128,2048]{1,0:T(8,128)(2,1)S(1)}, bf16[128,2048]{1,0:T(8,128)(2,1)S(1)}, u32[]{:S(2)}, u32[]{:S(2)}) %collective-permute-start.59) | collective-permute-done | bytes 524320 | tf_op jit(solution)/shard_map/normed_two_rows/ppermute | solution.py:30
  266.7 13.8 %collective-permute-done.62 = bf16[128,2048]{1,0:T(8,128)(2,1)S(1)} collective-permute-done((bf16[128,2048]{1,0:T(8,128)(2,1)S(1)}, bf16[128,2048]{1,0:T(8,128)(2,1)S(1)}, u32[]{:S(2)}, u32[]{:S(2)}) %collective-permute-start.62) | collective-permute-done | bytes 524320 | tf_op jit(solution)/shard_map/normed_two_rows/ppermute | solution.py:30
  282.5 3.2 fusion.226
  285.7 3.2 fusion.225
  288.9 4.3 multiply_convert_fusion
  297.3 3.4 convolution_convert_fusion.3
  304.7 8.4 %collective-permute-done.75 = bf16[128,2048]{1,0:T(8,128)(2,1)S(1)} collective-permute-done((bf16[128,2048]{1,0:T(8,128)(2,1)S(1)}, bf16[128,2048]{1,0:T(8,128)(2,1)S(1)}, u32[]{:S(2)}, u32[]{:S(2)}) %collective-permute-start.75) | collective-permute-done | bytes 524320 | tf_op jit(solution)/shard_map/ffn_grad_sum/ppermute | solution.py:30
  313.3 3.4 convolution_convert_fusion.2
  322.6 5.6 collective-permute-done.77
  328.8 3.4 convolution_convert_fusion.1
  344.7 4.4 collective-permute-done.84
  349.1 8.6 %collective-permute-done.83 = bf16[128,2048]{1,0:T(8,128)(2,1)S(1)} collective-permute-done((bf16[128,2048]{1,0:T(8,128)(2,1)S(1)}, bf16[128,2048]{1,0:T(8,128)(2,1)S(1)}, u32[]{:S(2)}, u32[]{:S(2)}) %collective-permute-start.83) | collective-permute-done | bytes 524320 | tf_op jit(solution)/shard_map/ffn_grad_sum/ppermute | solution.py:30
  357.7 5.2 collective-permute-done.81
  371.5 4.9 collective-permute-done.87
  381.2 6.8 %convolution_convert_fusion = bf16[1024,2048]{1,0:T(8,128)(2,1)} fusion(bf16[1024,704]{0,1:T(8,128)(2,1)S(1)} %bitcast_select_fusion, bf16[704,2048]{1,0:T(8,128)(2,1)} %copy-done.67), kind=kOutput, calls=%fused_computation.19 | convolution fusion | flops 2954887168 | bytes 8519680 | tf_op jit(solution)/shard_map/branch_rows/dot_general | solution.py:249
  397.8 4.0 collective-permute-done.88.refs_2_
  411.0 23.0 %attention_backward.1 = (bf16[2,512,256]{2,1,0:T(8,128)(2,1)}, bf16[4,2,512,256]{3,2,1,0:T(8,128)(2,1)}, bf16[4,2,512,256]{3,2,1,0:T(8,128)(2,1)}) custom-call(s32[16]{0:T(128)} %select_reduce_fusion.place_ref, s32[4]{0:T(128)} %bitcast.224, s32[1]{0:T(128)} %bitcast.1.core_ref, bf16[2,512,256]{2,1,0:T(8,128)(2,1)} %bitcast.222, ...), custom_call_target="tpu_custom_call" | custom-call | flops 128849018880 | bytes 8388608 | tf_op jit(solution)/shard_map/attention_backward/pallas_call | solution.py:515
  438.2 15.8 %collective-permute-start.104 = (bf16[1024,256]{1,0:T(8,128)(2,1)S(1)}, bf16[1024,256]{1,0:T(8,128)(2,1)S(1)}, u32[]{:S(2)}, u32[]{:S(2)}) collective-permute-start(bf16[1024,256]{1,0:T(8,128)(2,1)S(1)} %bitcast.198), channel_id=1, source_target_pairs={{0,4},{4,0},{1,5},{5,1},{2,6},{6,2},{3,7},{7,3},{8,12},{12,8},{9,1... | collective-permute-start | bytes 1572872 | tf_op jit(solution)/shard_map/normed_sum/ppermute | solution.py:30
  467.5 3.3 collective-permute-done.99
  473.4 11.2 %collective-permute-done.108 = bf16[1024,256]{1,0:T(8,128)(2,1)S(1)} collective-permute-done((bf16[1024,256]{1,0:T(8,128)(2,1)S(1)}, bf16[1024,256]{1,0:T(8,128)(2,1)S(1)}, u32[]{:S(2)}, u32[]{:S(2)}) %collective-permute-start.108) | collective-permute-done | bytes 524320 | tf_op jit(solution)/shard_map/normed_sum/ppermute | solution.py:30
  492.0 6.8 %collective-permute-done.110 = bf16[1024,256]{1,0:T(8,128)(2,1)S(1)} collective-permute-done((bf16[1024,256]{1,0:T(8,128)(2,1)S(1)}, bf16[1024,256]{1,0:T(8,128)(2,1)S(1)}, u32[]{:S(2)}, u32[]{:S(2)}) %collective-permute-start.110) | collective-permute-done | bytes 524320 | tf_op jit(solution)/shard_map/normed_sum/ppermute | solution.py:30
  499.3 2.7 collective-permute-done.107
  510.7 6.2 %convolution_convert_fusion.4 = bf16[2048,512]{0,1:T(8,128)(2,1)} fusion(bf16[1024,2048]{1,0:T(8,128)(2,1)} %copy-done.75, bf16[1024,256]{1,0:T(8,128)(2,1)} %copy-done.26, bf16[1024,256]{1,0:T(8,128)(2,1)} %copy-done.28), kind=kOutput, calls=%fused_computation.23 | convolution fusion | flops 2150629376 | bytes 7340032 | tf_op jit(solution)/shard_map/key_value_weight_sum/dot_general | solution.py:259
  528.4 5.0 collective-permute-done.117
  540.9 3.5 collective-permute-done.116
  554.2 8.3 %collective-permute-done.132 = bf16[256,512]{0,1:T(8,128)(2,1)S(1)} collective-permute-done((bf16[256,512]{0,1:T(8,128)(2,1)S(1)}, bf16[256,512]{0,1:T(8,128)(2,1)S(1)}, u32[]{:S(2)}, u32[]{:S(2)}) %collective-permute-start.132) | collective-permute-done | bytes 262176 | tf_op jit(solution)/shard_map/shared_sum/ppermute | solution.py:30
  562.8 3.4 collective-permute-start.134
  571.8 11.5 %collective-permute-start.130 = (bf16[256,512]{0,1:T(8,128)(2,1)}, bf16[256,512]{0,1:T(8,128)(2,1)}, u32[]{:S(2)}, u32[]{:S(2)}) collective-permute-start(bf16[256,512]{0,1:T(8,128)(2,1)} %get-tuple-element.471), channel_id=1, source_target_pairs={{0,20},{1,0},{2,28},{3,8},{4,4},{5,16},{6,12},{7,24},{8,29},{9,9},... | collective-permute-start | bytes 786440 | tf_op jit(solution)/shard_map/weight_layout/ppermute | solution.py:826
  584.5 3.4 all-to-all-start
  591.1 4.0 all-to-all-done
  (673 shorter events, 238.2 us)
Async XLA Ops:
  7.2 501.9 %reduce-scatter.2.cloned.1.call-start = ((), (), s32[]{:S(2)}) async-start(), calls=%async_computation.2 | async-start | bytes 4718592 | tf_op jit(solution)/shard_map/ffn_sum/reduce_scatter | solution.py:785
  14.6 16.7 %collective-permute-start.1 = (bf16[64,1536]{1,0:T(8,128)(2,1)S(1)}, bf16[64,1536]{1,0:T(8,128)(2,1)S(1)}, u32[]{:S(2)}, u32[]{:S(2)}) collective-permute-start(bf16[64,1536]{1,0:T(8,128)(2,1)S(1)} %pad_maximum_fusion.14), channel_id=1, source_target_pairs={{0,16},{8,24},{16,0},{24,8},{1,17},{9,25},{17,1},{25,9},{2,18},{10... | collective-permute-start | bytes 589832 | tf_op jit(solution)/shard_map/weight_columns/ppermute | solution.py:30
  14.7 16.6 %collective-permute-start = (bf16[64,1536]{1,0:T(8,128)(2,1)S(1)}, bf16[64,1536]{1,0:T(8,128)(2,1)S(1)}, u32[]{:S(2)}, u32[]{:S(2)}) collective-permute-start(bf16[64,1536]{1,0:T(8,128)(2,1)S(1)} %pad_maximum_fusion.13), channel_id=1, source_target_pairs={{0,8},{8,16},{16,24},{24,0},{1,9},{9,17},{17,25},{25,1},{2,10},{10... | collective-permute-start | bytes 589832 | tf_op jit(solution)/shard_map/weight_columns/ppermute | solution.py:30
  17.7 17.1 %collective-permute-start.5 = (bf16[64,768]{1,0:T(8,128)(2,1)S(1)}, bf16[64,768]{1,0:T(8,128)(2,1)S(1)}, u32[]{:S(2)}, u32[]{:S(2)}) collective-permute-start(bf16[64,768]{1,0:T(8,128)(2,1)S(1)} %pad_maximum_fusion.16), channel_id=1, source_target_pairs={{0,1},{1,0},{2,3},{3,2},{4,5},{5,4},{6,7},{7,6},{8,9},{9,8},{10,11... | collective-permute-start | bytes 294920 | tf_op jit(solution)/shard_map/weight_columns/ppermute | solution.py:30
  19.0 71.2 %collective-permute-start.27 = (bf16[128,2048]{1,0:T(8,128)(2,1)}, bf16[128,2048]{1,0:T(8,128)(2,1)}, u32[]{:S(2)}, u32[]{:S(2)}) collective-permute-start(bf16[128,2048]{1,0:T(8,128)(2,1)} %fusion.23), channel_id=1, source_target_pairs={{0,1},{1,0},{2,3},{3,2},{4,5},{5,4},{6,7},{7,6},{8,9},{9,8},{10,11... | collective-permute-start | bytes 1572872 | tf_op jit(solution)/shard_map/shared_rows/ppermute | solution.py:30
  37.9 17.7 %collective-permute-start.3 = (bf16[128,2048]{1,0:T(8,128)(2,1)}, bf16[128,2048]{1,0:T(8,128)(2,1)}, u32[]{:S(2)}, u32[]{:S(2)}) collective-permute-start(bf16[128,2048]{1,0:T(8,128)(2,1)} %fusion.23), channel_id=1, source_target_pairs={{0,8},{8,16},{16,24},{24,0},{1,9},{9,17},{17,25},{25,1},{2,10},{10... | collective-permute-start | bytes 1572872 | tf_op jit(solution)/shard_map/shared_rows/ppermute | solution.py:30
  54.5 18.4 %collective-permute-start.16 = (bf16[4,64,768]{2,1,0:T(8,128)(2,1)S(1)}, bf16[4,64,768]{2,1,0:T(8,128)(2,1)S(1)}, u32[]{:S(2)}, u32[]{:S(2)}) collective-permute-start(bf16[4,64,768]{2,1,0:T(8,128)(2,1)S(1)} %pad_maximum_fusion.12.refs_4_), channel_id=1, source_target_pairs={{0,2},{2,0},{1,3},{3,1},{4,6},{6,4},{5,7},{7,5},{8,10},{10,8},{9,1... | collective-permute-start | bytes 1179656 | tf_op jit(solution)/shard_map/shared_rows/ppermute | solution.py:30
  55.1 17.9 %collective-permute-start.17 = (bf16[4,64,768]{2,1,0:T(8,128)(2,1)S(1)}, bf16[4,64,768]{2,1,0:T(8,128)(2,1)S(1)}, u32[]{:S(2)}, u32[]{:S(2)}) collective-permute-start(bf16[4,64,768]{2,1,0:T(8,128)(2,1)S(1)} %pad_maximum_fusion.12.refs_4_), channel_id=1, source_target_pairs={{0,4},{4,0},{1,5},{5,1},{2,6},{6,2},{3,7},{7,3},{8,12},{12,8},{9,1... | collective-permute-start | bytes 1179656 | tf_op jit(solution)/shard_map/shared_rows/ppermute | solution.py:30
  71.2 16.1 %collective-permute-start.13 = (bf16[128,2048]{1,0:T(8,128)(2,1)}, bf16[128,2048]{1,0:T(8,128)(2,1)S(1)}, u32[]{:S(2)}, u32[]{:S(2)}) collective-permute-start(bf16[128,2048]{1,0:T(8,128)(2,1)} %collective-permute-done.4), channel_id=1, source_target_pairs={{0,8},{8,16},{16,24},{24,0},{1,9},{9,17},{17,25},{25,1},{2,10},{10... | collective-permute-start | bytes 1572872 | tf_op jit(solution)/shard_map/shared_rows/ppermute | solution.py:30
  76.2 77.7 %collective-permute-start.35 = (bf16[128,2048]{1,0:T(8,128)(2,1)}, bf16[128,2048]{1,0:T(8,128)(2,1)}, u32[]{:S(2)}, u32[]{:S(2)}) collective-permute-start(bf16[128,2048]{1,0:T(8,128)(2,1)} %fusion.30), channel_id=1, source_target_pairs={{0,1},{1,0},{2,3},{3,2},{4,5},{5,4},{6,7},{7,6},{8,9},{9,8},{10,11... | collective-permute-start | bytes 1572872 | tf_op jit(solution)/shard_map/normed_rows/ppermute | solution.py:30
  87.5 16.2 %collective-permute-start.20 = (bf16[128,2048]{1,0:T(8,128)(2,1)S(1)}, bf16[128,2048]{1,0:T(8,128)(2,1)S(1)}, u32[]{:S(2)}, u32[]{:S(2)}) collective-permute-start(bf16[128,2048]{1,0:T(8,128)(2,1)S(1)} %copy-done.50), channel_id=1, source_target_pairs={{0,8},{8,16},{16,24},{24,0},{1,9},{9,17},{17,25},{25,1},{2,10},{10... | collective-permute-start | bytes 1572872 | tf_op jit(solution)/shard_map/normed_rows/ppermute | solution.py:30
  149.8 23.4 %collective-permute-start.46 = (bf16[128,2048]{1,0:T(8,128)(2,1)}, bf16[128,2048]{1,0:T(8,128)(2,1)}, u32[]{:S(2)}, u32[]{:S(2)}) collective-permute-start(bf16[128,2048]{1,0:T(8,128)(2,1)} %get-tuple-element.194), channel_id=1, source_target_pairs={{0,2},{2,0},{1,3},{3,1},{4,6},{6,4},{5,7},{7,5},{8,10},{10,8},{9,1... | collective-permute-start | bytes 1572872 | tf_op jit(solution)/shard_map/grad_output_rows/ppermute | solution.py:30
  150.3 23.4 %collective-permute-start.47 = (bf16[128,2048]{1,0:T(8,128)(2,1)}, bf16[128,2048]{1,0:T(8,128)(2,1)}, u32[]{:S(2)}, u32[]{:S(2)}) collective-permute-start(bf16[128,2048]{1,0:T(8,128)(2,1)} %get-tuple-element.194), channel_id=1, source_target_pairs={{0,4},{4,0},{1,5},{5,1},{2,6},{6,2},{3,7},{7,3},{8,12},{12,8},{9,1... | collective-permute-start | bytes 1572872 | tf_op jit(solution)/shard_map/grad_output_rows/ppermute | solution.py:30
  150.3 23.4 %collective-permute-start.43 = (bf16[128,2048]{1,0:T(8,128)(2,1)S(1)}, bf16[128,2048]{1,0:T(8,128)(2,1)}, u32[]{:S(2)}, u32[]{:S(2)}) collective-permute-start(bf16[128,2048]{1,0:T(8,128)(2,1)S(1)} %copy-done.30), channel_id=1, source_target_pairs={{0,24},{8,0},{16,8},{24,16},{1,25},{9,1},{17,9},{25,17},{2,26},{10... | collective-permute-start | bytes 1572872 | tf_op jit(solution)/shard_map/grad_output_rows/ppermute | solution.py:30
  150.3 23.4 %collective-permute-start.42 = (bf16[128,2048]{1,0:T(8,128)(2,1)}, bf16[128,2048]{1,0:T(8,128)(2,1)}, u32[]{:S(2)}, u32[]{:S(2)}) collective-permute-start(bf16[128,2048]{1,0:T(8,128)(2,1)} %collective-permute-done.41), channel_id=1, source_target_pairs={{0,8},{8,16},{16,24},{24,0},{1,9},{9,17},{17,25},{25,1},{2,10},{10... | collective-permute-start | bytes 1572872 | tf_op jit(solution)/shard_map/grad_output_rows/ppermute | solution.py:30
  174.5 20.1 %collective-permute-start.51 = (bf16[128,2048]{1,0:T(8,128)(2,1)S(1)}, bf16[128,2048]{1,0:T(8,128)(2,1)S(1)}, u32[]{:S(2)}, u32[]{:S(2)}) collective-permute-start(bf16[128,2048]{1,0:T(8,128)(2,1)S(1)} %get-tuple-element.198), channel_id=1, source_target_pairs={{0,4},{4,0},{1,5},{5,1},{2,6},{6,2},{3,7},{7,3},{8,12},{12,8},{9,1... | collective-permute-start | bytes 1572872 | tf_op jit(solution)/shard_map/attention_sum/ppermute | solution.py:30
  183.2 16.7 %collective-permute-start.44 = (bf16[128,2048]{1,0:T(8,128)(2,1)S(1)}, bf16[128,2048]{1,0:T(8,128)(2,1)S(1)}, u32[]{:S(2)}, u32[]{:S(2)}) collective-permute-start(bf16[128,2048]{1,0:T(8,128)(2,1)S(1)} %convolution_convert_fusion.13), channel_id=1, source_target_pairs={{0,1},{1,0},{2,3},{3,2},{4,5},{5,4},{6,7},{7,6},{8,9},{9,8},{10,11... | collective-permute-start | bytes 1572872 | tf_op jit(solution)/shard_map/attention_sum/ppermute | solution.py:30
  198.2 20.4 %collective-permute-start.54 = (bf16[128,2048]{1,0:T(8,128)(2,1)S(1)}, bf16[128,2048]{1,0:T(8,128)(2,1)S(1)}, u32[]{:S(2)}, u32[]{:S(2)}) collective-permute-start(bf16[128,2048]{1,0:T(8,128)(2,1)S(1)} %get-tuple-element.202), channel_id=1, source_target_pairs={{0,2},{2,0},{1,3},{3,1},{4,6},{6,4},{5,7},{7,5},{8,10},{10,8},{9,1... | collective-permute-start | bytes 1572872 | tf_op jit(solution)/shard_map/attention_sum/ppermute | solution.py:30
  199.9 18.7 %collective-permute-start.55 = (bf16[128,2048]{1,0:T(8,128)(2,1)S(1)}, bf16[128,2048]{1,0:T(8,128)(2,1)S(1)}, u32[]{:S(2)}, u32[]{:S(2)}) collective-permute-start(bf16[128,2048]{1,0:T(8,128)(2,1)S(1)} %get-tuple-element.202), channel_id=1, source_target_pairs={{0,4},{4,0},{1,5},{5,1},{2,6},{6,2},{3,7},{7,3},{8,12},{12,8},{9,1... | collective-permute-start | bytes 1572872 | tf_op jit(solution)/shard_map/attention_sum/ppermute | solution.py:30
  202.3 16.2 %collective-permute-start.49 = (bf16[128,2048]{1,0:T(8,128)(2,1)S(1)}, bf16[128,2048]{1,0:T(8,128)(2,1)S(1)}, u32[]{:S(2)}, u32[]{:S(2)}) collective-permute-start(bf16[128,2048]{1,0:T(8,128)(2,1)S(1)} %add_convert_fusion.23), channel_id=1, source_target_pairs={{0,8},{8,16},{16,24},{24,0},{1,9},{9,17},{17,25},{25,1},{2,10},{10... | collective-permute-start | bytes 1572872 | tf_op jit(solution)/shard_map/attention_sum/ppermute | solution.py:30
  234.5 48.0 %collective-permute-start.66 = (bf16[128,2048]{1,0:T(8,128)(2,1)S(1)}, bf16[128,2048]{1,0:T(8,128)(2,1)S(1)}, u32[]{:S(2)}, u32[]{:S(2)}) collective-permute-start(bf16[128,2048]{1,0:T(8,128)(2,1)S(1)} %multiply_convert_fusion.3), channel_id=1, source_target_pairs={{0,1},{1,0},{2,3},{3,2},{4,5},{5,4},{6,7},{7,6},{8,9},{9,8},{10,11... | collective-permute-start | bytes 1572872 | tf_op jit(solution)/shard_map/normed_two_rows/ppermute | solution.py:30
  234.6 16.1 %collective-permute-start.56 = (bf16[128,2048]{1,0:T(8,128)(2,1)S(1)}, bf16[128,2048]{1,0:T(8,128)(2,1)S(1)}, u32[]{:S(2)}, u32[]{:S(2)}) collective-permute-start(bf16[128,2048]{1,0:T(8,128)(2,1)S(1)} %multiply_convert_fusion.3), channel_id=1, source_target_pairs={{0,8},{8,16},{16,24},{24,0},{1,9},{9,17},{17,25},{25,1},{2,10},{10... | collective-permute-start | bytes 1572872 | tf_op jit(solution)/shard_map/normed_two_rows/ppermute | solution.py:30
  234.6 16.1 %collective-permute-start.61 = (bf16[128,2048]{1,0:T(8,128)(2,1)S(1)}, bf16[128,2048]{1,0:T(8,128)(2,1)S(1)}, u32[]{:S(2)}, u32[]{:S(2)}) collective-permute-start(bf16[128,2048]{1,0:T(8,128)(2,1)S(1)} %collective-permute-done.50), channel_id=1, source_target_pairs={{0,4},{4,0},{1,5},{5,1},{2,6},{6,2},{3,7},{7,3},{8,12},{12,8},{9,1... | collective-permute-start | bytes 1572872 | tf_op jit(solution)/shard_map/normed_two_rows/ppermute | solution.py:30
  250.7 30.0 %collective-permute-start.63 = (bf16[128,2048]{1,0:T(8,128)(2,1)S(1)}, bf16[128,2048]{1,0:T(8,128)(2,1)S(1)}, u32[]{:S(2)}, u32[]{:S(2)}) collective-permute-start(bf16[128,2048]{1,0:T(8,128)(2,1)S(1)} %collective-permute-done.56), channel_id=1, source_target_pairs={{0,1},{1,0},{2,3},{3,2},{4,5},{5,4},{6,7},{7,6},{8,9},{9,8},{10,11... | collective-permute-start | bytes 1572872 | tf_op jit(solution)/shard_map/normed_two_rows/ppermute | solution.py:30
  336.5 21.2 %collective-permute-start.83 = (bf16[128,2048]{1,0:T(8,128)(2,1)S(1)}, bf16[128,2048]{1,0:T(8,128)(2,1)S(1)}, u32[]{:S(2)}, u32[]{:S(2)}) collective-permute-start(bf16[128,2048]{1,0:T(8,128)(2,1)S(1)} %get-tuple-element.238), channel_id=1, source_target_pairs={{0,2},{2,0},{1,3},{3,1},{4,6},{6,4},{5,7},{7,5},{8,10},{10,8},{9,1... | collective-permute-start | bytes 1572872 | tf_op jit(solution)/shard_map/ffn_grad_sum/ppermute | solution.py:30
  337.6 20.0 %collective-permute-start.82 = (bf16[128,2048]{1,0:T(8,128)(2,1)S(1)}, bf16[128,2048]{1,0:T(8,128)(2,1)S(1)}, u32[]{:S(2)}, u32[]{:S(2)}) collective-permute-start(bf16[128,2048]{1,0:T(8,128)(2,1)S(1)} %pad_maximum_fusion.5), channel_id=1, source_target_pairs={{0,4},{4,0},{1,5},{5,1},{2,6},{6,2},{3,7},{7,3},{8,12},{12,8},{9,1... | collective-permute-start | bytes 1572872 | tf_op jit(solution)/shard_map/ffn_grad_sum/ppermute | solution.py:30
  341.7 21.2 %collective-permute-start.81 = (bf16[128,2048]{1,0:T(8,128)(2,1)S(1)}, bf16[128,2048]{1,0:T(8,128)(2,1)S(1)}, u32[]{:S(2)}, u32[]{:S(2)}) collective-permute-start(bf16[128,2048]{1,0:T(8,128)(2,1)S(1)} %pad_maximum_fusion.4), channel_id=1, source_target_pairs={{0,4},{4,0},{1,5},{5,1},{2,6},{6,2},{3,7},{7,3},{8,12},{12,8},{9,1... | collective-permute-start | bytes 1572872 | tf_op jit(solution)/shard_map/ffn_grad_sum/ppermute | solution.py:30
  344.7 26.8 %collective-permute-start.80 = (bf16[128,2048]{1,0:T(8,128)(2,1)S(1)}, bf16[128,2048]{1,0:T(8,128)(2,1)}, u32[]{:S(2)}, u32[]{:S(2)}) collective-permute-start(bf16[128,2048]{1,0:T(8,128)(2,1)S(1)} %get-tuple-element.285.refs_3_), channel_id=1, source_target_pairs={{0,8},{8,16},{16,24},{24,0},{1,9},{9,17},{17,25},{25,1},{2,10},{10... | collective-permute-start | bytes 1572872 | tf_op jit(solution)/shard_map/branch_rows/ppermute | solution.py:30
  349.1 59.9 %collective-permute-start.92 = (bf16[128,2048]{1,0:T(8,128)(2,1)S(1)}, bf16[128,2048]{1,0:T(8,128)(2,1)}, u32[]{:S(2)}, u32[]{:S(2)}) collective-permute-start(bf16[128,2048]{1,0:T(8,128)(2,1)S(1)} %get-tuple-element.285.refs_3_), channel_id=1, source_target_pairs={{0,1},{1,0},{2,3},{3,2},{4,5},{5,4},{6,7},{7,6},{8,9},{9,8},{10,11... | collective-permute-start | bytes 1572872 | tf_op jit(solution)/shard_map/branch_rows/ppermute | solution.py:30
  371.5 16.6 %collective-permute-start.85 = (bf16[128,2048]{1,0:T(8,128)(2,1)}, bf16[128,2048]{1,0:T(8,128)(2,1)}, u32[]{:S(2)}, u32[]{:S(2)}) collective-permute-start(bf16[128,2048]{1,0:T(8,128)(2,1)} %collective-permute-done.80.refs_0_), channel_id=1, source_target_pairs={{0,8},{8,16},{16,24},{24,0},{1,9},{9,17},{17,25},{25,1},{2,10},{10... | collective-permute-start | bytes 1572872 | tf_op jit(solution)/shard_map/branch_rows/ppermute | solution.py:30
  405.4 31.9 %collective-permute-start.100 = (bf16[128,2048]{1,0:T(8,128)(2,1)S(1)}, bf16[128,2048]{1,0:T(8,128)(2,1)S(1)}, u32[]{:S(2)}, u32[]{:S(2)}) collective-permute-start(bf16[128,2048]{1,0:T(8,128)(2,1)S(1)} %add_convert_fusion.14), channel_id=1, source_target_pairs={{0,4},{4,0},{1,5},{5,1},{2,6},{6,2},{3,7},{7,3},{8,12},{12,8},{9,1... | collective-permute-start | bytes 1572872 | tf_op jit(solution)/shard_map/unit_weight_sums/ppermute | solution.py:30
  409.0 28.4 %collective-permute-start.101 = (bf16[144,2048]{1,0:T(8,128)(2,1)S(1)}, bf16[144,2048]{1,0:T(8,128)(2,1)S(1)}, u32[]{:S(2)}, u32[]{:S(2)}) collective-permute-start(bf16[144,2048]{1,0:T(8,128)(2,1)S(1)} %add_convert_fusion.2), channel_id=1, source_target_pairs={{0,2},{2,0},{1,3},{3,1},{4,6},{6,4},{5,7},{7,5},{8,10},{10,8},{9,1... | collective-permute-start | bytes 1769480 | tf_op jit(solution)/shard_map/unit_weight_sums/ppermute | solution.py:30
  435.5 18.6 %collective-permute-start.93 = (bf16[128,2048]{1,0:T(8,128)(2,1)S(1)}, bf16[128,2048]{1,0:T(8,128)(2,1)S(1)}, u32[]{:S(2)}, u32[]{:S(2)}) collective-permute-start(bf16[128,2048]{1,0:T(8,128)(2,1)S(1)} %convolution_convert_fusion.10), channel_id=1, source_target_pairs={{0,1},{1,0},{2,3},{3,2},{4,5},{5,4},{6,7},{7,6},{8,9},{9,8},{10,11... | collective-permute-start | bytes 1572872 | tf_op jit(solution)/shard_map/normed_sum/ppermute | solution.py:30
  437.4 33.6 %collective-permute-start.105 = (bf16[1024,256]{1,0:T(8,128)(2,1)S(1)}, bf16[1024,256]{1,0:T(8,128)(2,1)S(1)}, u32[]{:S(2)}, u32[]{:S(2)}) collective-permute-start(bf16[1024,256]{1,0:T(8,128)(2,1)S(1)} %bitcast.197), channel_id=1, source_target_pairs={{0,2},{2,0},{1,3},{3,1},{4,6},{6,4},{5,7},{7,5},{8,10},{10,8},{9,1... | collective-permute-start | bytes 1572872 | tf_op jit(solution)/shard_map/normed_sum/ppermute | solution.py:30
  438.2 32.8 %collective-permute-start.104 = (bf16[1024,256]{1,0:T(8,128)(2,1)S(1)}, bf16[1024,256]{1,0:T(8,128)(2,1)S(1)}, u32[]{:S(2)}, u32[]{:S(2)}) collective-permute-start(bf16[1024,256]{1,0:T(8,128)(2,1)S(1)} %bitcast.198), channel_id=1, source_target_pairs={{0,4},{4,0},{1,5},{5,1},{2,6},{6,2},{3,7},{7,3},{8,12},{12,8},{9,1... | collective-permute-start | bytes 1572872 | tf_op jit(solution)/shard_map/normed_sum/ppermute | solution.py:30
  454.5 16.3 %collective-permute-start.99 = (bf16[128,2048]{1,0:T(8,128)(2,1)S(1)}, bf16[128,2048]{1,0:T(8,128)(2,1)S(1)}, u32[]{:S(2)}, u32[]{:S(2)}) collective-permute-start(bf16[128,2048]{1,0:T(8,128)(2,1)S(1)} %fusion.9), channel_id=1, source_target_pairs={{0,8},{8,16},{16,24},{24,0},{1,9},{9,17},{17,25},{25,1},{2,10},{10... | collective-permute-start | bytes 1572872 | tf_op jit(solution)/shard_map/normed_sum/ppermute | solution.py:30
  502.0 26.4 %collective-permute-start.120 = (bf16[256,512]{0,1:T(8,128)(2,1)}, bf16[256,512]{0,1:T(8,128)(2,1)}, u32[]{:S(2)}, u32[]{:S(2)}) collective-permute-start(bf16[256,512]{0,1:T(8,128)(2,1)} %get-tuple-element.293), channel_id=1, source_target_pairs={{0,2},{2,0},{1,3},{3,1},{4,6},{6,4},{5,7},{7,5},{8,10},{10,8},{9,1... | collective-permute-start | bytes 786440 | tf_op jit(solution)/shard_map/shared_sum/ppermute | solution.py:30
  505.1 23.3 %collective-permute-start.119 = (bf16[256,512]{0,1:T(8,128)(2,1)}, bf16[256,512]{0,1:T(8,128)(2,1)S(1)}, u32[]{:S(2)}, u32[]{:S(2)}) collective-permute-start(bf16[256,512]{0,1:T(8,128)(2,1)} %get-tuple-element.292), channel_id=1, source_target_pairs={{0,2},{2,0},{1,3},{3,1},{4,6},{6,4},{5,7},{7,5},{8,10},{10,8},{9,1... | collective-permute-start | bytes 786440 | tf_op jit(solution)/shard_map/shared_sum/ppermute | solution.py:30
  505.7 22.7 %collective-permute-start.118 = (bf16[256,512]{0,1:T(8,128)(2,1)}, bf16[256,512]{0,1:T(8,128)(2,1)}, u32[]{:S(2)}, u32[]{:S(2)}) collective-permute-start(bf16[256,512]{0,1:T(8,128)(2,1)} %get-tuple-element.291), channel_id=1, source_target_pairs={{0,4},{4,0},{1,5},{5,1},{2,6},{6,2},{3,7},{7,3},{8,12},{12,8},{9,1... | collective-permute-start | bytes 786440 | tf_op jit(solution)/shard_map/shared_sum/ppermute | solution.py:30
  509.1 17.9 %collective-permute-start.114 = (bf16[128,2048]{1,0:T(8,128)(2,1)}, bf16[128,2048]{1,0:T(8,128)(2,1)}, u32[]{:S(2)}, u32[]{:S(2)}) collective-permute-start(bf16[128,2048]{1,0:T(8,128)(2,1)} %fusion.10), channel_id=1, source_target_pairs={{0,8},{8,16},{16,24},{24,0},{1,9},{9,17},{17,25},{25,1},{2,10},{10... | collective-permute-start | bytes 1572872 | tf_op jit(solution)/shard_map/shared_sum/ppermute | solution.py:30
  528.3 16.1 %collective-permute-start.116 = (bf16[128,2048]{1,0:T(8,128)(2,1)S(1)}, bf16[128,2048]{1,0:T(8,128)(2,1)S(1)}, u32[]{:S(2)}, u32[]{:S(2)}) collective-permute-start(bf16[128,2048]{1,0:T(8,128)(2,1)S(1)} %add_convert_fusion.10), channel_id=1, source_target_pairs={{0,8},{8,16},{16,24},{24,0},{1,9},{9,17},{17,25},{25,1},{2,10},{10... | collective-permute-start | bytes 1572872 | tf_op jit(solution)/shard_map/shared_sum/ppermute | solution.py:30
  544.6 24.4 %collective-permute-start.122 = (bf16[128,2048]{1,0:T(8,128)(2,1)S(1)}, bf16[128,2048]{1,0:T(8,128)(2,1)S(1)}, u32[]{:S(2)}, u32[]{:S(2)}) collective-permute-start(bf16[128,2048]{1,0:T(8,128)(2,1)S(1)} %add_convert_fusion.9), channel_id=1, source_target_pairs={{0,8},{8,16},{16,24},{24,0},{1,9},{9,17},{17,25},{25,1},{2,10},{10... | collective-permute-start | bytes 1572872 | tf_op jit(solution)/shard_map/shared_sum/ppermute | solution.py:30
  548.4 17.8 %collective-permute-start.127 = (bf16[256,512]{0,1:T(8,128)(2,1)S(1)}, bf16[256,512]{0,1:T(8,128)(2,1)S(1)}, u32[]{:S(2)}, u32[]{:S(2)}) collective-permute-start(bf16[256,512]{0,1:T(8,128)(2,1)S(1)} %get-tuple-element.303), channel_id=1, source_target_pairs={{0,4},{4,0},{1,5},{5,1},{2,6},{6,2},{3,7},{7,3},{8,12},{12,8},{9,1... | collective-permute-start | bytes 786440 | tf_op jit(solution)/shard_map/shared_sum/ppermute | solution.py:30
  549.4 17.7 %collective-permute-start.128 = (bf16[256,512]{0,1:T(8,128)(2,1)S(1)}, bf16[256,512]{0,1:T(8,128)(2,1)S(1)}, u32[]{:S(2)}, u32[]{:S(2)}) collective-permute-start(bf16[256,512]{0,1:T(8,128)(2,1)S(1)} %get-tuple-element.306), channel_id=1, source_target_pairs={{0,2},{2,0},{1,3},{3,1},{4,6},{6,4},{5,7},{7,5},{8,10},{10,8},{9,1... | collective-permute-start | bytes 786440 | tf_op jit(solution)/shard_map/shared_sum/ppermute | solution.py:30
  562.8 20.6 %collective-permute-start.134 = (bf16[256,512]{0,1:T(8,128)(2,1)S(1)}, bf16[256,512]{0,1:T(8,128)(2,1)S(1)}, u32[]{:S(2)}, u32[]{:S(2)}) collective-permute-start(bf16[256,512]{0,1:T(8,128)(2,1)S(1)} %broadcast_select_fusion.1), channel_id=1, source_target_pairs={{0,20},{1,0},{2,28},{3,8},{4,4},{5,16},{6,12},{7,24},{8,29},{9,9},... | collective-permute-start | bytes 786440 | tf_op jit(solution)/shard_map/weight_layout/ppermute | solution.py:826
  566.3 17.1 %collective-permute-start.133 = (bf16[256,512]{0,1:T(8,128)(2,1)S(1)}, bf16[256,512]{0,1:T(8,128)(2,1)S(1)}, u32[]{:S(2)}, u32[]{:S(2)}) collective-permute-start(bf16[256,512]{0,1:T(8,128)(2,1)S(1)} %get-tuple-element.392), channel_id=1, source_target_pairs={{0,0},{1,20},{2,8},{3,28},{4,16},{5,4},{6,24},{7,12},{8,9},{9,29},... | collective-permute-start | bytes 786440 | tf_op jit(solution)/shard_map/weight_layout/ppermute | solution.py:826
  570.3 25.6 %collective-permute-start.129 = (bf16[256,512]{0,1:T(8,128)(2,1)}, bf16[256,512]{0,1:T(8,128)(2,1)S(1)}, u32[]{:S(2)}, u32[]{:S(2)}) collective-permute-start(bf16[256,512]{0,1:T(8,128)(2,1)} %get-tuple-element.470), channel_id=1, source_target_pairs={{0,0},{1,20},{2,8},{3,28},{4,16},{5,4},{6,24},{7,12},{8,9},{9,29},... | collective-permute-start | bytes 786440 | tf_op jit(solution)/shard_map/weight_layout/ppermute | solution.py:826
  571.8 24.0 %collective-permute-start.130 = (bf16[256,512]{0,1:T(8,128)(2,1)}, bf16[256,512]{0,1:T(8,128)(2,1)}, u32[]{:S(2)}, u32[]{:S(2)}) collective-permute-start(bf16[256,512]{0,1:T(8,128)(2,1)} %get-tuple-element.471), channel_id=1, source_target_pairs={{0,20},{1,0},{2,28},{3,8},{4,4},{5,16},{6,12},{7,24},{8,29},{9,9},... | collective-permute-start | bytes 786440 | tf_op jit(solution)/shard_map/weight_layout/ppermute | solution.py:826
  (174 other events, 1883.9 us)
Sparse Core Ops, SparseCore 0:
  401.9 47.7 reduce-scatter.1

commit v6 on v5

--- a/solution.py
+++ b/solution.py
@@ -75,6 +75,23 @@
         yield wanted
         total = add_low(merged[(step + 1) % size], got[-1])
     return total, add_low(near_total, far[-1])
+
+
+def sum_joined_task(first, second):
+    if lax.axis_size("x") > 2:
+        return (yield from sum_task(first, second))
+    rows = first[0].shape[0]
+    over_x, over_y, got, far = [], [], [], []
+    yield [
+        ("x", jnp.concatenate([second[3], second[2]]), over_x),
+        ("y", jnp.concatenate([first[3], first[1]]), over_y),
+    ]
+    far_total = add_low(second[1], over_x[-1][:rows])
+    near_total = add_low(second[0], over_x[-1][rows:])
+    merged = add_low(first[2], over_y[-1][:rows])
+    own = add_low(first[0], over_y[-1][rows:])
+    yield [("x", merged, got), ("y", far_total, far)]
+    return add_low(own, got[-1]), add_low(near_total, far[-1])
 
 
 class Ticks:
@@ -765,7 +782,7 @@
         unit_window(grad_gate_act, group_in)
         unit_window(grad_up_act, group_in)
         unit_sum_tasks = [ticks.add(sum_task(chunk_parts(0), chunk_parts(1)))]
-        unit_window(hidden, group_grad, room=2)
+        unit_window(hidden, group_grad)
         unit_sum_tasks.append(ticks.add(sum_task(chunk_parts(2), chunk_parts(3))))
         grad_ffn = ffn_grad_sum.finish()
 
@@ -805,7 +822,7 @@
         ]
 
     def chunk_sums(values):
-        return sum_task(side_parts(values, 0), side_parts(values, 1))
+        return sum_joined_task(side_parts(values, 0), side_parts(values, 1))
 
     to_layout = [
         [
@@ -834,7 +851,7 @@
 
     with jax.named_scope("grad_keys_values"):
         keys_task = ticks.add(
-            sum_task(unit_parts(key_terms), unit_parts(value_terms)), urgent=True
+            sum_joined_task(unit_parts(key_terms), unit_parts(value_terms)), urgent=True
         )
     with jax.named_scope("normed_sum"):
         normed_sum = RowSum(
@@ -844,6 +861,9 @@
         sent = normed_sum.sent
     with jax.named_scope("query_weight_sum"):
         query_terms = matmul_left_t(after(group_normed, sent), grad_queries).astype(LOW)
+    with jax.named_scope("normed_sum"):
+        normed_sum.step()
+        sent = normed_sum.sent
     with jax.named_scope("out_weight_sum"):
         group_branch = jnp.concatenate(after(branch_both, sent), axis=0)
         out_terms = matmul_left_t(group_branch, mixed).astype(LOW)

time: 612 us -> 606 us (level)
  waiting for transfers between devices: 263 us -> 249 us
  starting transfers between devices: 123 us -> 112 us
  Pallas kernels: 38.4 us -> 47.3 us
    ppermute x131 -> x125, starting transfers between devices: 102 us -> 86.1 us  [hop(): lax.ppermute(values, axis, [(i, (i + steps) % size) for i in range(size)])]
    ppermute x131 -> x125, waiting for transfers between devices: 259 us -> 245 us  [hop(): lax.ppermute(values, axis, [(i, (i + steps) % size) for i in range(size)])]
    pallas_call x1, Pallas kernels: 23 us -> 29.1 us  [attention_backward(): pl.pallas_call(backward_kernel, out_shape=(jax.ShapeDtypeStruct(own_shape...]
    unnamed x231 -> x229, local copies, waits for them, and re-layouts: 21.8 us -> 26.7 us
  transfers between devices with their start and end apart: 137 -> 131, of which waited for: 62 -> 52; matrix products, arithmetic and copies ran while one was open for 23% -> 24% of each run, Pallas kernels for 6% -> 8%
where the time goes in v6:
time: 606 us; the launch traced here: 597 us
  waiting for transfers between devices  249 us (41%)
  starting transfers between devices  112 us (18%)
  matrix products  68.5 us (11%)
  local copies, waits for them, and re-layouts  53.4 us (9%)
  other arithmetic  47.6 us (8%)
  Pallas kernels  47.3 us (8%)
  between operations  20 us (3%)
    ppermute x125, waiting for transfers between devices, hop(): lax.ppermute(values, axis, [(i, (i + steps) % size) for i in range(size)])  245 us
    ppermute x125, starting transfers between devices, hop(): lax.ppermute(values, axis, [(i, (i + steps) % size) for i in range(size)])  86.1 us
    pallas_call x1, Pallas kernels, attention_backward(): pl.pallas_call(backward_kernel, out_shape=(jax.ShapeDtypeStruct(own_shape...  29.1 us
    unnamed x229, local copies, waits for them, and re-layouts  26.7 us
    dot_general x28, matrix products, matmul(): return jnp.dot(left_side, right_side, preferred_element_type=HIGH)  25.6 us
    dot_general x27, matrix products, matmul_right_t(): lax.dot_general(left_side, right_side, (((1,), (1,)), ((), ())), preferre...  25.6 us
    ppermute x4, starting transfers between devices, layout(): got = [lax.ppermute(sent[flip], ALL, to_layout[flip]) for flip in range(2)]  17.7 us
    dot_general x6, matrix products, matmul_left_t(): lax.dot_general(left_side, right_side, (((0,), (0,)), ((), ())), preferre...  17.3 us
  transfers between devices with their start and end apart: 131, of which 52 were waited for; matrix products, arithmetic and copies ran while one was open for 24% of the time, Pallas kernels for 8%

profile of v6, /device:TPU:0, one launch (start us, length us, event | category | flops | bytes accessed | tf_op | source)
XLA Modules:
  0.0 597.3 jit_solution(12532641477527867685)
XLA Ops:
  9.4 5.1 collective-permute-start.2
  23.6 7.7 %collective-permute-done.1 = bf16[64,1536]{1,0:T(8,128)(2,1)S(1)} collective-permute-done((bf16[64,1536]{1,0:T(8,128)(2,1)S(1)}, bf16[64,1536]{1,0:T(8,128)(2,1)S(1)}, u32[]{:S(2)}, u32[]{:S(2)}) %collective-permute-start.1) | collective-permute-done | bytes 196640 | tf_op jit(solution)/shard_map/weight_columns/ppermute | solution.py:30
  38.9 3.2 collective-permute-done.10
  43.2 9.4 %collective-permute-done.7.refs_1_ = bf16[4,64,768]{2,1,0:T(8,128)(2,1)S(1)} collective-permute-done((bf16[4,64,768]{2,1,0:T(8,128)(2,1)S(1)}, bf16[4,64,768]{2,1,0:T(8,128)(2,1)S(1)}, u32[]{:S(2)}, u32[]{:S(2)}) %collective-permute-start.7) | collective-permute-done | bytes 393248 | tf_op jit(solution)/shard_map/shared_rows/ppermute | solution.py:30
  60.4 6.4 %collective-permute-done.19 = bf16[32,2048]{1,0:T(8,128)(2,1)S(1)} collective-permute-done((bf16[32,2048]{1,0:T(8,128)(2,1)S(1)}, bf16[32,2048]{1,0:T(8,128)(2,1)S(1)}, u32[]{:S(2)}, u32[]{:S(2)}) %collective-permute-start.19) | collective-permute-done | bytes 131104 | tf_op jit(solution)/shard_map/shared_rows/ppermute | solution.py:30
  77.4 6.9 %collective-permute-done.22.refs_7_ = bf16[4,64,768]{2,1,0:T(8,128)(2,1)S(1)} collective-permute-done((bf16[4,64,768]{2,1,0:T(8,128)(2,1)S(1)}, bf16[4,64,768]{2,1,0:T(8,128)(2,1)S(1)}, u32[]{:S(2)}, u32[]{:S(2)}) %collective-permute-start.22) | collective-permute-done | bytes 393248 | tf_op jit(solution)/shard_map/shared_rows/ppermute | solution.py:30
  87.5 2.5 collective-permute-start.20
  95.7 8.1 %collective-permute-done.20 = bf16[128,2048]{1,0:T(8,128)(2,1)S(1)} collective-permute-done((bf16[128,2048]{1,0:T(8,128)(2,1)S(1)}, bf16[128,2048]{1,0:T(8,128)(2,1)S(1)}, u32[]{:S(2)}, u32[]{:S(2)}) %collective-permute-start.20) | collective-permute-done | bytes 524320 | tf_op jit(solution)/shard_map/normed_rows/ppermute | solution.py:30
  109.7 9.5 %collective-permute-done.23 = bf16[128,2048]{1,0:T(8,128)(2,1)} collective-permute-done((bf16[128,2048]{1,0:T(8,128)(2,1)S(1)}, bf16[128,2048]{1,0:T(8,128)(2,1)}, u32[]{:S(2)}, u32[]{:S(2)}) %collective-permute-start.23) | collective-permute-done | bytes 524320 | tf_op jit(solution)/shard_map/normed_rows/ppermute | solution.py:30
  124.0 9.8 %collective-permute-done.31 = bf16[128,2048]{1,0:T(8,128)(2,1)S(1)} collective-permute-done((bf16[128,2048]{1,0:T(8,128)(2,1)}, bf16[128,2048]{1,0:T(8,128)(2,1)S(1)}, u32[]{:S(2)}, u32[]{:S(2)}) %collective-permute-start.31) | collective-permute-done | bytes 524320 | tf_op jit(solution)/shard_map/normed_rows/ppermute | solution.py:30
  137.8 2.8 pad_maximum_fusion.1
  140.6 5.3 collective-permute-done.38
  156.7 16.1 %attention_forward.1 = (bf16[2,512,256]{2,1,0:T(8,128)(2,1)}, f32[2,8,1024]{2,1,0:T(8,128)}) custom-call(s32[16]{0:T(128)} %select_reduce_fusion.place_ref, s32[4]{0:T(128)} %bitcast.223, s32[1]{0:T(128)} %bitcast.1.core_ref, bf16[2,512,256]{2,1,0:T(8,128)(2,1)} %bitcast.221, bf16[4,2,512,256]{3,2,1,0:T(8,128)(2,1)} %bitcast.190, ...), custom_call_target="tpu_custom_call" | custom-call | flops 21474836480 | bytes 4194304 | tf_op jit(solution)/shard_map/attention_forward/pallas_call | solution.py:488
  176.1 5.4 collective-permute-start.51
  186.3 3.7 collective-permute-done.50
  190.0 3.7 collective-permute-done.51
  193.7 3.6 collective-permute-done.45
  203.5 14.0 %collective-permute-done.49 = bf16[128,2048]{1,0:T(8,128)(2,1)S(1)} collective-permute-done((bf16[128,2048]{1,0:T(8,128)(2,1)S(1)}, bf16[128,2048]{1,0:T(8,128)(2,1)S(1)}, u32[]{:S(2)}, u32[]{:S(2)}) %collective-permute-start.49) | collective-permute-done | bytes 524320 | tf_op jit(solution)/shard_map/attention_sum/ppermute | solution.py:30
  222.5 10.5 %collective-permute-done.53 = bf16[128,2048]{1,0:T(8,128)(2,1)S(1)} collective-permute-done((bf16[128,2048]{1,0:T(8,128)(2,1)S(1)}, bf16[128,2048]{1,0:T(8,128)(2,1)S(1)}, u32[]{:S(2)}, u32[]{:S(2)}) %collective-permute-start.53) | collective-permute-done | bytes 524320 | tf_op jit(solution)/shard_map/attention_sum/ppermute | solution.py:30
  236.3 13.4 %collective-permute-done.56 = bf16[128,2048]{1,0:T(8,128)(2,1)S(1)} collective-permute-done((bf16[128,2048]{1,0:T(8,128)(2,1)S(1)}, bf16[128,2048]{1,0:T(8,128)(2,1)S(1)}, u32[]{:S(2)}, u32[]{:S(2)}) %collective-permute-start.56) | collective-permute-done | bytes 524320 | tf_op jit(solution)/shard_map/normed_two_rows/ppermute | solution.py:30
  252.1 13.0 %collective-permute-done.59 = bf16[128,2048]{1,0:T(8,128)(2,1)S(1)} collective-permute-done((bf16[128,2048]{1,0:T(8,128)(2,1)S(1)}, bf16[128,2048]{1,0:T(8,128)(2,1)S(1)}, u32[]{:S(2)}, u32[]{:S(2)}) %collective-permute-start.59) | collective-permute-done | bytes 524320 | tf_op jit(solution)/shard_map/normed_two_rows/ppermute | solution.py:30
  265.8 14.0 %collective-permute-done.62 = bf16[128,2048]{1,0:T(8,128)(2,1)S(1)} collective-permute-done((bf16[128,2048]{1,0:T(8,128)(2,1)S(1)}, bf16[128,2048]{1,0:T(8,128)(2,1)S(1)}, u32[]{:S(2)}, u32[]{:S(2)}) %collective-permute-start.62) | collective-permute-done | bytes 524320 | tf_op jit(solution)/shard_map/normed_two_rows/ppermute | solution.py:30
  281.8 3.2 fusion.226
  285.0 3.2 fusion.225
  288.2 4.3 multiply_convert_fusion
  296.6 3.4 convolution_convert_fusion.3
  304.9 7.5 %collective-permute-done.75 = bf16[128,2048]{1,0:T(8,128)(2,1)S(1)} collective-permute-done((bf16[128,2048]{1,0:T(8,128)(2,1)S(1)}, bf16[128,2048]{1,0:T(8,128)(2,1)S(1)}, u32[]{:S(2)}, u32[]{:S(2)}) %collective-permute-start.75) | collective-permute-done | bytes 524320 | tf_op jit(solution)/shard_map/ffn_grad_sum/ppermute | solution.py:30
  312.5 3.4 convolution_convert_fusion.2
  321.9 5.6 collective-permute-done.77
  327.6 3.4 convolution_convert_fusion.1
  352.1 7.6 %collective-permute-done.80.refs_0_ = bf16[128,2048]{1,0:T(8,128)(2,1)} collective-permute-done((bf16[128,2048]{1,0:T(8,128)(2,1)S(1)}, bf16[128,2048]{1,0:T(8,128)(2,1)}, u32[]{:S(2)}, u32[]{:S(2)}) %collective-permute-start.80) | collective-permute-done | bytes 524320 | tf_op jit(solution)/shard_map/branch_rows/ppermute | solution.py:30
  365.0 12.0 %collective-permute-done.83.refs_1_ = bf16[128,2048]{1,0:T(8,128)(2,1)} collective-permute-done((bf16[128,2048]{1,0:T(8,128)(2,1)}, bf16[128,2048]{1,0:T(8,128)(2,1)}, u32[]{:S(2)}, u32[]{:S(2)}) %collective-permute-start.83) | collective-permute-done | bytes 524320 | tf_op jit(solution)/shard_map/branch_rows/ppermute | solution.py:30
  379.1 6.8 %convolution_convert_fusion = bf16[1024,2048]{1,0:T(8,128)(2,1)} fusion(bf16[1024,704]{0,1:T(8,128)(2,1)S(1)} %bitcast_select_fusion, bf16[704,2048]{1,0:T(8,128)(2,1)} %copy-done.66), kind=kOutput, calls=%fused_computation.19 | convolution fusion | flops 2954887168 | bytes 8519680 | tf_op jit(solution)/shard_map/branch_rows/dot_general | solution.py:266
  386.0 5.6 collective-permute-done.86.refs_2_
  395.8 9.0 %collective-permute-done.94 = bf16[144,2048]{1,0:T(8,128)(2,1)S(1)} collective-permute-done((bf16[144,2048]{1,0:T(8,128)(2,1)S(1)}, bf16[144,2048]{1,0:T(8,128)(2,1)S(1)}, u32[]{:S(2)}, u32[]{:S(2)}) %collective-permute-start.94) | collective-permute-done | bytes 589856 | tf_op jit(solution)/shard_map/branch_rows/ppermute | solution.py:30
  408.9 29.1 %attention_backward.1 = (bf16[2,512,256]{2,1,0:T(8,128)(2,1)}, bf16[4,2,512,256]{3,2,1,0:T(8,128)(2,1)}, bf16[4,2,512,256]{3,2,1,0:T(8,128)(2,1)}) custom-call(s32[16]{0:T(128)} %select_reduce_fusion.place_ref, s32[4]{0:T(128)} %bitcast.224, s32[1]{0:T(128)} %bitcast.1.core_ref, bf16[2,512,256]{2,1,0:T(8,128)(2,1)} %bitcast.222, ...), custom_call_target="tpu_custom_call" | custom-call | flops 128849018880 | bytes 8388608 | tf_op jit(solution)/shard_map/attention_backward/pallas_call | solution.py:532
  443.5 8.2 %collective-permute-start.104 = (bf16[2048,256]{1,0:T(8,128)(2,1)S(1)}, bf16[2048,256]{1,0:T(8,128)(2,1)S(1)}, u32[]{:S(2)}, u32[]{:S(2)}) collective-permute-start(bf16[2048,256]{1,0:T(8,128)(2,1)S(1)} %pad_maximum_fusion.2), channel_id=1, source_target_pairs={{0,4},{4,0},{1,5},{5,1},{2,6},{6,2},{3,7},{7,3},{8,12},{12,8},{9,1... | collective-permute-start | bytes 3145736 | tf_op jit(solution)/shard_map/normed_sum/ppermute | solution.py:30
  464.7 3.4 collective-permute-done.97
  484.1 10.4 %collective-permute-done.108 = bf16[1024,256]{1,0:T(8,128)(2,1)S(1)} collective-permute-done((bf16[1024,256]{1,0:T(8,128)(2,1)S(1)}, bf16[1024,256]{1,0:T(8,128)(2,1)S(1)}, u32[]{:S(2)}, u32[]{:S(2)}) %collective-permute-start.108) | collective-permute-done | bytes 524320 | tf_op jit(solution)/shard_map/normed_sum/ppermute | solution.py:30
  496.6 2.4 collective-permute-done.107
  504.6 4.6 convolution_convert_fusion.4
  512.2 3.0 fusion.35
  525.9 9.8 %collective-permute-done.114 = bf16[128,2048]{1,0:T(8,128)(2,1)S(1)} collective-permute-done((bf16[128,2048]{1,0:T(8,128)(2,1)S(1)}, bf16[128,2048]{1,0:T(8,128)(2,1)S(1)}, u32[]{:S(2)}, u32[]{:S(2)}) %collective-permute-start.114) | collective-permute-done | bytes 524320 | tf_op jit(solution)/shard_map/shared_sum/ppermute | solution.py:30
  541.8 7.2 %collective-permute-done.126 = bf16[256,512]{0,1:T(8,128)(2,1)S(1)} collective-permute-done((bf16[256,512]{0,1:T(8,128)(2,1)S(1)}, bf16[256,512]{0,1:T(8,128)(2,1)S(1)}, u32[]{:S(2)}, u32[]{:S(2)}) %collective-permute-start.126) | collective-permute-done | bytes 262176 | tf_op jit(solution)/shard_map/shared_sum/ppermute | solution.py:30
  549.3 5.9 collective-permute-start.128
  560.8 9.4 %collective-permute-start.124 = (bf16[256,512]{0,1:T(8,128)(2,1)}, bf16[256,512]{0,1:T(8,128)(2,1)}, u32[]{:S(2)}, u32[]{:S(2)}) collective-permute-start(bf16[256,512]{0,1:T(8,128)(2,1)} %get-tuple-element.451), channel_id=1, source_target_pairs={{0,20},{1,0},{2,28},{3,8},{4,4},{5,16},{6,12},{7,24},{8,29},{9,9},... | collective-permute-start | bytes 786440 | tf_op jit(solution)/shard_map/weight_layout/ppermute | solution.py:843
  571.2 8.1 %all-to-all-start = ((f32[32,1,192]{2,1,0:T(1,128)}), f32[32,1,192]{2,1,0:T(1,128)S(1)}, u32[]{:S(2)}, u32[]{:S(2)}) async-start(f32[32,1,192]{2,1,0:T(1,128)} %all_to_all.8), calls=%async_computation.1 | async-start | bytes 65536 | tf_op jit(solution)/shard_map/all_to_all | solution.py:917
  582.5 4.0 all-to-all-done
  (665 shorter events, 223.2 us)
Async XLA Ops:
  7.2 496.7 %reduce-scatter.2.cloned.1.call-start = ((), (), s32[]{:S(2)}) async-start(), calls=%async_computation.2 | async-start | bytes 4718592 | tf_op jit(solution)/shard_map/ffn_sum/reduce_scatter | solution.py:802
  14.6 16.7 %collective-permute-start.1 = (bf16[64,1536]{1,0:T(8,128)(2,1)S(1)}, bf16[64,1536]{1,0:T(8,128)(2,1)S(1)}, u32[]{:S(2)}, u32[]{:S(2)}) collective-permute-start(bf16[64,1536]{1,0:T(8,128)(2,1)S(1)} %pad_maximum_fusion.20), channel_id=1, source_target_pairs={{0,16},{8,24},{16,0},{24,8},{1,17},{9,25},{17,1},{25,9},{2,18},{10... | collective-permute-start | bytes 589832 | tf_op jit(solution)/shard_map/weight_columns/ppermute | solution.py:30
  14.7 16.6 %collective-permute-start = (bf16[64,1536]{1,0:T(8,128)(2,1)S(1)}, bf16[64,1536]{1,0:T(8,128)(2,1)S(1)}, u32[]{:S(2)}, u32[]{:S(2)}) collective-permute-start(bf16[64,1536]{1,0:T(8,128)(2,1)S(1)} %pad_maximum_fusion.19), channel_id=1, source_target_pairs={{0,8},{8,16},{16,24},{24,0},{1,9},{9,17},{17,25},{25,1},{2,10},{10... | collective-permute-start | bytes 589832 | tf_op jit(solution)/shard_map/weight_columns/ppermute | solution.py:30
  17.7 17.1 %collective-permute-start.5 = (bf16[64,768]{1,0:T(8,128)(2,1)S(1)}, bf16[64,768]{1,0:T(8,128)(2,1)S(1)}, u32[]{:S(2)}, u32[]{:S(2)}) collective-permute-start(bf16[64,768]{1,0:T(8,128)(2,1)S(1)} %pad_maximum_fusion.22), channel_id=1, source_target_pairs={{0,1},{1,0},{2,3},{3,2},{4,5},{5,4},{6,7},{7,6},{8,9},{9,8},{10,11... | collective-permute-start | bytes 294920 | tf_op jit(solution)/shard_map/weight_columns/ppermute | solution.py:30
  19.0 71.2 %collective-permute-start.27 = (bf16[128,2048]{1,0:T(8,128)(2,1)}, bf16[128,2048]{1,0:T(8,128)(2,1)}, u32[]{:S(2)}, u32[]{:S(2)}) collective-permute-start(bf16[128,2048]{1,0:T(8,128)(2,1)} %fusion.23), channel_id=1, source_target_pairs={{0,1},{1,0},{2,3},{3,2},{4,5},{5,4},{6,7},{7,6},{8,9},{9,8},{10,11... | collective-permute-start | bytes 1572872 | tf_op jit(solution)/shard_map/shared_rows/ppermute | solution.py:30
  37.9 17.7 %collective-permute-start.3 = (bf16[128,2048]{1,0:T(8,128)(2,1)}, bf16[128,2048]{1,0:T(8,128)(2,1)}, u32[]{:S(2)}, u32[]{:S(2)}) collective-permute-start(bf16[128,2048]{1,0:T(8,128)(2,1)} %fusion.23), channel_id=1, source_target_pairs={{0,8},{8,16},{16,24},{24,0},{1,9},{9,17},{17,25},{25,1},{2,10},{10... | collective-permute-start | bytes 1572872 | tf_op jit(solution)/shard_map/shared_rows/ppermute | solution.py:30
  54.5 18.4 %collective-permute-start.16 = (bf16[4,64,768]{2,1,0:T(8,128)(2,1)S(1)}, bf16[4,64,768]{2,1,0:T(8,128)(2,1)S(1)}, u32[]{:S(2)}, u32[]{:S(2)}) collective-permute-start(bf16[4,64,768]{2,1,0:T(8,128)(2,1)S(1)} %pad_maximum_fusion.18.refs_4_), channel_id=1, source_target_pairs={{0,2},{2,0},{1,3},{3,1},{4,6},{6,4},{5,7},{7,5},{8,10},{10,8},{9,1... | collective-permute-start | bytes 1179656 | tf_op jit(solution)/shard_map/shared_rows/ppermute | solution.py:30
  55.1 17.9 %collective-permute-start.17 = (bf16[4,64,768]{2,1,0:T(8,128)(2,1)S(1)}, bf16[4,64,768]{2,1,0:T(8,128)(2,1)S(1)}, u32[]{:S(2)}, u32[]{:S(2)}) collective-permute-start(bf16[4,64,768]{2,1,0:T(8,128)(2,1)S(1)} %pad_maximum_fusion.18.refs_4_), channel_id=1, source_target_pairs={{0,4},{4,0},{1,5},{5,1},{2,6},{6,2},{3,7},{7,3},{8,12},{12,8},{9,1... | collective-permute-start | bytes 1179656 | tf_op jit(solution)/shard_map/shared_rows/ppermute | solution.py:30
  71.2 16.1 %collective-permute-start.13 = (bf16[128,2048]{1,0:T(8,128)(2,1)}, bf16[128,2048]{1,0:T(8,128)(2,1)S(1)}, u32[]{:S(2)}, u32[]{:S(2)}) collective-permute-start(bf16[128,2048]{1,0:T(8,128)(2,1)} %collective-permute-done.4), channel_id=1, source_target_pairs={{0,8},{8,16},{16,24},{24,0},{1,9},{9,17},{17,25},{25,1},{2,10},{10... | collective-permute-start | bytes 1572872 | tf_op jit(solution)/shard_map/shared_rows/ppermute | solution.py:30
  76.2 77.3 %collective-permute-start.35 = (bf16[128,2048]{1,0:T(8,128)(2,1)}, bf16[128,2048]{1,0:T(8,128)(2,1)}, u32[]{:S(2)}, u32[]{:S(2)}) collective-permute-start(bf16[128,2048]{1,0:T(8,128)(2,1)} %fusion.30), channel_id=1, source_target_pairs={{0,1},{1,0},{2,3},{3,2},{4,5},{5,4},{6,7},{7,6},{8,9},{9,8},{10,11... | collective-permute-start | bytes 1572872 | tf_op jit(solution)/shard_map/normed_rows/ppermute | solution.py:30
  87.5 16.2 %collective-permute-start.20 = (bf16[128,2048]{1,0:T(8,128)(2,1)S(1)}, bf16[128,2048]{1,0:T(8,128)(2,1)S(1)}, u32[]{:S(2)}, u32[]{:S(2)}) collective-permute-start(bf16[128,2048]{1,0:T(8,128)(2,1)S(1)} %copy-done.49), channel_id=1, source_target_pairs={{0,8},{8,16},{16,24},{24,0},{1,9},{9,17},{17,25},{25,1},{2,10},{10... | collective-permute-start | bytes 1572872 | tf_op jit(solution)/shard_map/normed_rows/ppermute | solution.py:30
  149.7 25.8 %collective-permute-start.46 = (bf16[128,2048]{1,0:T(8,128)(2,1)}, bf16[128,2048]{1,0:T(8,128)(2,1)}, u32[]{:S(2)}, u32[]{:S(2)}) collective-permute-start(bf16[128,2048]{1,0:T(8,128)(2,1)} %get-tuple-element.184), channel_id=1, source_target_pairs={{0,2},{2,0},{1,3},{3,1},{4,6},{6,4},{5,7},{7,5},{8,10},{10,8},{9,1... | collective-permute-start | bytes 1572872 | tf_op jit(solution)/shard_map/grad_output_rows/ppermute | solution.py:30
  150.2 25.9 %collective-permute-start.47 = (bf16[128,2048]{1,0:T(8,128)(2,1)}, bf16[128,2048]{1,0:T(8,128)(2,1)}, u32[]{:S(2)}, u32[]{:S(2)}) collective-permute-start(bf16[128,2048]{1,0:T(8,128)(2,1)} %get-tuple-element.184), channel_id=1, source_target_pairs={{0,4},{4,0},{1,5},{5,1},{2,6},{6,2},{3,7},{7,3},{8,12},{12,8},{9,1... | collective-permute-start | bytes 1572872 | tf_op jit(solution)/shard_map/grad_output_rows/ppermute | solution.py:30
  150.2 25.9 %collective-permute-start.43 = (bf16[128,2048]{1,0:T(8,128)(2,1)S(1)}, bf16[128,2048]{1,0:T(8,128)(2,1)}, u32[]{:S(2)}, u32[]{:S(2)}) collective-permute-start(bf16[128,2048]{1,0:T(8,128)(2,1)S(1)} %copy-done.31), channel_id=1, source_target_pairs={{0,24},{8,0},{16,8},{24,16},{1,25},{9,1},{17,9},{25,17},{2,26},{10... | collective-permute-start | bytes 1572872 | tf_op jit(solution)/shard_map/grad_output_rows/ppermute | solution.py:30
  150.2 25.9 %collective-permute-start.42 = (bf16[128,2048]{1,0:T(8,128)(2,1)}, bf16[128,2048]{1,0:T(8,128)(2,1)}, u32[]{:S(2)}, u32[]{:S(2)}) collective-permute-start(bf16[128,2048]{1,0:T(8,128)(2,1)} %collective-permute-done.41), channel_id=1, source_target_pairs={{0,8},{8,16},{16,24},{24,0},{1,9},{9,17},{17,25},{25,1},{2,10},{10... | collective-permute-start | bytes 1572872 | tf_op jit(solution)/shard_map/grad_output_rows/ppermute | solution.py:30
  176.1 17.5 %collective-permute-start.51 = (bf16[128,2048]{1,0:T(8,128)(2,1)S(1)}, bf16[128,2048]{1,0:T(8,128)(2,1)S(1)}, u32[]{:S(2)}, u32[]{:S(2)}) collective-permute-start(bf16[128,2048]{1,0:T(8,128)(2,1)S(1)} %get-tuple-element.188), channel_id=1, source_target_pairs={{0,4},{4,0},{1,5},{5,1},{2,6},{6,2},{3,7},{7,3},{8,12},{12,8},{9,1... | collective-permute-start | bytes 1572872 | tf_op jit(solution)/shard_map/attention_sum/ppermute | solution.py:30
  182.3 16.7 %collective-permute-start.44 = (bf16[128,2048]{1,0:T(8,128)(2,1)S(1)}, bf16[128,2048]{1,0:T(8,128)(2,1)S(1)}, u32[]{:S(2)}, u32[]{:S(2)}) collective-permute-start(bf16[128,2048]{1,0:T(8,128)(2,1)S(1)} %convolution_convert_fusion.13), channel_id=1, source_target_pairs={{0,1},{1,0},{2,3},{3,2},{4,5},{5,4},{6,7},{7,6},{8,9},{9,8},{10,11... | collective-permute-start | bytes 1572872 | tf_op jit(solution)/shard_map/attention_sum/ppermute | solution.py:30
  197.3 20.4 %collective-permute-start.54 = (bf16[128,2048]{1,0:T(8,128)(2,1)S(1)}, bf16[128,2048]{1,0:T(8,128)(2,1)S(1)}, u32[]{:S(2)}, u32[]{:S(2)}) collective-permute-start(bf16[128,2048]{1,0:T(8,128)(2,1)S(1)} %get-tuple-element.192), channel_id=1, source_target_pairs={{0,2},{2,0},{1,3},{3,1},{4,6},{6,4},{5,7},{7,5},{8,10},{10,8},{9,1... | collective-permute-start | bytes 1572872 | tf_op jit(solution)/shard_map/attention_sum/ppermute | solution.py:30
  199.0 18.7 %collective-permute-start.55 = (bf16[128,2048]{1,0:T(8,128)(2,1)S(1)}, bf16[128,2048]{1,0:T(8,128)(2,1)S(1)}, u32[]{:S(2)}, u32[]{:S(2)}) collective-permute-start(bf16[128,2048]{1,0:T(8,128)(2,1)S(1)} %get-tuple-element.192), channel_id=1, source_target_pairs={{0,4},{4,0},{1,5},{5,1},{2,6},{6,2},{3,7},{7,3},{8,12},{12,8},{9,1... | collective-permute-start | bytes 1572872 | tf_op jit(solution)/shard_map/attention_sum/ppermute | solution.py:30
  201.3 16.2 %collective-permute-start.49 = (bf16[128,2048]{1,0:T(8,128)(2,1)S(1)}, bf16[128,2048]{1,0:T(8,128)(2,1)S(1)}, u32[]{:S(2)}, u32[]{:S(2)}) collective-permute-start(bf16[128,2048]{1,0:T(8,128)(2,1)S(1)} %add_convert_fusion.23), channel_id=1, source_target_pairs={{0,8},{8,16},{16,24},{24,0},{1,9},{9,17},{17,25},{25,1},{2,10},{10... | collective-permute-start | bytes 1572872 | tf_op jit(solution)/shard_map/attention_sum/ppermute | solution.py:30
  217.7 16.0 %collective-permute-start.57 = (bf16[144,2048]{1,0:T(8,128)(2,1)S(1)}, bf16[144,2048]{1,0:T(8,128)(2,1)S(1)}, u32[]{:S(2)}, u32[]{:S(2)}) collective-permute-start(bf16[144,2048]{1,0:T(8,128)(2,1)S(1)} %pad_slice_fusion), channel_id=1, source_target_pairs={{0,2},{2,0},{1,3},{3,1},{4,6},{6,4},{5,7},{7,5},{8,10},{10,8},{9,1... | collective-permute-start | bytes 1769480 | tf_op jit(solution)/shard_map/attention_sum/ppermute | solution.py:30
  233.6 48.2 %collective-permute-start.66 = (bf16[128,2048]{1,0:T(8,128)(2,1)S(1)}, bf16[128,2048]{1,0:T(8,128)(2,1)S(1)}, u32[]{:S(2)}, u32[]{:S(2)}) collective-permute-start(bf16[128,2048]{1,0:T(8,128)(2,1)S(1)} %multiply_convert_fusion.3), channel_id=1, source_target_pairs={{0,1},{1,0},{2,3},{3,2},{4,5},{5,4},{6,7},{7,6},{8,9},{9,8},{10,11... | collective-permute-start | bytes 1572872 | tf_op jit(solution)/shard_map/normed_two_rows/ppermute | solution.py:30
  233.6 16.1 %collective-permute-start.56 = (bf16[128,2048]{1,0:T(8,128)(2,1)S(1)}, bf16[128,2048]{1,0:T(8,128)(2,1)S(1)}, u32[]{:S(2)}, u32[]{:S(2)}) collective-permute-start(bf16[128,2048]{1,0:T(8,128)(2,1)S(1)} %multiply_convert_fusion.3), channel_id=1, source_target_pairs={{0,8},{8,16},{16,24},{24,0},{1,9},{9,17},{17,25},{25,1},{2,10},{10... | collective-permute-start | bytes 1572872 | tf_op jit(solution)/shard_map/normed_two_rows/ppermute | solution.py:30
  233.7 16.1 %collective-permute-start.61 = (bf16[128,2048]{1,0:T(8,128)(2,1)S(1)}, bf16[128,2048]{1,0:T(8,128)(2,1)S(1)}, u32[]{:S(2)}, u32[]{:S(2)}) collective-permute-start(bf16[128,2048]{1,0:T(8,128)(2,1)S(1)} %collective-permute-done.50), channel_id=1, source_target_pairs={{0,4},{4,0},{1,5},{5,1},{2,6},{6,2},{3,7},{7,3},{8,12},{12,8},{9,1... | collective-permute-start | bytes 1572872 | tf_op jit(solution)/shard_map/normed_two_rows/ppermute | solution.py:30
  249.8 30.3 %collective-permute-start.63 = (bf16[128,2048]{1,0:T(8,128)(2,1)S(1)}, bf16[128,2048]{1,0:T(8,128)(2,1)S(1)}, u32[]{:S(2)}, u32[]{:S(2)}) collective-permute-start(bf16[128,2048]{1,0:T(8,128)(2,1)S(1)} %collective-permute-done.56), channel_id=1, source_target_pairs={{0,1},{1,0},{2,3},{3,2},{4,5},{5,4},{6,7},{7,6},{8,9},{9,8},{10,11... | collective-permute-start | bytes 1572872 | tf_op jit(solution)/shard_map/normed_two_rows/ppermute | solution.py:30
  296.4 16.0 %collective-permute-start.75 = (bf16[128,2048]{1,0:T(8,128)(2,1)S(1)}, bf16[128,2048]{1,0:T(8,128)(2,1)S(1)}, u32[]{:S(2)}, u32[]{:S(2)}) collective-permute-start(bf16[128,2048]{1,0:T(8,128)(2,1)S(1)} %add_convert_fusion.21), channel_id=1, source_target_pairs={{0,8},{8,16},{16,24},{24,0},{1,9},{9,17},{17,25},{25,1},{2,10},{10... | collective-permute-start | bytes 1572872 | tf_op jit(solution)/shard_map/ffn_grad_sum/ppermute | solution.py:30
  343.5 62.2 %collective-permute-start.90 = (bf16[128,2048]{1,0:T(8,128)(2,1)S(1)}, bf16[128,2048]{1,0:T(8,128)(2,1)}, u32[]{:S(2)}, u32[]{:S(2)}) collective-permute-start(bf16[128,2048]{1,0:T(8,128)(2,1)S(1)} %get-tuple-element.273.refs_3_), channel_id=1, source_target_pairs={{0,1},{1,0},{2,3},{3,2},{4,5},{5,4},{6,7},{7,6},{8,9},{9,8},{10,11... | collective-permute-start | bytes 1572872 | tf_op jit(solution)/shard_map/branch_rows/ppermute | solution.py:30
  343.5 16.2 %collective-permute-start.80 = (bf16[128,2048]{1,0:T(8,128)(2,1)S(1)}, bf16[128,2048]{1,0:T(8,128)(2,1)}, u32[]{:S(2)}, u32[]{:S(2)}) collective-permute-start(bf16[128,2048]{1,0:T(8,128)(2,1)S(1)} %get-tuple-element.273.refs_3_), channel_id=1, source_target_pairs={{0,8},{8,16},{16,24},{24,0},{1,9},{9,17},{17,25},{25,1},{2,10},{10... | collective-permute-start | bytes 1572872 | tf_op jit(solution)/shard_map/branch_rows/ppermute | solution.py:30
  359.7 17.6 %collective-permute-start.93 = (bf16[128,2048]{1,0:T(8,128)(2,1)}, bf16[128,2048]{1,0:T(8,128)(2,1)}, u32[]{:S(2)}, u32[]{:S(2)}) collective-permute-start(bf16[128,2048]{1,0:T(8,128)(2,1)} %pad_maximum_fusion.8), channel_id=1, source_target_pairs={{0,2},{2,0},{1,3},{3,1},{4,6},{6,4},{5,7},{7,5},{8,10},{10,8},{9,1... | collective-permute-start | bytes 1572872 | tf_op jit(solution)/shard_map/branch_rows/ppermute | solution.py:30
  360.7 16.7 %collective-permute-start.92 = (bf16[144,2048]{1,0:T(8,128)(2,1)}, bf16[144,2048]{1,0:T(8,128)(2,1)}, u32[]{:S(2)}, u32[]{:S(2)}) collective-permute-start(bf16[144,2048]{1,0:T(8,128)(2,1)} %get-tuple-element.237), channel_id=1, source_target_pairs={{0,4},{4,0},{1,5},{5,1},{2,6},{6,2},{3,7},{7,3},{8,12},{12,8},{9,1... | collective-permute-start | bytes 1769480 | tf_op jit(solution)/shard_map/branch_rows/ppermute | solution.py:30
  365.0 41.8 %collective-permute-start.87 = (bf16[128,2048]{1,0:T(8,128)(2,1)}, bf16[128,2048]{1,0:T(8,128)(2,1)}, u32[]{:S(2)}, u32[]{:S(2)}) collective-permute-start(bf16[128,2048]{1,0:T(8,128)(2,1)} %collective-permute-done.80.refs_0_), channel_id=1, source_target_pairs={{0,1},{1,0},{2,3},{3,2},{4,5},{5,4},{6,7},{7,6},{8,9},{9,8},{10,11... | collective-permute-start | bytes 1572872 | tf_op jit(solution)/shard_map/branch_rows/ppermute | solution.py:30
  386.0 22.6 %collective-permute-start.88 = (bf16[128,2048]{1,0:T(8,128)(2,1)}, bf16[128,2048]{1,0:T(8,128)(2,1)}, u32[]{:S(2)}, u32[]{:S(2)}) collective-permute-start(bf16[128,2048]{1,0:T(8,128)(2,1)} %collective-permute-done.83.refs_1_), channel_id=1, source_target_pairs={{0,1},{1,0},{2,3},{3,2},{4,5},{5,4},{6,7},{7,6},{8,9},{9,8},{10,11... | collective-permute-start | bytes 1572872 | tf_op jit(solution)/shard_map/branch_rows/ppermute | solution.py:30
  392.4 16.5 %collective-permute-start.89 = (bf16[128,2048]{1,0:T(8,128)(2,1)}, bf16[128,2048]{1,0:T(8,128)(2,1)}, u32[]{:S(2)}, u32[]{:S(2)}) collective-permute-start(bf16[128,2048]{1,0:T(8,128)(2,1)} %collective-permute-done.86.refs_2_), channel_id=1, source_target_pairs={{0,1},{1,0},{2,3},{3,2},{4,5},{5,4},{6,7},{7,6},{8,9},{9,8},{10,11... | collective-permute-start | bytes 1572872 | tf_op jit(solution)/shard_map/branch_rows/ppermute | solution.py:30
  404.8 37.1 %collective-permute-start.98 = (bf16[128,2048]{1,0:T(8,128)(2,1)}, bf16[128,2048]{1,0:T(8,128)(2,1)S(1)}, u32[]{:S(2)}, u32[]{:S(2)}) collective-permute-start(bf16[128,2048]{1,0:T(8,128)(2,1)} %add_convert_fusion.16), channel_id=1, source_target_pairs={{0,4},{4,0},{1,5},{5,1},{2,6},{6,2},{3,7},{7,3},{8,12},{12,8},{9,1... | collective-permute-start | bytes 1572872 | tf_op jit(solution)/shard_map/unit_weight_sums/ppermute | solution.py:30
  405.7 36.3 %collective-permute-start.99 = (bf16[128,2048]{1,0:T(8,128)(2,1)}, bf16[128,2048]{1,0:T(8,128)(2,1)}, u32[]{:S(2)}, u32[]{:S(2)}) collective-permute-start(bf16[128,2048]{1,0:T(8,128)(2,1)} %add_convert_fusion.15), channel_id=1, source_target_pairs={{0,2},{2,0},{1,3},{3,1},{4,6},{6,4},{5,7},{7,5},{8,10},{10,8},{9,1... | collective-permute-start | bytes 1572872 | tf_op jit(solution)/shard_map/unit_weight_sums/ppermute | solution.py:30
  406.8 35.2 %collective-permute-start.100 = (bf16[128,2048]{1,0:T(8,128)(2,1)}, bf16[128,2048]{1,0:T(8,128)(2,1)S(1)}, u32[]{:S(2)}, u32[]{:S(2)}) collective-permute-start(bf16[128,2048]{1,0:T(8,128)(2,1)} %add_convert_fusion.14), channel_id=1, source_target_pairs={{0,4},{4,0},{1,5},{5,1},{2,6},{6,2},{3,7},{7,3},{8,12},{12,8},{9,1... | collective-permute-start | bytes 1572872 | tf_op jit(solution)/shard_map/unit_weight_sums/ppermute | solution.py:30
  408.5 35.0 %collective-permute-start.101 = (bf16[144,2048]{1,0:T(8,128)(2,1)S(1)}, bf16[144,2048]{1,0:T(8,128)(2,1)S(1)}, u32[]{:S(2)}, u32[]{:S(2)}) collective-permute-start(bf16[144,2048]{1,0:T(8,128)(2,1)S(1)} %add_convert_fusion.2), channel_id=1, source_target_pairs={{0,2},{2,0},{1,3},{3,1},{4,6},{6,4},{5,7},{7,5},{8,10},{10,8},{9,1... | collective-permute-start | bytes 1769480 | tf_op jit(solution)/shard_map/unit_weight_sums/ppermute | solution.py:30
  443.5 36.4 %collective-permute-start.105 = (bf16[2048,256]{1,0:T(8,128)(2,1)S(1)}, bf16[2048,256]{1,0:T(8,128)(2,1)S(1)}, u32[]{:S(2)}, u32[]{:S(2)}) collective-permute-start(bf16[2048,256]{1,0:T(8,128)(2,1)S(1)} %pad_maximum_fusion.3), channel_id=1, source_target_pairs={{0,2},{2,0},{1,3},{3,1},{4,6},{6,4},{5,7},{7,5},{8,10},{10,8},{9,1... | collective-permute-start | bytes 3145736 | tf_op jit(solution)/shard_map/normed_sum/ppermute | solution.py:30
  443.5 36.6 %collective-permute-start.104 = (bf16[2048,256]{1,0:T(8,128)(2,1)S(1)}, bf16[2048,256]{1,0:T(8,128)(2,1)S(1)}, u32[]{:S(2)}, u32[]{:S(2)}) collective-permute-start(bf16[2048,256]{1,0:T(8,128)(2,1)S(1)} %pad_maximum_fusion.2), channel_id=1, source_target_pairs={{0,4},{4,0},{1,5},{5,1},{2,6},{6,2},{3,7},{7,3},{8,12},{12,8},{9,1... | collective-permute-start | bytes 3145736 | tf_op jit(solution)/shard_map/normed_sum/ppermute | solution.py:30
  484.1 17.0 %collective-permute-start.106 = (bf16[128,2048]{1,0:T(8,128)(2,1)S(1)}, bf16[128,2048]{1,0:T(8,128)(2,1)S(1)}, u32[]{:S(2)}, u32[]{:S(2)}) collective-permute-start(bf16[128,2048]{1,0:T(8,128)(2,1)S(1)} %convolution_convert_fusion.7), channel_id=1, source_target_pairs={{0,1},{1,0},{2,3},{3,2},{4,5},{5,4},{6,7},{7,6},{8,9},{9,8},{10,11... | collective-permute-start | bytes 1572872 | tf_op jit(solution)/shard_map/normed_sum/ppermute | solution.py:30
  498.9 21.5 %collective-permute-start.116 = (bf16[512,512]{0,1:T(8,128)(2,1)}, bf16[512,512]{0,1:T(8,128)(2,1)}, u32[]{:S(2)}, u32[]{:S(2)}) collective-permute-start(bf16[512,512]{0,1:T(8,128)(2,1)} %pad_maximum_fusion.11), channel_id=1, source_target_pairs={{0,2},{2,0},{1,3},{3,1},{4,6},{6,4},{5,7},{7,5},{8,10},{10,8},{9,1... | collective-permute-start | bytes 1572872 | tf_op jit(solution)/shard_map/shared_sum/ppermute | solution.py:30
  499.3 21.2 %collective-permute-start.115 = (bf16[512,512]{0,1:T(8,128)(2,1)}, bf16[512,512]{0,1:T(8,128)(2,1)}, u32[]{:S(2)}, u32[]{:S(2)}) collective-permute-start(bf16[512,512]{0,1:T(8,128)(2,1)} %pad_maximum_fusion.10), channel_id=1, source_target_pairs={{0,4},{4,0},{1,5},{5,1},{2,6},{6,2},{3,7},{7,3},{8,12},{12,8},{9,1... | collective-permute-start | bytes 1572872 | tf_op jit(solution)/shard_map/shared_sum/ppermute | solution.py:30
  535.8 22.1 %collective-permute-start.118 = (bf16[128,2048]{1,0:T(8,128)(2,1)S(1)}, bf16[128,2048]{1,0:T(8,128)(2,1)S(1)}, u32[]{:S(2)}, u32[]{:S(2)}) collective-permute-start(bf16[128,2048]{1,0:T(8,128)(2,1)S(1)} %add_convert_fusion.9), channel_id=1, source_target_pairs={{0,8},{8,16},{16,24},{24,0},{1,9},{9,17},{17,25},{25,1},{2,10},{10... | collective-permute-start | bytes 1572872 | tf_op jit(solution)/shard_map/shared_sum/ppermute | solution.py:30
  535.9 19.3 %collective-permute-start.121 = (bf16[256,512]{0,1:T(8,128)(2,1)S(1)}, bf16[256,512]{0,1:T(8,128)(2,1)S(1)}, u32[]{:S(2)}, u32[]{:S(2)}) collective-permute-start(bf16[256,512]{0,1:T(8,128)(2,1)S(1)} %get-tuple-element.286), channel_id=1, source_target_pairs={{0,4},{4,0},{1,5},{5,1},{2,6},{6,2},{3,7},{7,3},{8,12},{12,8},{9,1... | collective-permute-start | bytes 786440 | tf_op jit(solution)/shard_map/shared_sum/ppermute | solution.py:30
  536.3 19.8 %collective-permute-start.122 = (bf16[256,512]{0,1:T(8,128)(2,1)S(1)}, bf16[256,512]{0,1:T(8,128)(2,1)S(1)}, u32[]{:S(2)}, u32[]{:S(2)}) collective-permute-start(bf16[256,512]{0,1:T(8,128)(2,1)S(1)} %get-tuple-element.288), channel_id=1, source_target_pairs={{0,2},{2,0},{1,3},{3,1},{4,6},{6,4},{5,7},{7,5},{8,10},{10,8},{9,1... | collective-permute-start | bytes 786440 | tf_op jit(solution)/shard_map/shared_sum/ppermute | solution.py:30
  549.3 20.9 %collective-permute-start.128 = (bf16[256,512]{0,1:T(8,128)(2,1)S(1)}, bf16[256,512]{0,1:T(8,128)(2,1)S(1)}, u32[]{:S(2)}, u32[]{:S(2)}) collective-permute-start(bf16[256,512]{0,1:T(8,128)(2,1)S(1)} %broadcast_select_fusion.1), channel_id=1, source_target_pairs={{0,20},{1,0},{2,28},{3,8},{4,4},{5,16},{6,12},{7,24},{8,29},{9,9},... | collective-permute-start | bytes 786440 | tf_op jit(solution)/shard_map/weight_layout/ppermute | solution.py:843
  559.2 28.0 %collective-permute-start.123 = (bf16[256,512]{0,1:T(8,128)(2,1)}, bf16[256,512]{0,1:T(8,128)(2,1)S(1)}, u32[]{:S(2)}, u32[]{:S(2)}) collective-permute-start(bf16[256,512]{0,1:T(8,128)(2,1)} %get-tuple-element.450), channel_id=1, source_target_pairs={{0,0},{1,20},{2,8},{3,28},{4,16},{5,4},{6,24},{7,12},{8,9},{9,29},... | collective-permute-start | bytes 786440 | tf_op jit(solution)/shard_map/weight_layout/ppermute | solution.py:843
  560.8 26.4 %collective-permute-start.124 = (bf16[256,512]{0,1:T(8,128)(2,1)}, bf16[256,512]{0,1:T(8,128)(2,1)}, u32[]{:S(2)}, u32[]{:S(2)}) collective-permute-start(bf16[256,512]{0,1:T(8,128)(2,1)} %get-tuple-element.451), channel_id=1, source_target_pairs={{0,20},{1,0},{2,28},{3,8},{4,4},{5,16},{6,12},{7,24},{8,29},{9,9},... | collective-permute-start | bytes 786440 | tf_op jit(solution)/shard_map/weight_layout/ppermute | solution.py:843
  (167 other events, 1832.5 us)
Sparse Core Ops, SparseCore 0:
  395.9 48.2 reduce-scatter.1

commit v7 on v6

--- a/solution.py
+++ b/solution.py
@@ -714,11 +714,11 @@
     with jax.named_scope("grad_output_rows"):
         grad_blocks += ticks.tick((grad_blocks[-1], 1), (grad_output, -1))
     mixed, lse = attention_forward(scalars, queries, keys_all, values_all)
-    with jax.named_scope("grad_output_rows"):
-        group_grad = ticks.join_cores(grad_blocks)
     with jax.named_scope("attention_sum"):
         attention_sum = RowSum(ticks, lambda v: matmul(v, weight_out), [mixed], rows_local)
         residual = state_rows + attention_sum.finish()
+    with jax.named_scope("grad_output_rows"):
+        group_grad = ticks.join_cores(list(after(tuple(grad_blocks), attention_sum.sent)))
     plain_two, factor_two, normed_two = normalize(residual, ffn_gain)
     with jax.named_scope("normed_two_rows"):
         group_in = ticks.gather_rows(normed_two.astype(LOW))

time: 606 us -> 600 us (0.990)
    unnamed x229 -> x227, local copies, waits for them, and re-layouts: 26.7 us -> 23.9 us
  transfers between devices with their start and end apart: 131 -> 131, of which waited for: 52 -> 52; matrix products, arithmetic and copies ran while one was open for 24% -> 24% of each run, Pallas kernels for 8% -> 7%
where the time goes in v7:
time: 600 us; the launch traced here: 591 us
  waiting for transfers between devices  249 us (42%)
  starting transfers between devices  111 us (18%)
  matrix products  68.5 us (11%)
  local copies, waits for them, and re-layouts  50.6 us (8%)
  other arithmetic  47.8 us (8%)
  Pallas kernels  44 us (7%)
  between operations  20.1 us (3%)
    ppermute x125, waiting for transfers between devices, hop(): lax.ppermute(values, axis, [(i, (i + steps) % size) for i in range(size)])  245 us
    ppermute x125, starting transfers between devices, hop(): lax.ppermute(values, axis, [(i, (i + steps) % size) for i in range(size)])  86.8 us
    pallas_call x1, Pallas kernels, attention_backward(): pl.pallas_call(backward_kernel, out_shape=(jax.ShapeDtypeStruct(own_shape...  26.9 us
    dot_general x28, matrix products, matmul(): return jnp.dot(left_side, right_side, preferred_element_type=HIGH)  25.6 us
    dot_general x27, matrix products, matmul_right_t(): lax.dot_general(left_side, right_side, (((1,), (1,)), ((), ())), preferre...  25.6 us
    unnamed x227, local copies, waits for them, and re-layouts  23.9 us
    ppermute x4, starting transfers between devices, layout(): got = [lax.ppermute(sent[flip], ALL, to_layout[flip]) for flip in range(2)]  17.7 us
    dot_general x6, matrix products, matmul_left_t(): lax.dot_general(left_side, right_side, (((0,), (0,)), ((), ())), preferre...  17.3 us
  transfers between devices with their start and end apart: 131, of which 52 were waited for; matrix products, arithmetic and copies ran while one was open for 24% of the time, Pallas kernels for 7%

profile of v7, /device:TPU:0, one launch (start us, length us, event | category | flops | bytes accessed | tf_op | source)
XLA Modules:
  0.0 590.9 jit_solution(11347731814174737275)
XLA Ops:
  9.4 5.1 collective-permute-start.2
  23.6 7.6 %collective-permute-done.1 = bf16[64,1536]{1,0:T(8,128)(2,1)S(1)} collective-permute-done((bf16[64,1536]{1,0:T(8,128)(2,1)S(1)}, bf16[64,1536]{1,0:T(8,128)(2,1)S(1)}, u32[]{:S(2)}, u32[]{:S(2)}) %collective-permute-start.1) | collective-permute-done | bytes 196640 | tf_op jit(solution)/shard_map/weight_columns/ppermute | solution.py:30
  38.9 3.2 collective-permute-done.10
  43.2 9.4 %collective-permute-done.7.refs_1_ = bf16[4,64,768]{2,1,0:T(8,128)(2,1)S(1)} collective-permute-done((bf16[4,64,768]{2,1,0:T(8,128)(2,1)S(1)}, bf16[4,64,768]{2,1,0:T(8,128)(2,1)S(1)}, u32[]{:S(2)}, u32[]{:S(2)}) %collective-permute-start.7) | collective-permute-done | bytes 393248 | tf_op jit(solution)/shard_map/shared_rows/ppermute | solution.py:30
  60.4 6.4 %collective-permute-done.19 = bf16[32,2048]{1,0:T(8,128)(2,1)S(1)} collective-permute-done((bf16[32,2048]{1,0:T(8,128)(2,1)S(1)}, bf16[32,2048]{1,0:T(8,128)(2,1)S(1)}, u32[]{:S(2)}, u32[]{:S(2)}) %collective-permute-start.19) | collective-permute-done | bytes 131104 | tf_op jit(solution)/shard_map/shared_rows/ppermute | solution.py:30
  77.4 6.9 %collective-permute-done.22.refs_7_ = bf16[4,64,768]{2,1,0:T(8,128)(2,1)S(1)} collective-permute-done((bf16[4,64,768]{2,1,0:T(8,128)(2,1)S(1)}, bf16[4,64,768]{2,1,0:T(8,128)(2,1)S(1)}, u32[]{:S(2)}, u32[]{:S(2)}) %collective-permute-start.22) | collective-permute-done | bytes 393248 | tf_op jit(solution)/shard_map/shared_rows/ppermute | solution.py:30
  95.7 8.1 %collective-permute-done.20 = bf16[128,2048]{1,0:T(8,128)(2,1)S(1)} collective-permute-done((bf16[128,2048]{1,0:T(8,128)(2,1)S(1)}, bf16[128,2048]{1,0:T(8,128)(2,1)S(1)}, u32[]{:S(2)}, u32[]{:S(2)}) %collective-permute-start.20) | collective-permute-done | bytes 524320 | tf_op jit(solution)/shard_map/normed_rows/ppermute | solution.py:30
  109.7 9.4 %collective-permute-done.23 = bf16[128,2048]{1,0:T(8,128)(2,1)S(1)} collective-permute-done((bf16[128,2048]{1,0:T(8,128)(2,1)S(1)}, bf16[128,2048]{1,0:T(8,128)(2,1)S(1)}, u32[]{:S(2)}, u32[]{:S(2)}) %collective-permute-start.23) | collective-permute-done | bytes 524320 | tf_op jit(solution)/shard_map/normed_rows/ppermute | solution.py:30
  122.9 10.8 %collective-permute-done.31 = bf16[128,2048]{1,0:T(8,128)(2,1)} collective-permute-done((bf16[128,2048]{1,0:T(8,128)(2,1)S(1)}, bf16[128,2048]{1,0:T(8,128)(2,1)}, u32[]{:S(2)}, u32[]{:S(2)}) %collective-permute-start.31) | collective-permute-done | bytes 524320 | tf_op jit(solution)/shard_map/normed_rows/ppermute | solution.py:30
  139.7 5.9 collective-permute-done.38
  147.2 5.4 collective-permute-done.41
  158.1 15.0 %attention_forward.1 = (bf16[2,512,256]{2,1,0:T(8,128)(2,1)}, f32[2,8,1024]{2,1,0:T(8,128)}) custom-call(s32[16]{0:T(128)} %select_reduce_fusion.place_ref, s32[4]{0:T(128)} %bitcast.223, s32[1]{0:T(128)} %bitcast.1.core_ref, bf16[2,512,256]{2,1,0:T(8,128)(2,1)} %bitcast.221, bf16[4,2,512,256]{3,2,1,0:T(8,128)(2,1)} %bitcast.190, ...), custom_call_target="tpu_custom_call" | custom-call | flops 21474836480 | bytes 4194304 | tf_op jit(solution)/shard_map/attention_forward/pallas_call | solution.py:488
  174.9 3.4 collective-permute-start.50
  178.2 4.4 collective-permute-start.51
  184.6 6.2 %collective-permute-done.50 = bf16[128,2048]{1,0:T(8,128)(2,1)S(1)} collective-permute-done((bf16[128,2048]{1,0:T(8,128)(2,1)S(1)}, bf16[128,2048]{1,0:T(8,128)(2,1)S(1)}, u32[]{:S(2)}, u32[]{:S(2)}) %collective-permute-start.50) | collective-permute-done | bytes 524320 | tf_op jit(solution)/shard_map/attention_sum/ppermute | solution.py:30
  190.8 4.1 collective-permute-done.51
  194.9 3.6 collective-permute-done.45
  203.3 11.7 %collective-permute-done.49 = bf16[128,2048]{1,0:T(8,128)(2,1)S(1)} collective-permute-done((bf16[128,2048]{1,0:T(8,128)(2,1)S(1)}, bf16[128,2048]{1,0:T(8,128)(2,1)S(1)}, u32[]{:S(2)}, u32[]{:S(2)}) %collective-permute-start.49) | collective-permute-done | bytes 524320 | tf_op jit(solution)/shard_map/attention_sum/ppermute | solution.py:30
  222.3 6.3 %collective-permute-done.53 = bf16[128,2048]{1,0:T(8,128)(2,1)S(1)} collective-permute-done((bf16[128,2048]{1,0:T(8,128)(2,1)S(1)}, bf16[128,2048]{1,0:T(8,128)(2,1)S(1)}, u32[]{:S(2)}, u32[]{:S(2)}) %collective-permute-start.53) | collective-permute-done | bytes 524320 | tf_op jit(solution)/shard_map/attention_sum/ppermute | solution.py:30
  233.5 13.0 %collective-permute-done.56 = bf16[128,2048]{1,0:T(8,128)(2,1)S(1)} collective-permute-done((bf16[128,2048]{1,0:T(8,128)(2,1)S(1)}, bf16[128,2048]{1,0:T(8,128)(2,1)S(1)}, u32[]{:S(2)}, u32[]{:S(2)}) %collective-permute-start.56) | collective-permute-done | bytes 524320 | tf_op jit(solution)/shard_map/normed_two_rows/ppermute | solution.py:30
  248.7 12.7 %collective-permute-done.59 = bf16[128,2048]{1,0:T(8,128)(2,1)S(1)} collective-permute-done((bf16[128,2048]{1,0:T(8,128)(2,1)S(1)}, bf16[128,2048]{1,0:T(8,128)(2,1)S(1)}, u32[]{:S(2)}, u32[]{:S(2)}) %collective-permute-start.59) | collective-permute-done | bytes 524320 | tf_op jit(solution)/shard_map/normed_two_rows/ppermute | solution.py:30
  262.4 13.4 %collective-permute-done.62 = bf16[128,2048]{1,0:T(8,128)(2,1)S(1)} collective-permute-done((bf16[128,2048]{1,0:T(8,128)(2,1)S(1)}, bf16[128,2048]{1,0:T(8,128)(2,1)S(1)}, u32[]{:S(2)}, u32[]{:S(2)}) %collective-permute-start.62) | collective-permute-done | bytes 524320 | tf_op jit(solution)/shard_map/normed_two_rows/ppermute | solution.py:30
  277.9 3.2 fusion.226
  281.1 3.2 fusion.225
  284.3 4.3 multiply_convert_fusion
  292.7 3.4 convolution_convert_fusion.3
  300.9 7.5 %collective-permute-done.75 = bf16[128,2048]{1,0:T(8,128)(2,1)S(1)} collective-permute-done((bf16[128,2048]{1,0:T(8,128)(2,1)S(1)}, bf16[128,2048]{1,0:T(8,128)(2,1)S(1)}, u32[]{:S(2)}, u32[]{:S(2)}) %collective-permute-start.75) | collective-permute-done | bytes 524320 | tf_op jit(solution)/shard_map/ffn_grad_sum/ppermute | solution.py:30
  308.6 3.4 convolution_convert_fusion.2
  317.9 5.6 collective-permute-done.77
  323.7 3.4 convolution_convert_fusion.1
  347.4 8.4 %collective-permute-done.80.refs_0_ = bf16[128,2048]{1,0:T(8,128)(2,1)} collective-permute-done((bf16[128,2048]{1,0:T(8,128)(2,1)S(1)}, bf16[128,2048]{1,0:T(8,128)(2,1)}, u32[]{:S(2)}, u32[]{:S(2)}) %collective-permute-start.80) | collective-permute-done | bytes 524320 | tf_op jit(solution)/shard_map/branch_rows/ppermute | solution.py:30
  360.9 12.0 %collective-permute-done.83.refs_1_ = bf16[128,2048]{1,0:T(8,128)(2,1)} collective-permute-done((bf16[128,2048]{1,0:T(8,128)(2,1)}, bf16[128,2048]{1,0:T(8,128)(2,1)}, u32[]{:S(2)}, u32[]{:S(2)}) %collective-permute-start.83) | collective-permute-done | bytes 524320 | tf_op jit(solution)/shard_map/branch_rows/ppermute | solution.py:30
  374.4 6.9 %convolution_convert_fusion = bf16[1024,2048]{1,0:T(8,128)(2,1)} fusion(bf16[1024,704]{0,1:T(8,128)(2,1)S(1)} %bitcast_select_fusion, bf16[704,2048]{1,0:T(8,128)(2,1)} %copy-done.65), kind=kOutput, calls=%fused_computation.19 | convolution fusion | flops 2954887168 | bytes 8519680 | tf_op jit(solution)/shard_map/branch_rows/dot_general | solution.py:266
  381.3 6.2 %collective-permute-done.86.refs_2_ = bf16[128,2048]{1,0:T(8,128)(2,1)} collective-permute-done((bf16[128,2048]{1,0:T(8,128)(2,1)}, bf16[128,2048]{1,0:T(8,128)(2,1)}, u32[]{:S(2)}, u32[]{:S(2)}) %collective-permute-start.86) | collective-permute-done | bytes 524320 | tf_op jit(solution)/shard_map/branch_rows/ppermute | solution.py:30
  391.9 8.8 %collective-permute-done.94 = bf16[144,2048]{1,0:T(8,128)(2,1)S(1)} collective-permute-done((bf16[144,2048]{1,0:T(8,128)(2,1)S(1)}, bf16[144,2048]{1,0:T(8,128)(2,1)S(1)}, u32[]{:S(2)}, u32[]{:S(2)}) %collective-permute-start.94) | collective-permute-done | bytes 589856 | tf_op jit(solution)/shard_map/branch_rows/ppermute | solution.py:30
  404.8 26.9 %attention_backward.1 = (bf16[2,512,256]{2,1,0:T(8,128)(2,1)}, bf16[4,2,512,256]{3,2,1,0:T(8,128)(2,1)}, bf16[4,2,512,256]{3,2,1,0:T(8,128)(2,1)}) custom-call(s32[16]{0:T(128)} %select_reduce_fusion.place_ref, s32[4]{0:T(128)} %bitcast.224, s32[1]{0:T(128)} %bitcast.1.core_ref, bf16[2,512,256]{2,1,0:T(8,128)(2,1)} %bitcast.222, ...), custom_call_target="tpu_custom_call" | custom-call | flops 128849018880 | bytes 8388608 | tf_op jit(solution)/shard_map/attention_backward/pallas_call | solution.py:532
  437.1 4.9 collective-permute-start.105
  442.1 5.4 collective-permute-start.104
  460.3 3.2 collective-permute-done.97
  479.2 10.7 %collective-permute-done.108 = bf16[1024,256]{1,0:T(8,128)(2,1)S(1)} collective-permute-done((bf16[1024,256]{1,0:T(8,128)(2,1)S(1)}, bf16[1024,256]{1,0:T(8,128)(2,1)S(1)}, u32[]{:S(2)}, u32[]{:S(2)}) %collective-permute-start.108) | collective-permute-done | bytes 524320 | tf_op jit(solution)/shard_map/normed_sum/ppermute | solution.py:30
  500.0 4.6 convolution_convert_fusion.4
  507.6 3.0 fusion.35
  520.4 10.7 %collective-permute-done.114 = bf16[128,2048]{1,0:T(8,128)(2,1)S(1)} collective-permute-done((bf16[128,2048]{1,0:T(8,128)(2,1)S(1)}, bf16[128,2048]{1,0:T(8,128)(2,1)S(1)}, u32[]{:S(2)}, u32[]{:S(2)}) %collective-permute-start.114) | collective-permute-done | bytes 524320 | tf_op jit(solution)/shard_map/shared_sum/ppermute | solution.py:30
  537.2 7.2 %collective-permute-done.126 = bf16[256,512]{0,1:T(8,128)(2,1)S(1)} collective-permute-done((bf16[256,512]{0,1:T(8,128)(2,1)S(1)}, bf16[256,512]{0,1:T(8,128)(2,1)S(1)}, u32[]{:S(2)}, u32[]{:S(2)}) %collective-permute-start.126) | collective-permute-done | bytes 262176 | tf_op jit(solution)/shard_map/shared_sum/ppermute | solution.py:30
  544.7 5.3 collective-permute-start.128
  555.6 10.0 %collective-permute-start.124 = (bf16[256,512]{0,1:T(8,128)(2,1)}, bf16[256,512]{0,1:T(8,128)(2,1)}, u32[]{:S(2)}, u32[]{:S(2)}) collective-permute-start(bf16[256,512]{0,1:T(8,128)(2,1)} %get-tuple-element.459), channel_id=1, source_target_pairs={{0,20},{1,0},{2,28},{3,8},{4,4},{5,16},{6,12},{7,24},{8,29},{9,9},... | collective-permute-start | bytes 786440 | tf_op jit(solution)/shard_map/weight_layout/ppermute | solution.py:843
  566.7 6.2 %all-to-all-start = ((f32[32,1,192]{2,1,0:T(1,128)}), f32[32,1,192]{2,1,0:T(1,128)S(1)}, u32[]{:S(2)}, u32[]{:S(2)}) async-start(f32[32,1,192]{2,1,0:T(1,128)} %all_to_all.8), calls=%async_computation.1 | async-start | bytes 65536 | tf_op jit(solution)/shard_map/all_to_all | solution.py:917
  576.1 4.0 all-to-all-done
  (663 shorter events, 220.6 us)
Async XLA Ops:
  7.2 492.1 %reduce-scatter.2.cloned.1.call-start = ((), (), s32[]{:S(2)}) async-start(), calls=%async_computation.2 | async-start | bytes 4718592 | tf_op jit(solution)/shard_map/ffn_sum/reduce_scatter | solution.py:802
  14.6 16.7 %collective-permute-start.1 = (bf16[64,1536]{1,0:T(8,128)(2,1)S(1)}, bf16[64,1536]{1,0:T(8,128)(2,1)S(1)}, u32[]{:S(2)}, u32[]{:S(2)}) collective-permute-start(bf16[64,1536]{1,0:T(8,128)(2,1)S(1)} %pad_maximum_fusion.20), channel_id=1, source_target_pairs={{0,16},{8,24},{16,0},{24,8},{1,17},{9,25},{17,1},{25,9},{2,18},{10... | collective-permute-start | bytes 589832 | tf_op jit(solution)/shard_map/weight_columns/ppermute | solution.py:30
  14.7 16.6 %collective-permute-start = (bf16[64,1536]{1,0:T(8,128)(2,1)S(1)}, bf16[64,1536]{1,0:T(8,128)(2,1)S(1)}, u32[]{:S(2)}, u32[]{:S(2)}) collective-permute-start(bf16[64,1536]{1,0:T(8,128)(2,1)S(1)} %pad_maximum_fusion.19), channel_id=1, source_target_pairs={{0,8},{8,16},{16,24},{24,0},{1,9},{9,17},{17,25},{25,1},{2,10},{10... | collective-permute-start | bytes 589832 | tf_op jit(solution)/shard_map/weight_columns/ppermute | solution.py:30
  17.7 17.1 %collective-permute-start.5 = (bf16[64,768]{1,0:T(8,128)(2,1)S(1)}, bf16[64,768]{1,0:T(8,128)(2,1)S(1)}, u32[]{:S(2)}, u32[]{:S(2)}) collective-permute-start(bf16[64,768]{1,0:T(8,128)(2,1)S(1)} %pad_maximum_fusion.22), channel_id=1, source_target_pairs={{0,1},{1,0},{2,3},{3,2},{4,5},{5,4},{6,7},{7,6},{8,9},{9,8},{10,11... | collective-permute-start | bytes 294920 | tf_op jit(solution)/shard_map/weight_columns/ppermute | solution.py:30
  19.0 71.2 %collective-permute-start.27 = (bf16[128,2048]{1,0:T(8,128)(2,1)}, bf16[128,2048]{1,0:T(8,128)(2,1)}, u32[]{:S(2)}, u32[]{:S(2)}) collective-permute-start(bf16[128,2048]{1,0:T(8,128)(2,1)} %fusion.23), channel_id=1, source_target_pairs={{0,1},{1,0},{2,3},{3,2},{4,5},{5,4},{6,7},{7,6},{8,9},{9,8},{10,11... | collective-permute-start | bytes 1572872 | tf_op jit(solution)/shard_map/shared_rows/ppermute | solution.py:30
  37.9 17.7 %collective-permute-start.3 = (bf16[128,2048]{1,0:T(8,128)(2,1)}, bf16[128,2048]{1,0:T(8,128)(2,1)}, u32[]{:S(2)}, u32[]{:S(2)}) collective-permute-start(bf16[128,2048]{1,0:T(8,128)(2,1)} %fusion.23), channel_id=1, source_target_pairs={{0,8},{8,16},{16,24},{24,0},{1,9},{9,17},{17,25},{25,1},{2,10},{10... | collective-permute-start | bytes 1572872 | tf_op jit(solution)/shard_map/shared_rows/ppermute | solution.py:30
  54.5 18.4 %collective-permute-start.16 = (bf16[4,64,768]{2,1,0:T(8,128)(2,1)S(1)}, bf16[4,64,768]{2,1,0:T(8,128)(2,1)S(1)}, u32[]{:S(2)}, u32[]{:S(2)}) collective-permute-start(bf16[4,64,768]{2,1,0:T(8,128)(2,1)S(1)} %pad_maximum_fusion.18.refs_4_), channel_id=1, source_target_pairs={{0,2},{2,0},{1,3},{3,1},{4,6},{6,4},{5,7},{7,5},{8,10},{10,8},{9,1... | collective-permute-start | bytes 1179656 | tf_op jit(solution)/shard_map/shared_rows/ppermute | solution.py:30
  55.1 17.9 %collective-permute-start.17 = (bf16[4,64,768]{2,1,0:T(8,128)(2,1)S(1)}, bf16[4,64,768]{2,1,0:T(8,128)(2,1)S(1)}, u32[]{:S(2)}, u32[]{:S(2)}) collective-permute-start(bf16[4,64,768]{2,1,0:T(8,128)(2,1)S(1)} %pad_maximum_fusion.18.refs_4_), channel_id=1, source_target_pairs={{0,4},{4,0},{1,5},{5,1},{2,6},{6,2},{3,7},{7,3},{8,12},{12,8},{9,1... | collective-permute-start | bytes 1179656 | tf_op jit(solution)/shard_map/shared_rows/ppermute | solution.py:30
  71.2 16.1 %collective-permute-start.13 = (bf16[128,2048]{1,0:T(8,128)(2,1)}, bf16[128,2048]{1,0:T(8,128)(2,1)S(1)}, u32[]{:S(2)}, u32[]{:S(2)}) collective-permute-start(bf16[128,2048]{1,0:T(8,128)(2,1)} %collective-permute-done.4), channel_id=1, source_target_pairs={{0,8},{8,16},{16,24},{24,0},{1,9},{9,17},{17,25},{25,1},{2,10},{10... | collective-permute-start | bytes 1572872 | tf_op jit(solution)/shard_map/shared_rows/ppermute | solution.py:30
  76.2 78.6 %collective-permute-start.35 = (bf16[128,2048]{1,0:T(8,128)(2,1)}, bf16[128,2048]{1,0:T(8,128)(2,1)}, u32[]{:S(2)}, u32[]{:S(2)}) collective-permute-start(bf16[128,2048]{1,0:T(8,128)(2,1)} %fusion.30), channel_id=1, source_target_pairs={{0,1},{1,0},{2,3},{3,2},{4,5},{5,4},{6,7},{7,6},{8,9},{9,8},{10,11... | collective-permute-start | bytes 1572872 | tf_op jit(solution)/shard_map/normed_rows/ppermute | solution.py:30
  87.5 16.2 %collective-permute-start.20 = (bf16[128,2048]{1,0:T(8,128)(2,1)S(1)}, bf16[128,2048]{1,0:T(8,128)(2,1)S(1)}, u32[]{:S(2)}, u32[]{:S(2)}) collective-permute-start(bf16[128,2048]{1,0:T(8,128)(2,1)S(1)} %copy-done.49), channel_id=1, source_target_pairs={{0,8},{8,16},{16,24},{24,0},{1,9},{9,17},{17,25},{25,1},{2,10},{10... | collective-permute-start | bytes 1572872 | tf_op jit(solution)/shard_map/normed_rows/ppermute | solution.py:30
  136.5 16.0 %collective-permute-start.41 = (bf16[128,2048]{1,0:T(8,128)(2,1)S(1)}, bf16[128,2048]{1,0:T(8,128)(2,1)}, u32[]{:S(2)}, u32[]{:S(2)}) collective-permute-start(bf16[128,2048]{1,0:T(8,128)(2,1)S(1)} %copy-done.31), channel_id=1, source_target_pairs={{0,8},{8,16},{16,24},{24,0},{1,9},{9,17},{17,25},{25,1},{2,10},{10... | collective-permute-start | bytes 1572872 | tf_op jit(solution)/shard_map/grad_output_rows/ppermute | solution.py:30
  136.7 15.9 %collective-permute-start.34 = (bf16[128,2048]{1,0:T(8,128)(2,1)}, bf16[128,2048]{1,0:T(8,128)(2,1)S(1)}, u32[]{:S(2)}, u32[]{:S(2)}) collective-permute-start(bf16[128,2048]{1,0:T(8,128)(2,1)} %collective-permute-done.31), channel_id=1, source_target_pairs={{0,1},{1,0},{2,3},{3,2},{4,5},{5,4},{6,7},{7,6},{8,9},{9,8},{10,11... | collective-permute-start | bytes 1572872 | tf_op jit(solution)/shard_map/normed_rows/ppermute | solution.py:30
  152.5 22.3 %collective-permute-start.46 = (bf16[128,2048]{1,0:T(8,128)(2,1)S(1)}, bf16[128,2048]{1,0:T(8,128)(2,1)}, u32[]{:S(2)}, u32[]{:S(2)}) collective-permute-start(bf16[128,2048]{1,0:T(8,128)(2,1)S(1)} %get-tuple-element.188), channel_id=1, source_target_pairs={{0,2},{2,0},{1,3},{3,1},{4,6},{6,4},{5,7},{7,5},{8,10},{10,8},{9,1... | collective-permute-start | bytes 1572872 | tf_op jit(solution)/shard_map/grad_output_rows/ppermute | solution.py:30
  152.6 22.3 %collective-permute-start.47 = (bf16[128,2048]{1,0:T(8,128)(2,1)S(1)}, bf16[128,2048]{1,0:T(8,128)(2,1)S(1)}, u32[]{:S(2)}, u32[]{:S(2)}) collective-permute-start(bf16[128,2048]{1,0:T(8,128)(2,1)S(1)} %get-tuple-element.188), channel_id=1, source_target_pairs={{0,4},{4,0},{1,5},{5,1},{2,6},{6,2},{3,7},{7,3},{8,12},{12,8},{9,1... | collective-permute-start | bytes 1572872 | tf_op jit(solution)/shard_map/grad_output_rows/ppermute | solution.py:30
  152.6 22.3 %collective-permute-start.43 = (bf16[128,2048]{1,0:T(8,128)(2,1)S(1)}, bf16[128,2048]{1,0:T(8,128)(2,1)}, u32[]{:S(2)}, u32[]{:S(2)}) collective-permute-start(bf16[128,2048]{1,0:T(8,128)(2,1)S(1)} %copy-done.31), channel_id=1, source_target_pairs={{0,24},{8,0},{16,8},{24,16},{1,25},{9,1},{17,9},{25,17},{2,26},{10... | collective-permute-start | bytes 1572872 | tf_op jit(solution)/shard_map/grad_output_rows/ppermute | solution.py:30
  152.6 22.3 %collective-permute-start.42 = (bf16[128,2048]{1,0:T(8,128)(2,1)}, bf16[128,2048]{1,0:T(8,128)(2,1)}, u32[]{:S(2)}, u32[]{:S(2)}) collective-permute-start(bf16[128,2048]{1,0:T(8,128)(2,1)} %collective-permute-done.41), channel_id=1, source_target_pairs={{0,8},{8,16},{16,24},{24,0},{1,9},{9,17},{17,25},{25,1},{2,10},{10... | collective-permute-start | bytes 1572872 | tf_op jit(solution)/shard_map/grad_output_rows/ppermute | solution.py:30
  174.9 15.9 %collective-permute-start.50 = (bf16[128,2048]{1,0:T(8,128)(2,1)S(1)}, bf16[128,2048]{1,0:T(8,128)(2,1)S(1)}, u32[]{:S(2)}, u32[]{:S(2)}) collective-permute-start(bf16[128,2048]{1,0:T(8,128)(2,1)S(1)} %get-tuple-element.192), channel_id=1, source_target_pairs={{0,2},{2,0},{1,3},{3,1},{4,6},{6,4},{5,7},{7,5},{8,10},{10,8},{9,1... | collective-permute-start | bytes 1572872 | tf_op jit(solution)/shard_map/attention_sum/ppermute | solution.py:30
  178.2 16.7 %collective-permute-start.51 = (bf16[128,2048]{1,0:T(8,128)(2,1)S(1)}, bf16[128,2048]{1,0:T(8,128)(2,1)S(1)}, u32[]{:S(2)}, u32[]{:S(2)}) collective-permute-start(bf16[128,2048]{1,0:T(8,128)(2,1)S(1)} %get-tuple-element.192), channel_id=1, source_target_pairs={{0,4},{4,0},{1,5},{5,1},{2,6},{6,2},{3,7},{7,3},{8,12},{12,8},{9,1... | collective-permute-start | bytes 1572872 | tf_op jit(solution)/shard_map/attention_sum/ppermute | solution.py:30
  183.3 16.8 %collective-permute-start.44 = (bf16[128,2048]{1,0:T(8,128)(2,1)S(1)}, bf16[128,2048]{1,0:T(8,128)(2,1)S(1)}, u32[]{:S(2)}, u32[]{:S(2)}) collective-permute-start(bf16[128,2048]{1,0:T(8,128)(2,1)S(1)} %convolution_convert_fusion.13), channel_id=1, source_target_pairs={{0,1},{1,0},{2,3},{3,2},{4,5},{5,4},{6,7},{7,6},{8,9},{9,8},{10,11... | collective-permute-start | bytes 1572872 | tf_op jit(solution)/shard_map/attention_sum/ppermute | solution.py:30
  198.5 16.7 %collective-permute-start.54 = (bf16[128,2048]{1,0:T(8,128)(2,1)S(1)}, bf16[128,2048]{1,0:T(8,128)(2,1)S(1)}, u32[]{:S(2)}, u32[]{:S(2)}) collective-permute-start(bf16[128,2048]{1,0:T(8,128)(2,1)S(1)} %get-tuple-element.196), channel_id=1, source_target_pairs={{0,2},{2,0},{1,3},{3,1},{4,6},{6,4},{5,7},{7,5},{8,10},{10,8},{9,1... | collective-permute-start | bytes 1572872 | tf_op jit(solution)/shard_map/attention_sum/ppermute | solution.py:30
  198.9 16.3 %collective-permute-start.55 = (bf16[128,2048]{1,0:T(8,128)(2,1)S(1)}, bf16[128,2048]{1,0:T(8,128)(2,1)S(1)}, u32[]{:S(2)}, u32[]{:S(2)}) collective-permute-start(bf16[128,2048]{1,0:T(8,128)(2,1)S(1)} %get-tuple-element.196), channel_id=1, source_target_pairs={{0,4},{4,0},{1,5},{5,1},{2,6},{6,2},{3,7},{7,3},{8,12},{12,8},{9,1... | collective-permute-start | bytes 1572872 | tf_op jit(solution)/shard_map/attention_sum/ppermute | solution.py:30
  215.2 16.1 %collective-permute-start.57 = (bf16[144,2048]{1,0:T(8,128)(2,1)S(1)}, bf16[144,2048]{1,0:T(8,128)(2,1)S(1)}, u32[]{:S(2)}, u32[]{:S(2)}) collective-permute-start(bf16[144,2048]{1,0:T(8,128)(2,1)S(1)} %pad_slice_fusion), channel_id=1, source_target_pairs={{0,2},{2,0},{1,3},{3,1},{4,6},{6,4},{5,7},{7,5},{8,10},{10,8},{9,1... | collective-permute-start | bytes 1769480 | tf_op jit(solution)/shard_map/attention_sum/ppermute | solution.py:30
  229.8 48.0 %collective-permute-start.66 = (bf16[128,2048]{1,0:T(8,128)(2,1)S(1)}, bf16[128,2048]{1,0:T(8,128)(2,1)S(1)}, u32[]{:S(2)}, u32[]{:S(2)}) collective-permute-start(bf16[128,2048]{1,0:T(8,128)(2,1)S(1)} %multiply_convert_fusion.3), channel_id=1, source_target_pairs={{0,1},{1,0},{2,3},{3,2},{4,5},{5,4},{6,7},{7,6},{8,9},{9,8},{10,11... | collective-permute-start | bytes 1572872 | tf_op jit(solution)/shard_map/normed_two_rows/ppermute | solution.py:30
  246.5 29.5 %collective-permute-start.63 = (bf16[128,2048]{1,0:T(8,128)(2,1)S(1)}, bf16[128,2048]{1,0:T(8,128)(2,1)S(1)}, u32[]{:S(2)}, u32[]{:S(2)}) collective-permute-start(bf16[128,2048]{1,0:T(8,128)(2,1)S(1)} %collective-permute-done.56), channel_id=1, source_target_pairs={{0,1},{1,0},{2,3},{3,2},{4,5},{5,4},{6,7},{7,6},{8,9},{9,8},{10,11... | collective-permute-start | bytes 1572872 | tf_op jit(solution)/shard_map/normed_two_rows/ppermute | solution.py:30
  292.4 16.0 %collective-permute-start.75 = (bf16[128,2048]{1,0:T(8,128)(2,1)S(1)}, bf16[128,2048]{1,0:T(8,128)(2,1)S(1)}, u32[]{:S(2)}, u32[]{:S(2)}) collective-permute-start(bf16[128,2048]{1,0:T(8,128)(2,1)S(1)} %add_convert_fusion.21), channel_id=1, source_target_pairs={{0,8},{8,16},{16,24},{24,0},{1,9},{9,17},{17,25},{25,1},{2,10},{10... | collective-permute-start | bytes 1572872 | tf_op jit(solution)/shard_map/ffn_grad_sum/ppermute | solution.py:30
  339.6 62.2 %collective-permute-start.90 = (bf16[128,2048]{1,0:T(8,128)(2,1)S(1)}, bf16[128,2048]{1,0:T(8,128)(2,1)}, u32[]{:S(2)}, u32[]{:S(2)}) collective-permute-start(bf16[128,2048]{1,0:T(8,128)(2,1)S(1)} %get-tuple-element.281.refs_3_), channel_id=1, source_target_pairs={{0,1},{1,0},{2,3},{3,2},{4,5},{5,4},{6,7},{7,6},{8,9},{9,8},{10,11... | collective-permute-start | bytes 1572872 | tf_op jit(solution)/shard_map/branch_rows/ppermute | solution.py:30
  339.6 16.2 %collective-permute-start.80 = (bf16[128,2048]{1,0:T(8,128)(2,1)S(1)}, bf16[128,2048]{1,0:T(8,128)(2,1)}, u32[]{:S(2)}, u32[]{:S(2)}) collective-permute-start(bf16[128,2048]{1,0:T(8,128)(2,1)S(1)} %get-tuple-element.281.refs_3_), channel_id=1, source_target_pairs={{0,8},{8,16},{16,24},{24,0},{1,9},{9,17},{17,25},{25,1},{2,10},{10... | collective-permute-start | bytes 1572872 | tf_op jit(solution)/shard_map/branch_rows/ppermute | solution.py:30
  355.8 17.5 %collective-permute-start.93 = (bf16[128,2048]{1,0:T(8,128)(2,1)}, bf16[128,2048]{1,0:T(8,128)(2,1)}, u32[]{:S(2)}, u32[]{:S(2)}) collective-permute-start(bf16[128,2048]{1,0:T(8,128)(2,1)} %pad_maximum_fusion.8), channel_id=1, source_target_pairs={{0,2},{2,0},{1,3},{3,1},{4,6},{6,4},{5,7},{7,5},{8,10},{10,8},{9,1... | collective-permute-start | bytes 1572872 | tf_op jit(solution)/shard_map/branch_rows/ppermute | solution.py:30
  356.7 16.6 %collective-permute-start.92 = (bf16[144,2048]{1,0:T(8,128)(2,1)}, bf16[144,2048]{1,0:T(8,128)(2,1)}, u32[]{:S(2)}, u32[]{:S(2)}) collective-permute-start(bf16[144,2048]{1,0:T(8,128)(2,1)} %get-tuple-element.245), channel_id=1, source_target_pairs={{0,4},{4,0},{1,5},{5,1},{2,6},{6,2},{3,7},{7,3},{8,12},{12,8},{9,1... | collective-permute-start | bytes 1769480 | tf_op jit(solution)/shard_map/branch_rows/ppermute | solution.py:30
  360.9 41.9 %collective-permute-start.87 = (bf16[128,2048]{1,0:T(8,128)(2,1)}, bf16[128,2048]{1,0:T(8,128)(2,1)}, u32[]{:S(2)}, u32[]{:S(2)}) collective-permute-start(bf16[128,2048]{1,0:T(8,128)(2,1)} %collective-permute-done.80.refs_0_), channel_id=1, source_target_pairs={{0,1},{1,0},{2,3},{3,2},{4,5},{5,4},{6,7},{7,6},{8,9},{9,8},{10,11... | collective-permute-start | bytes 1572872 | tf_op jit(solution)/shard_map/branch_rows/ppermute | solution.py:30
  381.3 22.6 %collective-permute-start.88 = (bf16[128,2048]{1,0:T(8,128)(2,1)}, bf16[128,2048]{1,0:T(8,128)(2,1)}, u32[]{:S(2)}, u32[]{:S(2)}) collective-permute-start(bf16[128,2048]{1,0:T(8,128)(2,1)} %collective-permute-done.83.refs_1_), channel_id=1, source_target_pairs={{0,1},{1,0},{2,3},{3,2},{4,5},{5,4},{6,7},{7,6},{8,9},{9,8},{10,11... | collective-permute-start | bytes 1572872 | tf_op jit(solution)/shard_map/branch_rows/ppermute | solution.py:30
  388.4 16.4 %collective-permute-start.89 = (bf16[128,2048]{1,0:T(8,128)(2,1)}, bf16[128,2048]{1,0:T(8,128)(2,1)}, u32[]{:S(2)}, u32[]{:S(2)}) collective-permute-start(bf16[128,2048]{1,0:T(8,128)(2,1)} %collective-permute-done.86.refs_2_), channel_id=1, source_target_pairs={{0,1},{1,0},{2,3},{3,2},{4,5},{5,4},{6,7},{7,6},{8,9},{9,8},{10,11... | collective-permute-start | bytes 1572872 | tf_op jit(solution)/shard_map/branch_rows/ppermute | solution.py:30
  400.7 34.8 %collective-permute-start.98 = (bf16[128,2048]{1,0:T(8,128)(2,1)}, bf16[128,2048]{1,0:T(8,128)(2,1)S(1)}, u32[]{:S(2)}, u32[]{:S(2)}) collective-permute-start(bf16[128,2048]{1,0:T(8,128)(2,1)} %add_convert_fusion.16), channel_id=1, source_target_pairs={{0,4},{4,0},{1,5},{5,1},{2,6},{6,2},{3,7},{7,3},{8,12},{12,8},{9,1... | collective-permute-start | bytes 1572872 | tf_op jit(solution)/shard_map/unit_weight_sums/ppermute | solution.py:30
  401.7 33.8 %collective-permute-start.99 = (bf16[128,2048]{1,0:T(8,128)(2,1)}, bf16[128,2048]{1,0:T(8,128)(2,1)}, u32[]{:S(2)}, u32[]{:S(2)}) collective-permute-start(bf16[128,2048]{1,0:T(8,128)(2,1)} %add_convert_fusion.15), channel_id=1, source_target_pairs={{0,2},{2,0},{1,3},{3,1},{4,6},{6,4},{5,7},{7,5},{8,10},{10,8},{9,1... | collective-permute-start | bytes 1572872 | tf_op jit(solution)/shard_map/unit_weight_sums/ppermute | solution.py:30
  402.8 32.7 %collective-permute-start.100 = (bf16[128,2048]{1,0:T(8,128)(2,1)}, bf16[128,2048]{1,0:T(8,128)(2,1)S(1)}, u32[]{:S(2)}, u32[]{:S(2)}) collective-permute-start(bf16[128,2048]{1,0:T(8,128)(2,1)} %add_convert_fusion.14), channel_id=1, source_target_pairs={{0,4},{4,0},{1,5},{5,1},{2,6},{6,2},{3,7},{7,3},{8,12},{12,8},{9,1... | collective-permute-start | bytes 1572872 | tf_op jit(solution)/shard_map/unit_weight_sums/ppermute | solution.py:30
  403.8 33.3 %collective-permute-start.101 = (bf16[144,2048]{1,0:T(8,128)(2,1)S(1)}, bf16[144,2048]{1,0:T(8,128)(2,1)S(1)}, u32[]{:S(2)}, u32[]{:S(2)}) collective-permute-start(bf16[144,2048]{1,0:T(8,128)(2,1)S(1)} %add_convert_fusion.2), channel_id=1, source_target_pairs={{0,2},{2,0},{1,3},{3,1},{4,6},{6,4},{5,7},{7,5},{8,10},{10,8},{9,1... | collective-permute-start | bytes 1769480 | tf_op jit(solution)/shard_map/unit_weight_sums/ppermute | solution.py:30
  437.1 38.2 %collective-permute-start.105 = (bf16[2048,256]{1,0:T(8,128)(2,1)S(1)}, bf16[2048,256]{1,0:T(8,128)(2,1)S(1)}, u32[]{:S(2)}, u32[]{:S(2)}) collective-permute-start(bf16[2048,256]{1,0:T(8,128)(2,1)S(1)} %pad_maximum_fusion.3), channel_id=1, source_target_pairs={{0,2},{2,0},{1,3},{3,1},{4,6},{6,4},{5,7},{7,5},{8,10},{10,8},{9,1... | collective-permute-start | bytes 3145736 | tf_op jit(solution)/shard_map/normed_sum/ppermute | solution.py:30
  442.1 33.4 %collective-permute-start.104 = (bf16[2048,256]{1,0:T(8,128)(2,1)S(1)}, bf16[2048,256]{1,0:T(8,128)(2,1)S(1)}, u32[]{:S(2)}, u32[]{:S(2)}) collective-permute-start(bf16[2048,256]{1,0:T(8,128)(2,1)S(1)} %pad_maximum_fusion.2), channel_id=1, source_target_pairs={{0,4},{4,0},{1,5},{5,1},{2,6},{6,2},{3,7},{7,3},{8,12},{12,8},{9,1... | collective-permute-start | bytes 3145736 | tf_op jit(solution)/shard_map/normed_sum/ppermute | solution.py:30
  479.1 17.3 %collective-permute-start.106 = (bf16[128,2048]{1,0:T(8,128)(2,1)S(1)}, bf16[128,2048]{1,0:T(8,128)(2,1)S(1)}, u32[]{:S(2)}, u32[]{:S(2)}) collective-permute-start(bf16[128,2048]{1,0:T(8,128)(2,1)S(1)} %convolution_convert_fusion.7), channel_id=1, source_target_pairs={{0,1},{1,0},{2,3},{3,2},{4,5},{5,4},{6,7},{7,6},{8,9},{9,8},{10,11... | collective-permute-start | bytes 1572872 | tf_op jit(solution)/shard_map/normed_sum/ppermute | solution.py:30
  493.0 22.5 %collective-permute-start.116 = (bf16[512,512]{0,1:T(8,128)(2,1)}, bf16[512,512]{0,1:T(8,128)(2,1)}, u32[]{:S(2)}, u32[]{:S(2)}) collective-permute-start(bf16[512,512]{0,1:T(8,128)(2,1)} %pad_maximum_fusion.11), channel_id=1, source_target_pairs={{0,2},{2,0},{1,3},{3,1},{4,6},{6,4},{5,7},{7,5},{8,10},{10,8},{9,1... | collective-permute-start | bytes 1572872 | tf_op jit(solution)/shard_map/shared_sum/ppermute | solution.py:30
  494.7 20.8 %collective-permute-start.115 = (bf16[512,512]{0,1:T(8,128)(2,1)}, bf16[512,512]{0,1:T(8,128)(2,1)}, u32[]{:S(2)}, u32[]{:S(2)}) collective-permute-start(bf16[512,512]{0,1:T(8,128)(2,1)} %pad_maximum_fusion.10), channel_id=1, source_target_pairs={{0,4},{4,0},{1,5},{5,1},{2,6},{6,2},{3,7},{7,3},{8,12},{12,8},{9,1... | collective-permute-start | bytes 1572872 | tf_op jit(solution)/shard_map/shared_sum/ppermute | solution.py:30
  531.2 21.5 %collective-permute-start.118 = (bf16[128,2048]{1,0:T(8,128)(2,1)S(1)}, bf16[128,2048]{1,0:T(8,128)(2,1)S(1)}, u32[]{:S(2)}, u32[]{:S(2)}) collective-permute-start(bf16[128,2048]{1,0:T(8,128)(2,1)S(1)} %add_convert_fusion.9), channel_id=1, source_target_pairs={{0,8},{8,16},{16,24},{24,0},{1,9},{9,17},{17,25},{25,1},{2,10},{10... | collective-permute-start | bytes 1572872 | tf_op jit(solution)/shard_map/shared_sum/ppermute | solution.py:30
  531.3 18.7 %collective-permute-start.121 = (bf16[256,512]{0,1:T(8,128)(2,1)S(1)}, bf16[256,512]{0,1:T(8,128)(2,1)S(1)}, u32[]{:S(2)}, u32[]{:S(2)}) collective-permute-start(bf16[256,512]{0,1:T(8,128)(2,1)S(1)} %get-tuple-element.294), channel_id=1, source_target_pairs={{0,4},{4,0},{1,5},{5,1},{2,6},{6,2},{3,7},{7,3},{8,12},{12,8},{9,1... | collective-permute-start | bytes 786440 | tf_op jit(solution)/shard_map/shared_sum/ppermute | solution.py:30
  531.7 19.2 %collective-permute-start.122 = (bf16[256,512]{0,1:T(8,128)(2,1)S(1)}, bf16[256,512]{0,1:T(8,128)(2,1)S(1)}, u32[]{:S(2)}, u32[]{:S(2)}) collective-permute-start(bf16[256,512]{0,1:T(8,128)(2,1)S(1)} %get-tuple-element.296), channel_id=1, source_target_pairs={{0,2},{2,0},{1,3},{3,1},{4,6},{6,4},{5,7},{7,5},{8,10},{10,8},{9,1... | collective-permute-start | bytes 786440 | tf_op jit(solution)/shard_map/shared_sum/ppermute | solution.py:30
  544.7 20.9 %collective-permute-start.128 = (bf16[256,512]{0,1:T(8,128)(2,1)S(1)}, bf16[256,512]{0,1:T(8,128)(2,1)S(1)}, u32[]{:S(2)}, u32[]{:S(2)}) collective-permute-start(bf16[256,512]{0,1:T(8,128)(2,1)S(1)} %broadcast_select_fusion.1), channel_id=1, source_target_pairs={{0,20},{1,0},{2,28},{3,8},{4,4},{5,16},{6,12},{7,24},{8,29},{9,9},... | collective-permute-start | bytes 786440 | tf_op jit(solution)/shard_map/weight_layout/ppermute | solution.py:843
  554.0 26.8 %collective-permute-start.123 = (bf16[256,512]{0,1:T(8,128)(2,1)}, bf16[256,512]{0,1:T(8,128)(2,1)S(1)}, u32[]{:S(2)}, u32[]{:S(2)}) collective-permute-start(bf16[256,512]{0,1:T(8,128)(2,1)} %get-tuple-element.458), channel_id=1, source_target_pairs={{0,0},{1,20},{2,8},{3,28},{4,16},{5,4},{6,24},{7,12},{8,9},{9,29},... | collective-permute-start | bytes 786440 | tf_op jit(solution)/shard_map/weight_layout/ppermute | solution.py:843
  555.6 25.2 %collective-permute-start.124 = (bf16[256,512]{0,1:T(8,128)(2,1)}, bf16[256,512]{0,1:T(8,128)(2,1)}, u32[]{:S(2)}, u32[]{:S(2)}) collective-permute-start(bf16[256,512]{0,1:T(8,128)(2,1)} %get-tuple-element.459), channel_id=1, source_target_pairs={{0,20},{1,0},{2,28},{3,8},{4,4},{5,16},{6,12},{7,24},{8,29},{9,9},... | collective-permute-start | bytes 786440 | tf_op jit(solution)/shard_map/weight_layout/ppermute | solution.py:843
  (166 other events, 1797.6 us)
Sparse Core Ops, SparseCore 0:
  392.0 47.6 reduce-scatter.1
